TPU v7x, 128 devices: a whole 4x4x4 slice. The times are simulated.
128 devices in a mesh: ctx: 32 (over x, z_hi, y), fsdp: 4 (over z_lo, core).
Axes of the slice: x: 4, y: 4, z: 4 (z_hi: 2, z_lo: 2; z = z_hi * 2 + z_lo), core: 2. Of those that a mesh axis runs over, the one named last changes fastest.
Arguments:
- layer_input: bfloat16 [4, 32, 1, 2, 64, 1024], P('fsdp', 'ctx'), may hold values from -6 to 6
- routes: int32 [4, 32, 1, 2, 64, 8], P('fsdp', 'ctx'), may hold values from 0 to 31, all different within a row; in each aligned block of 128 rows (0 to 127, 128 to 255, ..., all dimensions but the last counted through in order) at most 64 rows name the same one
- gates: float32 [4, 32, 1, 2, 64, 8], P('fsdp', 'ctx'), may hold values from 0.1 to 0.3
- cotangent: bfloat16 [4, 32, 1, 2, 64, 1024], P('fsdp', 'ctx'), may hold values from -6 to 6
- norm_attn: float32 [1024], P(('ctx', 'fsdp')), may hold values from 0.5 to 1.5
- query_key_value_weight: float32 [1024, 2048], P(('ctx', 'fsdp')), may hold values from -0.1875 to 0.1875
- output_weight: float32 [1024, 1024], P(('ctx', 'fsdp')), may hold values from -6 to 6
- norm_ffn: float32 [1024], P(('ctx', 'fsdp')), may hold values from 0.5 to 1.5
- exp_gate: float32 [32, 1024, 512], P('ctx', 'fsdp'), may hold values from -0.1875 to 0.1875
- exp_up: float32 [32, 1024, 512], P('ctx', 'fsdp'), may hold values from -0.1875 to 0.1875
- exp_down: float32 [32, 512, 1024], P('ctx', 'fsdp'), may hold values from -0.5 to 0.5
Outputs:
- layer_output: bfloat16 [4, 32, 1, 2, 64, 1024], P('fsdp', 'ctx')
- input_grad: float32 [4, 32, 1, 2, 64, 1024], P('fsdp', 'ctx')
- grad_norm_attn: float32 [1024], P(('ctx', 'fsdp'))
- grad_w_qkv: float32 [1024, 2048], P(('ctx', 'fsdp'))
- grad_w_out: float32 [1024, 1024], P(('ctx', 'fsdp'))
- grad_norm_ffn: float32 [1024], P(('ctx', 'fsdp'))
- grad_exp_gate: float32 [32, 1024, 512], P('ctx', 'fsdp')
- grad_exp_up: float32 [32, 1024, 512], P('ctx', 'fsdp')
- grad_exp_down: float32 [32, 512, 1024], P('ctx', 'fsdp')
Inputs may be any that keep to these rules, and one draw needn't show every extreme that they name: `routes`: each token names 8 different experts. In the rows of one device (the entries that share f and c), no expert is named more than 64 times, a bound that some block reaches.
All inputs are finite; a program needn't handle non-finite values.
Results may differ from a plain program's by a relative error of at most 0.024.
Values may be sent and summed in bfloat16 or wider, within the bound.
No kernel may reach another device: no remote copies, remote signals or barrier semaphores. Data moves between devices by JAX's collectives and lax.ppermute only.
A program may use at most 192 MiB of HBM per device.

v0:
```python
import jax
import jax.numpy as jnp
from jax import lax
from jax.sharding import PartitionSpec as P

HEADS = 16
KV_HEADS = 8
HEAD_DIM = 64


EPSILON = 1e-06
ROPE_BASE = 10000.0
MASKED = -1e30


def for_sending(value):
    return jax.tree.map(lambda a: a.astype(jnp.bfloat16) if a.dtype == jnp.float32 else a, value)


def rope_tables(positions, width):
    half = width // 2
    frequency = ROPE_BASE ** (-(jnp.arange(half, dtype=jnp.float32) * 2.0 / width))
    angle = positions.astype(jnp.float32)[:, None] * frequency[None, :]
    return (jnp.cos(angle), jnp.sin(angle))


def rotate(values, cosine, sine):
    half = values.shape[-1] // 2
    first = values[..., :half]
    second = values[..., half:]
    cosine = cosine[:, None, :]
    sine = sine[:, None, :]
    return jnp.concatenate(
        [first * cosine - second * sine, second * cosine + first * sine], axis=-1
    )


def unrotate(grads, cosine, sine):
    half = grads.shape[-1] // 2
    first = grads[..., :half]
    second = grads[..., half:]
    cosine = cosine[:, None, :]
    sine = sine[:, None, :]
    return jnp.concatenate(
        [first * cosine + second * sine, second * cosine - first * sine], axis=-1
    )


def block_positions(first, count, ctx_count, block_len):
    device = first + jnp.arange(count, dtype=jnp.int32)
    offset = jnp.arange(block_len, dtype=jnp.int32)
    front = device[:, None] * block_len + offset[None, :]
    back = (2 * ctx_count - 1 - device)[:, None] * block_len + offset[None, :]
    return jnp.stack([front, back], axis=1).reshape(-1)


def scores_of(queries, keys, query_pos, key_pos):
    count, heads, size = queries.shape
    kv_heads = keys.shape[1]
    grouped = queries.reshape(count, kv_heads, heads // kv_heads, size)
    raw_scores = jnp.einsum(
        "qkgd,tkd->kgqt", grouped, keys, preferred_element_type=jnp.float32
    ) * size ** (-0.5)
    causal = key_pos[None, :] <= query_pos[:, None]
    return (jnp.where(causal[None, None], raw_scores, MASKED), grouped)


def split_pairs(pairs):
    count, both = pairs.shape
    half = both // 2
    keys = pairs[:, :half].reshape(count, KV_HEADS, half // KV_HEADS)
    values = pairs[:, half:].reshape(count, KV_HEADS, half // KV_HEADS)
    return (keys, values)


def key_blocks(pairs, key_pos):
    total = pairs.shape[0]
    key_block = min(512, total)
    number = total // key_block
    return (pairs.reshape(number, key_block, pairs.shape[1]), key_pos.reshape(number, key_block))


def attend_forward(queries, pairs, query_pos, key_pos):
    count, heads, size = queries.shape
    groups = heads // KV_HEADS
    blocks, positions = key_blocks(pairs, key_pos)

    def stat_step(carry, item):
        peak, total = carry
        keys, values = split_pairs(item[0])
        scores, grouped = scores_of(queries, keys, query_pos, item[1])
        new_peak = jnp.maximum(peak, jnp.max(scores, axis=-1))
        total = total * jnp.exp(peak - new_peak) + jnp.sum(
            jnp.exp(scores - new_peak[..., None]), axis=-1
        )
        return ((new_peak, total), None)

    start_peak = jnp.full((KV_HEADS, groups, count), MASKED, jnp.float32)
    start_total = jnp.zeros((KV_HEADS, groups, count), jnp.float32)
    (peak, total), _ = lax.scan(stat_step, (start_peak, start_total), (blocks, positions))
    log_total = peak + jnp.log(total)

    def mix_step(running, item):
        keys, values = split_pairs(item[0])
        scores, grouped = scores_of(queries, keys, query_pos, item[1])
        weights = jnp.exp(scores - log_total[..., None]).astype(jnp.bfloat16)
        return (
            running
            + jnp.einsum("kgqt,tkd->qkgd", weights, values, preferred_element_type=jnp.float32),
            None,
        )

    start_mix = jnp.zeros((count, KV_HEADS, groups, size), jnp.float32)
    mixed, _ = lax.scan(mix_step, start_mix, (blocks, positions))
    return (mixed.reshape(count, -1), log_total)


def attend_backward(queries, pairs, query_pos, key_pos, log_total, out_grad, delta):
    keys, values = split_pairs(pairs)
    scores, grouped = scores_of(queries, keys, query_pos, key_pos)
    weights = jnp.exp(scores - log_total[..., None])
    grad_grouped = out_grad.reshape(grouped.shape)
    weight_grad = jnp.einsum(
        "qkgd,tkd->kgqt", grad_grouped, values, preferred_element_type=jnp.float32
    )
    score_grad = (weights * (weight_grad - delta[..., None])).astype(jnp.bfloat16)
    return (weights, score_grad, keys, grouped, grad_grouped, delta)


def query_grads(score_grad, keys, scale):
    mixed = (
        jnp.einsum("kgqt,tkd->qkgd", score_grad, keys, preferred_element_type=jnp.float32) * scale
    )
    return mixed.reshape(mixed.shape[0], -1)


def pair_grads(weights, score_grad, grouped, grad_grouped, scale):
    key_grad = (
        jnp.einsum("kgqt,qkgd->tkd", score_grad, grouped, preferred_element_type=jnp.float32)
        * scale
    )
    value_grad = jnp.einsum(
        "kgqt,qkgd->tkd",
        weights.astype(jnp.bfloat16),
        grad_grouped,
        preferred_element_type=jnp.float32,
    )
    count = key_grad.shape[0]
    return jnp.concatenate([key_grad.reshape(count, -1), value_grad.reshape(count, -1)], axis=-1)


def backward_blocks(queries, pairs, query_pos, key_pos, log_total, out_grad, scale):
    count, heads, size = queries.shape
    groups = heads // KV_HEADS
    blocks, positions = key_blocks(pairs, key_pos)
    grad_grouped = out_grad.reshape(count, KV_HEADS, groups, size)

    def delta_step(running, item):
        keys, values = split_pairs(item[0])
        scores, grouped = scores_of(queries, keys, query_pos, item[1])
        weights = jnp.exp(scores - log_total[..., None])
        weight_grad = jnp.einsum(
            "qkgd,tkd->kgqt", grad_grouped, values, preferred_element_type=jnp.float32
        )
        return (running + jnp.sum(weights * weight_grad, axis=-1), None)

    delta, _ = lax.scan(
        delta_step, jnp.zeros((KV_HEADS, groups, count), jnp.float32), (blocks, positions)
    )

    def grad_step(running, item):
        outcome = attend_backward(queries, item[0], query_pos, item[1], log_total, out_grad, delta)
        running = running + query_grads(outcome[1], outcome[2], scale)
        return (running, pair_grads(outcome[0], outcome[1], outcome[3], outcome[4], scale))

    query_grad, pair_blocks = lax.scan(
        grad_step, jnp.zeros((count, heads * size), jnp.float32), (blocks, positions)
    )
    return (query_grad, pair_blocks.reshape(pairs.shape[0], -1), delta)


def on_device(
    layer_input,
    routes,
    gates,
    cotangent,
    norm_attn,
    query_key_value_weight,
    output_weight,
    norm_ffn,
    exp_gate,
    exp_up,
    exp_down,
):
    ctx_count = lax.axis_size("ctx")
    ctx_index = lax.axis_index("ctx")
    seqs = layer_input.shape[2]
    block_len = layer_input.shape[4]
    width = layer_input.shape[5]
    kv_width = KV_HEADS * HEAD_DIM
    per_seq = 2 * block_len
    token_rows = seqs * per_seq
    top_count = routes.shape[-1]
    scale = HEAD_DIM ** (-0.5)
    x_rows = layer_input.reshape(token_rows, width).astype(jnp.float32)

    def attn_masters():
        return (
            query_key_value_weight.astype(jnp.bfloat16),
            output_weight.astype(jnp.bfloat16),
            norm_attn.astype(jnp.bfloat16),
            norm_ffn.astype(jnp.bfloat16),
        )

    w_qkv_b, w_out_b, gain_attn, gain_ffn = lax.all_gather(
        for_sending(attn_masters()), ("ctx", "fsdp"), axis=0, tiled=True
    )
    scale_attn = lax.rsqrt(jnp.mean(x_rows * x_rows, axis=-1, keepdims=True) + EPSILON)
    normed_attn = x_rows * scale_attn
    attention_hidden = (normed_attn * gain_attn.astype(jnp.float32)).astype(jnp.bfloat16)
    projected_rows = jnp.dot(attention_hidden, w_qkv_b, preferred_element_type=jnp.float32)
    query_pos = block_positions(ctx_index, 1, ctx_count, block_len)
    key_pos = block_positions(0, ctx_count, ctx_count, block_len)
    cosine, sine = rope_tables(query_pos, HEAD_DIM)
    cosine = jnp.tile(cosine, (seqs, 1))
    sine = jnp.tile(sine, (seqs, 1))
    queries = rotate(
        projected_rows[:, :width].reshape(token_rows, HEADS, HEAD_DIM), cosine, sine
    ).astype(jnp.bfloat16)
    keys_rot = rotate(
        projected_rows[:, width : width + kv_width].reshape(token_rows, KV_HEADS, HEAD_DIM),
        cosine,
        sine,
    ).astype(jnp.bfloat16)
    pairs_local = jnp.concatenate(
        [
            keys_rot.reshape(token_rows, kv_width),
            projected_rows[:, width + kv_width :].astype(jnp.bfloat16),
        ],
        axis=-1,
    )
    pairs_all = lax.all_gather(
        pairs_local.reshape(1, seqs, per_seq, 2 * kv_width), "ctx", axis=0, tiled=True
    )
    pairs_seq = jnp.swapaxes(pairs_all, 0, 1).reshape(seqs, ctx_count * per_seq, 2 * kv_width)
    query_seq = queries.reshape(seqs, per_seq, HEADS, HEAD_DIM)

    def forward_one(item):
        return attend_forward(item[0], item[1], query_pos, key_pos)

    attn_seq, log_seq = lax.map(forward_one, (query_seq, pairs_seq))
    attention_reduced = attn_seq.reshape(token_rows, width).astype(jnp.bfloat16)
    middle_output = x_rows + jnp.dot(attention_reduced, w_out_b, preferred_element_type=jnp.float32)
    scale_ffn = lax.rsqrt(jnp.mean(middle_output * middle_output, axis=-1, keepdims=True) + EPSILON)
    normed_ffn = middle_output * scale_ffn
    hidden_ffn = (normed_ffn * gain_ffn.astype(jnp.float32)).astype(jnp.bfloat16)
    local_experts = exp_gate.shape[0]
    expert_count = local_experts * ctx_count
    capacity = min(token_rows, 2 * token_rows * top_count // expert_count)
    picks = routes.reshape(token_rows * top_count)
    one_hot = (picks[:, None] == jnp.arange(expert_count, dtype=jnp.int32)[None, :]).astype(
        jnp.int32
    )
    earlier = jnp.cumsum(one_hot, axis=0) - one_hot
    rank = jnp.sum(earlier * one_hot, axis=1)
    target = picks * capacity + rank
    owner = jnp.arange(token_rows * top_count, dtype=jnp.int32) // top_count
    slot_weights = gates.reshape(token_rows, top_count)

    def to_experts(slot_rows):
        buffer = jnp.zeros((expert_count * capacity, width), jnp.bfloat16).at[target].set(slot_rows)
        return buffer.reshape(expert_count, capacity, width)

    def owner_layout(arrived):
        grouped = arrived.reshape(ctx_count, local_experts, capacity, width)
        return jnp.swapaxes(grouped, 0, 1).reshape(local_experts, ctx_count * capacity, width)

    def source_layout(result):
        grouped = result.reshape(local_experts, ctx_count, capacity, width)
        return jnp.swapaxes(grouped, 0, 1).reshape(expert_count, capacity, width)

    def to_tokens(returned):
        return (
            returned.reshape(expert_count * capacity, width)[target]
            .astype(jnp.float32)
            .reshape(token_rows, top_count, width)
        )

    slot_input = owner_layout(
        lax.all_to_all(
            to_experts(hidden_ffn[owner]), "ctx", split_axis=0, concat_axis=0, tiled=True
        )
    )
    gate_full, up_full, down_full = (
        lax.all_gather(exp_gate.astype(jnp.bfloat16), "fsdp", axis=1, tiled=True),
        lax.all_gather(exp_up.astype(jnp.bfloat16), "fsdp", axis=1, tiled=True),
        lax.all_gather(exp_down.astype(jnp.bfloat16), "fsdp", axis=1, tiled=True),
    )
    gate_hidden = jnp.einsum(
        "end,edf->enf", slot_input, gate_full, preferred_element_type=jnp.float32
    )
    up_hidden = jnp.einsum("end,edf->enf", slot_input, up_full, preferred_element_type=jnp.float32)
    sigmoid_gate = jax.nn.sigmoid(gate_hidden)
    swished = gate_hidden * sigmoid_gate
    activated = (swished * up_hidden).astype(jnp.bfloat16)
    slot_out = jnp.einsum(
        "enf,efd->end", activated, down_full, preferred_element_type=jnp.float32
    ).astype(jnp.bfloat16)
    returned = lax.all_to_all(
        source_layout(slot_out), "ctx", split_axis=0, concat_axis=0, tiled=True
    )
    moe = jnp.sum(to_tokens(returned) * slot_weights[..., None], axis=1)
    layer_output = (middle_output + moe).astype(jnp.bfloat16).reshape(layer_input.shape)
    grad_out = cotangent.reshape(token_rows, width).astype(jnp.float32)
    slot_grads = (
        (slot_weights[..., None] * grad_out[:, None, :])
        .reshape(token_rows * top_count, width)
        .astype(jnp.bfloat16)
    )
    slot_grad_in = owner_layout(
        lax.all_to_all(to_experts(slot_grads), "ctx", split_axis=0, concat_axis=0, tiled=True)
    )
    act_grad = jnp.einsum(
        "end,efd->enf", slot_grad_in, down_full, preferred_element_type=jnp.float32
    )
    grad_down_local = jnp.einsum(
        "enf,end->efd", activated, slot_grad_in, preferred_element_type=jnp.float32
    )
    gate_grad = (
        act_grad * up_hidden * sigmoid_gate * (1.0 + gate_hidden * (1.0 - sigmoid_gate))
    ).astype(jnp.bfloat16)
    up_grad = (act_grad * swished).astype(jnp.bfloat16)
    grad_gate_local = jnp.einsum(
        "end,enf->edf", slot_input, gate_grad, preferred_element_type=jnp.float32
    )
    grad_up_local = jnp.einsum(
        "end,enf->edf", slot_input, up_grad, preferred_element_type=jnp.float32
    )
    input_slot = jnp.einsum(
        "enf,edf->end", gate_grad, gate_full, preferred_element_type=jnp.float32
    )
    input_slot = (
        input_slot
        + jnp.einsum("enf,edf->end", up_grad, up_full, preferred_element_type=jnp.float32)
    ).astype(jnp.bfloat16)
    came_back = lax.all_to_all(
        source_layout(input_slot), "ctx", split_axis=0, concat_axis=0, tiled=True
    )
    hidden_grad = jnp.sum(to_tokens(came_back), axis=1)
    grad_exp_gate, grad_exp_up, grad_exp_down = (
        lax.psum_scatter(
            grad_gate_local.astype(jnp.bfloat16), "fsdp", scatter_dimension=1, tiled=True
        ).astype(jnp.float32),
        lax.psum_scatter(
            grad_up_local.astype(jnp.bfloat16), "fsdp", scatter_dimension=1, tiled=True
        ).astype(jnp.float32),
        lax.psum_scatter(
            grad_down_local.astype(jnp.bfloat16), "fsdp", scatter_dimension=1, tiled=True
        ).astype(jnp.float32),
    )
    grad_gain_ffn = jnp.sum(hidden_grad * normed_ffn, axis=0)
    normed_grad = hidden_grad * gain_ffn.astype(jnp.float32)
    mid_grad = (
        grad_out
        + scale_ffn * normed_grad
        - middle_output
        * scale_ffn**3
        * jnp.mean(normed_grad * middle_output, axis=-1, keepdims=True)
    )
    w_qkv_b, w_out_b, gain_attn, gain_ffn = lax.all_gather(
        for_sending(attn_masters()), ("ctx", "fsdp"), axis=0, tiled=True
    )
    branch_grad = mid_grad.astype(jnp.bfloat16)
    grad_w_out = jnp.einsum(
        "rd,re->de", attention_reduced, branch_grad, preferred_element_type=jnp.float32
    )
    out_grad = lax.dot_general(
        branch_grad, w_out_b, (((1,), (1,)), ((), ())), preferred_element_type=jnp.float32
    ).astype(jnp.bfloat16)
    out_seq = out_grad.reshape(seqs, per_seq, HEADS, HEAD_DIM)

    def backward_one(item):
        outcome = backward_blocks(item[0], item[1], query_pos, key_pos, item[2], item[3], scale)
        return (outcome[0], outcome[1])

    query_grad, pair_grad = lax.map(backward_one, (query_seq, pairs_seq, log_seq, out_seq))
    pair_terms = jnp.swapaxes(pair_grad.reshape(seqs, ctx_count, per_seq, 2 * kv_width), 0, 1)
    pair_own = (
        lax.psum_scatter(pair_terms.astype(jnp.bfloat16), "ctx", scatter_dimension=0, tiled=True)
        .astype(jnp.float32)
        .reshape(token_rows, 2 * kv_width)
    )
    query_rows_grad = query_grad.reshape(token_rows, HEADS, HEAD_DIM)
    key_rows_grad = pair_own[:, :kv_width].reshape(token_rows, KV_HEADS, HEAD_DIM)
    proj_grad = jnp.concatenate(
        [
            unrotate(query_rows_grad, cosine, sine).reshape(token_rows, width),
            unrotate(key_rows_grad, cosine, sine).reshape(token_rows, kv_width),
            pair_own[:, kv_width:],
        ],
        axis=-1,
    ).astype(jnp.bfloat16)
    grad_w_qkv = jnp.einsum(
        "rd,re->de", attention_hidden, proj_grad, preferred_element_type=jnp.float32
    )
    hidden_grad_attn = lax.dot_general(
        proj_grad, w_qkv_b, (((1,), (1,)), ((), ())), preferred_element_type=jnp.float32
    )
    grad_gain_attn = jnp.sum(hidden_grad_attn * normed_attn, axis=0)
    normed_grad_attn = hidden_grad_attn * gain_attn.astype(jnp.float32)
    input_grad = (
        mid_grad
        + scale_attn * normed_grad_attn
        - x_rows * scale_attn**3 * jnp.mean(normed_grad_attn * x_rows, axis=-1, keepdims=True)
    )
    grad_qkv_own, grad_out_own, grad_norm_attn, grad_norm_ffn = (
        lax.psum_scatter(grad_w_qkv, ("ctx", "fsdp"), scatter_dimension=0, tiled=True),
        lax.psum_scatter(grad_w_out, ("ctx", "fsdp"), scatter_dimension=0, tiled=True),
        lax.psum_scatter(grad_gain_attn, ("ctx", "fsdp"), scatter_dimension=0, tiled=True),
        lax.psum_scatter(grad_gain_ffn, ("ctx", "fsdp"), scatter_dimension=0, tiled=True),
    )
    return (
        layer_output,
        input_grad.reshape(layer_input.shape),
        grad_norm_attn,
        grad_qkv_own,
        grad_out_own,
        grad_norm_ffn,
        grad_exp_gate,
        grad_exp_up,
        grad_exp_down,
    )


def solution(mesh):
    in_specs = (
        P("fsdp", "ctx", None, None, None, None),
        P("fsdp", "ctx", None, None, None, None),
        P("fsdp", "ctx", None, None, None, None),
        P("fsdp", "ctx", None, None, None, None),
        P(("ctx", "fsdp")),
        P(("ctx", "fsdp"), None),
        P(("ctx", "fsdp"), None),
        P(("ctx", "fsdp")),
        P("ctx", "fsdp", None),
        P("ctx", "fsdp", None),
        P("ctx", "fsdp", None),
    )
    out_specs = (
        P("fsdp", "ctx", None, None, None, None),
        P("fsdp", "ctx", None, None, None, None),
        P(("ctx", "fsdp")),
        P(("ctx", "fsdp"), None),
        P(("ctx", "fsdp"), None),
        P(("ctx", "fsdp")),
        P("ctx", "fsdp", None),
        P("ctx", "fsdp", None),
        P("ctx", "fsdp", None),
    )
    return jax.shard_map(
        on_device, mesh=mesh, in_specs=in_specs, out_specs=out_specs, check_vma=False
    )
```

profile of v0, /device:TPU:1, one launch (start us, length us, event | category | flops | bytes accessed | tf_op | source)
XLA Modules:
  0.0 2536.7 jit_solution(17529047592162189228)
XLA Ops:
  12.6 68.7 %all-reduce.5 = (bf16[1024]{0:T(1024)(128)(2,1)S(1)}, bf16[1024]{0:T(1024)(128)(2,1)S(1)}) all-reduce(bf16[1024]{0:T(1024)(128)(2,1)S(1)} %dynamic-update-slice, bf16[1024]{0:T(1024)(128)(2,1)S(1)} %dynamic-update-slice.1), channel_id=1, replica_groups=mesh['ctx'=32,'fsdp'=4] {'ctx','fsdp'}, use_global_device_ids=true, to_apply=%add | all-reduce | flops 2048 | bytes 8192
  83.1 128.9 %all-gather.8.cloned.1.call-done = bf16[1024,2048]{1,0:T(8,128)(2,1)} async-done(((bf16[8,2048]{1,0:T(8,128)(2,1)}), bf16[1024,2048]{1,0:T(8,128)(2,1)}) %all-gather.8.cloned.1.call-update) | async-done | bytes 4194320 | tf_op jit(solution)/shard_map/all_gather | solution.py:215
  217.8 9.2 reduce-window.6
  227.9 91.8 %all-gather.18.cloned.1.call-done = bf16[4096,1024]{1,0:T(8,128)(2,1)} async-done(((bf16[128,1024]{1,0:T(8,128)(2,1)}), bf16[4096,1024]{1,0:T(8,128)(2,1)}) %all-gather.18.cloned.1.call-update) | async-done | bytes 8388624 | tf_op jit(solution)/shard_map/all_gather | solution.py:242
  319.7 11.4 copy.68
  331.2 26.2 %while.76 = (s32[]{:T(128)}, f32[8,2,128]{2,1,0:T(2,128)S(1)}, f32[8,2,128]{2,1,0:T(2,128)S(1)}, s32[8,512]{1,0:T(8,128)S(1)}, s32[1,2,64]{2,1,0:T(2,128)}, /*in...) while((s32[]{:T(128)}, f32[8,2,128]{2,1,0:T(2,128)S(1)}, ...), condition=%wide.wide.region_4.5_spmd.clone, body=%wide.wide.region_1.4_spmd.clone.sunk | while | flops 141633536 | bytes 12630656 | solution.py:100
  357.4 25.0 while.77
  382.4 131.8 %all-gather.10.cloned.1.call-done = bf16[1024,1024]{1,0:T(8,128)(2,1)} async-done(((bf16[8,1024]{1,0:T(8,128)(2,1)}), bf16[1024,1024]{1,0:T(8,128)(2,1)}) %all-gather.10.cloned.1.call-update) | async-done | bytes 2097168 | tf_op jit(solution)/shard_map/all_gather | solution.py:215
  516.5 15.5 scatter_custom_fusion
  539.8 8.4 scatter_custom_fusion.1
  548.2 47.2 %all-to-all-done = bf16[32,64,1024]{2,1,0:T(8,128)(2,1)} async-done(((bf16[32,64,1024]{2,1,0:T(8,128)(2,1)}), bf16[32,64,1024]{2,1,0:T(8,128)(2,1)}, u32[]{:S(2)}, u32[]{:S(2)}) %all-to-all-start) | async-done | bytes 4194336 | tf_op jit(solution)/shard_map/all_to_all | solution.py:290
  595.4 8.6 all-to-all-start.2
  606.1 6.8 fusion.46
  612.9 47.5 %all-gather.12.cloned.1.call-done = bf16[1,1024,512]{2,1,0:T(8,128)(2,1)} async-done(((bf16[1,256,512]{2,1,0:T(8,128)(2,1)}), bf16[1,1024,512]{2,1,0:T(8,128)(2,1)}) %all-gather.12.cloned.1.call-update) | async-done | bytes 1048592 | tf_op jit(solution)/shard_map/all_gather | solution.py:295
  660.4 6.8 fusion.50
  667.2 17.7 all-gather.16.cloned.1.call-done
  684.9 11.2 multiply_convert_fusion
  700.5 9.5 all-to-all-start.1
  718.9 58.8 %all-to-all-done.1 = bf16[32,64,1024]{2,1,0:T(8,128)(2,1)} async-done(((bf16[32,64,1024]{2,1,0:T(8,128)(2,1)}), bf16[32,64,1024]{2,1,0:T(8,128)(2,1)}, u32[]{:S(2)}, u32[]{:S(2)}) %all-to-all-start.1) | async-done | bytes 4194336 | tf_op jit(solution)/shard_map/all_to_all | solution.py:309
  777.7 7.1 all-to-all-start.3
  785.1 8.7 gather_fusion
  793.8 49.1 %all-to-all-done.3 = bf16[32,64,1024]{2,1,0:T(8,128)(2,1)} async-done(((bf16[32,64,1024]{2,1,0:T(8,128)(2,1)}), bf16[32,64,1024]{2,1,0:T(8,128)(2,1)}, u32[]{:S(2)}, u32[]{:S(2)}) %all-to-all-start.3) | async-done | bytes 4194336 | tf_op jit(solution)/shard_map/all_to_all | solution.py:346
  842.9 7.7 gather_fusion.1
  857.4 37.0 %while.78 = (s32[]{:T(128)}, f32[8,2,128]{2,1,0:T(2,128)S(1)}, s32[8,512]{1,0:T(8,128)S(1)}, s32[1,2,64]{2,1,0:T(2,128)}, bf16[8,512,1024]{1,2,0:T(8,128)(2,1)},...) while((s32[]{:T(128)}, f32[8,2,128]{2,1,0:T(2,128)S(1)}, ...), condition=%wide.wide.region_18.19_spmd.clone, body=%wide.wide.region_16.18_spmd.clone.sunk | while | flops 273745920 | bytes 14334599 | solution.py:167
  894.4 78.7 %while.79 = (s32[]{:T(128)}, f32[128,1024]{0,1:T(8,128)S(1)}, bf16[8,512,1024]{2,1,0:T(8,128)(2,1)}, bf16[8,512,1024]{1,2,0:T(8,128)(2,1)}, s32[8,512]{1,0:T(8,1...) while((s32[]{:T(128)}, f32[128,1024]{0,1:T(8,128)S(1)}, ...), condition=%wide.wide.region_20.21_spmd.clone, body=%wide.wide.region_19.20_spmd.clone.sunk | while | flops 684654592 | bytes 35355288 | solution.py:176
  995.8 157.3 %reduce-scatter.7.cloned.1.call-done = bf16[1,1,128,1024]{3,2,0,1:T(8,128)(2,1)} async-done(((bf16[32,1,128,1024]{3,2,0,1:T(8,128)(2,1)}), bf16[1,1,128,1024]{3,2,0,1:T(8,128)(2,1)}) %reduce-scatter.7.cloned.1.call-update) | async-done | bytes 262160 | tf_op jit(solution)/shard_map/reduce_scatter | solution.py:389
  1159.6 35.2 %reduce-scatter.17.cloned.1.call-done = bf16[1,128,1024]{2,1,0:T(8,128)(2,1)} async-done(((bf16[1,512,1024]{2,1,0:T(8,128)(2,1)}), bf16[1,128,1024]{2,1,0:T(8,128)(2,1)}) %reduce-scatter.17.cloned.1.call-update) | async-done | bytes 262160 | tf_op jit(solution)/shard_map/reduce_scatter | solution.py:357
  1196.5 22.3 reduce-scatter.15.cloned.1.call-done
  1220.6 22.2 reduce-scatter.13.cloned.1.call-done
  1248.4 65.9 %all-reduce.4 = (f32[1024]{0:T(1024)S(1)}, f32[1024]{0:T(1024)S(1)}) all-reduce(f32[1024]{0:T(1024)S(1)} %get-tuple-element.439, f32[1024]{0:T(1024)S(1)} %get-tuple-element.437), channel_id=4, replica_groups=mesh['ctx'=32,'fsdp'=4] {'ctx','fsdp'}, use_global_device_ids=true, to_apply=%region_24.25.clone | all-reduce | flops 2048 | bytes 16384
  1316.4 565.9 %reduce-scatter.11.cloned.1.call-done = f32[8,1024]{1,0:T(8,128)} async-done(((f32[1024,1024]{1,0:T(8,128)}), f32[8,1024]{1,0:T(8,128)}) %reduce-scatter.11.cloned.1.call-update) | async-done | bytes 32784 | tf_op jit(solution)/shard_map/reduce_scatter | solution.py:418
  1882.3 646.8 %reduce-scatter.9.cloned.1.call-done = f32[8,2048]{1,0:T(8,128)} async-done(((f32[1024,2048]{1,0:T(8,128)}), f32[8,2048]{1,0:T(8,128)}) %reduce-scatter.9.cloned.1.call-update) | async-done | bytes 65552 | tf_op jit(solution)/shard_map/reduce_scatter | solution.py:417
  (473 shorter events, 250.0 us)
Async XLA Ops:
  8.0 204.0 %all-gather.8.cloned.1.call-start = ((), (), s32[]{:S(2)}) async-start(), calls=%async_computation.10 | async-start | bytes 4227072 | tf_op jit(solution)/shard_map/all_gather | solution.py:215
  9.5 310.2 %all-gather.18.cloned.1.call-start = ((), (), s32[]{:S(2)}) async-start(), calls=%async_computation.21 | async-start | bytes 8650752 | tf_op jit(solution)/shard_map/all_gather | solution.py:242
  12.1 203.9 %copy-start.23 = (f32[128]{0:T(128)}, f32[128]{0:T(128)S(1)}, u32[]{:S(2)}) copy-start(f32[128]{0:T(128)S(1)} %rsqrt.26) | copy-start | bytes 1540
  12.1 204.8 %copy-start.25 = (s32[1,2,64]{2,1,0:T(2,128)}, s32[1,2,64]{2,1,0:T(2,128)S(1)}, u32[]{:S(2)}) copy-start(s32[1,2,64]{2,1,0:T(2,128)S(1)} %get-tuple-element.1015) | copy-start | bytes 1540
  81.9 145.8 %copy-start.14 = (f32[128,32]{0,1:T(8,128)}, f32[128,32]{0,1:T(8,128)S(1)}, u32[]{:S(2)}) copy-start(f32[128,32]{0,1:T(8,128)S(1)} %get-tuple-element.534) | copy-start | bytes 49156
  81.9 145.8 %copy-start.16 = (f32[128,32]{0,1:T(8,128)}, f32[128,32]{0,1:T(8,128)S(1)}, u32[]{:S(2)}) copy-start(f32[128,32]{0,1:T(8,128)S(1)} %get-tuple-element.535) | copy-start | bytes 49156
  83.0 133.0 %copy-start.5 = (bf16[128,1024]{1,0:T(8,128)(2,1)}, bf16[128,1024]{1,0:T(8,128)(2,1)S(1)}, u32[]{:S(2)}) copy-start(bf16[128,1024]{1,0:T(8,128)(2,1)S(1)} %fusion.57) | copy-start | bytes 786436
  83.1 133.0 %copy-start.21 = (f32[8,1024]{1,0:T(8,128)S(1)}, f32[8,1024]{1,0:T(8,128)}, u32[]{:S(2)}) copy-start(f32[8,1024]{1,0:T(8,128)} %param.25) | copy-start | bytes 98308
  83.1 133.9 %copy-start.20 = (s32[1,1,1,2,64,8]{4,5,3,2,1,0:T(8,128)S(1)}, s32[1,1,1,2,64,8]{4,5,3,2,1,0:T(8,128)}, u32[]{:S(2)}) copy-start(s32[1,1,1,2,64,8]{4,5,3,2,1,0:T(8,128)} %param.20) | copy-start | bytes 12292
  216.0 298.2 %all-gather.10.cloned.1.call-start = ((), (), s32[]{:S(2)}) async-start(), calls=%async_computation.11 | async-start | bytes 2113536 | tf_op jit(solution)/shard_map/all_gather | solution.py:215
  357.4 156.8 %copy-start.3 = (bf16[1,1,1,2,64,1024]{5,4,3,2,1,0:T(8,128)(2,1)S(1)}, bf16[1,1,1,2,64,1024]{5,4,3,2,1,0:T(8,128)(2,1)}, u32[]{:S(2)}) copy-start(bf16[1,1,1,2,64,1024]{5,4,3,2,1,0:T(8,128)(2,1)} %param.19) | copy-start | bytes 786436
  382.4 149.6 %copy-start.7 = (bf16[128,8,2,64]{0,3,2,1:T(8,128)(2,1)}, bf16[128,8,2,64]{0,3,2,1:T(8,128)(2,1)S(1)}, u32[]{:S(2)}) copy-start(bf16[128,8,2,64]{0,3,2,1:T(8,128)(2,1)S(1)} %convert_element_type.195) | copy-start | bytes 786436
  516.4 335.7 %copy-start.2 = (f32[128,1024]{1,0:T(8,128)}, f32[128,1024]{1,0:T(8,128)S(1)}, u32[]{:S(2)}) copy-start(f32[128,1024]{1,0:T(8,128)S(1)} %get-tuple-element.539) | copy-start | bytes 1572868
  532.0 63.4 %all-to-all-start = ((bf16[32,64,1024]{2,1,0:T(8,128)(2,1)}), bf16[32,64,1024]{2,1,0:T(8,128)(2,1)}, u32[]{:S(2)}, u32[]{:S(2)}) async-start(bf16[32,64,1024]{2,1,0:T(8,128)(2,1)} %bitcast.447), calls=%async_computation | async-start | bytes 8388608 | tf_op jit(solution)/shard_map/all_to_all | solution.py:290
  538.7 67.4 %all-gather.14.cloned.1.call-start = ((), (), s32[]{:S(2)}) async-start(), calls=%async_computation.13 | async-start | bytes 1310720 | tf_op jit(solution)/shard_map/all_gather | solution.py:296
  595.4 9.9 copy-start.13
  595.4 89.5 %all-to-all-start.2 = ((bf16[32,64,1024]{2,1,0:T(8,128)(2,1)}), bf16[32,64,1024]{2,1,0:T(8,128)(2,1)}, u32[]{:S(2)}, u32[]{:S(2)}) async-start(bf16[32,64,1024]{2,1,0:T(8,128)(2,1)} %bitcast.446), calls=%async_computation.2 | async-start | bytes 8388608 | tf_op jit(solution)/shard_map/all_to_all | solution.py:321
  604.0 56.4 %all-gather.12.cloned.1.call-start = ((), (), s32[]{:S(2)}) async-start(), calls=%async_computation.12 | async-start | bytes 1310720 | tf_op jit(solution)/shard_map/all_gather | solution.py:295
  604.8 80.0 %all-gather.16.cloned.1.call-start = ((), (), s32[]{:S(2)}) async-start(), calls=%async_computation.14 | async-start | bytes 1310720 | tf_op jit(solution)/shard_map/all_gather | solution.py:297
  684.9 11.2 copy-start.29
  700.5 9.6 copy-start.28
  700.5 77.2 %all-to-all-start.1 = ((bf16[32,64,1024]{2,1,0:T(8,128)(2,1)}), bf16[32,64,1024]{2,1,0:T(8,128)(2,1)}, u32[]{:S(2)}, u32[]{:S(2)}) async-start(bf16[32,64,1024]{2,1,0:T(8,128)(2,1)} %bitcast.456), calls=%async_computation.1 | async-start | bytes 8388608 | tf_op jit(solution)/shard_map/all_to_all | solution.py:309
  777.7 65.3 %all-to-all-start.3 = ((bf16[32,64,1024]{2,1,0:T(8,128)(2,1)}), bf16[32,64,1024]{2,1,0:T(8,128)(2,1)}, u32[]{:S(2)}, u32[]{:S(2)}) async-start(bf16[32,64,1024]{2,1,0:T(8,128)(2,1)} %bitcast.455), calls=%async_computation.3 | async-start | bytes 8388608 | tf_op jit(solution)/shard_map/all_to_all | solution.py:346
  784.8 368.2 %reduce-scatter.7.cloned.1.call-start = ((), (), s32[]{:S(2)}) async-start(), calls=%async_computation.15 | async-start | bytes 8650752 | tf_op jit(solution)/shard_map/reduce_scatter | solution.py:389
  973.2 221.6 %reduce-scatter.17.cloned.1.call-start = ((), (), s32[]{:S(2)}) async-start(), calls=%async_computation.20 | async-start | bytes 1310720 | tf_op jit(solution)/shard_map/reduce_scatter | solution.py:357
  980.3 238.5 %reduce-scatter.15.cloned.1.call-start = ((), (), s32[]{:S(2)}) async-start(), calls=%async_computation.19 | async-start | bytes 1310720 | tf_op jit(solution)/shard_map/reduce_scatter | solution.py:354
  986.8 256.0 %reduce-scatter.13.cloned.1.call-start = ((), (), s32[]{:S(2)}) async-start(), calls=%async_computation.18 | async-start | bytes 1310720 | tf_op jit(solution)/shard_map/reduce_scatter | solution.py:351
  992.5 889.8 %reduce-scatter.11.cloned.1.call-start = ((), (), s32[]{:S(2)}) async-start(), calls=%async_computation.17 | async-start | bytes 4227072 | tf_op jit(solution)/shard_map/reduce_scatter | solution.py:418
  995.3 159.1 %copy-start.6 = (bf16[128,1024]{1,0:T(8,128)(2,1)S(1)}, bf16[128,1024]{1,0:T(8,128)(2,1)}, u32[]{:S(2)}) copy-start(bf16[128,1024]{1,0:T(8,128)(2,1)} %copy-done.5) | copy-start | bytes 786436
  995.3 1533.8 %reduce-scatter.9.cloned.1.call-start = ((), (), s32[]{:S(2)}) async-start(), calls=%async_computation.16 | async-start | bytes 8454144 | tf_op jit(solution)/shard_map/reduce_scatter | solution.py:417
  1159.0 85.6 %copy-start.4 = (bf16[1,1,1,2,64,1024]{5,4,3,2,1,0:T(8,128)(2,1)S(1)}, bf16[1,1,1,2,64,1024]{5,4,3,2,1,0:T(8,128)(2,1)}, u32[]{:S(2)}) copy-start(bf16[1,1,1,2,64,1024]{5,4,3,2,1,0:T(8,128)(2,1)} %param.19) | copy-start | bytes 786436
  1159.0 85.6 %copy-start.19 = (f32[1024]{0:T(1024)S(1)}, f32[1024]{0:T(1024)}, u32[]{:S(2)}) copy-start(f32[1024]{0:T(1024)} %copy-done.18) | copy-start | bytes 12292
  (18 other events, 81.9 us)
Sparse Core Ops, SparseCore 0:
  11.1 200.7 all-gather.7
  216.1 103.5 all-gather.17
  322.1 192.1 all-gather.9
  973.3 179.7 reduce-scatter.6
  1155.3 39.3 reduce-scatter.16
  1197.1 21.6 reduce-scatter.14
  1221.2 21.5 reduce-scatter.12
  1245.8 636.4 reduce-scatter.10
  1885.3 643.8 reduce-scatter.8
Sparse Core Ops, SparseCore 1:
  541.4 53.6 all-gather.13
  606.7 53.7 all-gather.11
  662.5 22.3 all-gather.15
where the time goes:
time: 2550 us; the launch traced here: 2540 us
  waiting for transfers between devices  2020 us (79%)
  matrix products  168 us (7%)
  blocking collectives  135 us (5%)
  local copies, waits for them, and re-layouts  107 us (4%)
  other arithmetic  52.5 us (2%)
  starting transfers between devices  33.1 us (1%)
    reduce_scatter x1, waiting for transfers between devices, on_device(): lax.psum_scatter(grad_w_qkv, ('ctx', 'fsdp'), scatter_dimension=0, tiled=...  647 us
    reduce_scatter x1, waiting for transfers between devices, on_device(): lax.psum_scatter(grad_w_out, ('ctx', 'fsdp'), scatter_dimension=0, tiled=...  566 us
    all_gather x2, waiting for transfers between devices, on_device(): lax.all_gather(for_sending(attn_masters()), ('ctx', 'fsdp'), axis=0, tile...  261 us
    reduce_scatter x1, waiting for transfers between devices, on_device(): lax.psum_scatter(pair_terms.astype(jnp.bfloat16), 'ctx', scatter_dimensio...  157 us
    unnamed x2, blocking collectives  135 us
    all_gather x1, waiting for transfers between devices, on_device(): lax.all_gather(pairs_local.reshape(1, seqs, per_seq, 2 * kv_width), 'ctx'...  91.8 us
    all_to_all x1, waiting for transfers between devices, on_device(): lax.all_to_all(source_layout(slot_out), 'ctx', split_axis=0, concat_axis=...  58.8 us
  transfers between devices with their start and end apart: 16, of which 14 were waited for; matrix products, arithmetic and copies ran while one was open for 6% of the time, Pallas kernels for 0%

commit v1 on v0

v1 whole, which is shorter than its diff:
```python
import functools

import jax
import jax.numpy as jnp
import numpy as np
from jax import lax
from jax.experimental import pallas as pl
from jax.experimental.pallas import tpu as pltpu
from jax.sharding import Mesh
from jax.sharding import PartitionSpec as P

WIDTH = 1024
EPSILON = 1e-06
ROPE_BASE = 10000.0
MASKED = -1e30
BF = jnp.bfloat16
F32 = jnp.float32
CTX = ("x", "zh", "y")
HEAD_AXES = ("x", "zh")
FSDP = ("zl", "core")
ALL = CTX + FSDP
VMEM_LIMIT = 56 * 1024 * 1024

NT = (((1,), (1,)), ((), ()))
TN = (((0,), (0,)), ((), ()))


def mm(a, b, dims=None):
    if dims is None:
        return jnp.dot(a, b, preferred_element_type=F32)
    return lax.dot_general(a, b, dims, preferred_element_type=F32)


def lane(shape):
    return lax.broadcasted_iota(jnp.int32, shape, len(shape) - 1)


def row(shape):
    return lax.broadcasted_iota(jnp.int32, shape, len(shape) - 2)


def call(kernel, out_shape, cost, **kw):
    flops, bytes_accessed = cost
    return pl.pallas_call(
        kernel,
        out_shape=out_shape,
        compiler_params=pltpu.CompilerParams(vmem_limit_bytes=VMEM_LIMIT),
        cost_estimate=pl.CostEstimate(
            flops=int(flops), bytes_accessed=int(bytes_accessed), transcendentals=0
        ),
        **kw,
    )


def sds(shape, dtype):
    return jax.ShapeDtypeStruct(shape, dtype)


VM = pl.BlockSpec(memory_space=pltpu.VMEM)
SM = pl.BlockSpec(memory_space=pltpu.SMEM)


def slice_matrix():
    table = np.zeros((512, 512), np.float32)
    for k in range(512):
        section, place = k // 128, k % 128
        if section < 2:
            pair, part = section, place // 64
        else:
            pair, part = place // 64, section
        feat = place % 64
        f = (feat % 32) // 8
        column = pair * 64 + part * 16 + (feat // 32) * 8 + feat % 8
        table[k, f * 128 + column] = 1.0
    return table


def head_matrix():
    table = np.zeros((4, 128, 768), np.float32)
    for f in range(4):
        for block in range(2):
            for part in range(4):
                for j in range(16):
                    feat = (j // 8) * 32 + 8 * f + j % 8
                    source = block * 64 + part * 16 + j
                    if part == 2:
                        target = block * 128 + feat
                    elif part == 3:
                        target = block * 128 + 64 + feat
                    else:
                        target = 256 + block * 256 + part * 128 + feat
                    table[f, source, target] = 1.0
    return table


def kernel_route(picks_ref, gates_ref, rank_ref, gate_ref):
    experts = row((32, 128))
    gate = jnp.zeros((32, 128), F32)
    chosen = jnp.zeros((32, 128), F32)
    for k in range(8):
        hit = picks_ref[k : k + 1, :] == experts
        gate = gate + jnp.where(hit, gates_ref[k : k + 1, :], 0.0)
        chosen = chosen + jnp.where(hit, 1.0, 0.0)
    before = jnp.where(row((128, 128)) < lane((128, 128)), 1.0, 0.0).astype(BF)
    rank = mm(chosen.astype(BF), before)
    rank_ref[...] = jnp.where(chosen > 0.5, rank, -1.0)
    gate_ref[...] = gate


def kernel_slices(w_ref, gains_ref, table_ref, out_ref):
    w = w_ref[...].astype(BF).astype(F32)
    parts = []
    for p in range(4):
        parts.append(
            jnp.concatenate(
                [
                    w[:, 256 * p : 256 * p + 256],
                    w[:, 1024 + 128 * p : 1152 + 128 * p],
                    w[:, 1536 + 128 * p : 1664 + 128 * p],
                ],
                axis=1,
            )
        )
    stacked = jnp.concatenate(parts, axis=0).astype(BF)
    cut = mm(stacked, table_ref[...])
    for f in range(4):
        for p in range(4):
            out_ref[f, :, 128 * p : 128 * p + 128] = cut[
                8 * p : 8 * p + 8, 128 * f : 128 * f + 128
            ].astype(BF)
        out_ref[f, :, 512:640] = gains_ref[...].astype(BF)


def kernel_project(x_ref, w_ref, cos_ref, sin_ref, msg_ref, hidden_ref, gains_ref):
    gains = jnp.transpose(w_ref[:, 512:640].astype(F32))
    gains_ref[...] = gains[:8]
    for s in range(4):
        x = x_ref[128 * s : 128 * s + 128, :].astype(F32)
        scale = lax.rsqrt(jnp.mean(x * x, axis=-1, keepdims=True) + EPSILON)
        hidden_ref[128 * s : 128 * s + 128, :] = (x * scale * gains[0:1]).astype(BF)
    proj = mm(hidden_ref[...], w_ref[:, 0:512])
    ahead = pltpu.roll(proj, 512 - 8, 1)
    behind = pltpu.roll(proj, 8, 1)
    partner = jnp.where((lane((512, 512)) // 8) % 2 == 0, ahead, behind)
    cos = jnp.concatenate([cos_ref[...]] * 4, axis=0)
    sin = jnp.concatenate([sin_ref[...]] * 4, axis=0)
    turned = proj * cos + partner * sin
    low = lane((64, 128)) < 64
    for s in range(4):
        for p in range(4):
            front = turned[128 * s : 128 * s + 64, 128 * p : 128 * p + 128]
            back = turned[128 * s + 64 : 128 * s + 128, 128 * p : 128 * p + 128]
            msg_ref[8 * p + s] = jnp.where(low, front, pltpu.roll(back, 64, 1)).astype(BF)
            msg_ref[8 * p + 4 + s] = jnp.where(low, pltpu.roll(front, 64, 1), back).astype(BF)


def kernel_heads(msg_ref, table_ref, kv_ref, q_ref):
    out = jnp.zeros((512, 768), F32)
    for f in range(4):
        out = out + mm(msg_ref[:, f].reshape(512, 128), table_ref[f])
    pairs = out[:, 0:256].astype(BF)
    for half in range(2):
        block = pairs[:, 128 * half : 128 * half + 128]
        for y in range(4):
            kv_ref[y, 512 * half : 512 * half + 512, :] = block
    queries = (out[:, 256:768] * 0.125).astype(BF)
    for half in range(2):
        for head in range(2):
            at = 256 * half + 128 * head
            q_ref[half, :, head] = queries[:, at : at + 128].reshape(8, 64, 128)


def tile_positions(tile, mine):
    front = tile < 4
    i = jnp.where(front, tile, tile - 4)
    q = lane((1, 256))
    k = row((512, 1))
    k = lax.broadcasted_iota(jnp.int32, (512, 1), 0)
    q_front = (8 * i + 4 * (q // 128) + mine) * 64 + q % 64
    q_back = (63 - 8 * i - 4 * (q // 128) - mine) * 64 + q % 64
    k_front = 512 * i + k
    k_back = (59 - 8 * i + 4 * (k // 256) - (k % 256) // 64) * 64 + k % 64
    count = jnp.where(front, i + 1, 8 - i)
    return jnp.where(front, q_front, q_back), jnp.where(front, k_front, k_back), count


def kernel_attend(mine_ref, kv_ref, q_ref, msg_ref, log_ref, out_ref, keys_ref, turned_ref):
    tile = pl.program_id(0)

    @pl.when(tile == 0)
    def _():
        for group in range(16):
            half, place = (0, group) if group < 8 else (1, 15 - group)
            for y in range(4):
                at = 256 * group + 64 * y
                keys_ref[at : at + 64, :] = kv_ref[y, half, place]
        for c in range(8):
            turned_ref[:, 512 * c : 512 * c + 512] = jnp.transpose(
                keys_ref[512 * c : 512 * c + 512, :].astype(F32)
            ).astype(BF)

    q = q_ref[...]
    q_pos, k_pos, count = tile_positions(tile, mine_ref[0])

    def step(c, carry, last):
        peak, total, mixed = carry
        at = pl.multiple_of(c * 512, 512)
        scores = mm(keys_ref[pl.ds(at, 512), :], q, NT)
        if last:
            scores = jnp.where(k_pos <= q_pos, scores, MASKED)
        higher = jnp.maximum(peak, jnp.max(scores, axis=0, keepdims=True))
        weights = jnp.exp(scores - higher)
        fade = jnp.exp(peak - higher)
        total = total * fade + jnp.sum(weights, axis=0, keepdims=True)
        mixed = mixed * fade + mm(turned_ref[64:128, pl.ds(at, 512)], weights.astype(BF))
        return higher, total, mixed

    start = (
        jnp.full((1, 256), MASKED, F32),
        jnp.zeros((1, 256), F32),
        jnp.zeros((64, 256), F32),
    )
    carry = lax.fori_loop(0, count - 1, lambda c, v: step(c, v, False), start)
    peak, total, mixed = step(count - 1, carry, True)
    log_ref[0] = jnp.broadcast_to(peak + jnp.log(total), (8, 256))
    mixed = mixed / total
    out = jnp.transpose(jnp.concatenate([jnp.zeros((64, 256), F32), mixed], axis=0))
    out_ref[...] = out
    low = lane((64, 128)) < 64
    for a in range(2):
        first = out[128 * a : 128 * a + 64]
        second = out[128 * a + 64 : 128 * a + 128]
        msg_ref[a, 0] = jnp.where(low, pltpu.roll(first, 64, 1), second).astype(BF)


def kernel_attend_back(
    mine_ref, keys_ref, turned_ref, q_ref, grad_ref, log_ref, out_ref, dq_ref, dkv_ref, sum_ref
):
    tile = pl.program_id(0)

    @pl.when(tile == 0)
    def _():
        sum_ref[...] = jnp.zeros_like(sum_ref)

    q = q_ref[...]
    low = lane((64, 128)) < 64
    pieces = []
    for a in range(2):
        both = grad_ref[a, 0].astype(F32)
        pieces.append(jnp.where(low, 0.0, pltpu.roll(both, 64, 1)))
        pieces.append(jnp.where(low, 0.0, both))
    grad = jnp.concatenate(pieces, axis=0)
    delta = jnp.sum(jnp.transpose(grad * out_ref[...]), axis=0, keepdims=True)
    grad = grad.astype(BF)
    q_pos, k_pos, count = tile_positions(tile, mine_ref[0])
    log_total = log_ref[0][0:1]

    def step(c, dq, last):
        at = pl.multiple_of(c * 512, 512)
        keys = keys_ref[pl.ds(at, 512), :]
        scores = mm(keys, q, NT)
        if last:
            scores = jnp.where(k_pos <= q_pos, scores, MASKED)
        weights = jnp.exp(scores - log_total)
        slope = (weights * (mm(keys, grad, NT) - delta)).astype(BF)
        sum_ref[pl.ds(at, 512), :] += mm(slope, q) + mm(weights.astype(BF), grad)
        return dq + mm(turned_ref[0:64, pl.ds(at, 512)], slope)

    dq = lax.fori_loop(0, count - 1, lambda c, v: step(c, v, False), jnp.zeros((64, 256), F32))
    dq = step(count - 1, dq, True)
    dq_ref[...] = jnp.transpose(jnp.concatenate([dq * 0.125, jnp.zeros((64, 256), F32)], axis=0))

    @pl.when(tile == 7)
    def _():
        for group in range(16):
            half, place = (0, group) if group < 8 else (1, 15 - group)
            for y in range(4):
                at = 256 * group + 64 * y
                dkv_ref[y, half, place] = sum_ref[at : at + 64, :].astype(BF)


def kernel_middle(
    o_ref, w_ref, x_ref, gains_ref, rank_ref, slots_ref, mid_ref, rows_ref, hidden_ref
):
    @pl.when(pl.program_id(0) == 0)
    def _():
        for g in range(8):
            rows_ref[:, 128 * g : 128 * g + 128] = o_ref[g].reshape(128, 128)
        mid = x_ref[...].astype(F32) + mm(rows_ref[...], w_ref[...])
        mid_ref[...] = mid
        scale = lax.rsqrt(jnp.mean(mid * mid, axis=-1, keepdims=True) + EPSILON)
        hidden_ref[...] = (mid * scale * gains_ref[1:2]).astype(BF)

    slot = lax.broadcasted_iota(jnp.int32, (64, 128), 0).astype(F32)
    for j in range(4):
        rank = rank_ref[pl.ds(4 * pl.program_id(0) + j, 1), :]
        pick = jnp.where(slot == rank, 1.0, 0.0).astype(BF)
        slots_ref[j] = mm(pick, hidden_ref[...]).astype(BF)


def kernel_experts(
    h_ref, dy_ref, gate_ref, w_ref, ys_ref, dxs_ref, grad_ref, gu_ref, v_ref, rank_ref, ggu_ref, gv_ref
):
    step = pl.program_id(0)

    @pl.when(step == 0)
    def _():
        for f in range(4):
            gu_ref[256 * f : 256 * f + 256, :] = w_ref[f, 0:256, :]
            v_ref[128 * f : 128 * f + 128, :] = w_ref[f, 256:384, :]
        before = jnp.where(row((128, 128)) < lane((128, 128)), 1.0, 0.0).astype(BF)
        chosen = gate_ref[...] > 0.0
        rank = mm(jnp.where(chosen, 1.0, 0.0).astype(BF), before)
        rank_ref[...] = jnp.where(chosen, rank, -1.0)
        ggu_ref[...] = jnp.zeros_like(ggu_ref)
        gv_ref[...] = jnp.zeros_like(gv_ref)

    slot = lax.broadcasted_iota(jnp.int32, (64, 128), 0).astype(F32)
    grads = []
    for j in range(4):
        source = 4 * step + j
        pick = slot == rank_ref[pl.ds(source, 1), :]
        weight = jnp.sum(
            jnp.where(pick, gate_ref[pl.ds(source, 1), :], 0.0), axis=1, keepdims=True
        )
        rows = mm(jnp.where(pick, 1.0, 0.0).astype(BF), dy_ref[j])
        grads.append((rows * weight).astype(BF))
    dys = jnp.concatenate(grads, axis=0)
    h = h_ref[...].reshape(256, WIDTH)
    both = mm(h, gu_ref[...])
    gate_h, up_h = both[:, :512], both[:, 512:]
    sig = jax.nn.sigmoid(gate_h)
    swished = gate_h * sig
    act = (swished * up_h).astype(BF)
    ys_ref[...] = mm(act, v_ref[...]).astype(BF).reshape(4, 64, WIDTH)
    dact = mm(dys, v_ref[...], NT)
    dgate = (dact * up_h * sig * (1.0 + gate_h * (1.0 - sig))).astype(BF)
    dup = (dact * swished).astype(BF)
    dboth = jnp.concatenate([dgate, dup], axis=1)
    dxs_ref[...] = mm(dboth, gu_ref[...], NT).astype(BF).reshape(4, 64, WIDTH)
    ggu_ref[...] += mm(h, dboth, TN)
    gv_ref[...] += mm(act, dys, TN)

    @pl.when(step == 7)
    def _():
        for f in range(4):
            grad_ref[f, 0:256, :] = ggu_ref[256 * f : 256 * f + 256, :].astype(BF)
            grad_ref[f, 256:384, :] = gv_ref[128 * f : 128 * f + 128, :].astype(BF)


def kernel_middle_back(
    dxs_ref, rank_ref, mid_ref, cot_ref, gains_ref, w_ref, dmid_ref, low_ref, msg_ref, ggain_ref, sum_ref
):
    step = pl.program_id(0)

    @pl.when(step == 0)
    def _():
        sum_ref[...] = jnp.zeros_like(sum_ref)

    slot = lax.broadcasted_iota(jnp.int32, (64, 128), 0).astype(F32)
    picks = []
    for j in range(4):
        picks.append(jnp.where(slot == rank_ref[pl.ds(4 * step + j, 1), :], 1.0, 0.0))
    picks = jnp.concatenate(picks, axis=0).astype(BF)
    sum_ref[...] += mm(picks, dxs_ref[...].reshape(256, WIDTH), TN)

    @pl.when(step == 7)
    def _():
        mid = mid_ref[...]
        scale = lax.rsqrt(jnp.mean(mid * mid, axis=-1, keepdims=True) + EPSILON)
        dh = sum_ref[...]
        ggain_ref[...] = jnp.broadcast_to(
            jnp.sum(dh * (mid * scale), axis=0, keepdims=True), (8, WIDTH)
        )
        dn = dh * gains_ref[1:2]
        dmid = (
            cot_ref[...].astype(F32)
            + scale * dn
            - mid * (scale * scale * scale) * jnp.mean(dn * mid, axis=-1, keepdims=True)
        )
        dmid_ref[...] = dmid
        low = dmid.astype(BF)
        low_ref[...] = low
        grad = mm(low, w_ref[...], NT).astype(BF)
        for g in range(8):
            msg_ref[g] = grad[:, 128 * g : 128 * g + 128].reshape(2, 64, 128)


def kernel_slices_back(dkv_ref, dq_ref, cos_ref, sin_ref, table_ref, msg_ref):
    def unrotate(w, cos, sin):
        partner = jnp.where(
            lane(w.shape) % 64 < 32, pltpu.roll(w, 96, 1), pltpu.roll(w, 32, 1)
        )
        return (w * cos - partner * sin).astype(BF)

    cos, sin = cos_ref[...], sin_ref[...]
    dkv = dkv_ref[0].astype(F32)
    for y in range(1, 4):
        dkv = dkv + dkv_ref[y].astype(F32)
    dkv = unrotate(dkv, cos, sin)
    parts = [dkv[0:512], dkv[512:1024]]
    for half in range(2):
        table_cos = cos[512 * half : 512 * half + 512]
        table_sin = sin[512 * half : 512 * half + 512]
        for head in range(2):
            parts.append(
                unrotate(dq_ref[half, :, head].reshape(512, 128), table_cos, table_sin)
            )
    whole = jnp.concatenate(parts, axis=1)
    for f in range(4):
        msg_ref[:, f] = mm(whole, table_ref[f], NT).astype(BF).reshape(8, 64, 128)


def kernel_project_back(
    msg_ref, x_ref, hidden_ref, w_ref, gains_ref, ggain_ref, o_ref, da_ref, grads_ref, dh_ref, d_ref
):
    low = lane((64, 128)) < 64
    for s in range(4):
        for p in range(4):
            even = msg_ref[8 * p + s].astype(F32)
            odd = msg_ref[8 * p + 4 + s].astype(F32)
            d_ref[128 * s : 128 * s + 64, 128 * p : 128 * p + 128] = jnp.where(
                low, even, pltpu.roll(odd, 64, 1)
            ).astype(BF)
            d_ref[128 * s + 64 : 128 * s + 128, 128 * p : 128 * p + 128] = jnp.where(
                low, pltpu.roll(even, 64, 1), odd
            ).astype(BF)
    grads_ref[:, 0:512] = mm(hidden_ref[...], d_ref[...], TN).astype(BF)
    total = jnp.zeros((1, WIDTH), F32)
    for s in range(4):
        part = mm(d_ref[128 * s : 128 * s + 128, :], w_ref[:, 0:512], NT)
        dh_ref[128 * s : 128 * s + 128, :] = part.astype(BF)
        x = x_ref[128 * s : 128 * s + 128, :].astype(F32)
        scale = lax.rsqrt(jnp.mean(x * x, axis=-1, keepdims=True) + EPSILON)
        total = total + jnp.sum(part * (x * scale), axis=0, keepdims=True)
    which = lax.broadcasted_iota(jnp.int32, (128, WIDTH), 0)
    both = jnp.where(which == 0, total, jnp.where(which == 1, ggain_ref[0:1], 0.0))
    grads_ref[:, 512:640] = jnp.transpose(both).astype(BF)
    for g in range(8):
        part = jnp.zeros((128, 256), F32)
        for s in range(4):
            part = part + mm(
                o_ref[s, g].reshape(128, 128), da_ref[128 * s : 128 * s + 128, :], TN
            )
        grads_ref[128 * g : 128 * g + 128, 640:896] = part.astype(BF)


def kernel_total(parts_ref, table_ref, qkv_ref, out_ref, gains_ref, sum_ref):
    step = pl.program_id(0)

    @pl.when(step == 0)
    def _():
        sum_ref[...] = jnp.zeros_like(sum_ref)

    sum_ref[...] += jnp.sum(parts_ref[...].astype(F32), axis=0)

    @pl.when(step == 3)
    def _():
        rows = []
        for p in range(4):
            rows.append(
                jnp.concatenate(
                    [sum_ref[f, :, 128 * p : 128 * p + 128] for f in range(4)], axis=1
                )
            )
        rest = jnp.concatenate(rows, axis=0)
        whole = jnp.zeros((32, 512), F32)
        for _ in range(3):
            part = rest.astype(BF)
            rest = rest - part.astype(F32)
            whole = whole + mm(part, table_ref[...], NT)
        for p in range(4):
            piece = whole[8 * p : 8 * p + 8]
            qkv_ref[:, 256 * p : 256 * p + 256] = piece[:, 0:256]
            qkv_ref[:, 1024 + 128 * p : 1152 + 128 * p] = piece[:, 256:384]
            qkv_ref[:, 1536 + 128 * p : 1664 + 128 * p] = piece[:, 384:512]
        for f in range(4):
            out_ref[:, 256 * f : 256 * f + 256] = sum_ref[f, :, 640:896]
        gains_ref[...] = (
            sum_ref[0, :, 512:640]
            + sum_ref[1, :, 512:640]
            + sum_ref[2, :, 512:640]
            + sum_ref[3, :, 512:640]
        )


def kernel_input_grad(dh_ref, x_ref, dmid_ref, gains_ref, out_ref):
    x = x_ref[...].astype(F32)
    scale = lax.rsqrt(jnp.mean(x * x, axis=-1, keepdims=True) + EPSILON)
    dn = dh_ref[...].astype(F32) * gains_ref[0:1]
    out_ref[...] = (
        dmid_ref[...]
        + scale * dn
        - x * (scale * scale * scale) * jnp.mean(dn * x, axis=-1, keepdims=True)
    )


def kernel_output(ys_ref, rank_ref, gate_ref, mid_ref, out_ref, sum_ref):
    step = pl.program_id(0)

    @pl.when(step == 0)
    def _():
        sum_ref[...] = mid_ref[...]

    slot = lax.broadcasted_iota(jnp.int32, (64, 128), 0).astype(F32)
    picks = []
    for j in range(4):
        hit = slot == rank_ref[pl.ds(4 * step + j, 1), :]
        picks.append(jnp.where(hit, gate_ref[pl.ds(4 * step + j, 1), :], 0.0))
    picks = jnp.concatenate(picks, axis=0)
    high = picks.astype(BF)
    rest = (picks - high.astype(F32)).astype(BF)
    ys = ys_ref[...].reshape(256, WIDTH)
    sum_ref[...] += mm(high, ys, TN) + mm(rest, ys, TN)

    @pl.when(step == 7)
    def _():
        out_ref[...] = sum_ref[...].astype(BF)


def angles(positions, features):
    frequency = ROPE_BASE ** (-(features.astype(F32) * 2.0 / 64))
    return positions.astype(F32)[:, None] * frequency[None, :]


def whole(shape):
    return pl.BlockSpec(shape, lambda t: (0,) * len(shape))


def exchange(value, axes):
    return lax.all_to_all(value, axes, split_axis=0, concat_axis=0, tiled=True)


def gather(value, axes):
    return lax.all_gather(value, axes, axis=0, tiled=True)


def on_device(
    layer_input,
    routes,
    gates,
    cotangent,
    norm_attn,
    query_key_value_weight,
    output_weight,
    norm_ffn,
    exp_gate,
    exp_up,
    exp_down,
):
    head_index = lax.axis_index(HEAD_AXES)
    mine = lax.axis_index("y")
    ctx_index = lax.axis_index(CTX)
    part_index = lax.axis_index(FSDP)
    x = layer_input.reshape(128, WIDTH)
    cot = cotangent.reshape(128, WIDTH)
    slice_table = jnp.asarray(slice_matrix(), BF)
    head_table = jnp.asarray(head_matrix(), BF)

    x_all = gather(x, FSDP)
    rank, gate = call(
        kernel_route,
        (sds((32, 128), F32), sds((32, 128), F32)),
        (1e6, 1e5),
        in_specs=[VM, VM],
        out_specs=(VM, VM),
    )(routes.reshape(128, 8).T, gates.reshape(128, 8).T)
    which = lax.broadcasted_iota(jnp.int32, (8, 128), 1)
    gain_rows = jnp.where(
        which == 0, norm_attn[:, None], jnp.where(which == 1, norm_ffn[:, None], 0.0)
    )
    slices = call(
        kernel_slices,
        sds((4, 8, 640), BF),
        (2e7, 1e6),
        in_specs=[VM, VM, VM],
        out_specs=VM,
    )(query_key_value_weight, gain_rows, slice_table)
    slices = jnp.broadcast_to(slices[None], (32, 4, 8, 640)).reshape(128, 8, 640)
    w_slice = exchange(slices, ALL).reshape(WIDTH, 640)
    out_copies = jnp.broadcast_to(output_weight.astype(BF)[None], (128, 8, WIDTH))
    w_out = exchange(out_copies, ALL).reshape(WIDTH, WIDTH)
    cot_all = gather(cot, CTX)
    gate_all = gather(gate, CTX).reshape(32, 32, 128)
    expert_weights = jnp.concatenate(
        [
            jnp.concatenate([exp_gate[0], exp_up[0]], axis=1),
            exp_down[0],
        ],
        axis=0,
    ).astype(BF)
    expert_all = gather(expert_weights, FSDP).reshape(4, 384, WIDTH)

    offset = jnp.arange(64, dtype=jnp.int32)
    token_pos = jnp.concatenate([ctx_index * 64 + offset, (63 - ctx_index) * 64 + offset])
    column = jnp.arange(512, dtype=jnp.int32)
    angle = angles(token_pos, 8 * part_index + column % 8)
    is_value = (column // 16) % 4 == 3
    sign = jnp.where((column // 8) % 2 == 0, -1.0, 1.0)
    cos_slice = jnp.where(is_value, 1.0, jnp.cos(angle))
    sin_slice = jnp.where(is_value, 0.0, jnp.sin(angle) * sign)
    msg, hidden, gains = call(
        kernel_project,
        (sds((32, 64, 128), BF), sds((512, WIDTH), BF), sds((8, WIDTH), F32)),
        (6e8, 4e6),
        in_specs=[VM] * 4,
        out_specs=(VM, VM, VM),
    )(x_all, w_slice, cos_slice, sin_slice)
    msg = exchange(msg, HEAD_AXES + FSDP)

    kv_copies, queries = call(
        kernel_heads,
        (sds((4, 1024, 128), BF), sds((2, 8, 2, 64, 128), BF)),
        (4e8, 3e6),
        in_specs=[VM, VM],
        out_specs=(VM, VM),
    )(msg.reshape(8, 4, 64, 128), head_table)
    queries = queries.reshape(2048, 128)
    kv = exchange(kv_copies, ("y",)).reshape(4, 2, 8, 64, 128)
    mine_ref = mine.astype(jnp.int32).reshape(1)
    msg_spec = pl.BlockSpec((2, 1, 64, 128), lambda t: (t % 4, t // 4, 0, 0))
    row_spec = pl.BlockSpec((256, 128), lambda t: (t, 0))
    log_spec = pl.BlockSpec((1, 8, 256), lambda t: (t, 0, 0))
    o_msg, log_total, o_rows, keys, turned = call(
        kernel_attend,
        (
            sds((8, 2, 64, 128), BF),
            sds((8, 8, 256), F32),
            sds((2048, 128), F32),
            sds((4096, 128), BF),
            sds((128, 4096), BF),
        ),
        (1e10, 5e6),
        grid=(8,),
        in_specs=[SM, whole((4, 2, 8, 64, 128)), row_spec],
        out_specs=(msg_spec, log_spec, row_spec, whole((4096, 128)), whole((128, 4096))),
    )(mine_ref, kv, queries)
    o_heads = exchange(o_msg, HEAD_AXES)
    o_all = gather(o_heads, FSDP).reshape(4, 8, 2, 64, 128)

    slots, mid = call(
        kernel_middle,
        (sds((32, 64, WIDTH), BF), sds((128, WIDTH), F32)),
        (9e8, 8e6),
        grid=(8,),
        in_specs=[
            whole((8, 2, 64, 128)),
            whole((WIDTH, WIDTH)),
            whole((128, WIDTH)),
            whole((8, WIDTH)),
            whole((32, 128)),
        ],
        out_specs=(
            pl.BlockSpec((4, 64, WIDTH), lambda t: (t, 0, 0)),
            whole((128, WIDTH)),
        ),
        scratch_shapes=[pltpu.VMEM((128, WIDTH), BF), pltpu.VMEM((128, WIDTH), BF)],
    )(o_heads, w_out, x, gains, rank)
    slots = exchange(slots, CTX)
    gate_mine = lax.dynamic_index_in_dim(gate_all, ctx_index, axis=1, keepdims=False)
    slot_spec = pl.BlockSpec((4, 64, WIDTH), lambda t: (t, 0, 0))
    ys, dxs, expert_grads = call(
        kernel_experts,
        (sds((32, 64, WIDTH), BF), sds((32, 64, WIDTH), BF), sds((4, 384, WIDTH), BF)),
        (2e10, 3e7),
        grid=(8,),
        in_specs=[
            slot_spec,
            pl.BlockSpec((4, 128, WIDTH), lambda t: (t, 0, 0)),
            whole((32, 128)),
            whole((4, 384, WIDTH)),
        ],
        out_specs=(slot_spec, slot_spec, whole((4, 384, WIDTH))),
        scratch_shapes=[
            pltpu.VMEM((WIDTH, WIDTH), BF),
            pltpu.VMEM((512, WIDTH), BF),
            pltpu.VMEM((32, 128), F32),
            pltpu.VMEM((WIDTH, WIDTH), F32),
            pltpu.VMEM((512, WIDTH), F32),
        ],
    )(slots, cot_all.reshape(32, 128, WIDTH), gate_mine, expert_all)
    dxs = exchange(dxs, CTX)
    expert_own = lax.psum_scatter(
        expert_grads.reshape(4 * 384, WIDTH), FSDP, scatter_dimension=0, tiled=True
    ).astype(F32)

    dmid, dmid_low, grad_msg, gain_ffn_part = call(
        kernel_middle_back,
        (
            sds((128, WIDTH), F32),
            sds((128, WIDTH), BF),
            sds((8, 2, 64, 128), BF),
            sds((8, WIDTH), F32),
        ),
        (9e8, 8e6),
        grid=(8,),
        in_specs=[
            slot_spec,
            whole((32, 128)),
            whole((128, WIDTH)),
            whole((128, WIDTH)),
            whole((8, WIDTH)),
            whole((WIDTH, WIDTH)),
        ],
        out_specs=(
            whole((128, WIDTH)),
            whole((128, WIDTH)),
            whole((8, 2, 64, 128)),
            whole((8, WIDTH)),
        ),
        scratch_shapes=[pltpu.VMEM((128, WIDTH), F32)],
    )(dxs, rank, mid, cot, gains, w_out)
    grad_heads = exchange(grad_msg, HEAD_AXES)
    da_all = gather(dmid_low, FSDP)

    ys, grad_heads = lax.optimization_barrier((ys, grad_heads))
    ys = exchange(ys, CTX)
    layer_output = call(
        kernel_output,
        sds((128, WIDTH), BF),
        (1e9, 5e6),
        grid=(8,),
        in_specs=[slot_spec, whole((32, 128)), whole((32, 128)), whole((128, WIDTH))],
        out_specs=whole((128, WIDTH)),
        scratch_shapes=[pltpu.VMEM((128, WIDTH), F32)],
    )(ys, rank, gate, mid)

    dq, dkv = call(
        kernel_attend_back,
        (sds((2048, 128), F32), sds((4, 2, 8, 64, 128), BF)),
        (2e10, 7e6),
        grid=(8,),
        in_specs=[
            SM,
            whole((4096, 128)),
            whole((128, 4096)),
            row_spec,
            msg_spec,
            log_spec,
            row_spec,
        ],
        out_specs=(row_spec, whole((4, 2, 8, 64, 128))),
        scratch_shapes=[pltpu.VMEM((4096, 128), F32)],
    )(mine_ref, keys, turned, queries, grad_heads, log_total, o_rows)
    dkv = exchange(dkv.reshape(4, 1024, 128), ("y",))

    block = 4 * jnp.arange(8, dtype=jnp.int32)[:, None] + mine
    quarter_pos = jnp.concatenate(
        [
            (block * 64 + offset[None, :]).reshape(-1),
            ((63 - block) * 64 + offset[None, :]).reshape(-1),
        ]
    )
    column = jnp.arange(128, dtype=jnp.int32)
    angle = angles(quarter_pos, column % 32)
    sign = jnp.where(column % 64 < 32, -1.0, 1.0)
    cos_heads = jnp.where(column >= 64, 1.0, jnp.cos(angle))
    sin_heads = jnp.where(column >= 64, 0.0, jnp.sin(angle) * sign)
    back = call(
        kernel_slices_back,
        sds((8, 4, 64, 128), BF),
        (4e8, 5e6),
        in_specs=[VM] * 5,
        out_specs=VM,
    )(dkv, dq.reshape(2, 8, 2, 64, 128), cos_heads, sin_heads, head_table)
    back = exchange(back.reshape(32, 64, 128), HEAD_AXES + FSDP)

    da_part = lax.dynamic_slice_in_dim(da_all, part_index * 256, 256, axis=1)
    grads, dh = call(
        kernel_project_back,
        (sds((WIDTH, 896), BF), sds((512, WIDTH), BF)),
        (1.5e9, 8e6),
        in_specs=[VM] * 8,
        out_specs=(VM, VM),
        scratch_shapes=[pltpu.VMEM((512, 512), BF)],
    )(back, x_all, hidden, w_slice, gains, gain_ffn_part, o_all, da_part)
    dh = lax.psum_scatter(dh, FSDP, scatter_dimension=0, tiled=True)
    grads = exchange(grads.reshape(128, 8, 896), ALL)
    grad_qkv, grad_out, grad_gains = call(
        kernel_total,
        (sds((8, 2048), F32), sds((8, WIDTH), F32), sds((8, 128), F32)),
        (1e8, 4e6),
        grid=(4,),
        in_specs=[pl.BlockSpec((8, 4, 8, 896), lambda t: (t, 0, 0, 0)), whole((512, 512))],
        out_specs=(whole((8, 2048)), whole((8, WIDTH)), whole((8, 128))),
        scratch_shapes=[pltpu.VMEM((4, 8, 896), F32)],
    )(grads.reshape(32, 4, 8, 896), slice_table)
    input_grad = call(
        kernel_input_grad,
        sds((128, WIDTH), F32),
        (1e6, 2e6),
        in_specs=[VM] * 4,
        out_specs=VM,
    )(dh, x, dmid, gains)
    return (
        layer_output.reshape(layer_input.shape),
        input_grad.reshape(layer_input.shape),
        grad_gains[:, 0],
        grad_qkv,
        grad_out,
        grad_gains[:, 1],
        expert_own[0:256, 0:512][None],
        expert_own[0:256, 512:1024][None],
        expert_own[256:384][None],
    )


def solution(mesh):
    parts = Mesh(mesh.devices.reshape(4, 2, 4, 2, 2), ALL)
    tokens = P(FSDP, CTX, None, None, None, None)
    experts = P(CTX, FSDP, None)
    in_specs = (
        tokens,
        tokens,
        tokens,
        tokens,
        P(ALL),
        P(ALL, None),
        P(ALL, None),
        P(ALL),
        experts,
        experts,
        experts,
    )
    out_specs = (
        tokens,
        tokens,
        P(ALL),
        P(ALL, None),
        P(ALL, None),
        P(ALL),
        experts,
        experts,
        experts,
    )
    return jax.shard_map(
        on_device, mesh=parts, in_specs=in_specs, out_specs=out_specs, check_vma=False
    )
```

time: 2550 us -> 574 us (0.23)
  waiting for transfers between devices: 2020 us -> 121 us
  matrix products: 168 us -> 0 us
  Pallas kernels: 0 us -> 128 us
  local copies, waits for them, and re-layouts: 107 us -> 15 us
  blocking collectives: 135 us -> 216 us
  other arithmetic: 52.5 us -> 10.5 us
  starting transfers between devices: 33.1 us -> 64.9 us
    reduce_scatter x6 -> x2, waiting for transfers between devices: 1450 us -> 48.1 us  [the longest x1 48.1 us: on_device(): dh = lax.psum_scatter(dh, FSDP, scatter_dimension=0, tiled=True)]
    all_gather x6 -> x5, waiting for transfers between devices: 418 us -> 0.03 us  [gather(): return lax.all_gather(value, axes, axis=0, tiled=True)]
    dot_general x87 -> x0, matrix products: 168 us -> none  [the longest x8 19.3 us: attend_backward(): jnp.einsum('qkgd,tkd->kgqt', grad_grouped, values, preferred_element_type...]
    unnamed x2 -> x0, blocking collectives: 135 us -> none
    pallas_call x0 -> x14, Pallas kernels: none -> 128 us  [the longest x1 30.1 us: on_device(): call(kernel_experts, (sds((32, 64, WIDTH), BF), sds((32, 64, WIDTH), BF),...]
    all_gather x0 -> x1, blocking collectives: none -> 125 us  [gather(): return lax.all_gather(value, axes, axis=0, tiled=True)]
    all_to_all x0 -> x3, blocking collectives: none -> 90.4 us  [exchange(): return lax.all_to_all(value, axes, split_axis=0, concat_axis=0, tiled=True)]
    all_to_all x4 -> x9, waiting for transfers between devices: 155 us -> 70.1 us  [exchange(): return lax.all_to_all(value, axes, split_axis=0, concat_axis=0, tiled=True)]
  transfers between devices with their start and end apart: 16 -> 16, of which waited for: 14 -> 8; matrix products, arithmetic and copies ran while one was open for 6% -> 4% of each run, Pallas kernels for 0% -> 14%
where the time goes in v1:
time: 574 us; the launch traced here: 570 us
  blocking collectives  216 us (38%)
  Pallas kernels  128 us (22%)
  waiting for transfers between devices  121 us (21%)
  starting transfers between devices  64.9 us (11%)
  local copies, waits for them, and re-layouts  15 us (3%)
  between operations  14.4 us (3%)
  other arithmetic  10.5 us (2%)
    all_gather x1, blocking collectives, gather(): return lax.all_gather(value, axes, axis=0, tiled=True)  125 us
    all_to_all x3, blocking collectives, exchange(): return lax.all_to_all(value, axes, split_axis=0, concat_axis=0, tiled=True)  90.4 us
    all_to_all x9, waiting for transfers between devices, exchange(): return lax.all_to_all(value, axes, split_axis=0, concat_axis=0, tiled=True)  70.1 us
    all_to_all x9, starting transfers between devices, exchange(): return lax.all_to_all(value, axes, split_axis=0, concat_axis=0, tiled=True)  64.6 us
    reduce_scatter x1, waiting for transfers between devices, on_device(): dh = lax.psum_scatter(dh, FSDP, scatter_dimension=0, tiled=True)  48.1 us
    pallas_call x1, Pallas kernels, on_device(): call(kernel_experts, (sds((32, 64, WIDTH), BF), sds((32, 64, WIDTH), BF),...  30.1 us
    pallas_call x1, Pallas kernels, on_device(): call(kernel_attend, (sds((8, 2, 64, 128), BF), sds((8, 8, 256), F32), sds...  24.6 us
    pallas_call x1, Pallas kernels, on_device(): call(kernel_attend_back, (sds((2048, 128), F32), sds((4, 2, 8, 64, 128),...  22.8 us
  transfers between devices with their start and end apart: 16, of which 8 were waited for; matrix products, arithmetic and copies ran while one was open for 4% of the time, Pallas kernels for 14%

profile of v1, /device:TPU:1, one launch (start us, length us, event | category | flops | bytes accessed | tf_op | source)
XLA Modules:
  0.0 569.7 jit_solution(13767021404778656168)
XLA Ops:
  16.6 11.5 %all-to-all-start = ((bf16[128,8,640]{2,1,0:T(8,128)(2,1)}), bf16[128,8,640]{2,1,0:T(8,128)(2,1)S(1)}, u32[]{:S(2)}, u32[]{:S(2)}) async-start(bf16[128,8,640]{2,1,0:T(8,128)(2,1)} %bitcast.2), calls=%async_computation | async-start | bytes 2621440 | tf_op jit(solution)/shard_map/all_to_all | solution.py:531
  30.1 20.0 %all-to-all-done = bf16[128,8,640]{2,1,0:T(8,128)(2,1)S(1)} async-done(((bf16[128,8,640]{2,1,0:T(8,128)(2,1)}), bf16[128,8,640]{2,1,0:T(8,128)(2,1)S(1)}, u32[]{:S(2)}, u32[]{:S(2)}) %all-to-all-start) | async-done | bytes 1310752 | tf_op jit(solution)/shard_map/all_to_all | solution.py:531
  51.2 4.2 shard_map.197
  55.4 16.6 %all_to_all.60 = bf16[32,64,128]{2,1,0:T(8,128)(2,1)} all-to-all(bf16[32,64,128]{2,1,0:T(8,128)(2,1)} %get-tuple-element.39), channel_id=1, replica_groups=mesh['x'=4,'zh'=2,'y'=4,'zl'=2,'core'=2] {'x','zh','zl','core'}, dimensions={0} | all-to-all | bytes 1048576 | tf_op jit(solution)/shard_map/all_to_all | solution.py:531
  72.0 3.3 shard_map.198
  75.2 3.5 all-to-all-start.2
  78.8 15.3 %all-to-all-done.2 = bf16[4,1024,128]{2,1,0:T(8,128)(2,1)S(1)} async-done(((bf16[4,1024,128]{2,1,0:T(8,128)(2,1)}), bf16[4,1024,128]{2,1,0:T(8,128)(2,1)S(1)}, u32[]{:S(2)}, u32[]{:S(2)}) %all-to-all-start.2) | async-done | bytes 1048608 | tf_op jit(solution)/shard_map/all_to_all | solution.py:531
  95.7 5.3 all-to-all-start.4
  101.1 24.6 %shard_map.199 = (bf16[8,2,64,128]{3,2,1,0:T(8,128)(2,1)}, f32[8,8,256]{2,1,0:T(8,128)}, f32[2048,128]{1,0:T(8,128)}, bf16[4096,128]{1,0:T(8,128)(2,1)}, bf16[128,4096]{1,0:T(8,128)(2,1)}) custom-call(s32[1]{0:T(128)} %bitcast.mine_ref, bf16[4,2,8,64,128]{4,3,2,1,0:T(8,128)(2,1)} %bitcast.57, bf16[2048,128]{1,0:T(8,128)(2,1)} %bitcast.68), custom_call_target="tpu_custom_call" | custom-call | flops 10000000000 | bytes 5000000 | tf_op jit(solution)/shard_map/pallas_call | solution.py:624
  125.7 7.0 %all-to-all-done.4 = bf16[128,8,1024]{2,1,0:T(8,128)(2,1)S(1)} async-done(((bf16[128,8,1024]{2,1,0:T(8,128)(2,1)}), bf16[128,8,1024]{2,1,0:T(8,128)(2,1)S(1)}, u32[]{:S(2)}, u32[]{:S(2)}) %all-to-all-start.4) | async-done | bytes 2097184 | tf_op jit(solution)/shard_map/all_to_all | solution.py:531
  132.7 3.6 all-to-all-start.3
  139.2 4.6 all-to-all-done.3.o_ref
  144.5 7.0 %shard_map.201 = (bf16[32,64,1024]{2,1,0:T(8,128)(2,1)}, f32[128,1024]{1,0:T(8,128)}) custom-call(bf16[8,2,64,128]{3,2,1,0:T(8,128)(2,1)} %copy-done.4, bf16[1024,1024]{1,0:T(8,128)(2,1)} %bitcast.42, bf16[128,1024]{1,0:T(8,128)(2,1)} %bitcast.54, f32[8,1024]{1,0:T(8,128)} %get-tuple-element.43.gains_ref, f32[32,128]{1,0:T(8,128)} %get-tuple-element.44.rank_ref), custom_call_target="tpu_custom_call" | custom-call | flops 900000000 | bytes 8000000 | tf_op jit(solution)/shard_map/pallas_call | solution.py:641
  151.5 5.0 all-to-all-start.5
  156.6 125.4 %all_gather.20 = f32[1024,128]{1,0:T(8,128)S(1)} all-gather(f32[32,128]{1,0:T(8,128)S(1)} %copy-done.7), channel_id=1, replica_groups=mesh['x'=4,'zh'=2,'y'=4,'zl'=2,'core'=2] {'x','zh','y'}, dimensions={0}, use_global_device_ids=true | all-gather | bytes 540672 | tf_op jit(solution)/shard_map/all_gather | solution.py:535
  282.6 30.1 %shard_map.202 = (bf16[32,64,1024]{2,1,0:T(8,128)(2,1)}, bf16[32,64,1024]{2,1,0:T(8,128)(2,1)}, bf16[4,384,1024]{2,1,0:T(8,128)(2,1)}) custom-call(bf16[32,64,1024]{2,1,0:T(8,128)(2,1)} %all-to-all-done.5.h_ref, bf16[32,128,1024]{2,1,0:T(8,128)(2,1)} %bitcast.65, f32[32,128]{1,0:T(8,128)} %bitcast.64, bf16[4,384,1024]{2,1,0:T(8,128)(2,1)} %bitcast.66), custom_call_target="tpu_custom_call" | custom-call | flops 20000000000 | bytes 30000000 | tf_op jit(solution)/shard_map/pallas_call | solution.py:662
  312.7 41.5 %all_to_all.61.dxs_ref = bf16[32,64,1024]{2,1,0:T(8,128)(2,1)} all-to-all(bf16[32,64,1024]{2,1,0:T(8,128)(2,1)} %get-tuple-element.48), channel_id=1, replica_groups=mesh['x'=4,'zh'=2,'y'=4,'zl'=2,'core'=2] {'x','zh','y'}, dimensions={0} | all-to-all | bytes 8388608 | tf_op jit(solution)/shard_map/all_to_all | solution.py:531
  354.2 8.6 %shard_map.203 = (f32[128,1024]{1,0:T(8,128)}, bf16[128,1024]{1,0:T(8,128)(2,1)}, bf16[8,2,64,128]{3,2,1,0:T(8,128)(2,1)}, f32[8,1024]{1,0:T(8,128)}) custom-call(bf16[32,64,1024]{2,1,0:T(8,128)(2,1)} %all_to_all.61.dxs_ref, f32[32,128]{1,0:T(8,128)} %get-tuple-element.44.rank_ref, f32[128,1024]{1,0:T(8,128)} %get-tuple-element.49.mid_ref, ...), custom_call_target="tpu_custom_call" | custom-call | flops 900000000 | bytes 8000000 | tf_op jit(solution)/shard_map/pallas_call | solution.py:687
  363.5 4.3 all-to-all-start.7
  368.4 6.7 %all-to-all-done.7.grad_ref = bf16[8,2,64,128]{3,2,1,0:T(8,128)(2,1)S(1)} async-done(((bf16[8,2,64,128]{3,2,1,0:T(8,128)(2,1)}), bf16[8,2,64,128]{3,2,1,0:T(8,128)(2,1)S(1)}, u32[]{:S(2)}, u32[]{:S(2)}) %all-to-all-start.7) | async-done | bytes 262176 | tf_op jit(solution)/shard_map/all_to_all | solution.py:531
  375.8 22.8 %shard_map.205 = (f32[2048,128]{1,0:T(8,128)}, bf16[4,2,8,64,128]{4,3,2,1,0:T(8,128)(2,1)}) custom-call(s32[1]{0:T(128)} %bitcast.mine_ref, bf16[4096,128]{1,0:T(8,128)(2,1)} %get-tuple-element.52.keys_ref, bf16[128,4096]{1,0:T(8,128)(2,1)} %get-tuple-element.53.turned_ref, bf16[2048,128]{1,0:T(8,128)(2,1)} %bitcast.69, bf16[8,2,64,128]{3,2,1,0:T(8,128)(2,1)} %copy-done.6, ...), custom_call_target="tpu_custom_call" | custom-call | flops 20000000000 | bytes 7000000 | tf_op jit(solution)/shard_map/pallas_call | solution.py:728
  398.6 4.2 all-to-all-start.9
  406.1 6.5 %all-to-all-done.9.dkv_ref = bf16[4,1024,128]{2,1,0:T(8,128)(2,1)S(1)} async-done(((bf16[4,1024,128]{2,1,0:T(8,128)(2,1)}), bf16[4,1024,128]{2,1,0:T(8,128)(2,1)S(1)}, u32[]{:S(2)}, u32[]{:S(2)}) %all-to-all-start.9) | async-done | bytes 1048608 | tf_op jit(solution)/shard_map/all_to_all | solution.py:531
  413.5 4.3 shard_map.206
  417.8 22.3 %all-to-all-start.10 = ((bf16[32,64,128]{2,1,0:T(8,128)(2,1)}), bf16[32,64,128]{2,1,0:T(8,128)(2,1)S(1)}, u32[]{:S(2)}, u32[]{:S(2)}) async-start(bf16[32,64,128]{2,1,0:T(8,128)(2,1)} %bitcast.48), calls=%async_computation.10 | async-start | bytes 1048576 | tf_op jit(solution)/shard_map/all_to_all | solution.py:531
  441.9 9.9 %all-to-all-done.10.msg_ref = bf16[32,64,128]{2,1,0:T(8,128)(2,1)S(1)} async-done(((bf16[32,64,128]{2,1,0:T(8,128)(2,1)}), bf16[32,64,128]{2,1,0:T(8,128)(2,1)S(1)}, u32[]{:S(2)}, u32[]{:S(2)}) %all-to-all-start.10) | async-done | bytes 524320 | tf_op jit(solution)/shard_map/all_to_all | solution.py:531
  452.6 6.6 %shard_map.207 = (bf16[1024,896]{1,0:T(8,128)(2,1)}, bf16[512,1024]{1,0:T(8,128)(2,1)}) custom-call(bf16[32,64,128]{2,1,0:T(8,128)(2,1)} %copy-done.5, bf16[512,1024]{1,0:T(8,128)(2,1)} %all-gather.6.cloned.1.call-done.x_ref, bf16[512,1024]{1,0:T(8,128)(2,1)} %get-tuple-element.59.hidden_ref, bf16[1024,640]{1,0:T(8,128)(2,1)} %bitcast.46, ...), custom_call_target="tpu_custom_call" | custom-call | flops 1500000000 | bytes 8000000 | tf_op jit(solution)/shard_map/pallas_call | solution.py:769
  459.1 32.3 %all_to_all.62 = bf16[128,8,896]{2,1,0:T(8,128)(2,1)} all-to-all(bf16[128,8,896]{2,1,0:T(8,128)(2,1)} %bitcast.49), channel_id=1, replica_groups=mesh['x'=4,'zh'=2,'y'=4,'zl'=2,'core'=2] {'x','zh','y','zl','core'}, dimensions={0} | all-to-all | bytes 3670016 | tf_op jit(solution)/shard_map/all_to_all | solution.py:531
  491.4 4.9 all-to-all-start.8
  500.3 3.7 shard_map.209
  505.5 48.1 %reduce-scatter.3.cloned.1.call-done.dh_ref = bf16[128,1024]{1,0:T(8,128)(2,1)} async-done(((bf16[512,1024]{1,0:T(8,128)(2,1)}), bf16[128,1024]{1,0:T(8,128)(2,1)}) %reduce-scatter.3.cloned.1.call-update) | async-done | bytes 262160 | tf_op jit(solution)/shard_map/reduce_scatter | solution.py:777
  555.8 7.0 %shard_map.204 = bf16[128,1024]{1,0:T(8,128)(2,1)} custom-call(bf16[32,64,1024]{2,1,0:T(8,128)(2,1)} %all-to-all-done.8.ys_ref, f32[32,128]{1,0:T(8,128)} %get-tuple-element.44.rank_ref, f32[32,128]{1,0:T(8,128)} %get-tuple-element.46.gate_ref, f32[128,1024]{1,0:T(8,128)} %get-tuple-element.49.mid_ref), custom_call_target="tpu_custom_call" | custom-call | flops 1000000000 | bytes 5000000 | tf_op jit(solution)/shard_map/pallas_call | solution.py:718
  (83 shorter events, 34.5 us)
Async XLA Ops:
  7.2 43.0 %all-gather.6.cloned.1.call-start = ((), (), s32[]{:S(2)}) async-start(), calls=%async_computation.14 | async-start | bytes 1310720 | tf_op jit(solution)/shard_map/all_gather | solution.py:535
  7.9 274.7 %all-gather.10.cloned.1.call-start = ((), (), s32[]{:S(2)}) async-start(), calls=%async_computation.16 | async-start | bytes 3932160 | tf_op jit(solution)/shard_map/all_gather | solution.py:535
  9.0 3.1 copy-start.11
  9.0 3.1 copy-start.12
  11.4 271.2 %all-gather.8.cloned.1.call-start = ((), (), s32[]{:S(2)}) async-start(), calls=%async_computation.15 | async-start | bytes 8650752 | tf_op jit(solution)/shard_map/all_gather | solution.py:535
  16.6 33.5 %all-to-all-start = ((bf16[128,8,640]{2,1,0:T(8,128)(2,1)}), bf16[128,8,640]{2,1,0:T(8,128)(2,1)S(1)}, u32[]{:S(2)}, u32[]{:S(2)}) async-start(bf16[128,8,640]{2,1,0:T(8,128)(2,1)} %bitcast.2), calls=%async_computation | async-start | bytes 2621440 | tf_op jit(solution)/shard_map/all_to_all | solution.py:531
  50.1 1.1 copy-start.1
  72.0 6.8 %copy-start.8 = (f32[8,1024]{1,0:T(8,128)S(1)}, f32[8,1024]{1,0:T(8,128)}, u32[]{:S(2)}) copy-start(f32[8,1024]{1,0:T(8,128)} %param.19) | copy-start | bytes 98308
  75.2 18.9 %all-to-all-start.2 = ((bf16[4,1024,128]{2,1,0:T(8,128)(2,1)}), bf16[4,1024,128]{2,1,0:T(8,128)(2,1)S(1)}, u32[]{:S(2)}, u32[]{:S(2)}) async-start(bf16[4,1024,128]{2,1,0:T(8,128)(2,1)} %get-tuple-element.40), calls=%async_computation.2 | async-start | bytes 2097152 | tf_op jit(solution)/shard_map/all_to_all | solution.py:531
  94.1 1.6 copy-start.3
  95.7 37.0 %all-to-all-start.4 = ((bf16[128,8,1024]{2,1,0:T(8,128)(2,1)}), bf16[128,8,1024]{2,1,0:T(8,128)(2,1)S(1)}, u32[]{:S(2)}, u32[]{:S(2)}) async-start(bf16[128,8,1024]{2,1,0:T(8,128)(2,1)} %broadcast_in_dim.105), calls=%async_computation.4 | async-start | bytes 4194304 | tf_op jit(solution)/shard_map/all_to_all | solution.py:531
  101.0 35.3 %copy-start.9 = (s32[1,1,1,2,64,8]{4,5,3,2,1,0:T(8,128)S(1)}, s32[1,1,1,2,64,8]{4,5,3,2,1,0:T(8,128)}, u32[]{:S(2)}) copy-start(s32[1,1,1,2,64,8]{4,5,3,2,1,0:T(8,128)} %param.14) | copy-start | bytes 12292
  101.0 36.0 %copy-start.10 = (f32[1,1,1,2,64,8]{4,5,3,2,1,0:T(8,128)S(1)}, f32[1,1,1,2,64,8]{4,5,3,2,1,0:T(8,128)}, u32[]{:S(2)}) copy-start(f32[1,1,1,2,64,8]{4,5,3,2,1,0:T(8,128)} %param.15) | copy-start | bytes 12292
  132.7 11.1 %copy-start = (bf16[128,8,1024]{2,1,0:T(8,128)(2,1)}, bf16[128,8,1024]{2,1,0:T(8,128)(2,1)S(1)}, u32[]{:S(2)}) copy-start(bf16[128,8,1024]{2,1,0:T(8,128)(2,1)S(1)} %all-to-all-done.4) | copy-start | bytes 6291460
  132.7 11.1 %all-to-all-start.3 = ((bf16[8,2,64,128]{3,2,1,0:T(8,128)(2,1)}), bf16[8,2,64,128]{3,2,1,0:T(8,128)(2,1)S(1)}, u32[]{:S(2)}, u32[]{:S(2)}) async-start(bf16[8,2,64,128]{3,2,1,0:T(8,128)(2,1)} %get-tuple-element.42), calls=%async_computation.3 | async-start | bytes 524288 | tf_op jit(solution)/shard_map/all_to_all | solution.py:531
  143.8 0.7 copy-start.4
  151.5 5.1 copy-start.7
  151.5 131.1 %all-to-all-start.5 = ((bf16[32,64,1024]{2,1,0:T(8,128)(2,1)}), bf16[32,64,1024]{2,1,0:T(8,128)(2,1)}, u32[]{:S(2)}, u32[]{:S(2)}) async-start(bf16[32,64,1024]{2,1,0:T(8,128)(2,1)} %get-tuple-element.45), calls=%async_computation.5 | async-start | bytes 8388608 | tf_op jit(solution)/shard_map/all_to_all | solution.py:531
  156.5 283.6 %all-gather.14.cloned.1.call-start = ((), (), s32[]{:S(2)}) async-start(), calls=%async_computation.18 | async-start | bytes 1310720 | tf_op jit(solution)/shard_map/all_gather | solution.py:535
  362.9 79.0 %all-gather.12.cloned.1.call-start = ((), (), s32[]{:S(2)}) async-start(), calls=%async_computation.17 | async-start | bytes 1310720 | tf_op jit(solution)/shard_map/all_gather | solution.py:535
  363.5 11.6 %all-to-all-start.7 = ((bf16[8,2,64,128]{3,2,1,0:T(8,128)(2,1)}), bf16[8,2,64,128]{3,2,1,0:T(8,128)(2,1)S(1)}, u32[]{:S(2)}, u32[]{:S(2)}) async-start(bf16[8,2,64,128]{3,2,1,0:T(8,128)(2,1)} %get-tuple-element.50), calls=%async_computation.7 | async-start | bytes 524288 | tf_op jit(solution)/shard_map/all_to_all | solution.py:531
  367.8 129.3 %reduce-scatter.5.cloned.1.call-start = ((), (), s32[]{:S(2)}) async-start(), calls=%async_computation.20 | async-start | bytes 3932160 | tf_op jit(solution)/shard_map/reduce_scatter | solution.py:683
  375.1 0.7 copy-start.6
  398.6 14.0 %all-to-all-start.9 = ((bf16[4,1024,128]{2,1,0:T(8,128)(2,1)}), bf16[4,1024,128]{2,1,0:T(8,128)(2,1)S(1)}, u32[]{:S(2)}, u32[]{:S(2)}) async-start(bf16[4,1024,128]{2,1,0:T(8,128)(2,1)} %bitcast.56), calls=%async_computation.9 | async-start | bytes 2097152 | tf_op jit(solution)/shard_map/all_to_all | solution.py:531
  412.6 1.0 copy-start.2
  417.8 33.9 %all-to-all-start.10 = ((bf16[32,64,128]{2,1,0:T(8,128)(2,1)}), bf16[32,64,128]{2,1,0:T(8,128)(2,1)S(1)}, u32[]{:S(2)}, u32[]{:S(2)}) async-start(bf16[32,64,128]{2,1,0:T(8,128)(2,1)} %bitcast.48), calls=%async_computation.10 | async-start | bytes 1048576 | tf_op jit(solution)/shard_map/all_to_all | solution.py:531
  451.8 0.8 copy-start.5
  491.4 64.4 %all-to-all-start.8 = ((bf16[32,64,1024]{2,1,0:T(8,128)(2,1)}), bf16[32,64,1024]{2,1,0:T(8,128)(2,1)}, u32[]{:S(2)}, u32[]{:S(2)}) async-start(bf16[32,64,1024]{2,1,0:T(8,128)(2,1)} %get-tuple-element.51), calls=%async_computation.8 | async-start | bytes 8388608 | tf_op jit(solution)/shard_map/all_to_all | solution.py:531
  496.3 57.3 %reduce-scatter.3.cloned.1.call-start = ((), (), s32[]{:S(2)}) async-start(), calls=%async_computation.19 | async-start | bytes 1310720 | tf_op jit(solution)/shard_map/reduce_scatter | solution.py:777
Sparse Core Ops, SparseCore 0:
  9.7 37.8 all-gather.5
  49.2 44.7 all-gather.9
  97.1 165.2 all-gather.7
  363.0 35.3 all-gather.13
  400.5 21.1 all-gather.11
  423.9 43.3 reduce-scatter.4
  499.5 53.9 reduce-scatter.2

commit v2 on v1

--- a/solution.py
+++ b/solution.py
@@ -93,6 +93,10 @@
     return table
 
 
+def place(part_ref, r, size):
+    return pl.ds(pl.multiple_of(lax.bitwise_xor(part_ref[0], r) * size, size), size)
+
+
 def kernel_route(picks_ref, gates_ref, rank_ref, gate_ref):
     experts = row((32, 128))
     gate = jnp.zeros((32, 128), F32)
@@ -107,7 +111,7 @@
     gate_ref[...] = gate
 
 
-def kernel_slices(w_ref, gains_ref, table_ref, out_ref):
+def kernel_slices(w_ref, gains_ref, table_ref, gate_ref, out_weight_ref, out_ref):
     w = w_ref[...].astype(BF).astype(F32)
     parts = []
     for p in range(4):
@@ -123,21 +127,59 @@
         )
     stacked = jnp.concatenate(parts, axis=0).astype(BF)
     cut = mm(stacked, table_ref[...])
+    columns = []
     for f in range(4):
-        for p in range(4):
-            out_ref[f, :, 128 * p : 128 * p + 128] = cut[
-                8 * p : 8 * p + 8, 128 * f : 128 * f + 128
-            ].astype(BF)
-        out_ref[f, :, 512:640] = gains_ref[...].astype(BF)
-
-
-def kernel_project(x_ref, w_ref, cos_ref, sin_ref, msg_ref, hidden_ref, gains_ref):
+        columns.append(
+            jnp.concatenate(
+                [cut[8 * p : 8 * p + 8, 128 * f : 128 * f + 128] for p in range(4)], axis=1
+            ).astype(BF)
+        )
+    gains = gains_ref[...]
+    left = lane((8, 128)) < 64
+    sub = row((8, 128))
+    for c in range(32):
+        gate = gate_ref[c : c + 1, :]
+        high = gate.astype(BF).astype(F32)
+        middle = (gate - high).astype(BF).astype(F32)
+        rest = gate - high - middle
+        parts = jnp.where(
+            sub < 2, high, jnp.where(sub < 4, middle, jnp.where(sub < 6, rest, 0.0))
+        )
+        parts = jnp.where(sub % 2 == 0, pltpu.roll(parts, 64, 1), parts)
+        last = jnp.where(left, gains, parts).astype(BF)
+        for f in range(4):
+            out_ref[c, f, :, 0:512] = columns[f]
+            out_ref[c, f, :, 512:640] = last
+            out_ref[c, f, :, 640:896] = out_weight_ref[:, 256 * f : 256 * f + 256].astype(BF)
+
+
+def kernel_picks(rank_ref, gate_ref, pick_ref, turned_ref, high_ref, rest_ref):
+    slot = lax.broadcasted_iota(jnp.int32, (64, 128), 0).astype(F32)
+    for p in range(16):
+        picks, weights = [], []
+        for e in (2 * p, 2 * p + 1):
+            hit = slot == rank_ref[e : e + 1, :]
+            picks.append(jnp.where(hit, 1.0, 0.0))
+            weights.append(jnp.where(hit, gate_ref[e : e + 1, :], 0.0))
+        picks = jnp.concatenate(picks, axis=0)
+        weights = jnp.transpose(jnp.concatenate(weights, axis=0))
+        at = slice(128 * p, 128 * p + 128)
+        pick_ref[at, :] = picks.astype(BF)
+        turned_ref[:, at] = jnp.transpose(picks).astype(BF)
+        high = weights.astype(BF)
+        high_ref[:, at] = high
+        rest_ref[:, at] = (weights - high.astype(F32)).astype(BF)
+
+
+def kernel_project(
+    part_ref, x0_ref, x1_ref, x2_ref, x3_ref, w_ref, cos_ref, sin_ref, msg_ref, hidden_ref, gains_ref
+):
     gains = jnp.transpose(w_ref[:, 512:640].astype(F32))
     gains_ref[...] = gains[:8]
-    for s in range(4):
-        x = x_ref[128 * s : 128 * s + 128, :].astype(F32)
+    for r, x_ref in enumerate((x0_ref, x1_ref, x2_ref, x3_ref)):
+        x = x_ref[...].astype(F32)
         scale = lax.rsqrt(jnp.mean(x * x, axis=-1, keepdims=True) + EPSILON)
-        hidden_ref[128 * s : 128 * s + 128, :] = (x * scale * gains[0:1]).astype(BF)
+        hidden_ref[place(part_ref, r, 128), :] = (x * scale * gains[0:1]).astype(BF)
     proj = mm(hidden_ref[...], w_ref[:, 0:512])
     ahead = pltpu.roll(proj, 512 - 8, 1)
     behind = pltpu.roll(proj, 8, 1)
@@ -280,40 +322,79 @@
 
 
 def kernel_middle(
-    o_ref, w_ref, x_ref, gains_ref, rank_ref, slots_ref, mid_ref, rows_ref, hidden_ref
+    part_ref,
+    o_ref,
+    u0_ref,
+    u1_ref,
+    u2_ref,
+    u3_ref,
+    l0_ref,
+    l1_ref,
+    l2_ref,
+    l3_ref,
+    x_ref,
+    gains_ref,
+    pick_ref,
+    slots_ref,
+    mid_ref,
+    rows_ref,
+    hidden_ref,
 ):
     @pl.when(pl.program_id(0) == 0)
     def _():
         for g in range(8):
             rows_ref[:, 128 * g : 128 * g + 128] = o_ref[g].reshape(128, 128)
-        mid = x_ref[...].astype(F32) + mm(rows_ref[...], w_ref[...])
-        mid_ref[...] = mid
+        uppers = (u0_ref, u1_ref, u2_ref, u3_ref)
+        lowers = (l0_ref, l1_ref, l2_ref, l3_ref)
+        for r in range(4):
+            at = place(part_ref, r, 256)
+            mid_ref[:, at] = (
+                x_ref[:, at].astype(F32)
+                + mm(rows_ref[:, 0:512], uppers[r][...])
+                + mm(rows_ref[:, 512:1024], lowers[r][...])
+            )
+        mid = mid_ref[...]
         scale = lax.rsqrt(jnp.mean(mid * mid, axis=-1, keepdims=True) + EPSILON)
         hidden_ref[...] = (mid * scale * gains_ref[1:2]).astype(BF)
 
-    slot = lax.broadcasted_iota(jnp.int32, (64, 128), 0).astype(F32)
-    for j in range(4):
-        rank = rank_ref[pl.ds(4 * pl.program_id(0) + j, 1), :]
-        pick = jnp.where(slot == rank, 1.0, 0.0).astype(BF)
-        slots_ref[j] = mm(pick, hidden_ref[...]).astype(BF)
-
-
-def kernel_experts(
-    h_ref, dy_ref, gate_ref, w_ref, ys_ref, dxs_ref, grad_ref, gu_ref, v_ref, rank_ref, ggu_ref, gv_ref
+    slots_ref[...] = mm(pick_ref[...], hidden_ref[...]).astype(BF).reshape(4, 64, WIDTH)
+
+
+def kernel_experts_ready(
+    part_ref,
+    dy_ref,
+    parts_ref,
+    v0_ref,
+    v1_ref,
+    v2_ref,
+    v3_ref,
+    w0_ref,
+    w1_ref,
+    w2_ref,
+    w3_ref,
+    dys_ref,
+    dact_ref,
+    v_ref,
+    gu_ref,
+    rank_ref,
+    gate_ref,
 ):
     step = pl.program_id(0)
 
     @pl.when(step == 0)
     def _():
-        for f in range(4):
-            gu_ref[256 * f : 256 * f + 256, :] = w_ref[f, 0:256, :]
-            v_ref[128 * f : 128 * f + 128, :] = w_ref[f, 256:384, :]
+        for r, w_ref in enumerate((v0_ref, v1_ref, v2_ref, v3_ref)):
+            v_ref[place(part_ref, r, 128), :] = w_ref[...]
+        for r, w_ref in enumerate((w0_ref, w1_ref, w2_ref, w3_ref)):
+            gu_ref[place(part_ref, r, 256), :] = w_ref[...]
         before = jnp.where(row((128, 128)) < lane((128, 128)), 1.0, 0.0).astype(BF)
+        parts = [parts_ref[:, k, :].astype(F32) for k in range(6)]
+        even = parts[0] + parts[2] + parts[4]
+        odd = parts[1] + parts[3] + parts[5]
+        gate_ref[...] = jnp.where(lane((32, 128)) < 64, pltpu.roll(even, 64, 1), odd)
         chosen = gate_ref[...] > 0.0
         rank = mm(jnp.where(chosen, 1.0, 0.0).astype(BF), before)
         rank_ref[...] = jnp.where(chosen, rank, -1.0)
-        ggu_ref[...] = jnp.zeros_like(ggu_ref)
-        gv_ref[...] = jnp.zeros_like(gv_ref)
 
     slot = lax.broadcasted_iota(jnp.int32, (64, 128), 0).astype(F32)
     grads = []
@@ -326,20 +407,38 @@
         rows = mm(jnp.where(pick, 1.0, 0.0).astype(BF), dy_ref[j])
         grads.append((rows * weight).astype(BF))
     dys = jnp.concatenate(grads, axis=0)
-    h = h_ref[...].reshape(256, WIDTH)
-    both = mm(h, gu_ref[...])
+    dys_ref[...] = dys.reshape(4, 64, WIDTH)
+    dact_ref[...] = mm(dys, v_ref[...], NT)
+
+
+def kernel_experts(h_ref, gu_ref, dact_ref, act_ref, dboth_ref, dxs_ref):
+    both = mm(h_ref[...].reshape(256, WIDTH), gu_ref[...])
     gate_h, up_h = both[:, :512], both[:, 512:]
     sig = jax.nn.sigmoid(gate_h)
     swished = gate_h * sig
-    act = (swished * up_h).astype(BF)
-    ys_ref[...] = mm(act, v_ref[...]).astype(BF).reshape(4, 64, WIDTH)
-    dact = mm(dys, v_ref[...], NT)
+    act_ref[...] = (swished * up_h).astype(BF)
+    dact = dact_ref[...]
     dgate = (dact * up_h * sig * (1.0 + gate_h * (1.0 - sig))).astype(BF)
     dup = (dact * swished).astype(BF)
     dboth = jnp.concatenate([dgate, dup], axis=1)
+    dboth_ref[...] = dboth
     dxs_ref[...] = mm(dboth, gu_ref[...], NT).astype(BF).reshape(4, 64, WIDTH)
-    ggu_ref[...] += mm(h, dboth, TN)
-    gv_ref[...] += mm(act, dys, TN)
+
+
+def kernel_experts_after(
+    h_ref, act_ref, dys_ref, dboth_ref, v_ref, ys_ref, grad_ref, ggu_ref, gv_ref
+):
+    step = pl.program_id(0)
+
+    @pl.when(step == 0)
+    def _():
+        ggu_ref[...] = jnp.zeros_like(ggu_ref)
+        gv_ref[...] = jnp.zeros_like(gv_ref)
+
+    act = act_ref[...]
+    ys_ref[...] = mm(act, v_ref[...]).astype(BF).reshape(4, 64, WIDTH)
+    ggu_ref[...] += mm(h_ref[...].reshape(256, WIDTH), dboth_ref[...], TN)
+    gv_ref[...] += mm(act, dys_ref[...].reshape(256, WIDTH), TN)
 
     @pl.when(step == 7)
     def _():
@@ -349,22 +448,39 @@
 
 
 def kernel_middle_back(
-    dxs_ref, rank_ref, mid_ref, cot_ref, gains_ref, w_ref, dmid_ref, low_ref, msg_ref, ggain_ref, sum_ref
+    part_ref,
+    dxs_ref,
+    pick_ref,
+    mid_ref,
+    cot_ref,
+    gains_ref,
+    u0_ref,
+    u1_ref,
+    u2_ref,
+    u3_ref,
+    l0_ref,
+    l1_ref,
+    l2_ref,
+    l3_ref,
+    dmid_ref,
+    parts_ref,
+    msg_ref,
+    ggain_ref,
+    sum_ref,
+    low_ref,
 ):
     step = pl.program_id(0)
+    part = mm(pick_ref[...], dxs_ref[...].reshape(512, WIDTH))
 
     @pl.when(step == 0)
     def _():
-        sum_ref[...] = jnp.zeros_like(sum_ref)
-
-    slot = lax.broadcasted_iota(jnp.int32, (64, 128), 0).astype(F32)
-    picks = []
-    for j in range(4):
-        picks.append(jnp.where(slot == rank_ref[pl.ds(4 * step + j, 1), :], 1.0, 0.0))
-    picks = jnp.concatenate(picks, axis=0).astype(BF)
-    sum_ref[...] += mm(picks, dxs_ref[...].reshape(256, WIDTH), TN)
-
-    @pl.when(step == 7)
+        sum_ref[...] = part
+
+    @pl.when(step > 0)
+    def _():
+        sum_ref[...] += part
+
+    @pl.when(step == 3)
     def _():
         mid = mid_ref[...]
         scale = lax.rsqrt(jnp.mean(mid * mid, axis=-1, keepdims=True) + EPSILON)
@@ -379,11 +495,31 @@
             - mid * (scale * scale * scale) * jnp.mean(dn * mid, axis=-1, keepdims=True)
         )
         dmid_ref[...] = dmid
-        low = dmid.astype(BF)
-        low_ref[...] = low
-        grad = mm(low, w_ref[...], NT).astype(BF)
-        for g in range(8):
-            msg_ref[g] = grad[:, 128 * g : 128 * g + 128].reshape(2, 64, 128)
+        low_ref[...] = dmid.astype(BF)
+        uppers = (u0_ref, u1_ref, u2_ref, u3_ref)
+        lowers = (l0_ref, l1_ref, l2_ref, l3_ref)
+        for r in range(4):
+            parts_ref[r] = low_ref[:, place(part_ref, r, 256)]
+        for h, w_refs in enumerate((uppers, lowers)):
+            grad = mm(parts_ref[0], w_refs[0][...], NT)
+            for r in range(1, 4):
+                grad = grad + mm(parts_ref[r], w_refs[r][...], NT)
+            grad = grad.astype(BF)
+            for g in range(4):
+                msg_ref[4 * h + g] = grad[:, 128 * g : 128 * g + 128].reshape(2, 64, 128)
+
+
+def kernel_out_weight(
+    o0_ref, o1_ref, o2_ref, o3_ref, da0_ref, da1_ref, da2_ref, da3_ref, gain_ref, grad_ref
+):
+    which = lax.broadcasted_iota(jnp.int32, (128, WIDTH), 0)
+    grad_ref[:, 0:128] = jnp.transpose(jnp.where(which == 1, gain_ref[0:1], 0.0)).astype(BF)
+    pairs = ((o0_ref, da0_ref), (o1_ref, da1_ref), (o2_ref, da2_ref), (o3_ref, da3_ref))
+    for g in range(8):
+        part = jnp.zeros((128, 256), F32)
+        for o_ref, da_ref in pairs:
+            part = part + mm(o_ref[g].reshape(128, 128), da_ref[...], TN)
+        grad_ref[128 * g : 128 * g + 128, 128:384] = part.astype(BF)
 
 
 def kernel_slices_back(dkv_ref, dq_ref, cos_ref, sin_ref, table_ref, msg_ref):
@@ -393,27 +529,27 @@
         )
         return (w * cos - partner * sin).astype(BF)
 
-    cos, sin = cos_ref[...], sin_ref[...]
-    dkv = dkv_ref[0].astype(F32)
-    for y in range(1, 4):
-        dkv = dkv + dkv_ref[y].astype(F32)
-    dkv = unrotate(dkv, cos, sin)
-    parts = [dkv[0:512], dkv[512:1024]]
+    parts = []
     for half in range(2):
-        table_cos = cos[512 * half : 512 * half + 512]
-        table_sin = sin[512 * half : 512 * half + 512]
+        at = slice(512 * half, 512 * half + 512)
+        parts.append(unrotate(dkv_ref[at, :].astype(F32), cos_ref[at, :], sin_ref[at, :]))
+    for half in range(2):
+        at = slice(512 * half, 512 * half + 512)
         for head in range(2):
             parts.append(
-                unrotate(dq_ref[half, :, head].reshape(512, 128), table_cos, table_sin)
+                unrotate(dq_ref[half, :, head].reshape(512, 128), cos_ref[at, :], sin_ref[at, :])
             )
     whole = jnp.concatenate(parts, axis=1)
     for f in range(4):
         msg_ref[:, f] = mm(whole, table_ref[f], NT).astype(BF).reshape(8, 64, 128)
 
 
-def kernel_project_back(
-    msg_ref, x_ref, hidden_ref, w_ref, gains_ref, ggain_ref, o_ref, da_ref, grads_ref, dh_ref, d_ref
-):
+def kernel_hidden_grad(part_ref, d_ref, w_ref, h0_ref, h1_ref, h2_ref, h3_ref):
+    for r, h_ref in enumerate((h0_ref, h1_ref, h2_ref, h3_ref)):
+        h_ref[...] = mm(d_ref[place(part_ref, r, 128), :], w_ref[:, 0:512], NT).astype(BF)
+
+
+def kernel_grads(msg_ref, hidden_ref, w_ref, rest_ref, grads_ref, d_ref):
     low = lane((64, 128)) < 64
     for s in range(4):
         for p in range(4):
@@ -425,24 +561,27 @@
             d_ref[128 * s + 64 : 128 * s + 128, 128 * p : 128 * p + 128] = jnp.where(
                 low, pltpu.roll(even, 64, 1), odd
             ).astype(BF)
-    grads_ref[:, 0:512] = mm(hidden_ref[...], d_ref[...], TN).astype(BF)
-    total = jnp.zeros((1, WIDTH), F32)
-    for s in range(4):
-        part = mm(d_ref[128 * s : 128 * s + 128, :], w_ref[:, 0:512], NT)
-        dh_ref[128 * s : 128 * s + 128, :] = part.astype(BF)
-        x = x_ref[128 * s : 128 * s + 128, :].astype(F32)
-        scale = lax.rsqrt(jnp.mean(x * x, axis=-1, keepdims=True) + EPSILON)
-        total = total + jnp.sum(part * (x * scale), axis=0, keepdims=True)
-    which = lax.broadcasted_iota(jnp.int32, (128, WIDTH), 0)
-    both = jnp.where(which == 0, total, jnp.where(which == 1, ggain_ref[0:1], 0.0))
-    grads_ref[:, 512:640] = jnp.transpose(both).astype(BF)
-    for g in range(8):
-        part = jnp.zeros((128, 256), F32)
-        for s in range(4):
-            part = part + mm(
-                o_ref[s, g].reshape(128, 128), da_ref[128 * s : 128 * s + 128, :], TN
-            )
-        grads_ref[128 * g : 128 * g + 128, 640:896] = part.astype(BF)
+    total = mm(hidden_ref[...], d_ref[...], TN)
+    grads_ref[:, 0:512] = total.astype(BF)
+    gain = jnp.sum(total * w_ref[:, 0:512].astype(F32), axis=1, keepdims=True)
+    gain = gain / w_ref[:, 512:640].astype(F32)[:, 0:1]
+    rest = rest_ref[:, 0:128]
+    grads_ref[:, 512:640] = jnp.where(lane((WIDTH, 128)) == 0, gain.astype(BF), rest)
+    grads_ref[:, 640:896] = rest_ref[:, 128:384]
+
+
+def kernel_input_grad(d0_ref, d1_ref, d2_ref, d3_ref, x_ref, dmid_ref, gains_ref, out_ref):
+    dh = d0_ref[...].astype(F32)
+    for d_ref in (d1_ref, d2_ref, d3_ref):
+        dh = dh + d_ref[...].astype(F32)
+    x = x_ref[...].astype(F32)
+    scale = lax.rsqrt(jnp.mean(x * x, axis=-1, keepdims=True) + EPSILON)
+    dn = dh * gains_ref[0:1]
+    out_ref[...] = (
+        dmid_ref[...]
+        + scale * dn
+        - x * (scale * scale * scale) * jnp.mean(dn * x, axis=-1, keepdims=True)
+    )
 
 
 def kernel_total(parts_ref, table_ref, qkv_ref, out_ref, gains_ref, sum_ref):
@@ -484,36 +623,17 @@
         )
 
 
-def kernel_input_grad(dh_ref, x_ref, dmid_ref, gains_ref, out_ref):
-    x = x_ref[...].astype(F32)
-    scale = lax.rsqrt(jnp.mean(x * x, axis=-1, keepdims=True) + EPSILON)
-    dn = dh_ref[...].astype(F32) * gains_ref[0:1]
-    out_ref[...] = (
-        dmid_ref[...]
-        + scale * dn
-        - x * (scale * scale * scale) * jnp.mean(dn * x, axis=-1, keepdims=True)
-    )
-
-
-def kernel_output(ys_ref, rank_ref, gate_ref, mid_ref, out_ref, sum_ref):
+def kernel_output(ys_ref, high_ref, rest_ref, mid_ref, out_ref, sum_ref):
     step = pl.program_id(0)
 
     @pl.when(step == 0)
     def _():
         sum_ref[...] = mid_ref[...]
 
-    slot = lax.broadcasted_iota(jnp.int32, (64, 128), 0).astype(F32)
-    picks = []
-    for j in range(4):
-        hit = slot == rank_ref[pl.ds(4 * step + j, 1), :]
-        picks.append(jnp.where(hit, gate_ref[pl.ds(4 * step + j, 1), :], 0.0))
-    picks = jnp.concatenate(picks, axis=0)
-    high = picks.astype(BF)
-    rest = (picks - high.astype(F32)).astype(BF)
-    ys = ys_ref[...].reshape(256, WIDTH)
-    sum_ref[...] += mm(high, ys, TN) + mm(rest, ys, TN)
-
-    @pl.when(step == 7)
+    ys = ys_ref[...].reshape(512, WIDTH)
+    sum_ref[...] += mm(high_ref[...], ys) + mm(rest_ref[...], ys)
+
+    @pl.when(step == 3)
     def _():
         out_ref[...] = sum_ref[...].astype(BF)
 
@@ -533,6 +653,25 @@
 
 def gather(value, axes):
     return lax.all_gather(value, axes, axis=0, tiled=True)
+
+
+def after(value, marker):
+    return lax.optimization_barrier((value, marker))[0]
+
+
+def swap(value, axis):
+    return lax.ppermute(value, axis, [(0, 1), (1, 0)])
+
+
+def neighbours(value):
+    return value, swap(value, "core"), swap(value, "zl")
+
+
+def cross(parts):
+    here = [parts[0]]
+    for r in range(1, 4):
+        here.append(lax.ppermute(parts[r], FSDP, [(f, f ^ r) for f in range(4)]))
+    return here
 
 
 def on_device(
@@ -548,16 +687,18 @@
     exp_up,
     exp_down,
 ):
-    head_index = lax.axis_index(HEAD_AXES)
     mine = lax.axis_index("y")
     ctx_index = lax.axis_index(CTX)
     part_index = lax.axis_index(FSDP)
+    mine_ref = mine.astype(jnp.int32).reshape(1)
+    part_ref = part_index.astype(jnp.int32).reshape(1)
     x = layer_input.reshape(128, WIDTH)
     cot = cotangent.reshape(128, WIDTH)
     slice_table = jnp.asarray(slice_matrix(), BF)
     head_table = jnp.asarray(head_matrix(), BF)
 
-    x_all = gather(x, FSDP)
+    cot_all = gather(cot, CTX)
+    x_all = neighbours(x)
     rank, gate = call(
         kernel_route,
         (sds((32, 128), F32), sds((32, 128), F32)),
@@ -571,25 +712,25 @@
     )
     slices = call(
         kernel_slices,
-        sds((4, 8, 640), BF),
-        (2e7, 1e6),
-        in_specs=[VM, VM, VM],
+        sds((32, 4, 8, 896), BF),
+        (2e7, 3e6),
+        in_specs=[VM] * 5,
         out_specs=VM,
-    )(query_key_value_weight, gain_rows, slice_table)
-    slices = jnp.broadcast_to(slices[None], (32, 4, 8, 640)).reshape(128, 8, 640)
-    w_slice = exchange(slices, ALL).reshape(WIDTH, 640)
-    out_copies = jnp.broadcast_to(output_weight.astype(BF)[None], (128, 8, WIDTH))
-    w_out = exchange(out_copies, ALL).reshape(WIDTH, WIDTH)
-    cot_all = gather(cot, CTX)
-    gate_all = gather(gate, CTX).reshape(32, 32, 128)
-    expert_weights = jnp.concatenate(
-        [
-            jnp.concatenate([exp_gate[0], exp_up[0]], axis=1),
-            exp_down[0],
-        ],
-        axis=0,
-    ).astype(BF)
-    expert_all = gather(expert_weights, FSDP).reshape(4, 384, WIDTH)
+    )(query_key_value_weight, gain_rows, slice_table, gate, output_weight)
+    slices, rank, gate, x_all = lax.optimization_barrier((slices, rank, gate, x_all))
+    x_all = x_all + (swap(x_all[2], "core"),)
+    w_slice = exchange(slices.reshape(128, 8, 896), ALL)
+    gate_parts = lax.dynamic_slice(
+        w_slice.reshape(32, 4, 8, 896), (0, part_index, 0, 512), (32, 1, 8, 128)
+    ).reshape(32, 8, 128)
+    w_slice = w_slice.reshape(WIDTH, 896)
+    picks, picks_turned, picks_high, picks_rest = call(
+        kernel_picks,
+        (sds((2048, 128), BF),) + (sds((128, 2048), BF),) * 3,
+        (2e9, 4e6),
+        in_specs=[VM, VM],
+        out_specs=(VM,) * 4,
+    )(rank, gate)
 
     offset = jnp.arange(64, dtype=jnp.int32)
     token_pos = jnp.concatenate([ctx_index * 64 + offset, (63 - ctx_index) * 64 + offset])
@@ -603,9 +744,10 @@
         kernel_project,
         (sds((32, 64, 128), BF), sds((512, WIDTH), BF), sds((8, WIDTH), F32)),
         (6e8, 4e6),
-        in_specs=[VM] * 4,
+        in_specs=[SM] + [VM] * 7,
         out_specs=(VM, VM, VM),
-    )(x_all, w_slice, cos_slice, sin_slice)
+    )(part_ref, *x_all, w_slice, cos_slice, sin_slice)
+    out_upper = neighbours(w_slice[0:512, 640:896])
     msg = exchange(msg, HEAD_AXES + FSDP)
 
     kv_copies, queries = call(
@@ -616,8 +758,30 @@
         out_specs=(VM, VM),
     )(msg.reshape(8, 4, 64, 128), head_table)
     queries = queries.reshape(2048, 128)
+    kv_copies, out_upper = lax.optimization_barrier((kv_copies, out_upper))
+    out_lower = neighbours(after(w_slice[512:1024, 640:896], msg))
     kv = exchange(kv_copies, ("y",)).reshape(4, 2, 8, 64, 128)
-    mine_ref = mine.astype(jnp.int32).reshape(1)
+    block = 4 * jnp.arange(8, dtype=jnp.int32)[:, None] + mine
+    quarter_pos = jnp.concatenate(
+        [
+            (block * 64 + offset[None, :]).reshape(-1),
+            ((63 - block) * 64 + offset[None, :]).reshape(-1),
+        ]
+    )
+    column = jnp.arange(128, dtype=jnp.int32)
+    angle = angles(quarter_pos, column % 32)
+    sign = jnp.where(column % 64 < 32, -1.0, 1.0)
+    cos_heads = jnp.where(column >= 64, 1.0, jnp.cos(angle))
+    sin_heads = jnp.where(column >= 64, 0.0, jnp.sin(angle) * sign)
+    kv, out_lower, cos_heads, sin_heads = lax.optimization_barrier(
+        (kv, out_lower, cos_heads, sin_heads)
+    )
+    downs = neighbours(after(exp_down[0].astype(BF), kv))
+    gate_ups = jnp.concatenate([exp_gate[0], exp_up[0]], axis=1).astype(BF)
+    gate_ups = neighbours(after(gate_ups, kv))
+    out_upper = out_upper + (swap(after(out_upper[2], kv), "core"),)
+    out_lower = out_lower + (swap(out_lower[2], "core"),)
+    w_out = (*out_upper, *out_lower)
     msg_spec = pl.BlockSpec((2, 1, 64, 128), lambda t: (t % 4, t // 4, 0, 0))
     row_spec = pl.BlockSpec((256, 128), lambda t: (t, 0))
     log_spec = pl.BlockSpec((1, 8, 256), lambda t: (t, 0, 0))
@@ -635,96 +799,111 @@
         in_specs=[SM, whole((4, 2, 8, 64, 128)), row_spec],
         out_specs=(msg_spec, log_spec, row_spec, whole((4096, 128)), whole((128, 4096))),
     )(mine_ref, kv, queries)
+    o_msg, w_out, downs, gate_ups = lax.optimization_barrier((o_msg, w_out, downs, gate_ups))
+    downs = downs + (swap(downs[2], "core"),)
+    gate_ups = gate_ups + (swap(gate_ups[2], "core"),)
     o_heads = exchange(o_msg, HEAD_AXES)
-    o_all = gather(o_heads, FSDP).reshape(4, 8, 2, 64, 128)
-
+
+    slot_spec = pl.BlockSpec((4, 64, WIDTH), lambda t: (t, 0, 0))
+    out_specs = [whole((512, 256))] * 8
     slots, mid = call(
         kernel_middle,
         (sds((32, 64, WIDTH), BF), sds((128, WIDTH), F32)),
         (9e8, 8e6),
         grid=(8,),
-        in_specs=[
-            whole((8, 2, 64, 128)),
-            whole((WIDTH, WIDTH)),
+        in_specs=[SM, whole((8, 2, 64, 128))]
+        + out_specs
+        + [
             whole((128, WIDTH)),
             whole((8, WIDTH)),
-            whole((32, 128)),
+            pl.BlockSpec((256, 128), lambda t: (t, 0)),
         ],
-        out_specs=(
-            pl.BlockSpec((4, 64, WIDTH), lambda t: (t, 0, 0)),
-            whole((128, WIDTH)),
+        out_specs=(slot_spec, whole((128, WIDTH))),
+        scratch_shapes=[pltpu.VMEM((128, WIDTH), BF), pltpu.VMEM((128, WIDTH), BF)],
+    )(part_ref, o_heads, *w_out, x, gains, picks)
+    cot_all = after(cot_all, mid)
+    slots, downs, gate_ups = lax.optimization_barrier((slots, downs, gate_ups))
+    o_all = neighbours(after(o_heads, mid))
+    slots = exchange(slots, CTX)
+    dys, dact, down, gate_up = call(
+        kernel_experts_ready,
+        (
+            sds((32, 64, WIDTH), BF),
+            sds((2048, 512), F32),
+            sds((512, WIDTH), BF),
+            sds((WIDTH, WIDTH), BF),
         ),
-        scratch_shapes=[pltpu.VMEM((128, WIDTH), BF), pltpu.VMEM((128, WIDTH), BF)],
-    )(o_heads, w_out, x, gains, rank)
-    slots = exchange(slots, CTX)
-    gate_mine = lax.dynamic_index_in_dim(gate_all, ctx_index, axis=1, keepdims=False)
-    slot_spec = pl.BlockSpec((4, 64, WIDTH), lambda t: (t, 0, 0))
-    ys, dxs, expert_grads = call(
-        kernel_experts,
-        (sds((32, 64, WIDTH), BF), sds((32, 64, WIDTH), BF), sds((4, 384, WIDTH), BF)),
-        (2e10, 3e7),
+        (6e9, 2e7),
         grid=(8,),
         in_specs=[
+            SM,
+            pl.BlockSpec((4, 128, WIDTH), lambda t: (t, 0, 0)),
+            whole((32, 8, 128)),
+        ]
+        + [whole((128, WIDTH))] * 4
+        + [whole((256, WIDTH))] * 4,
+        out_specs=(
             slot_spec,
-            pl.BlockSpec((4, 128, WIDTH), lambda t: (t, 0, 0)),
-            whole((32, 128)),
-            whole((4, 384, WIDTH)),
-        ],
-        out_specs=(slot_spec, slot_spec, whole((4, 384, WIDTH))),
-        scratch_shapes=[
-            pltpu.VMEM((WIDTH, WIDTH), BF),
-            pltpu.VMEM((512, WIDTH), BF),
-            pltpu.VMEM((32, 128), F32),
-            pltpu.VMEM((WIDTH, WIDTH), F32),
-            pltpu.VMEM((512, WIDTH), F32),
-        ],
-    )(slots, cot_all.reshape(32, 128, WIDTH), gate_mine, expert_all)
+            pl.BlockSpec((256, 512), lambda t: (t, 0)),
+            whole((512, WIDTH)),
+            whole((WIDTH, WIDTH)),
+        ),
+        scratch_shapes=[pltpu.VMEM((32, 128), F32), pltpu.VMEM((32, 128), F32)],
+    )(part_ref, cot_all.reshape(32, 128, WIDTH), gate_parts, *downs, *gate_ups)
+    act_spec = pl.BlockSpec((256, 512), lambda t: (t, 0))
+    both_spec = pl.BlockSpec((256, WIDTH), lambda t: (t, 0))
+    act, dboth, dxs = call(
+        kernel_experts,
+        (sds((2048, 512), BF), sds((2048, WIDTH), BF), sds((32, 64, WIDTH), BF)),
+        (9e9, 2e7),
+        grid=(8,),
+        in_specs=[slot_spec, whole((WIDTH, WIDTH)), act_spec],
+        out_specs=(act_spec, both_spec, slot_spec),
+    )(slots, gate_up, dact)
+    ys, expert_grads = call(
+        kernel_experts_after,
+        (sds((32, 64, WIDTH), BF), sds((4, 384, WIDTH), BF)),
+        (9e9, 2e7),
+        grid=(8,),
+        in_specs=[slot_spec, act_spec, slot_spec, both_spec, whole((512, WIDTH))],
+        out_specs=(slot_spec, whole((4, 384, WIDTH))),
+        scratch_shapes=[pltpu.VMEM((WIDTH, WIDTH), F32), pltpu.VMEM((512, WIDTH), F32)],
+    )(slots, act, dys, dboth, down)
+    dxs, o_all = lax.optimization_barrier((dxs, o_all))
+    o_all = o_all + (swap(o_all[2], "core"),)
     dxs = exchange(dxs, CTX)
-    expert_own = lax.psum_scatter(
-        expert_grads.reshape(4 * 384, WIDTH), FSDP, scatter_dimension=0, tiled=True
-    ).astype(F32)
-
-    dmid, dmid_low, grad_msg, gain_ffn_part = call(
+    dxs, ys, expert_grads, o_all = lax.optimization_barrier((dxs, ys, expert_grads, o_all))
+
+    dmid, da_parts, grad_msg, gain_ffn_part = call(
         kernel_middle_back,
         (
             sds((128, WIDTH), F32),
-            sds((128, WIDTH), BF),
+            sds((4, 128, 256), BF),
             sds((8, 2, 64, 128), BF),
             sds((8, WIDTH), F32),
         ),
         (9e8, 8e6),
-        grid=(8,),
+        grid=(4,),
         in_specs=[
-            slot_spec,
-            whole((32, 128)),
+            SM,
+            pl.BlockSpec((8, 64, WIDTH), lambda t: (t, 0, 0)),
+            pl.BlockSpec((128, 512), lambda t: (0, t)),
             whole((128, WIDTH)),
             whole((128, WIDTH)),
             whole((8, WIDTH)),
-            whole((WIDTH, WIDTH)),
-        ],
+        ]
+        + out_specs,
         out_specs=(
             whole((128, WIDTH)),
-            whole((128, WIDTH)),
+            whole((4, 128, 256)),
             whole((8, 2, 64, 128)),
             whole((8, WIDTH)),
         ),
-        scratch_shapes=[pltpu.VMEM((128, WIDTH), F32)],
-    )(dxs, rank, mid, cot, gains, w_out)
+        scratch_shapes=[pltpu.VMEM((128, WIDTH), F32), pltpu.VMEM((128, WIDTH), BF)],
+    )(part_ref, dxs, picks_turned, mid, cot, gains, *w_out)
     grad_heads = exchange(grad_msg, HEAD_AXES)
-    da_all = gather(dmid_low, FSDP)
-
     ys, grad_heads = lax.optimization_barrier((ys, grad_heads))
     ys = exchange(ys, CTX)
-    layer_output = call(
-        kernel_output,
-        sds((128, WIDTH), BF),
-        (1e9, 5e6),
-        grid=(8,),
-        in_specs=[slot_spec, whole((32, 128)), whole((32, 128)), whole((128, WIDTH))],
-        out_specs=whole((128, WIDTH)),
-        scratch_shapes=[pltpu.VMEM((128, WIDTH), F32)],
-    )(ys, rank, gate, mid)
-
     dq, dkv = call(
         kernel_attend_back,
         (sds((2048, 128), F32), sds((4, 2, 8, 64, 128), BF)),
@@ -742,20 +921,36 @@
         out_specs=(row_spec, whole((4, 2, 8, 64, 128))),
         scratch_shapes=[pltpu.VMEM((4096, 128), F32)],
     )(mine_ref, keys, turned, queries, grad_heads, log_total, o_rows)
-    dkv = exchange(dkv.reshape(4, 1024, 128), ("y",))
-
-    block = 4 * jnp.arange(8, dtype=jnp.int32)[:, None] + mine
-    quarter_pos = jnp.concatenate(
-        [
-            (block * 64 + offset[None, :]).reshape(-1),
-            ((63 - block) * 64 + offset[None, :]).reshape(-1),
-        ]
+    da_here = cross(da_parts)
+    dkv = lax.psum_scatter(
+        dkv.reshape(4096, 128), ("y",), scatter_dimension=0, tiled=True
     )
-    column = jnp.arange(128, dtype=jnp.int32)
-    angle = angles(quarter_pos, column % 32)
-    sign = jnp.where(column % 64 < 32, -1.0, 1.0)
-    cos_heads = jnp.where(column >= 64, 1.0, jnp.cos(angle))
-    sin_heads = jnp.where(column >= 64, 0.0, jnp.sin(angle) * sign)
+    dkv, ys, da_here = lax.optimization_barrier((dkv, ys, da_here))
+    expert_own = lax.psum_scatter(
+        after(expert_grads, dkv).reshape(4 * 384, WIDTH), FSDP, scatter_dimension=0, tiled=True
+    ).astype(F32)
+    rest_part = call(
+        kernel_out_weight,
+        sds((WIDTH, 384), BF),
+        (3e8, 2e6),
+        in_specs=[VM] * 9,
+        out_specs=VM,
+    )(*o_all, *da_here, gain_ffn_part)
+    layer_output = call(
+        kernel_output,
+        sds((128, WIDTH), BF),
+        (1e9, 5e6),
+        grid=(4,),
+        in_specs=[
+            pl.BlockSpec((8, 64, WIDTH), lambda t: (t, 0, 0)),
+            pl.BlockSpec((128, 512), lambda t: (0, t)),
+            pl.BlockSpec((128, 512), lambda t: (0, t)),
+            whole((128, WIDTH)),
+        ],
+        out_specs=whole((128, WIDTH)),
+        scratch_shapes=[pltpu.VMEM((128, WIDTH), F32)],
+    )(ys, picks_high, picks_rest, mid)
+
     back = call(
         kernel_slices_back,
         sds((8, 4, 64, 128), BF),
@@ -765,16 +960,28 @@
     )(dkv, dq.reshape(2, 8, 2, 64, 128), cos_heads, sin_heads, head_table)
     back = exchange(back.reshape(32, 64, 128), HEAD_AXES + FSDP)
 
-    da_part = lax.dynamic_slice_in_dim(da_all, part_index * 256, 256, axis=1)
-    grads, dh = call(
-        kernel_project_back,
-        (sds((WIDTH, 896), BF), sds((512, WIDTH), BF)),
-        (1.5e9, 8e6),
-        in_specs=[VM] * 8,
+    grads, d_all = call(
+        kernel_grads,
+        (sds((WIDTH, 896), BF), sds((512, 512), BF)),
+        (6e8, 5e6),
+        in_specs=[VM] * 4,
         out_specs=(VM, VM),
-        scratch_shapes=[pltpu.VMEM((512, 512), BF)],
-    )(back, x_all, hidden, w_slice, gains, gain_ffn_part, o_all, da_part)
-    dh = lax.psum_scatter(dh, FSDP, scatter_dimension=0, tiled=True)
+    )(back, hidden, w_slice, rest_part)
+    dh_parts = call(
+        kernel_hidden_grad,
+        (sds((128, WIDTH), BF),) * 4,
+        (6e8, 5e6),
+        in_specs=[SM, VM, VM],
+        out_specs=(VM,) * 4,
+    )(part_ref, d_all, w_slice)
+    dh_here = cross(dh_parts)
+    input_grad = call(
+        kernel_input_grad,
+        sds((128, WIDTH), F32),
+        (1e6, 2e6),
+        in_specs=[VM] * 7,
+        out_specs=VM,
+    )(*dh_here, x, dmid, gains)
     grads = exchange(grads.reshape(128, 8, 896), ALL)
     grad_qkv, grad_out, grad_gains = call(
         kernel_total,
@@ -785,13 +992,6 @@
         out_specs=(whole((8, 2048)), whole((8, WIDTH)), whole((8, 128))),
         scratch_shapes=[pltpu.VMEM((4, 8, 896), F32)],
     )(grads.reshape(32, 4, 8, 896), slice_table)
-    input_grad = call(
-        kernel_input_grad,
-        sds((128, WIDTH), F32),
-        (1e6, 2e6),
-        in_specs=[VM] * 4,
-        out_specs=VM,
-    )(dh, x, dmid, gains)
     return (
         layer_output.reshape(layer_input.shape),
         input_grad.reshape(layer_input.shape),

time: 574 us -> 493 us (0.86)
  blocking collectives: 216 us -> 15.1 us
  waiting for transfers between devices: 121 us -> 206 us
  Pallas kernels: 128 us -> 146 us
  starting transfers between devices: 64.9 us -> 81.5 us
    all_gather x1 -> x0, blocking collectives: 125 us -> none  [gather(): return lax.all_gather(value, axes, axis=0, tiled=True)]
    all_to_all x3 -> x1, blocking collectives: 90.4 us -> 15.1 us  [exchange(): return lax.all_to_all(value, axes, split_axis=0, concat_axis=0, tiled=True)]
    all_to_all x9, waiting for transfers between devices: 70.1 us -> 131 us  [exchange(): return lax.all_to_all(value, axes, split_axis=0, concat_axis=0, tiled=True)]
    ppermute x0 -> x24, waiting for transfers between devices: none -> 60 us  [the longest x6 46.5 us: cross(): here.append(lax.ppermute(parts[r], FSDP, [(f, f ^ r) for f in range(4)]))]
    reduce_scatter x2, waiting for transfers between devices: 48.1 us -> 14.6 us  [the longest x1 14.6 us: on_device(): lax.psum_scatter(dkv.reshape(4096, 128), ('y',), scatter_dimension=0, til...]
    ppermute x0 -> x24, starting transfers between devices: none -> 23.8 us  [the longest x18 15.1 us: swap(): return lax.ppermute(value, axis, [(0, 1), (1, 0)])]
    pallas_call x4 -> x9, Pallas kernels: 47.2 us -> 66.5 us  [the longest x1 15.9 us: on_device(): call(kernel_experts_after, (sds((32, 64, WIDTH), BF), sds((4, 384, WIDTH)...]
    all_to_all x9, starting transfers between devices: 64.6 us -> 57.6 us  [exchange(): return lax.all_to_all(value, axes, split_axis=0, concat_axis=0, tiled=True)]
  transfers between devices with their start and end apart: 16 -> 36, of which waited for: 8 -> 15; matrix products, arithmetic and copies ran while one was open for 4% -> 3% of each run, Pallas kernels for 14% -> 29%
where the time goes in v2:
time: 493 us; the launch traced here: 490 us
  waiting for transfers between devices  206 us (42%)
  Pallas kernels  146 us (30%)
  starting transfers between devices  81.5 us (17%)
  local copies, waits for them, and re-layouts  17.9 us (4%)
  blocking collectives  15.1 us (3%)
  between operations  14.2 us (3%)
  other arithmetic  9.25 us (2%)
    all_to_all x9, waiting for transfers between devices, exchange(): return lax.all_to_all(value, axes, split_axis=0, concat_axis=0, tiled=True)  131 us
    all_to_all x9, starting transfers between devices, exchange(): return lax.all_to_all(value, axes, split_axis=0, concat_axis=0, tiled=True)  57.6 us
    ppermute x6, waiting for transfers between devices, cross(): here.append(lax.ppermute(parts[r], FSDP, [(f, f ^ r) for f in range(4)]))  46.5 us
    pallas_call x1, Pallas kernels, on_device(): call(kernel_attend, (sds((8, 2, 64, 128), BF), sds((8, 8, 256), F32), sds...  24.6 us
    pallas_call x1, Pallas kernels, on_device(): call(kernel_attend_back, (sds((2048, 128), F32), sds((4, 2, 8, 64, 128),...  22.9 us
    pallas_call x1, Pallas kernels, on_device(): call(kernel_experts_after, (sds((32, 64, WIDTH), BF), sds((4, 384, WIDTH)...  15.9 us
    all_to_all x1, blocking collectives, exchange(): return lax.all_to_all(value, axes, split_axis=0, concat_axis=0, tiled=True)  15.1 us
    ppermute x18, starting transfers between devices, swap(): return lax.ppermute(value, axis, [(0, 1), (1, 0)])  15.1 us
  transfers between devices with their start and end apart: 36, of which 15 were waited for; matrix products, arithmetic and copies ran while one was open for 3% of the time, Pallas kernels for 29%

profile of v2, /device:TPU:1, one launch (start us, length us, event | category | flops | bytes accessed | tf_op | source)
XLA Modules:
  0.0 490.3 jit_solution(8446591736271202109)
XLA Ops:
  19.3 9.9 %all-to-all-start = ((bf16[128,8,896]{2,1,0:T(8,128)(2,1)}), bf16[128,8,896]{2,1,0:T(8,128)(2,1)S(1)}, u32[]{:S(2)}, u32[]{:S(2)}) async-start(bf16[128,8,896]{2,1,0:T(8,128)(2,1)} %bitcast.54), calls=%async_computation | async-start | bytes 3670016 | tf_op jit(solution)/shard_map/all_to_all | solution.py:651
  32.3 25.1 %all-to-all-done = bf16[128,8,896]{2,1,0:T(8,128)(2,1)S(1)} async-done(((bf16[128,8,896]{2,1,0:T(8,128)(2,1)}), bf16[128,8,896]{2,1,0:T(8,128)(2,1)S(1)}, u32[]{:S(2)}, u32[]{:S(2)}) %all-to-all-start) | async-done | bytes 1835040 | tf_op jit(solution)/shard_map/all_to_all | solution.py:651
  58.7 4.6 shard_map.198
  63.3 5.0 %all-to-all-start.1 = ((bf16[32,64,128]{2,1,0:T(8,128)(2,1)}), bf16[32,64,128]{2,1,0:T(8,128)(2,1)S(1)}, u32[]{:S(2)}, u32[]{:S(2)}) async-start(bf16[32,64,128]{2,1,0:T(8,128)(2,1)} %get-tuple-element.123), calls=%async_computation.1 | async-start | bytes 1048576 | tf_op jit(solution)/shard_map/all_to_all | solution.py:651
  71.4 10.1 %all-to-all-done.1 = bf16[32,64,128]{2,1,0:T(8,128)(2,1)S(1)} async-done(((bf16[32,64,128]{2,1,0:T(8,128)(2,1)}), bf16[32,64,128]{2,1,0:T(8,128)(2,1)S(1)}, u32[]{:S(2)}, u32[]{:S(2)}) %all-to-all-start.1) | async-done | bytes 524320 | tf_op jit(solution)/shard_map/all_to_all | solution.py:651
  95.3 11.9 %collective-permute-done.6.l2_ref = bf16[512,256]{1,0:T(8,128)(2,1)} collective-permute-done((bf16[512,256]{1,0:T(8,128)(2,1)S(1)}, bf16[512,256]{1,0:T(8,128)(2,1)}, u32[]{:S(2)}, u32[]{:S(2)}) %collective-permute-start.6) | collective-permute-done | bytes 262176 | tf_op jit(solution)/shard_map/ppermute | solution.py:663
  114.7 24.6 %shard_map.200 = (bf16[8,2,64,128]{3,2,1,0:T(8,128)(2,1)}, f32[8,8,256]{2,1,0:T(8,128)}, f32[2048,128]{1,0:T(8,128)}, bf16[4096,128]{1,0:T(8,128)(2,1)}, bf16[128,4096]{1,0:T(8,128)(2,1)}) custom-call(s32[1]{0:T(128)} %bitcast.mine_ref, bf16[4,2,8,64,128]{4,3,2,1,0:T(8,128)(2,1)} %bitcast.67, bf16[2048,128]{1,0:T(8,128)(2,1)} %bitcast.75), custom_call_target="tpu_custom_call" | custom-call | flops 10000000000 | bytes 5000000 | tf_op jit(solution)/shard_map/pallas_call | solution.py:788
  141.3 6.3 %all-to-all-start.3 = ((bf16[8,2,64,128]{3,2,1,0:T(8,128)(2,1)}), bf16[8,2,64,128]{3,2,1,0:T(8,128)(2,1)S(1)}, u32[]{:S(2)}, u32[]{:S(2)}) async-start(bf16[8,2,64,128]{3,2,1,0:T(8,128)(2,1)} %get-tuple-element.141), calls=%async_computation.3 | async-start | bytes 524288 | tf_op jit(solution)/shard_map/all_to_all | solution.py:651
  150.3 5.5 %all-to-all-done.3.o_ref.o0_ref = bf16[8,2,64,128]{3,2,1,0:T(8,128)(2,1)S(1)} async-done(((bf16[8,2,64,128]{3,2,1,0:T(8,128)(2,1)}), bf16[8,2,64,128]{3,2,1,0:T(8,128)(2,1)S(1)}, u32[]{:S(2)}, u32[]{:S(2)}) %all-to-all-start.3) | async-done | bytes 262176 | tf_op jit(solution)/shard_map/all_to_all | solution.py:651
  156.5 7.9 %shard_map.202 = (bf16[32,64,1024]{2,1,0:T(8,128)(2,1)}, f32[128,1024]{1,0:T(8,128)}) custom-call(s32[1]{0:T(128)} %bitcast.1.part_ref, bf16[8,2,64,128]{3,2,1,0:T(8,128)(2,1)} %copy-done.6, bf16[512,256]{1,0:T(8,128)(2,1)} %copy-done.5, bf16[512,256]{1,0:T(8,128)(2,1)} %copy-done.12, bf16[512,256]{1,0:T(8,128)(2,1)} %copy-done.13, ...), custom_call_target="tpu_custom_call" | custom-call | flops 900000000 | bytes 8000000 | tf_op jit(solution)/shard_map/pallas_call | solution.py:809
  165.3 5.8 %all-to-all-start.4 = ((bf16[32,64,1024]{2,1,0:T(8,128)(2,1)}), bf16[32,64,1024]{2,1,0:T(8,128)(2,1)}, u32[]{:S(2)}, u32[]{:S(2)}) async-start(bf16[32,64,1024]{2,1,0:T(8,128)(2,1)} %get-tuple-element.161), calls=%async_computation.4 | async-start | bytes 8388608 | tf_op jit(solution)/shard_map/all_to_all | solution.py:651
  174.0 12.4 %shard_map.203 = (bf16[32,64,1024]{2,1,0:T(8,128)(2,1)}, f32[2048,512]{1,0:T(8,128)}, bf16[512,1024]{1,0:T(8,128)(2,1)}, bf16[1024,1024]{1,0:T(8,128)(2,1)}) custom-call(s32[1]{0:T(128)} %bitcast.1.part_ref, bf16[32,128,1024]{2,1,0:T(8,128)(2,1)} %bitcast.74, bf16[32,8,128]{2,1,0:T(8,128)(2,1)} %dynamic-slice_bitcast_fusion.parts_ref, ...), custom_call_target="tpu_custom_call" | custom-call | flops 6000000000 | bytes 20000000 | tf_op jit(solution)/shard_map/pallas_call | solution.py:828
  186.4 41.3 %all-to-all-done.4.h_ref = bf16[32,64,1024]{2,1,0:T(8,128)(2,1)} async-done(((bf16[32,64,1024]{2,1,0:T(8,128)(2,1)}), bf16[32,64,1024]{2,1,0:T(8,128)(2,1)}, u32[]{:S(2)}, u32[]{:S(2)}) %all-to-all-start.4) | async-done | bytes 4194336 | tf_op jit(solution)/shard_map/all_to_all | solution.py:651
  227.7 14.4 %shard_map.204 = (bf16[2048,512]{1,0:T(8,128)(2,1)}, bf16[2048,1024]{1,0:T(8,128)(2,1)}, bf16[32,64,1024]{2,1,0:T(8,128)(2,1)}) custom-call(bf16[32,64,1024]{2,1,0:T(8,128)(2,1)} %all-to-all-done.4.h_ref, bf16[1024,1024]{1,0:T(8,128)(2,1)} %get-tuple-element.172.gu_ref, f32[2048,512]{1,0:T(8,128)} %get-tuple-element.173.dact_ref), custom_call_target="tpu_custom_call" | custom-call | flops 8999999488 | bytes 20000000 | tf_op jit(solution)/shard_map/pallas_call | solution.py:855
  242.8 8.4 %all-to-all-start.5 = ((bf16[32,64,1024]{2,1,0:T(8,128)(2,1)}), bf16[32,64,1024]{2,1,0:T(8,128)(2,1)}, u32[]{:S(2)}, u32[]{:S(2)}) async-start(bf16[32,64,1024]{2,1,0:T(8,128)(2,1)} %get-tuple-element.176), calls=%async_computation.5 | async-start | bytes 8388608 | tf_op jit(solution)/shard_map/all_to_all | solution.py:651
  253.3 15.9 %shard_map.205 = (bf16[32,64,1024]{2,1,0:T(8,128)(2,1)}, bf16[4,384,1024]{2,1,0:T(8,128)(2,1)}) custom-call(bf16[32,64,1024]{2,1,0:T(8,128)(2,1)} %all-to-all-done.4.h_ref, bf16[2048,512]{1,0:T(8,128)(2,1)} %get-tuple-element.177.act_ref, bf16[32,64,1024]{2,1,0:T(8,128)(2,1)} %get-tuple-element.178.dys_ref, bf16[2048,1024]{1,0:T(8,128)(2,1)} %get-tuple-element.179.dboth_ref, ...), custom_call_target="tpu_custom_call" | custom-call | flops 8999999488 | bytes 20000000 | tf_op jit(solution)/shard_map/pallas_call | solution.py:863
  269.3 37.0 %all-to-all-done.5.dxs_ref = bf16[32,64,1024]{2,1,0:T(8,128)(2,1)} async-done(((bf16[32,64,1024]{2,1,0:T(8,128)(2,1)}), bf16[32,64,1024]{2,1,0:T(8,128)(2,1)}, u32[]{:S(2)}, u32[]{:S(2)}) %all-to-all-start.5) | async-done | bytes 4194336 | tf_op jit(solution)/shard_map/all_to_all | solution.py:651
  306.2 6.6 %shard_map.206 = (f32[128,1024]{1,0:T(8,128)}, bf16[4,128,256]{2,1,0:T(8,128)(2,1)}, bf16[8,2,64,128]{3,2,1,0:T(8,128)(2,1)}, f32[8,1024]{1,0:T(8,128)}) custom-call(s32[1]{0:T(128)} %bitcast.1.part_ref, bf16[32,64,1024]{2,1,0:T(8,128)(2,1)} %all-to-all-done.5.dxs_ref, bf16[128,2048]{1,0:T(8,128)(2,1)} %get-tuple-element.188.pick_ref, ...), custom_call_target="tpu_custom_call" | custom-call | flops 900000000 | bytes 8000000 | tf_op jit(solution)/shard_map/pallas_call | solution.py:877
  312.8 15.1 %all_to_all.50.grad_ref = bf16[8,2,64,128]{3,2,1,0:T(8,128)(2,1)} all-to-all(bf16[8,2,64,128]{3,2,1,0:T(8,128)(2,1)} %get-tuple-element.189), channel_id=1, replica_groups=mesh['x'=4,'zh'=2,'y'=4,'zl'=2,'core'=2] {'x','zh'}, dimensions={0} | all-to-all | bytes 524288 | tf_op jit(solution)/shard_map/all_to_all | solution.py:651
  328.0 5.1 %all-to-all-start.7 = ((bf16[32,64,1024]{2,1,0:T(8,128)(2,1)}), bf16[32,64,1024]{2,1,0:T(8,128)(2,1)}, u32[]{:S(2)}, u32[]{:S(2)}) async-start(bf16[32,64,1024]{2,1,0:T(8,128)(2,1)} %get-tuple-element.194), calls=%async_computation.8 | async-start | bytes 8388608 | tf_op jit(solution)/shard_map/all_to_all | solution.py:651
  333.2 22.9 %shard_map.207 = (f32[2048,128]{1,0:T(8,128)}, bf16[4,2,8,64,128]{4,3,2,1,0:T(8,128)(2,1)}) custom-call(s32[1]{0:T(128)} %bitcast.mine_ref, bf16[4096,128]{1,0:T(8,128)(2,1)} %get-tuple-element.129.keys_ref, bf16[128,4096]{1,0:T(8,128)(2,1)} %get-tuple-element.130.turned_ref, bf16[2048,128]{1,0:T(8,128)(2,1)} %bitcast.76, ...), custom_call_target="tpu_custom_call" | custom-call | flops 20000000000 | bytes 7000000 | tf_op jit(solution)/shard_map/pallas_call | solution.py:907
  356.8 4.4 collective-permute-start.18
  362.8 15.5 %collective-permute-done.19.da2_ref = bf16[128,256]{1,0:T(8,128)(2,1)S(1)} collective-permute-done((bf16[128,256]{1,0:T(8,128)(2,1)S(1)}, bf16[128,256]{1,0:T(8,128)(2,1)S(1)}, u32[]{:S(2)}, u32[]{:S(2)}) %collective-permute-start.19) | collective-permute-done | bytes 65568 | tf_op jit(solution)/shard_map/ppermute | solution.py:673
  380.7 14.6 %reduce-scatter.3.cloned.1.call-done.dkv_ref = bf16[1024,128]{1,0:T(8,128)(2,1)} async-done(((bf16[4096,128]{1,0:T(8,128)(2,1)}), bf16[1024,128]{1,0:T(8,128)(2,1)}) %reduce-scatter.3.cloned.1.call-update) | async-done | bytes 262160 | tf_op jit(solution)/shard_map/reduce_scatter | solution.py:925
  395.3 4.0 shard_map.209
  399.3 7.9 %all-to-all-start.8 = ((bf16[32,64,128]{2,1,0:T(8,128)(2,1)}), bf16[32,64,128]{2,1,0:T(8,128)(2,1)S(1)}, u32[]{:S(2)}, u32[]{:S(2)}) async-start(bf16[32,64,128]{2,1,0:T(8,128)(2,1)} %bitcast.57), calls=%async_computation.9 | async-start | bytes 1048576 | tf_op jit(solution)/shard_map/all_to_all | solution.py:651
  410.1 8.7 %all-to-all-done.8.msg_ref = bf16[32,64,128]{2,1,0:T(8,128)(2,1)S(1)} async-done(((bf16[32,64,128]{2,1,0:T(8,128)(2,1)}), bf16[32,64,128]{2,1,0:T(8,128)(2,1)S(1)}, u32[]{:S(2)}, u32[]{:S(2)}) %all-to-all-start.8) | async-done | bytes 524320 | tf_op jit(solution)/shard_map/all_to_all | solution.py:651
  419.6 5.3 %shard_map.211 = (bf16[1024,896]{1,0:T(8,128)(2,1)}, bf16[512,512]{1,0:T(8,128)(2,1)}) custom-call(bf16[32,64,128]{2,1,0:T(8,128)(2,1)} %copy-done.2, bf16[512,1024]{1,0:T(8,128)(2,1)} %get-tuple-element.203.hidden_ref, bf16[1024,896]{1,0:T(8,128)(2,1)} %bitcast.52, bf16[1024,384]{1,0:T(8,128)(2,1)} %shard_map.210.rest_ref), custom_call_target="tpu_custom_call" | custom-call | flops 600000000 | bytes 5000000 | tf_op jit(solution)/shard_map/pallas_call | solution.py:963
  424.9 5.7 %all-to-all-start.9 = ((bf16[128,8,896]{2,1,0:T(8,128)(2,1)}), bf16[128,8,896]{2,1,0:T(8,128)(2,1)S(1)}, u32[]{:S(2)}, u32[]{:S(2)}) async-start(bf16[128,8,896]{2,1,0:T(8,128)(2,1)} %bitcast.58), calls=%async_computation.10 | async-start | bytes 3670016 | tf_op jit(solution)/shard_map/all_to_all | solution.py:651
  437.2 5.0 %shard_map.208 = bf16[128,1024]{1,0:T(8,128)(2,1)} custom-call(bf16[32,64,1024]{2,1,0:T(8,128)(2,1)} %all-to-all-done.7.ys_ref, bf16[128,2048]{1,0:T(8,128)(2,1)} %get-tuple-element.197.high_ref, bf16[128,2048]{1,0:T(8,128)(2,1)} %get-tuple-element.198.rest_ref, f32[128,1024]{1,0:T(8,128)} %get-tuple-element.162.mid_ref), custom_call_target="tpu_custom_call" | custom-call | flops 1000000000 | bytes 5000000 | tf_op jit(solution)/shard_map/pallas_call | solution.py:939
  442.2 22.9 %collective-permute-done.22.d2_ref = bf16[128,1024]{1,0:T(8,128)(2,1)S(1)} collective-permute-done((bf16[128,1024]{1,0:T(8,128)(2,1)}, bf16[128,1024]{1,0:T(8,128)(2,1)S(1)}, u32[]{:S(2)}, u32[]{:S(2)}) %collective-permute-start.22) | collective-permute-done | bytes 262176 | tf_op jit(solution)/shard_map/ppermute | solution.py:673
  465.2 5.7 %collective-permute-done.23.d3_ref = bf16[128,1024]{1,0:T(8,128)(2,1)S(1)} collective-permute-done((bf16[128,1024]{1,0:T(8,128)(2,1)}, bf16[128,1024]{1,0:T(8,128)(2,1)S(1)}, u32[]{:S(2)}, u32[]{:S(2)}) %collective-permute-start.23) | collective-permute-done | bytes 262176 | tf_op jit(solution)/shard_map/ppermute | solution.py:673
  (165 shorter events, 80.6 us)
Async XLA Ops:
  7.2 166.8 %all-gather.2.cloned.1.call-start = ((), (), s32[]{:S(2)}) async-start(), calls=%async_computation.12 | async-start | bytes 8650752 | tf_op jit(solution)/shard_map/all_gather | solution.py:655
  7.9 11.4 %collective-permute-start = (bf16[128,1024]{1,0:T(8,128)(2,1)}, bf16[128,1024]{1,0:T(8,128)(2,1)S(1)}, u32[]{:S(2)}, u32[]{:S(2)}) collective-permute-start(bf16[128,1024]{1,0:T(8,128)(2,1)} %bitcast.60), channel_id=1, source_target_pairs={{0,1},{1,0},{2,3},{3,2},{4,5},{5,4},{6,7},{7,6},{8,9},{9,8},{10,11... | collective-permute-start | bytes 786440 | tf_op jit(solution)/shard_map/ppermute | solution.py:663
  9.4 9.9 %collective-permute-start.1 = (bf16[128,1024]{1,0:T(8,128)(2,1)}, bf16[128,1024]{1,0:T(8,128)(2,1)S(1)}, u32[]{:S(2)}, u32[]{:S(2)}) collective-permute-start(bf16[128,1024]{1,0:T(8,128)(2,1)} %bitcast.61), channel_id=1, source_target_pairs={{0,2},{2,0},{1,3},{3,1},{4,6},{6,4},{5,7},{7,5},{8,10},{10,8},{9,1... | collective-permute-start | bytes 786440 | tf_op jit(solution)/shard_map/ppermute | solution.py:663
  19.3 38.2 %all-to-all-start = ((bf16[128,8,896]{2,1,0:T(8,128)(2,1)}), bf16[128,8,896]{2,1,0:T(8,128)(2,1)S(1)}, u32[]{:S(2)}, u32[]{:S(2)}) async-start(bf16[128,8,896]{2,1,0:T(8,128)(2,1)} %bitcast.54), calls=%async_computation | async-start | bytes 3670016 | tf_op jit(solution)/shard_map/all_to_all | solution.py:651
  63.3 18.2 %all-to-all-start.1 = ((bf16[32,64,128]{2,1,0:T(8,128)(2,1)}), bf16[32,64,128]{2,1,0:T(8,128)(2,1)S(1)}, u32[]{:S(2)}, u32[]{:S(2)}) async-start(bf16[32,64,128]{2,1,0:T(8,128)(2,1)} %get-tuple-element.123), calls=%async_computation.1 | async-start | bytes 1048576 | tf_op jit(solution)/shard_map/all_to_all | solution.py:651
  69.4 16.1 %collective-permute-start.3 = (bf16[512,256]{1,0:T(8,128)(2,1)S(1)}, bf16[512,256]{1,0:T(8,128)(2,1)S(1)}, u32[]{:S(2)}, u32[]{:S(2)}) collective-permute-start(bf16[512,256]{1,0:T(8,128)(2,1)S(1)} %get-tuple-element.142.u0_ref), channel_id=1, source_target_pairs={{0,1},{1,0},{2,3},{3,2},{4,5},{5,4},{6,7},{7,6},{8,9},{9,8},{10,11... | collective-permute-start | bytes 786440 | tf_op jit(solution)/shard_map/ppermute | solution.py:663
  69.7 15.8 %collective-permute-start.4 = (bf16[512,256]{1,0:T(8,128)(2,1)S(1)}, bf16[512,256]{1,0:T(8,128)(2,1)S(1)}, u32[]{:S(2)}, u32[]{:S(2)}) collective-permute-start(bf16[512,256]{1,0:T(8,128)(2,1)S(1)} %get-tuple-element.142.u0_ref), channel_id=1, source_target_pairs={{0,2},{2,0},{1,3},{3,1},{4,6},{6,4},{5,7},{7,5},{8,10},{10,8},{9,1... | collective-permute-start | bytes 786440 | tf_op jit(solution)/shard_map/ppermute | solution.py:663
  86.2 23.8 %all-to-all-start.2 = ((bf16[4,1024,128]{2,1,0:T(8,128)(2,1)}), bf16[4,1024,128]{2,1,0:T(8,128)(2,1)S(1)}, u32[]{:S(2)}, u32[]{:S(2)}) async-start(bf16[4,1024,128]{2,1,0:T(8,128)(2,1)} %get-tuple-element.125), calls=%async_computation.2 | async-start | bytes 2097152 | tf_op jit(solution)/shard_map/all_to_all | solution.py:651
  93.4 13.8 %collective-permute-start.6 = (bf16[512,256]{1,0:T(8,128)(2,1)S(1)}, bf16[512,256]{1,0:T(8,128)(2,1)}, u32[]{:S(2)}, u32[]{:S(2)}) collective-permute-start(bf16[512,256]{1,0:T(8,128)(2,1)S(1)} %get-tuple-element.146.l0_ref), channel_id=1, source_target_pairs={{0,2},{2,0},{1,3},{3,1},{4,6},{6,4},{5,7},{7,5},{8,10},{10,8},{9,1... | collective-permute-start | bytes 786440 | tf_op jit(solution)/shard_map/ppermute | solution.py:663
  112.0 28.6 %collective-permute-start.11 = (bf16[256,1024]{1,0:T(8,128)(2,1)S(1)}, bf16[256,1024]{1,0:T(8,128)(2,1)S(1)}, u32[]{:S(2)}, u32[]{:S(2)}) collective-permute-start(bf16[256,1024]{1,0:T(8,128)(2,1)S(1)} %pad_maximum_fusion.w0_ref), channel_id=1, source_target_pairs={{0,1},{1,0},{2,3},{3,2},{4,5},{5,4},{6,7},{7,6},{8,9},{9,8},{10,11... | collective-permute-start | bytes 1572872 | tf_op jit(solution)/shard_map/ppermute | solution.py:663
  112.3 28.4 %collective-permute-start.12 = (bf16[256,1024]{1,0:T(8,128)(2,1)S(1)}, bf16[256,1024]{1,0:T(8,128)(2,1)}, u32[]{:S(2)}, u32[]{:S(2)}) collective-permute-start(bf16[256,1024]{1,0:T(8,128)(2,1)S(1)} %pad_maximum_fusion.w0_ref), channel_id=1, source_target_pairs={{0,2},{2,0},{1,3},{3,1},{4,6},{6,4},{5,7},{7,5},{8,10},{10,8},{9,1... | collective-permute-start | bytes 1572872 | tf_op jit(solution)/shard_map/ppermute | solution.py:663
  113.6 27.0 %collective-permute-start.10 = (bf16[128,1024]{1,0:T(8,128)(2,1)S(1)}, bf16[128,1024]{1,0:T(8,128)(2,1)S(1)}, u32[]{:S(2)}, u32[]{:S(2)}) collective-permute-start(bf16[128,1024]{1,0:T(8,128)(2,1)S(1)} %convert_bitcast_fusion.2.v0_ref), channel_id=1, source_target_pairs={{0,2},{2,0},{1,3},{3,1},{4,6},{6,4},{5,7},{7,5},{8,10},{10,8},{9,1... | collective-permute-start | bytes 786440 | tf_op jit(solution)/shard_map/ppermute | solution.py:663
  113.8 26.9 %collective-permute-start.9 = (bf16[128,1024]{1,0:T(8,128)(2,1)S(1)}, bf16[128,1024]{1,0:T(8,128)(2,1)S(1)}, u32[]{:S(2)}, u32[]{:S(2)}) collective-permute-start(bf16[128,1024]{1,0:T(8,128)(2,1)S(1)} %convert_bitcast_fusion.2.v0_ref), channel_id=1, source_target_pairs={{0,1},{1,0},{2,3},{3,2},{4,5},{5,4},{6,7},{7,6},{8,9},{9,8},{10,11... | collective-permute-start | bytes 786440 | tf_op jit(solution)/shard_map/ppermute | solution.py:663
  114.6 26.0 %collective-permute-start.8 = (bf16[512,256]{1,0:T(8,128)(2,1)}, bf16[512,256]{1,0:T(8,128)(2,1)S(1)}, u32[]{:S(2)}, u32[]{:S(2)}) collective-permute-start(bf16[512,256]{1,0:T(8,128)(2,1)} %collective-permute-done.6.l2_ref), channel_id=1, source_target_pairs={{0,1},{1,0},{2,3},{3,2},{4,5},{5,4},{6,7},{7,6},{8,9},{9,8},{10,11... | collective-permute-start | bytes 786440 | tf_op jit(solution)/shard_map/ppermute | solution.py:663
  140.7 23.8 %collective-permute-start.14 = (bf16[256,1024]{1,0:T(8,128)(2,1)}, bf16[256,1024]{1,0:T(8,128)(2,1)S(1)}, u32[]{:S(2)}, u32[]{:S(2)}) collective-permute-start(bf16[256,1024]{1,0:T(8,128)(2,1)} %collective-permute-done.12.w2_ref), channel_id=1, source_target_pairs={{0,1},{1,0},{2,3},{3,2},{4,5},{5,4},{6,7},{7,6},{8,9},{9,8},{10,11... | collective-permute-start | bytes 1572872 | tf_op jit(solution)/shard_map/ppermute | solution.py:663
  141.3 14.5 %all-to-all-start.3 = ((bf16[8,2,64,128]{3,2,1,0:T(8,128)(2,1)}), bf16[8,2,64,128]{3,2,1,0:T(8,128)(2,1)S(1)}, u32[]{:S(2)}, u32[]{:S(2)}) async-start(bf16[8,2,64,128]{3,2,1,0:T(8,128)(2,1)} %get-tuple-element.141), calls=%async_computation.3 | async-start | bytes 524288 | tf_op jit(solution)/shard_map/all_to_all | solution.py:651
  147.6 16.9 %collective-permute-start.13 = (bf16[128,1024]{1,0:T(8,128)(2,1)S(1)}, bf16[128,1024]{1,0:T(8,128)(2,1)S(1)}, u32[]{:S(2)}, u32[]{:S(2)}) collective-permute-start(bf16[128,1024]{1,0:T(8,128)(2,1)S(1)} %collective-permute-done.10.v2_ref), channel_id=1, source_target_pairs={{0,1},{1,0},{2,3},{3,2},{4,5},{5,4},{6,7},{7,6},{8,9},{9,8},{10,11... | collective-permute-start | bytes 786440 | tf_op jit(solution)/shard_map/ppermute | solution.py:663
  165.3 62.4 %all-to-all-start.4 = ((bf16[32,64,1024]{2,1,0:T(8,128)(2,1)}), bf16[32,64,1024]{2,1,0:T(8,128)(2,1)}, u32[]{:S(2)}, u32[]{:S(2)}) async-start(bf16[32,64,1024]{2,1,0:T(8,128)(2,1)} %get-tuple-element.161), calls=%async_computation.4 | async-start | bytes 8388608 | tf_op jit(solution)/shard_map/all_to_all | solution.py:651
  172.6 69.5 %collective-permute-start.15 = (bf16[8,2,64,128]{3,2,1,0:T(8,128)(2,1)S(1)}, bf16[8,2,64,128]{3,2,1,0:T(8,128)(2,1)S(1)}, u32[]{:S(2)}, u32[]{:S(2)}) collective-permute-start(bf16[8,2,64,128]{3,2,1,0:T(8,128)(2,1)S(1)} %copy-done.7), channel_id=1, source_target_pairs={{0,1},{1,0},{2,3},{3,2},{4,5},{5,4},{6,7},{7,6},{8,9},{9,8},{10,11... | collective-permute-start | bytes 786440 | tf_op jit(solution)/shard_map/ppermute | solution.py:663
  174.0 68.1 %collective-permute-start.16 = (bf16[8,2,64,128]{3,2,1,0:T(8,128)(2,1)S(1)}, bf16[8,2,64,128]{3,2,1,0:T(8,128)(2,1)S(1)}, u32[]{:S(2)}, u32[]{:S(2)}) collective-permute-start(bf16[8,2,64,128]{3,2,1,0:T(8,128)(2,1)S(1)} %copy-done.7), channel_id=1, source_target_pairs={{0,2},{2,0},{1,3},{3,1},{4,6},{6,4},{5,7},{7,5},{8,10},{10,8},{9,1... | collective-permute-start | bytes 786440 | tf_op jit(solution)/shard_map/ppermute | solution.py:663
  242.8 63.5 %all-to-all-start.5 = ((bf16[32,64,1024]{2,1,0:T(8,128)(2,1)}), bf16[32,64,1024]{2,1,0:T(8,128)(2,1)}, u32[]{:S(2)}, u32[]{:S(2)}) async-start(bf16[32,64,1024]{2,1,0:T(8,128)(2,1)} %get-tuple-element.176), calls=%async_computation.5 | async-start | bytes 8388608 | tf_op jit(solution)/shard_map/all_to_all | solution.py:651
  251.2 18.0 %collective-permute-start.17 = (bf16[8,2,64,128]{3,2,1,0:T(8,128)(2,1)S(1)}, bf16[8,2,64,128]{3,2,1,0:T(8,128)(2,1)S(1)}, u32[]{:S(2)}, u32[]{:S(2)}) collective-permute-start(bf16[8,2,64,128]{3,2,1,0:T(8,128)(2,1)S(1)} %collective-permute-done.16.o2_ref), channel_id=1, source_target_pairs={{0,1},{1,0},{2,3},{3,2},{4,5},{5,4},{6,7},{7,6},{8,9},{9,8},{10,11... | collective-permute-start | bytes 786440 | tf_op jit(solution)/shard_map/ppermute | solution.py:663
  328.0 67.3 %all-to-all-start.7 = ((bf16[32,64,1024]{2,1,0:T(8,128)(2,1)}), bf16[32,64,1024]{2,1,0:T(8,128)(2,1)}, u32[]{:S(2)}, u32[]{:S(2)}) async-start(bf16[32,64,1024]{2,1,0:T(8,128)(2,1)} %get-tuple-element.194), calls=%async_computation.8 | async-start | bytes 8388608 | tf_op jit(solution)/shard_map/all_to_all | solution.py:651
  333.1 62.2 %reduce-scatter.3.cloned.1.call-start = ((), (), s32[]{:S(2)}) async-start(), calls=%async_computation.13 | async-start | bytes 1310720 | tf_op jit(solution)/shard_map/reduce_scatter | solution.py:925
  356.1 124.4 %reduce-scatter.5.cloned.1.call-start = ((), (), s32[]{:S(2)}) async-start(), calls=%async_computation.14 | async-start | bytes 3932160 | tf_op jit(solution)/shard_map/reduce_scatter | solution.py:929
  361.2 17.2 %collective-permute-start.19 = (bf16[128,256]{1,0:T(8,128)(2,1)S(1)}, bf16[128,256]{1,0:T(8,128)(2,1)S(1)}, u32[]{:S(2)}, u32[]{:S(2)}) collective-permute-start(bf16[128,256]{1,0:T(8,128)(2,1)S(1)} %get-tuple-element.232), channel_id=1, source_target_pairs={{0,2},{1,3},{2,0},{3,1},{4,6},{5,7},{6,4},{7,5},{8,10},{9,11},{10,... | collective-permute-start | bytes 196616 | tf_op jit(solution)/shard_map/ppermute | solution.py:673
  361.2 19.5 %collective-permute-start.20 = (bf16[128,256]{1,0:T(8,128)(2,1)S(1)}, bf16[128,256]{1,0:T(8,128)(2,1)S(1)}, u32[]{:S(2)}, u32[]{:S(2)}) collective-permute-start(bf16[128,256]{1,0:T(8,128)(2,1)S(1)} %get-tuple-element.231), channel_id=1, source_target_pairs={{0,3},{1,2},{2,1},{3,0},{4,7},{5,6},{6,5},{7,4},{8,11},{9,10},{10,... | collective-permute-start | bytes 196616 | tf_op jit(solution)/shard_map/ppermute | solution.py:673
  399.3 19.5 %all-to-all-start.8 = ((bf16[32,64,128]{2,1,0:T(8,128)(2,1)}), bf16[32,64,128]{2,1,0:T(8,128)(2,1)S(1)}, u32[]{:S(2)}, u32[]{:S(2)}) async-start(bf16[32,64,128]{2,1,0:T(8,128)(2,1)} %bitcast.57), calls=%async_computation.9 | async-start | bytes 1048576 | tf_op jit(solution)/shard_map/all_to_all | solution.py:651
  424.9 49.2 %all-to-all-start.9 = ((bf16[128,8,896]{2,1,0:T(8,128)(2,1)}), bf16[128,8,896]{2,1,0:T(8,128)(2,1)S(1)}, u32[]{:S(2)}, u32[]{:S(2)}) async-start(bf16[128,8,896]{2,1,0:T(8,128)(2,1)} %bitcast.58), calls=%async_computation.10 | async-start | bytes 3670016 | tf_op jit(solution)/shard_map/all_to_all | solution.py:651
  434.5 7.7 %collective-permute-start.21 = (bf16[128,1024]{1,0:T(8,128)(2,1)}, bf16[128,1024]{1,0:T(8,128)(2,1)S(1)}, u32[]{:S(2)}, u32[]{:S(2)}) collective-permute-start(bf16[128,1024]{1,0:T(8,128)(2,1)} %get-tuple-element.215), channel_id=1, source_target_pairs={{0,1},{1,0},{2,3},{3,2},{4,5},{5,4},{6,7},{7,6},{8,9},{9,8},{10,11... | collective-permute-start | bytes 786440 | tf_op jit(solution)/shard_map/ppermute | solution.py:673
  435.6 29.6 %collective-permute-start.22 = (bf16[128,1024]{1,0:T(8,128)(2,1)}, bf16[128,1024]{1,0:T(8,128)(2,1)S(1)}, u32[]{:S(2)}, u32[]{:S(2)}) collective-permute-start(bf16[128,1024]{1,0:T(8,128)(2,1)} %get-tuple-element.216), channel_id=1, source_target_pairs={{0,2},{1,3},{2,0},{3,1},{4,6},{5,7},{6,4},{7,5},{8,10},{9,11},{10,... | collective-permute-start | bytes 786440 | tf_op jit(solution)/shard_map/ppermute | solution.py:673
  436.4 34.5 %collective-permute-start.23 = (bf16[128,1024]{1,0:T(8,128)(2,1)}, bf16[128,1024]{1,0:T(8,128)(2,1)S(1)}, u32[]{:S(2)}, u32[]{:S(2)}) collective-permute-start(bf16[128,1024]{1,0:T(8,128)(2,1)} %get-tuple-element.217), channel_id=1, source_target_pairs={{0,3},{1,2},{2,1},{3,0},{4,7},{5,6},{6,5},{7,4},{8,11},{9,10},{10,... | collective-permute-start | bytes 786440 | tf_op jit(solution)/shard_map/ppermute | solution.py:673
  (40 other events, 614.8 us)
Sparse Core Ops, SparseCore 0:
  11.1 136.2 all-gather.1
  356.2 39.0 reduce-scatter.2
  397.9 68.5 reduce-scatter.4

commit v3 on v2

--- a/solution.py
+++ b/solution.py
@@ -212,18 +212,19 @@
             q_ref[half, :, head] = queries[:, at : at + 128].reshape(8, 64, 128)
 
 
+CHUNKS = (1, 2, 3, 4, 8, 7, 6, 5)
+
+
 def tile_positions(tile, mine):
     front = tile < 4
     i = jnp.where(front, tile, tile - 4)
     q = lane((1, 256))
-    k = row((512, 1))
     k = lax.broadcasted_iota(jnp.int32, (512, 1), 0)
     q_front = (8 * i + 4 * (q // 128) + mine) * 64 + q % 64
     q_back = (63 - 8 * i - 4 * (q // 128) - mine) * 64 + q % 64
     k_front = 512 * i + k
     k_back = (59 - 8 * i + 4 * (k // 256) - (k % 256) // 64) * 64 + k % 64
-    count = jnp.where(front, i + 1, 8 - i)
-    return jnp.where(front, q_front, q_back), jnp.where(front, k_front, k_back), count
+    return jnp.where(front, q_front, q_back), jnp.where(front, k_front, k_back)
 
 
 def kernel_attend(mine_ref, kv_ref, q_ref, msg_ref, log_ref, out_ref, keys_ref, turned_ref):
@@ -242,37 +243,39 @@
             ).astype(BF)
 
     q = q_ref[...]
-    q_pos, k_pos, count = tile_positions(tile, mine_ref[0])
-
-    def step(c, carry, last):
-        peak, total, mixed = carry
-        at = pl.multiple_of(c * 512, 512)
-        scores = mm(keys_ref[pl.ds(at, 512), :], q, NT)
-        if last:
-            scores = jnp.where(k_pos <= q_pos, scores, MASKED)
-        higher = jnp.maximum(peak, jnp.max(scores, axis=0, keepdims=True))
-        weights = jnp.exp(scores - higher)
-        fade = jnp.exp(peak - higher)
-        total = total * fade + jnp.sum(weights, axis=0, keepdims=True)
-        mixed = mixed * fade + mm(turned_ref[64:128, pl.ds(at, 512)], weights.astype(BF))
-        return higher, total, mixed
-
-    start = (
-        jnp.full((1, 256), MASKED, F32),
-        jnp.zeros((1, 256), F32),
-        jnp.zeros((64, 256), F32),
-    )
-    carry = lax.fori_loop(0, count - 1, lambda c, v: step(c, v, False), start)
-    peak, total, mixed = step(count - 1, carry, True)
-    log_ref[0] = jnp.broadcast_to(peak + jnp.log(total), (8, 256))
-    mixed = mixed / total
-    out = jnp.transpose(jnp.concatenate([jnp.zeros((64, 256), F32), mixed], axis=0))
-    out_ref[...] = out
-    low = lane((64, 128)) < 64
-    for a in range(2):
-        first = out[128 * a : 128 * a + 64]
-        second = out[128 * a + 64 : 128 * a + 128]
-        msg_ref[a, 0] = jnp.where(low, pltpu.roll(first, 64, 1), second).astype(BF)
+    q_pos, k_pos = tile_positions(tile, mine_ref[0])
+
+    def run(count):
+        peak = jnp.full((1, 256), MASKED, F32)
+        total = jnp.zeros((1, 256), F32)
+        mixed = jnp.zeros((64, 256), F32)
+        later = mm(keys_ref[0:512, :], q, NT)
+        for c in range(count):
+            scores = later
+            if c + 1 < count:
+                later = mm(keys_ref[512 * c + 512 : 512 * c + 1024, :], q, NT)
+            else:
+                scores = jnp.where(k_pos <= q_pos, scores, MASKED)
+            higher = jnp.maximum(peak, jnp.max(scores, axis=0, keepdims=True))
+            weights = jnp.exp(scores - higher)
+            fade = jnp.exp(peak - higher)
+            total = total * fade + jnp.sum(weights, axis=0, keepdims=True)
+            mixed = mixed * fade + mm(
+                turned_ref[64:128, 512 * c : 512 * c + 512], weights.astype(BF)
+            )
+            peak = higher
+        log_ref[0] = jnp.broadcast_to(peak + jnp.log(total), (8, 256))
+        mixed = mixed / total
+        out = jnp.transpose(jnp.concatenate([jnp.zeros((64, 256), F32), mixed], axis=0))
+        out_ref[...] = out
+        low = lane((64, 128)) < 64
+        for a in range(2):
+            first = out[128 * a : 128 * a + 64]
+            second = out[128 * a + 64 : 128 * a + 128]
+            msg_ref[a, 0] = jnp.where(low, pltpu.roll(first, 64, 1), second).astype(BF)
+
+    for t, count in enumerate(CHUNKS):
+        pl.when(tile == t)(functools.partial(run, count))
 
 
 def kernel_attend_back(
@@ -294,11 +297,11 @@
     grad = jnp.concatenate(pieces, axis=0)
     delta = jnp.sum(jnp.transpose(grad * out_ref[...]), axis=0, keepdims=True)
     grad = grad.astype(BF)
-    q_pos, k_pos, count = tile_positions(tile, mine_ref[0])
+    q_pos, k_pos = tile_positions(tile, mine_ref[0])
     log_total = log_ref[0][0:1]
 
     def step(c, dq, last):
-        at = pl.multiple_of(c * 512, 512)
+        at = 512 * c
         keys = keys_ref[pl.ds(at, 512), :]
         scores = mm(keys, q, NT)
         if last:
@@ -308,9 +311,15 @@
         sum_ref[pl.ds(at, 512), :] += mm(slope, q) + mm(weights.astype(BF), grad)
         return dq + mm(turned_ref[0:64, pl.ds(at, 512)], slope)
 
-    dq = lax.fori_loop(0, count - 1, lambda c, v: step(c, v, False), jnp.zeros((64, 256), F32))
-    dq = step(count - 1, dq, True)
-    dq_ref[...] = jnp.transpose(jnp.concatenate([dq * 0.125, jnp.zeros((64, 256), F32)], axis=0))
+    def run(count):
+        dq = jnp.zeros((64, 256), F32)
+        for c in range(count):
+            dq = step(c, dq, c == count - 1)
+        dq = jnp.concatenate([dq * 0.125, jnp.zeros((64, 256), F32)], axis=0)
+        dq_ref[...] = jnp.transpose(dq)
+
+    for t, count in enumerate(CHUNKS):
+        pl.when(tile == t)(functools.partial(run, count))
 
     @pl.when(tile == 7)
     def _():
@@ -357,17 +366,16 @@
         scale = lax.rsqrt(jnp.mean(mid * mid, axis=-1, keepdims=True) + EPSILON)
         hidden_ref[...] = (mid * scale * gains_ref[1:2]).astype(BF)
 
-    slots_ref[...] = mm(pick_ref[...], hidden_ref[...]).astype(BF).reshape(4, 64, WIDTH)
+    for c in range(4):
+        at = slice(256 * c, 256 * c + 256)
+        rows = mm(pick_ref[...], hidden_ref[:, at]).astype(BF)
+        slots_ref[:, :, at] = rows.reshape(16, 64, 256)
 
 
 def kernel_experts_ready(
     part_ref,
     dy_ref,
     parts_ref,
-    v0_ref,
-    v1_ref,
-    v2_ref,
-    v3_ref,
     w0_ref,
     w1_ref,
     w2_ref,
@@ -383,10 +391,9 @@
 
     @pl.when(step == 0)
     def _():
-        for r, w_ref in enumerate((v0_ref, v1_ref, v2_ref, v3_ref)):
-            v_ref[place(part_ref, r, 128), :] = w_ref[...]
         for r, w_ref in enumerate((w0_ref, w1_ref, w2_ref, w3_ref)):
-            gu_ref[place(part_ref, r, 256), :] = w_ref[...]
+            gu_ref[place(part_ref, r, 256), :] = w_ref[0:256, :]
+            v_ref[place(part_ref, r, 128), :] = w_ref[256:384, :]
         before = jnp.where(row((128, 128)) < lane((128, 128)), 1.0, 0.0).astype(BF)
         parts = [parts_ref[:, k, :].astype(F32) for k in range(6)]
         even = parts[0] + parts[2] + parts[4]
@@ -404,7 +411,7 @@
         weight = jnp.sum(
             jnp.where(pick, gate_ref[pl.ds(source, 1), :], 0.0), axis=1, keepdims=True
         )
-        rows = mm(jnp.where(pick, 1.0, 0.0).astype(BF), dy_ref[j])
+        rows = mm(jnp.where(pick, 1.0, 0.0).astype(BF), dy_ref[0, j, 0])
         grads.append((rows * weight).astype(BF))
     dys = jnp.concatenate(grads, axis=0)
     dys_ref[...] = dys.reshape(4, 64, WIDTH)
@@ -412,7 +419,7 @@
 
 
 def kernel_experts(h_ref, gu_ref, dact_ref, act_ref, dboth_ref, dxs_ref):
-    both = mm(h_ref[...].reshape(256, WIDTH), gu_ref[...])
+    both = mm(h_ref[...].reshape(512, WIDTH), gu_ref[...])
     gate_h, up_h = both[:, :512], both[:, 512:]
     sig = jax.nn.sigmoid(gate_h)
     swished = gate_h * sig
@@ -422,7 +429,7 @@
     dup = (dact * swished).astype(BF)
     dboth = jnp.concatenate([dgate, dup], axis=1)
     dboth_ref[...] = dboth
-    dxs_ref[...] = mm(dboth, gu_ref[...], NT).astype(BF).reshape(4, 64, WIDTH)
+    dxs_ref[...] = mm(dboth, gu_ref[...], NT).astype(BF).reshape(8, 64, WIDTH)
 
 
 def kernel_experts_after(
@@ -470,7 +477,7 @@
     low_ref,
 ):
     step = pl.program_id(0)
-    part = mm(pick_ref[...], dxs_ref[...].reshape(512, WIDTH))
+    part = mm(pick_ref[...], dxs_ref[...].reshape(1024, WIDTH))
 
     @pl.when(step == 0)
     def _():
@@ -480,7 +487,7 @@
     def _():
         sum_ref[...] += part
 
-    @pl.when(step == 3)
+    @pl.when(step == 1)
     def _():
         mid = mid_ref[...]
         scale = lax.rsqrt(jnp.mean(mid * mid, axis=-1, keepdims=True) + EPSILON)
@@ -585,42 +592,36 @@
 
 
 def kernel_total(parts_ref, table_ref, qkv_ref, out_ref, gains_ref, sum_ref):
-    step = pl.program_id(0)
-
-    @pl.when(step == 0)
-    def _():
-        sum_ref[...] = jnp.zeros_like(sum_ref)
-
-    sum_ref[...] += jnp.sum(parts_ref[...].astype(F32), axis=0)
-
-    @pl.when(step == 3)
-    def _():
-        rows = []
-        for p in range(4):
-            rows.append(
-                jnp.concatenate(
-                    [sum_ref[f, :, 128 * p : 128 * p + 128] for f in range(4)], axis=1
-                )
-            )
-        rest = jnp.concatenate(rows, axis=0)
-        whole = jnp.zeros((32, 512), F32)
-        for _ in range(3):
-            part = rest.astype(BF)
-            rest = rest - part.astype(F32)
-            whole = whole + mm(part, table_ref[...], NT)
-        for p in range(4):
-            piece = whole[8 * p : 8 * p + 8]
-            qkv_ref[:, 256 * p : 256 * p + 256] = piece[:, 0:256]
-            qkv_ref[:, 1024 + 128 * p : 1152 + 128 * p] = piece[:, 256:384]
-            qkv_ref[:, 1536 + 128 * p : 1664 + 128 * p] = piece[:, 384:512]
-        for f in range(4):
-            out_ref[:, 256 * f : 256 * f + 256] = sum_ref[f, :, 640:896]
-        gains_ref[...] = (
-            sum_ref[0, :, 512:640]
-            + sum_ref[1, :, 512:640]
-            + sum_ref[2, :, 512:640]
-            + sum_ref[3, :, 512:640]
+    total = parts_ref[0].astype(F32)
+    for c in range(1, 32):
+        total = total + parts_ref[c].astype(F32)
+    sum_ref[...] = total
+    rows = []
+    for p in range(4):
+        rows.append(
+            jnp.concatenate([sum_ref[f, :, 128 * p : 128 * p + 128] for f in range(4)], axis=1)
         )
+    rest = jnp.concatenate(rows, axis=0)
+    parts = []
+    for _ in range(3):
+        part = rest.astype(BF)
+        rest = rest - part.astype(F32)
+        parts.append(part)
+    whole = mm(jnp.concatenate(parts, axis=0), table_ref[...], NT)
+    whole = whole[0:32] + whole[32:64] + whole[64:96]
+    for p in range(4):
+        piece = whole[8 * p : 8 * p + 8]
+        qkv_ref[:, 256 * p : 256 * p + 256] = piece[:, 0:256]
+        qkv_ref[:, 1024 + 128 * p : 1152 + 128 * p] = piece[:, 256:384]
+        qkv_ref[:, 1536 + 128 * p : 1664 + 128 * p] = piece[:, 384:512]
+    for f in range(4):
+        out_ref[:, 256 * f : 256 * f + 256] = sum_ref[f, :, 640:896]
+    gains_ref[...] = (
+        sum_ref[0, :, 512:640]
+        + sum_ref[1, :, 512:640]
+        + sum_ref[2, :, 512:640]
+        + sum_ref[3, :, 512:640]
+    )
 
 
 def kernel_output(ys_ref, high_ref, rest_ref, mid_ref, out_ref, sum_ref):
@@ -697,7 +698,6 @@
     slice_table = jnp.asarray(slice_matrix(), BF)
     head_table = jnp.asarray(head_matrix(), BF)
 
-    cot_all = gather(cot, CTX)
     x_all = neighbours(x)
     rank, gate = call(
         kernel_route,
@@ -719,7 +719,16 @@
     )(query_key_value_weight, gain_rows, slice_table, gate, output_weight)
     slices, rank, gate, x_all = lax.optimization_barrier((slices, rank, gate, x_all))
     x_all = x_all + (swap(x_all[2], "core"),)
+    offset = jnp.arange(64, dtype=jnp.int32)
+    token_pos = jnp.concatenate([ctx_index * 64 + offset, (63 - ctx_index) * 64 + offset])
+    column = jnp.arange(512, dtype=jnp.int32)
+    angle = angles(token_pos, 8 * part_index + column % 8)
+    is_value = (column // 16) % 4 == 3
+    sign = jnp.where((column // 8) % 2 == 0, -1.0, 1.0)
+    cos_slice = jnp.where(is_value, 1.0, jnp.cos(angle))
+    sin_slice = jnp.where(is_value, 0.0, jnp.sin(angle) * sign)
     w_slice = exchange(slices.reshape(128, 8, 896), ALL)
+    w_slice, cos_slice, sin_slice = lax.optimization_barrier((w_slice, cos_slice, sin_slice))
     gate_parts = lax.dynamic_slice(
         w_slice.reshape(32, 4, 8, 896), (0, part_index, 0, 512), (32, 1, 8, 128)
     ).reshape(32, 8, 128)
@@ -732,14 +741,6 @@
         out_specs=(VM,) * 4,
     )(rank, gate)
 
-    offset = jnp.arange(64, dtype=jnp.int32)
-    token_pos = jnp.concatenate([ctx_index * 64 + offset, (63 - ctx_index) * 64 + offset])
-    column = jnp.arange(512, dtype=jnp.int32)
-    angle = angles(token_pos, 8 * part_index + column % 8)
-    is_value = (column // 16) % 4 == 3
-    sign = jnp.where((column // 8) % 2 == 0, -1.0, 1.0)
-    cos_slice = jnp.where(is_value, 1.0, jnp.cos(angle))
-    sin_slice = jnp.where(is_value, 0.0, jnp.sin(angle) * sign)
     msg, hidden, gains = call(
         kernel_project,
         (sds((32, 64, 128), BF), sds((512, WIDTH), BF), sds((8, WIDTH), F32)),
@@ -747,6 +748,12 @@
         in_specs=[SM] + [VM] * 7,
         out_specs=(VM, VM, VM),
     )(part_ref, *x_all, w_slice, cos_slice, sin_slice)
+    across = swap(after(cot, w_slice), "zh")
+    first = lax.axis_index("zh") == 0
+    cot_pair = jnp.concatenate(
+        [jnp.where(first, cot, across), jnp.where(first, across, cot)], axis=0
+    )
+    cot_all = gather(after(cot_pair, msg), ("x", "y")).reshape(4, 4, 2, 128, WIDTH)
     out_upper = neighbours(w_slice[0:512, 640:896])
     msg = exchange(msg, HEAD_AXES + FSDP)
 
@@ -761,6 +768,9 @@
     kv_copies, out_upper = lax.optimization_barrier((kv_copies, out_upper))
     out_lower = neighbours(after(w_slice[512:1024, 640:896], msg))
     kv = exchange(kv_copies, ("y",)).reshape(4, 2, 8, 64, 128)
+    expert_weights = jnp.concatenate(
+        [jnp.concatenate([exp_gate[0], exp_up[0]], axis=1), exp_down[0]], axis=0
+    ).astype(BF)
     block = 4 * jnp.arange(8, dtype=jnp.int32)[:, None] + mine
     quarter_pos = jnp.concatenate(
         [
@@ -776,9 +786,7 @@
     kv, out_lower, cos_heads, sin_heads = lax.optimization_barrier(
         (kv, out_lower, cos_heads, sin_heads)
     )
-    downs = neighbours(after(exp_down[0].astype(BF), kv))
-    gate_ups = jnp.concatenate([exp_gate[0], exp_up[0]], axis=1).astype(BF)
-    gate_ups = neighbours(after(gate_ups, kv))
+    experts_all = neighbours(after(expert_weights, msg))
     out_upper = out_upper + (swap(after(out_upper[2], kv), "core"),)
     out_lower = out_lower + (swap(out_lower[2], "core"),)
     w_out = (*out_upper, *out_lower)
@@ -799,9 +807,8 @@
         in_specs=[SM, whole((4, 2, 8, 64, 128)), row_spec],
         out_specs=(msg_spec, log_spec, row_spec, whole((4096, 128)), whole((128, 4096))),
     )(mine_ref, kv, queries)
-    o_msg, w_out, downs, gate_ups = lax.optimization_barrier((o_msg, w_out, downs, gate_ups))
-    downs = downs + (swap(downs[2], "core"),)
-    gate_ups = gate_ups + (swap(gate_ups[2], "core"),)
+    o_msg, w_out, experts_all = lax.optimization_barrier((o_msg, w_out, experts_all))
+    experts_all = experts_all + (swap(experts_all[2], "core"),)
     o_heads = exchange(o_msg, HEAD_AXES)
 
     slot_spec = pl.BlockSpec((4, 64, WIDTH), lambda t: (t, 0, 0))
@@ -810,19 +817,19 @@
         kernel_middle,
         (sds((32, 64, WIDTH), BF), sds((128, WIDTH), F32)),
         (9e8, 8e6),
-        grid=(8,),
+        grid=(2,),
         in_specs=[SM, whole((8, 2, 64, 128))]
         + out_specs
         + [
             whole((128, WIDTH)),
             whole((8, WIDTH)),
-            pl.BlockSpec((256, 128), lambda t: (t, 0)),
+            pl.BlockSpec((1024, 128), lambda t: (t, 0)),
         ],
-        out_specs=(slot_spec, whole((128, WIDTH))),
+        out_specs=(pl.BlockSpec((16, 64, WIDTH), lambda t: (t, 0, 0)), whole((128, WIDTH))),
         scratch_shapes=[pltpu.VMEM((128, WIDTH), BF), pltpu.VMEM((128, WIDTH), BF)],
     )(part_ref, o_heads, *w_out, x, gains, picks)
     cot_all = after(cot_all, mid)
-    slots, downs, gate_ups = lax.optimization_barrier((slots, downs, gate_ups))
+    slots, experts_all = lax.optimization_barrier((slots, experts_all))
     o_all = neighbours(after(o_heads, mid))
     slots = exchange(slots, CTX)
     dys, dact, down, gate_up = call(
@@ -837,11 +844,10 @@
         grid=(8,),
         in_specs=[
             SM,
-            pl.BlockSpec((4, 128, WIDTH), lambda t: (t, 0, 0)),
+            pl.BlockSpec((1, 4, 1, 128, WIDTH), lambda t: (t // 2, 0, t % 2, 0, 0)),
             whole((32, 8, 128)),
         ]
-        + [whole((128, WIDTH))] * 4
-        + [whole((256, WIDTH))] * 4,
+        + [whole((384, WIDTH))] * 4,
         out_specs=(
             slot_spec,
             pl.BlockSpec((256, 512), lambda t: (t, 0)),
@@ -849,16 +855,24 @@
             whole((WIDTH, WIDTH)),
         ),
         scratch_shapes=[pltpu.VMEM((32, 128), F32), pltpu.VMEM((32, 128), F32)],
-    )(part_ref, cot_all.reshape(32, 128, WIDTH), gate_parts, *downs, *gate_ups)
+    )(part_ref, cot_all, gate_parts, *experts_all)
     act_spec = pl.BlockSpec((256, 512), lambda t: (t, 0))
     both_spec = pl.BlockSpec((256, WIDTH), lambda t: (t, 0))
     act, dboth, dxs = call(
         kernel_experts,
         (sds((2048, 512), BF), sds((2048, WIDTH), BF), sds((32, 64, WIDTH), BF)),
         (9e9, 2e7),
-        grid=(8,),
-        in_specs=[slot_spec, whole((WIDTH, WIDTH)), act_spec],
-        out_specs=(act_spec, both_spec, slot_spec),
+        grid=(4,),
+        in_specs=[
+            pl.BlockSpec((8, 64, WIDTH), lambda t: (t, 0, 0)),
+            whole((WIDTH, WIDTH)),
+            pl.BlockSpec((512, 512), lambda t: (t, 0)),
+        ],
+        out_specs=(
+            pl.BlockSpec((512, 512), lambda t: (t, 0)),
+            pl.BlockSpec((512, WIDTH), lambda t: (t, 0)),
+            pl.BlockSpec((8, 64, WIDTH), lambda t: (t, 0, 0)),
+        ),
     )(slots, gate_up, dact)
     ys, expert_grads = call(
         kernel_experts_after,
@@ -883,11 +897,11 @@
             sds((8, WIDTH), F32),
         ),
         (9e8, 8e6),
-        grid=(4,),
+        grid=(2,),
         in_specs=[
             SM,
-            pl.BlockSpec((8, 64, WIDTH), lambda t: (t, 0, 0)),
-            pl.BlockSpec((128, 512), lambda t: (0, t)),
+            pl.BlockSpec((16, 64, WIDTH), lambda t: (t, 0, 0)),
+            pl.BlockSpec((128, 1024), lambda t: (0, t)),
             whole((128, WIDTH)),
             whole((128, WIDTH)),
             whole((8, WIDTH)),
@@ -974,6 +988,15 @@
         in_specs=[SM, VM, VM],
         out_specs=(VM,) * 4,
     )(part_ref, d_all, w_slice)
+    grads = exchange(grads.reshape(128, 8, 896), ALL)
+    grad_qkv, grad_out, grad_gains = call(
+        kernel_total,
+        (sds((8, 2048), F32), sds((8, WIDTH), F32), sds((8, 128), F32)),
+        (1e8, 4e6),
+        in_specs=[VM, VM],
+        out_specs=(VM, VM, VM),
+        scratch_shapes=[pltpu.VMEM((4, 8, 896), F32)],
+    )(grads.reshape(32, 4, 8, 896), slice_table)
     dh_here = cross(dh_parts)
     input_grad = call(
         kernel_input_grad,
@@ -981,17 +1004,7 @@
         (1e6, 2e6),
         in_specs=[VM] * 7,
         out_specs=VM,
-    )(*dh_here, x, dmid, gains)
-    grads = exchange(grads.reshape(128, 8, 896), ALL)
-    grad_qkv, grad_out, grad_gains = call(
-        kernel_total,
-        (sds((8, 2048), F32), sds((8, WIDTH), F32), sds((8, 128), F32)),
-        (1e8, 4e6),
-        grid=(4,),
-        in_specs=[pl.BlockSpec((8, 4, 8, 896), lambda t: (t, 0, 0, 0)), whole((512, 512))],
-        out_specs=(whole((8, 2048)), whole((8, WIDTH)), whole((8, 128))),
-        scratch_shapes=[pltpu.VMEM((4, 8, 896), F32)],
-    )(grads.reshape(32, 4, 8, 896), slice_table)
+    )(*after(dh_here, grad_qkv), x, dmid, gains)
     return (
         layer_output.reshape(layer_input.shape),
         input_grad.reshape(layer_input.shape),

time: 493 us -> 487 us (0.988); the launches traced: 490 us -> 478 us
  Pallas kernels: 146 us -> 130 us
  waiting for transfers between devices: 206 us -> 214 us
    all_to_all x9, waiting for transfers between devices: 131 us -> 165 us  [exchange(): return lax.all_to_all(value, axes, split_axis=0, concat_axis=0, tiled=True)]
    ppermute x6, waiting for transfers between devices: 46.5 us -> 27.5 us  [cross(): here.append(lax.ppermute(parts[r], FSDP, [(f, f ^ r) for f in range(4)]))]
    ppermute x18 -> x16, waiting for transfers between devices: 13.5 us -> 4.37 us  [swap(): return lax.ppermute(value, axis, [(0, 1), (1, 0)])]
    pallas_call x1, Pallas kernels: 24.6 us -> 16.1 us  [on_device(): call(kernel_attend, (sds((8, 2, 64, 128), BF), sds((8, 8, 256), F32), sds...]
    ppermute x18 -> x16, starting transfers between devices: 15.1 us -> 13 us  [swap(): return lax.ppermute(value, axis, [(0, 1), (1, 0)])]
  transfers between devices with their start and end apart: 36 -> 34, of which waited for: 15 -> 15; matrix products, arithmetic and copies ran while one was open for 3% -> 3% of each run, Pallas kernels for 29% -> 26%
where the time goes in v3:
time: 487 us; the launch traced here: 478 us
  waiting for transfers between devices  214 us (44%)
  Pallas kernels  130 us (27%)
  starting transfers between devices  79.6 us (16%)
  local copies, waits for them, and re-layouts  16.1 us (3%)
  between operations  14.7 us (3%)
  blocking collectives  14.1 us (3%)
  other arithmetic  8.9 us (2%)
    all_to_all x9, waiting for transfers between devices, exchange(): return lax.all_to_all(value, axes, split_axis=0, concat_axis=0, tiled=True)  165 us
    all_to_all x9, starting transfers between devices, exchange(): return lax.all_to_all(value, axes, split_axis=0, concat_axis=0, tiled=True)  58.9 us
    ppermute x6, waiting for transfers between devices, cross(): here.append(lax.ppermute(parts[r], FSDP, [(f, f ^ r) for f in range(4)]))  27.5 us
    pallas_call x1, Pallas kernels, on_device(): call(kernel_attend_back, (sds((2048, 128), F32), sds((4, 2, 8, 64, 128),...  20.1 us
    reduce_scatter x1, waiting for transfers between devices, on_device(): lax.psum_scatter(dkv.reshape(4096, 128), ('y',), scatter_dimension=0, til...  17.1 us
    pallas_call x1, Pallas kernels, on_device(): call(kernel_attend, (sds((8, 2, 64, 128), BF), sds((8, 8, 256), F32), sds...  16.1 us
    pallas_call x1, Pallas kernels, on_device(): call(kernel_experts_after, (sds((32, 64, WIDTH), BF), sds((4, 384, WIDTH)...  15.9 us
    all_to_all x1, blocking collectives, exchange(): return lax.all_to_all(value, axes, split_axis=0, concat_axis=0, tiled=True)  14.1 us
  transfers between devices with their start and end apart: 34, of which 15 were waited for; matrix products, arithmetic and copies ran while one was open for 3% of the time, Pallas kernels for 26%

profile of v3, /device:TPU:1, one launch (start us, length us, event | category | flops | bytes accessed | tf_op | source)
XLA Modules:
  0.0 477.9 jit_solution(3114376048637939655)
XLA Ops:
  19.3 9.9 %all-to-all-start = ((bf16[128,8,896]{2,1,0:T(8,128)(2,1)}), bf16[128,8,896]{2,1,0:T(8,128)(2,1)S(1)}, u32[]{:S(2)}, u32[]{:S(2)}) async-start(bf16[128,8,896]{2,1,0:T(8,128)(2,1)} %bitcast.56), calls=%async_computation | async-start | bytes 3670016 | tf_op jit(solution)/shard_map/all_to_all | solution.py:652
  32.3 24.0 %all-to-all-done = bf16[128,8,896]{2,1,0:T(8,128)(2,1)S(1)} async-done(((bf16[128,8,896]{2,1,0:T(8,128)(2,1)}), bf16[128,8,896]{2,1,0:T(8,128)(2,1)S(1)}, u32[]{:S(2)}, u32[]{:S(2)}) %all-to-all-start) | async-done | bytes 1835040 | tf_op jit(solution)/shard_map/all_to_all | solution.py:652
  57.6 4.6 shard_map.198
  65.7 5.7 %all-to-all-start.1 = ((bf16[32,64,128]{2,1,0:T(8,128)(2,1)}), bf16[32,64,128]{2,1,0:T(8,128)(2,1)S(1)}, u32[]{:S(2)}, u32[]{:S(2)}) async-start(bf16[32,64,128]{2,1,0:T(8,128)(2,1)} %get-tuple-element.127), calls=%async_computation.1 | async-start | bytes 1048576 | tf_op jit(solution)/shard_map/all_to_all | solution.py:652
  74.5 11.9 %all-to-all-done.1 = bf16[32,64,128]{2,1,0:T(8,128)(2,1)S(1)} async-done(((bf16[32,64,128]{2,1,0:T(8,128)(2,1)}), bf16[32,64,128]{2,1,0:T(8,128)(2,1)S(1)}, u32[]{:S(2)}, u32[]{:S(2)}) %all-to-all-start.1) | async-done | bytes 524320 | tf_op jit(solution)/shard_map/all_to_all | solution.py:652
  102.0 15.3 %all-to-all-done.2 = bf16[4,1024,128]{2,1,0:T(8,128)(2,1)S(1)} async-done(((bf16[4,1024,128]{2,1,0:T(8,128)(2,1)}), bf16[4,1024,128]{2,1,0:T(8,128)(2,1)S(1)}, u32[]{:S(2)}, u32[]{:S(2)}) %all-to-all-start.2) | async-done | bytes 1048608 | tf_op jit(solution)/shard_map/all_to_all | solution.py:652
  118.3 16.1 %shard_map.200 = (bf16[8,2,64,128]{3,2,1,0:T(8,128)(2,1)}, f32[8,8,256]{2,1,0:T(8,128)}, f32[2048,128]{1,0:T(8,128)}, bf16[4096,128]{1,0:T(8,128)(2,1)}, bf16[128,4096]{1,0:T(8,128)(2,1)}) custom-call(s32[1]{0:T(128)} %bitcast.mine_ref, bf16[4,2,8,64,128]{4,3,2,1,0:T(8,128)(2,1)} %bitcast.67, bf16[2048,128]{1,0:T(8,128)(2,1)} %bitcast.77), custom_call_target="tpu_custom_call" | custom-call | flops 10000000000 | bytes 5000000 | tf_op jit(solution)/shard_map/pallas_call | solution.py:796
  140.8 5.8 %all-to-all-done.3.o_ref.o0_ref = bf16[8,2,64,128]{3,2,1,0:T(8,128)(2,1)S(1)} async-done(((bf16[8,2,64,128]{3,2,1,0:T(8,128)(2,1)}), bf16[8,2,64,128]{3,2,1,0:T(8,128)(2,1)S(1)}, u32[]{:S(2)}, u32[]{:S(2)}) %all-to-all-start.3) | async-done | bytes 262176 | tf_op jit(solution)/shard_map/all_to_all | solution.py:652
  147.3 5.2 %shard_map.202 = (bf16[32,64,1024]{2,1,0:T(8,128)(2,1)}, f32[128,1024]{1,0:T(8,128)}) custom-call(s32[1]{0:T(128)} %bitcast.1.part_ref, bf16[8,2,64,128]{3,2,1,0:T(8,128)(2,1)} %copy-done.7, bf16[512,256]{1,0:T(8,128)(2,1)} %copy-done.6, bf16[512,256]{1,0:T(8,128)(2,1)} %copy-done.14, bf16[512,256]{1,0:T(8,128)(2,1)} %copy-done.15, ...), custom_call_target="tpu_custom_call" | custom-call | flops 900000000 | bytes 8000000 | tf_op jit(solution)/shard_map/pallas_call | solution.py:816
  153.4 4.9 %all-to-all-start.4 = ((bf16[32,64,1024]{2,1,0:T(8,128)(2,1)}), bf16[32,64,1024]{2,1,0:T(8,128)(2,1)}, u32[]{:S(2)}, u32[]{:S(2)}) async-start(bf16[32,64,1024]{2,1,0:T(8,128)(2,1)} %get-tuple-element.161), calls=%async_computation.4 | async-start | bytes 8388608 | tf_op jit(solution)/shard_map/all_to_all | solution.py:652
  161.0 12.5 %shard_map.203 = (bf16[32,64,1024]{2,1,0:T(8,128)(2,1)}, f32[2048,512]{1,0:T(8,128)}, bf16[512,1024]{1,0:T(8,128)(2,1)}, bf16[1024,1024]{1,0:T(8,128)(2,1)}) custom-call(s32[1]{0:T(128)} %bitcast.1.part_ref, bf16[4,4,2,128,1024]{4,3,2,1,0:T(8,128)(2,1)} %bitcast.76, bf16[32,8,128]{2,1,0:T(8,128)(2,1)} %dynamic-slice_bitcast_fusion.parts_ref, ...), custom_call_target="tpu_custom_call" | custom-call | flops 6000000000 | bytes 20000000 | tf_op jit(solution)/shard_map/pallas_call | solution.py:835
  173.4 43.2 %all-to-all-done.4.h_ref = bf16[32,64,1024]{2,1,0:T(8,128)(2,1)} async-done(((bf16[32,64,1024]{2,1,0:T(8,128)(2,1)}), bf16[32,64,1024]{2,1,0:T(8,128)(2,1)}, u32[]{:S(2)}, u32[]{:S(2)}) %all-to-all-start.4) | async-done | bytes 4194336 | tf_op jit(solution)/shard_map/all_to_all | solution.py:652
  216.6 13.9 %shard_map.204 = (bf16[2048,512]{1,0:T(8,128)(2,1)}, bf16[2048,1024]{1,0:T(8,128)(2,1)}, bf16[32,64,1024]{2,1,0:T(8,128)(2,1)}) custom-call(bf16[32,64,1024]{2,1,0:T(8,128)(2,1)} %all-to-all-done.4.h_ref, bf16[1024,1024]{1,0:T(8,128)(2,1)} %get-tuple-element.170.gu_ref, f32[2048,512]{1,0:T(8,128)} %get-tuple-element.171.dact_ref), custom_call_target="tpu_custom_call" | custom-call | flops 8999999488 | bytes 20000000 | tf_op jit(solution)/shard_map/pallas_call | solution.py:861
  231.1 9.1 %all-to-all-start.5 = ((bf16[32,64,1024]{2,1,0:T(8,128)(2,1)}), bf16[32,64,1024]{2,1,0:T(8,128)(2,1)}, u32[]{:S(2)}, u32[]{:S(2)}) async-start(bf16[32,64,1024]{2,1,0:T(8,128)(2,1)} %get-tuple-element.174), calls=%async_computation.5 | async-start | bytes 8388608 | tf_op jit(solution)/shard_map/all_to_all | solution.py:652
  241.4 15.9 %shard_map.205 = (bf16[32,64,1024]{2,1,0:T(8,128)(2,1)}, bf16[4,384,1024]{2,1,0:T(8,128)(2,1)}) custom-call(bf16[32,64,1024]{2,1,0:T(8,128)(2,1)} %all-to-all-done.4.h_ref, bf16[2048,512]{1,0:T(8,128)(2,1)} %get-tuple-element.175.act_ref, bf16[32,64,1024]{2,1,0:T(8,128)(2,1)} %get-tuple-element.176.dys_ref, bf16[2048,1024]{1,0:T(8,128)(2,1)} %get-tuple-element.177.dboth_ref, ...), custom_call_target="tpu_custom_call" | custom-call | flops 8999999488 | bytes 20000000 | tf_op jit(solution)/shard_map/pallas_call | solution.py:877
  257.3 41.1 %all-to-all-done.5.dxs_ref = bf16[32,64,1024]{2,1,0:T(8,128)(2,1)} async-done(((bf16[32,64,1024]{2,1,0:T(8,128)(2,1)}), bf16[32,64,1024]{2,1,0:T(8,128)(2,1)}, u32[]{:S(2)}, u32[]{:S(2)}) %all-to-all-start.5) | async-done | bytes 4194336 | tf_op jit(solution)/shard_map/all_to_all | solution.py:652
  298.4 5.7 %shard_map.206 = (f32[128,1024]{1,0:T(8,128)}, bf16[4,128,256]{2,1,0:T(8,128)(2,1)}, bf16[8,2,64,128]{3,2,1,0:T(8,128)(2,1)}, f32[8,1024]{1,0:T(8,128)}) custom-call(s32[1]{0:T(128)} %bitcast.1.part_ref, bf16[32,64,1024]{2,1,0:T(8,128)(2,1)} %all-to-all-done.5.dxs_ref, bf16[128,2048]{1,0:T(8,128)(2,1)} %get-tuple-element.186.pick_ref, ...), custom_call_target="tpu_custom_call" | custom-call | flops 900000000 | bytes 8000000 | tf_op jit(solution)/shard_map/pallas_call | solution.py:891
  304.1 14.1 %all_to_all.50.grad_ref = bf16[8,2,64,128]{3,2,1,0:T(8,128)(2,1)} all-to-all(bf16[8,2,64,128]{3,2,1,0:T(8,128)(2,1)} %get-tuple-element.187), channel_id=1, replica_groups=mesh['x'=4,'zh'=2,'y'=4,'zl'=2,'core'=2] {'x','zh'}, dimensions={0} | all-to-all | bytes 524288 | tf_op jit(solution)/shard_map/all_to_all | solution.py:652
  318.2 6.4 %all-to-all-start.7 = ((bf16[32,64,1024]{2,1,0:T(8,128)(2,1)}), bf16[32,64,1024]{2,1,0:T(8,128)(2,1)}, u32[]{:S(2)}, u32[]{:S(2)}) async-start(bf16[32,64,1024]{2,1,0:T(8,128)(2,1)} %get-tuple-element.192), calls=%async_computation.8 | async-start | bytes 8388608 | tf_op jit(solution)/shard_map/all_to_all | solution.py:652
  324.7 20.1 %shard_map.207 = (f32[2048,128]{1,0:T(8,128)}, bf16[4,2,8,64,128]{4,3,2,1,0:T(8,128)(2,1)}) custom-call(s32[1]{0:T(128)} %bitcast.mine_ref, bf16[4096,128]{1,0:T(8,128)(2,1)} %get-tuple-element.133.keys_ref, bf16[128,4096]{1,0:T(8,128)(2,1)} %get-tuple-element.134.turned_ref, bf16[2048,128]{1,0:T(8,128)(2,1)} %bitcast.78, ...), custom_call_target="tpu_custom_call" | custom-call | flops 20000000000 | bytes 7000000 | tf_op jit(solution)/shard_map/pallas_call | solution.py:921
  350.5 15.9 %collective-permute-done.17.da2_ref = bf16[128,256]{1,0:T(8,128)(2,1)S(1)} collective-permute-done((bf16[128,256]{1,0:T(8,128)(2,1)S(1)}, bf16[128,256]{1,0:T(8,128)(2,1)S(1)}, u32[]{:S(2)}, u32[]{:S(2)}) %collective-permute-start.17) | collective-permute-done | bytes 65568 | tf_op jit(solution)/shard_map/ppermute | solution.py:674
  368.7 17.1 %reduce-scatter.3.cloned.1.call-done.dkv_ref = bf16[1024,128]{1,0:T(8,128)(2,1)} async-done(((bf16[4096,128]{1,0:T(8,128)(2,1)}), bf16[1024,128]{1,0:T(8,128)(2,1)}) %reduce-scatter.3.cloned.1.call-update) | async-done | bytes 262160 | tf_op jit(solution)/shard_map/reduce_scatter | solution.py:939
  385.8 4.0 shard_map.209
  389.8 10.1 %all-to-all-start.8 = ((bf16[32,64,128]{2,1,0:T(8,128)(2,1)}), bf16[32,64,128]{2,1,0:T(8,128)(2,1)S(1)}, u32[]{:S(2)}, u32[]{:S(2)}) async-start(bf16[32,64,128]{2,1,0:T(8,128)(2,1)} %bitcast.59), calls=%async_computation.9 | async-start | bytes 1048576 | tf_op jit(solution)/shard_map/all_to_all | solution.py:652
  402.9 8.6 %all-to-all-done.8.msg_ref = bf16[32,64,128]{2,1,0:T(8,128)(2,1)S(1)} async-done(((bf16[32,64,128]{2,1,0:T(8,128)(2,1)}), bf16[32,64,128]{2,1,0:T(8,128)(2,1)S(1)}, u32[]{:S(2)}, u32[]{:S(2)}) %all-to-all-start.8) | async-done | bytes 524320 | tf_op jit(solution)/shard_map/all_to_all | solution.py:652
  412.3 5.3 %shard_map.211 = (bf16[1024,896]{1,0:T(8,128)(2,1)}, bf16[512,512]{1,0:T(8,128)(2,1)}) custom-call(bf16[32,64,128]{2,1,0:T(8,128)(2,1)} %copy-done.2, bf16[512,1024]{1,0:T(8,128)(2,1)} %get-tuple-element.201.hidden_ref, bf16[1024,896]{1,0:T(8,128)(2,1)} %bitcast.54, bf16[1024,384]{1,0:T(8,128)(2,1)} %shard_map.210.rest_ref), custom_call_target="tpu_custom_call" | custom-call | flops 600000000 | bytes 5000000 | tf_op jit(solution)/shard_map/pallas_call | solution.py:977
  417.6 5.9 %all-to-all-start.9 = ((bf16[128,8,896]{2,1,0:T(8,128)(2,1)}), bf16[128,8,896]{2,1,0:T(8,128)(2,1)S(1)}, u32[]{:S(2)}, u32[]{:S(2)}) async-start(bf16[128,8,896]{2,1,0:T(8,128)(2,1)} %bitcast.60), calls=%async_computation.10 | async-start | bytes 3670016 | tf_op jit(solution)/shard_map/all_to_all | solution.py:652
  423.5 3.9 shard_map.212
  430.1 5.0 %shard_map.208 = bf16[128,1024]{1,0:T(8,128)(2,1)} custom-call(bf16[32,64,1024]{2,1,0:T(8,128)(2,1)} %all-to-all-done.7.ys_ref, bf16[128,2048]{1,0:T(8,128)(2,1)} %get-tuple-element.195.high_ref, bf16[128,2048]{1,0:T(8,128)(2,1)} %get-tuple-element.196.rest_ref, f32[128,1024]{1,0:T(8,128)} %get-tuple-element.164.mid_ref), custom_call_target="tpu_custom_call" | custom-call | flops 1000000000 | bytes 5000000 | tf_op jit(solution)/shard_map/pallas_call | solution.py:953
  435.1 15.5 %all-to-all-done.9 = bf16[128,8,896]{2,1,0:T(8,128)(2,1)S(1)} async-done(((bf16[128,8,896]{2,1,0:T(8,128)(2,1)}), bf16[128,8,896]{2,1,0:T(8,128)(2,1)S(1)}, u32[]{:S(2)}, u32[]{:S(2)}) %all-to-all-start.9) | async-done | bytes 1835040 | tf_op jit(solution)/shard_map/all_to_all | solution.py:652
  454.4 3.7 collective-permute-done.20.d2_ref
  458.1 5.7 %collective-permute-done.21.d3_ref = bf16[128,1024]{1,0:T(8,128)(2,1)S(1)} collective-permute-done((bf16[128,1024]{1,0:T(8,128)(2,1)}, bf16[128,1024]{1,0:T(8,128)(2,1)S(1)}, u32[]{:S(2)}, u32[]{:S(2)}) %collective-permute-start.21) | collective-permute-done | bytes 262176 | tf_op jit(solution)/shard_map/ppermute | solution.py:674
  (161 shorter events, 77.2 us)
Async XLA Ops:
  7.2 11.4 %collective-permute-start = (bf16[128,1024]{1,0:T(8,128)(2,1)}, bf16[128,1024]{1,0:T(8,128)(2,1)S(1)}, u32[]{:S(2)}, u32[]{:S(2)}) collective-permute-start(bf16[128,1024]{1,0:T(8,128)(2,1)} %bitcast.62), channel_id=1, source_target_pairs={{0,1},{1,0},{2,3},{3,2},{4,5},{5,4},{6,7},{7,6},{8,9},{9,8},{10,11... | collective-permute-start | bytes 786440 | tf_op jit(solution)/shard_map/ppermute | solution.py:664
  8.7 9.9 %collective-permute-start.1 = (bf16[128,1024]{1,0:T(8,128)(2,1)}, bf16[128,1024]{1,0:T(8,128)(2,1)S(1)}, u32[]{:S(2)}, u32[]{:S(2)}) collective-permute-start(bf16[128,1024]{1,0:T(8,128)(2,1)} %bitcast.63), channel_id=1, source_target_pairs={{0,2},{2,0},{1,3},{3,1},{4,6},{6,4},{5,7},{7,5},{8,10},{10,8},{9,1... | collective-permute-start | bytes 786440 | tf_op jit(solution)/shard_map/ppermute | solution.py:664
  19.3 37.0 %all-to-all-start = ((bf16[128,8,896]{2,1,0:T(8,128)(2,1)}), bf16[128,8,896]{2,1,0:T(8,128)(2,1)S(1)}, u32[]{:S(2)}, u32[]{:S(2)}) async-start(bf16[128,8,896]{2,1,0:T(8,128)(2,1)} %bitcast.56), calls=%async_computation | async-start | bytes 3670016 | tf_op jit(solution)/shard_map/all_to_all | solution.py:652
  29.2 131.8 %all-gather.2.cloned.1.call-start = ((), (), s32[]{:S(2)}) async-start(), calls=%async_computation.12 | async-start | bytes 8912896 | tf_op jit(solution)/shard_map/all_gather | solution.py:656
  29.3 27.5 %collective-permute-start.2 = (bf16[128,1024]{1,0:T(8,128)(2,1)S(1)}, bf16[128,1024]{1,0:T(8,128)(2,1)S(1)}, u32[]{:S(2)}, u32[]{:S(2)}) collective-permute-start(bf16[128,1024]{1,0:T(8,128)(2,1)S(1)} %collective-permute-done.1.x2_ref), channel_id=1, source_target_pairs={{0,1},{1,0},{2,3},{3,2},{4,5},{5,4},{6,7},{7,6},{8,9},{9,8},{10,11... | collective-permute-start | bytes 786440 | tf_op jit(solution)/shard_map/ppermute | solution.py:664
  56.3 8.2 %collective-permute-start.12 = (bf16[128,1024]{1,0:T(8,128)(2,1)S(1)}, bf16[128,1024]{1,0:T(8,128)(2,1)S(1)}, u32[]{:S(2)}, u32[]{:S(2)}) collective-permute-start(bf16[128,1024]{1,0:T(8,128)(2,1)S(1)} %bitcast.70), channel_id=1, source_target_pairs={{0,16},{16,0},{1,17},{17,1},{2,18},{18,2},{3,19},{19,3},{4,20},{20... | collective-permute-start | bytes 786440 | tf_op jit(solution)/shard_map/ppermute | solution.py:664
  65.7 20.6 %all-to-all-start.1 = ((bf16[32,64,128]{2,1,0:T(8,128)(2,1)}), bf16[32,64,128]{2,1,0:T(8,128)(2,1)S(1)}, u32[]{:S(2)}, u32[]{:S(2)}) async-start(bf16[32,64,128]{2,1,0:T(8,128)(2,1)} %get-tuple-element.127), calls=%async_computation.1 | async-start | bytes 1048576 | tf_op jit(solution)/shard_map/all_to_all | solution.py:652
  72.6 17.8 %collective-permute-start.3 = (bf16[512,256]{1,0:T(8,128)(2,1)S(1)}, bf16[512,256]{1,0:T(8,128)(2,1)S(1)}, u32[]{:S(2)}, u32[]{:S(2)}) collective-permute-start(bf16[512,256]{1,0:T(8,128)(2,1)S(1)} %get-tuple-element.145.u0_ref), channel_id=1, source_target_pairs={{0,1},{1,0},{2,3},{3,2},{4,5},{5,4},{6,7},{7,6},{8,9},{9,8},{10,11... | collective-permute-start | bytes 786440 | tf_op jit(solution)/shard_map/ppermute | solution.py:664
  72.9 17.6 %collective-permute-start.4 = (bf16[512,256]{1,0:T(8,128)(2,1)S(1)}, bf16[512,256]{1,0:T(8,128)(2,1)S(1)}, u32[]{:S(2)}, u32[]{:S(2)}) collective-permute-start(bf16[512,256]{1,0:T(8,128)(2,1)S(1)} %get-tuple-element.145.u0_ref), channel_id=1, source_target_pairs={{0,2},{2,0},{1,3},{3,1},{4,6},{6,4},{5,7},{7,5},{8,10},{10,8},{9,1... | collective-permute-start | bytes 786440 | tf_op jit(solution)/shard_map/ppermute | solution.py:664
  90.5 26.8 %all-to-all-start.2 = ((bf16[4,1024,128]{2,1,0:T(8,128)(2,1)}), bf16[4,1024,128]{2,1,0:T(8,128)(2,1)S(1)}, u32[]{:S(2)}, u32[]{:S(2)}) async-start(bf16[4,1024,128]{2,1,0:T(8,128)(2,1)} %get-tuple-element.129), calls=%async_computation.2 | async-start | bytes 2097152 | tf_op jit(solution)/shard_map/all_to_all | solution.py:652
  94.4 7.7 %collective-permute-start.6 = (bf16[512,256]{1,0:T(8,128)(2,1)S(1)}, bf16[512,256]{1,0:T(8,128)(2,1)S(1)}, u32[]{:S(2)}, u32[]{:S(2)}) collective-permute-start(bf16[512,256]{1,0:T(8,128)(2,1)S(1)} %get-tuple-element.149.l0_ref), channel_id=1, source_target_pairs={{0,2},{2,0},{1,3},{3,1},{4,6},{6,4},{5,7},{7,5},{8,10},{10,8},{9,1... | collective-permute-start | bytes 786440 | tf_op jit(solution)/shard_map/ppermute | solution.py:664
  98.1 36.3 %collective-permute-start.10 = (bf16[384,1024]{1,0:T(8,128)(2,1)S(1)}, bf16[384,1024]{1,0:T(8,128)(2,1)}, u32[]{:S(2)}, u32[]{:S(2)}) collective-permute-start(bf16[384,1024]{1,0:T(8,128)(2,1)S(1)} %pad_maximum_fusion.w0_ref), channel_id=1, source_target_pairs={{0,2},{2,0},{1,3},{3,1},{4,6},{6,4},{5,7},{7,5},{8,10},{10,8},{9,1... | collective-permute-start | bytes 2359304 | tf_op jit(solution)/shard_map/ppermute | solution.py:664
  99.0 35.4 %collective-permute-start.9 = (bf16[384,1024]{1,0:T(8,128)(2,1)S(1)}, bf16[384,1024]{1,0:T(8,128)(2,1)}, u32[]{:S(2)}, u32[]{:S(2)}) collective-permute-start(bf16[384,1024]{1,0:T(8,128)(2,1)S(1)} %pad_maximum_fusion.w0_ref), channel_id=1, source_target_pairs={{0,1},{1,0},{2,3},{3,2},{4,5},{5,4},{6,7},{7,6},{8,9},{9,8},{10,11... | collective-permute-start | bytes 2359304 | tf_op jit(solution)/shard_map/ppermute | solution.py:664
  117.3 17.1 %collective-permute-start.7 = (bf16[512,256]{1,0:T(8,128)(2,1)S(1)}, bf16[512,256]{1,0:T(8,128)(2,1)S(1)}, u32[]{:S(2)}, u32[]{:S(2)}) collective-permute-start(bf16[512,256]{1,0:T(8,128)(2,1)S(1)} %collective-permute-done.4.u2_ref), channel_id=1, source_target_pairs={{0,1},{1,0},{2,3},{3,2},{4,5},{5,4},{6,7},{7,6},{8,9},{9,8},{10,11... | collective-permute-start | bytes 786440 | tf_op jit(solution)/shard_map/ppermute | solution.py:664
  117.7 16.7 %collective-permute-start.8 = (bf16[512,256]{1,0:T(8,128)(2,1)S(1)}, bf16[512,256]{1,0:T(8,128)(2,1)S(1)}, u32[]{:S(2)}, u32[]{:S(2)}) collective-permute-start(bf16[512,256]{1,0:T(8,128)(2,1)S(1)} %collective-permute-done.6.l2_ref), channel_id=1, source_target_pairs={{0,1},{1,0},{2,3},{3,2},{4,5},{5,4},{6,7},{7,6},{8,9},{9,8},{10,11... | collective-permute-start | bytes 786440 | tf_op jit(solution)/shard_map/ppermute | solution.py:664
  134.5 18.1 %collective-permute-start.11 = (bf16[384,1024]{1,0:T(8,128)(2,1)}, bf16[384,1024]{1,0:T(8,128)(2,1)S(1)}, u32[]{:S(2)}, u32[]{:S(2)}) collective-permute-start(bf16[384,1024]{1,0:T(8,128)(2,1)} %collective-permute-done.10.w2_ref), channel_id=1, source_target_pairs={{0,1},{1,0},{2,3},{3,2},{4,5},{5,4},{6,7},{7,6},{8,9},{9,8},{10,11... | collective-permute-start | bytes 2359304 | tf_op jit(solution)/shard_map/ppermute | solution.py:664
  134.9 11.7 %all-to-all-start.3 = ((bf16[8,2,64,128]{3,2,1,0:T(8,128)(2,1)}), bf16[8,2,64,128]{3,2,1,0:T(8,128)(2,1)S(1)}, u32[]{:S(2)}, u32[]{:S(2)}) async-start(bf16[8,2,64,128]{3,2,1,0:T(8,128)(2,1)} %get-tuple-element.144), calls=%async_computation.3 | async-start | bytes 524288 | tf_op jit(solution)/shard_map/all_to_all | solution.py:652
  153.4 63.2 %all-to-all-start.4 = ((bf16[32,64,1024]{2,1,0:T(8,128)(2,1)}), bf16[32,64,1024]{2,1,0:T(8,128)(2,1)}, u32[]{:S(2)}, u32[]{:S(2)}) async-start(bf16[32,64,1024]{2,1,0:T(8,128)(2,1)} %get-tuple-element.161), calls=%async_computation.4 | async-start | bytes 8388608 | tf_op jit(solution)/shard_map/all_to_all | solution.py:652
  159.8 70.7 %collective-permute-start.13 = (bf16[8,2,64,128]{3,2,1,0:T(8,128)(2,1)S(1)}, bf16[8,2,64,128]{3,2,1,0:T(8,128)(2,1)S(1)}, u32[]{:S(2)}, u32[]{:S(2)}) collective-permute-start(bf16[8,2,64,128]{3,2,1,0:T(8,128)(2,1)S(1)} %copy-done.8), channel_id=1, source_target_pairs={{0,1},{1,0},{2,3},{3,2},{4,5},{5,4},{6,7},{7,6},{8,9},{9,8},{10,11... | collective-permute-start | bytes 786440 | tf_op jit(solution)/shard_map/ppermute | solution.py:664
  160.8 69.7 %collective-permute-start.14 = (bf16[8,2,64,128]{3,2,1,0:T(8,128)(2,1)S(1)}, bf16[8,2,64,128]{3,2,1,0:T(8,128)(2,1)S(1)}, u32[]{:S(2)}, u32[]{:S(2)}) collective-permute-start(bf16[8,2,64,128]{3,2,1,0:T(8,128)(2,1)S(1)} %copy-done.8), channel_id=1, source_target_pairs={{0,2},{2,0},{1,3},{3,1},{4,6},{6,4},{5,7},{7,5},{8,10},{10,8},{9,1... | collective-permute-start | bytes 786440 | tf_op jit(solution)/shard_map/ppermute | solution.py:664
  231.1 67.2 %all-to-all-start.5 = ((bf16[32,64,1024]{2,1,0:T(8,128)(2,1)}), bf16[32,64,1024]{2,1,0:T(8,128)(2,1)}, u32[]{:S(2)}, u32[]{:S(2)}) async-start(bf16[32,64,1024]{2,1,0:T(8,128)(2,1)} %get-tuple-element.174), calls=%async_computation.5 | async-start | bytes 8388608 | tf_op jit(solution)/shard_map/all_to_all | solution.py:652
  240.3 17.0 %collective-permute-start.15 = (bf16[8,2,64,128]{3,2,1,0:T(8,128)(2,1)S(1)}, bf16[8,2,64,128]{3,2,1,0:T(8,128)(2,1)S(1)}, u32[]{:S(2)}, u32[]{:S(2)}) collective-permute-start(bf16[8,2,64,128]{3,2,1,0:T(8,128)(2,1)S(1)} %collective-permute-done.14.o2_ref), channel_id=1, source_target_pairs={{0,1},{1,0},{2,3},{3,2},{4,5},{5,4},{6,7},{7,6},{8,9},{9,8},{10,11... | collective-permute-start | bytes 786440 | tf_op jit(solution)/shard_map/ppermute | solution.py:664
  318.2 67.6 %all-to-all-start.7 = ((bf16[32,64,1024]{2,1,0:T(8,128)(2,1)}), bf16[32,64,1024]{2,1,0:T(8,128)(2,1)}, u32[]{:S(2)}, u32[]{:S(2)}) async-start(bf16[32,64,1024]{2,1,0:T(8,128)(2,1)} %get-tuple-element.192), calls=%async_computation.8 | async-start | bytes 8388608 | tf_op jit(solution)/shard_map/all_to_all | solution.py:652
  324.6 61.1 %reduce-scatter.3.cloned.1.call-start = ((), (), s32[]{:S(2)}) async-start(), calls=%async_computation.13 | async-start | bytes 1310720 | tf_op jit(solution)/shard_map/reduce_scatter | solution.py:939
  344.8 122.9 %reduce-scatter.5.cloned.1.call-start = ((), (), s32[]{:S(2)}) async-start(), calls=%async_computation.14 | async-start | bytes 3932160 | tf_op jit(solution)/shard_map/reduce_scatter | solution.py:943
  348.8 17.6 %collective-permute-start.17 = (bf16[128,256]{1,0:T(8,128)(2,1)S(1)}, bf16[128,256]{1,0:T(8,128)(2,1)S(1)}, u32[]{:S(2)}, u32[]{:S(2)}) collective-permute-start(bf16[128,256]{1,0:T(8,128)(2,1)S(1)} %get-tuple-element.236), channel_id=1, source_target_pairs={{0,2},{1,3},{2,0},{3,1},{4,6},{5,7},{6,4},{7,5},{8,10},{9,11},{10,... | collective-permute-start | bytes 196616 | tf_op jit(solution)/shard_map/ppermute | solution.py:674
  348.9 19.8 %collective-permute-start.18 = (bf16[128,256]{1,0:T(8,128)(2,1)S(1)}, bf16[128,256]{1,0:T(8,128)(2,1)S(1)}, u32[]{:S(2)}, u32[]{:S(2)}) collective-permute-start(bf16[128,256]{1,0:T(8,128)(2,1)S(1)} %get-tuple-element.235), channel_id=1, source_target_pairs={{0,3},{1,2},{2,1},{3,0},{4,7},{5,6},{6,5},{7,4},{8,11},{9,10},{10,... | collective-permute-start | bytes 196616 | tf_op jit(solution)/shard_map/ppermute | solution.py:674
  389.8 21.8 %all-to-all-start.8 = ((bf16[32,64,128]{2,1,0:T(8,128)(2,1)}), bf16[32,64,128]{2,1,0:T(8,128)(2,1)S(1)}, u32[]{:S(2)}, u32[]{:S(2)}) async-start(bf16[32,64,128]{2,1,0:T(8,128)(2,1)} %bitcast.59), calls=%async_computation.9 | async-start | bytes 1048576 | tf_op jit(solution)/shard_map/all_to_all | solution.py:652
  417.6 33.0 %all-to-all-start.9 = ((bf16[128,8,896]{2,1,0:T(8,128)(2,1)}), bf16[128,8,896]{2,1,0:T(8,128)(2,1)S(1)}, u32[]{:S(2)}, u32[]{:S(2)}) async-start(bf16[128,8,896]{2,1,0:T(8,128)(2,1)} %bitcast.60), calls=%async_computation.10 | async-start | bytes 3670016 | tf_op jit(solution)/shard_map/all_to_all | solution.py:652
  427.4 27.0 %collective-permute-start.19 = (bf16[128,1024]{1,0:T(8,128)(2,1)}, bf16[128,1024]{1,0:T(8,128)(2,1)S(1)}, u32[]{:S(2)}, u32[]{:S(2)}) collective-permute-start(bf16[128,1024]{1,0:T(8,128)(2,1)} %get-tuple-element.213), channel_id=1, source_target_pairs={{0,1},{1,0},{2,3},{3,2},{4,5},{5,4},{6,7},{7,6},{8,9},{9,8},{10,11... | collective-permute-start | bytes 786440 | tf_op jit(solution)/shard_map/ppermute | solution.py:674
  428.4 29.7 %collective-permute-start.20 = (bf16[128,1024]{1,0:T(8,128)(2,1)}, bf16[128,1024]{1,0:T(8,128)(2,1)S(1)}, u32[]{:S(2)}, u32[]{:S(2)}) collective-permute-start(bf16[128,1024]{1,0:T(8,128)(2,1)} %get-tuple-element.214), channel_id=1, source_target_pairs={{0,2},{1,3},{2,0},{3,1},{4,6},{5,7},{6,4},{7,5},{8,10},{9,11},{10,... | collective-permute-start | bytes 786440 | tf_op jit(solution)/shard_map/ppermute | solution.py:674
  429.2 34.5 %collective-permute-start.21 = (bf16[128,1024]{1,0:T(8,128)(2,1)}, bf16[128,1024]{1,0:T(8,128)(2,1)S(1)}, u32[]{:S(2)}, u32[]{:S(2)}) collective-permute-start(bf16[128,1024]{1,0:T(8,128)(2,1)} %get-tuple-element.215), channel_id=1, source_target_pairs={{0,3},{1,2},{2,1},{3,0},{4,7},{5,6},{6,5},{7,4},{8,11},{9,10},{10,... | collective-permute-start | bytes 786440 | tf_op jit(solution)/shard_map/ppermute | solution.py:674
  (37 other events, 502.7 us)
Sparse Core Ops, SparseCore 0:
  65.6 77.8 all-gather.1
  345.0 40.7 reduce-scatter.2
  388.3 70.9 reduce-scatter.4

commit v4 on v3

--- a/solution.py
+++ b/solution.py
@@ -279,7 +279,7 @@
 
 
 def kernel_attend_back(
-    mine_ref, keys_ref, turned_ref, q_ref, grad_ref, log_ref, out_ref, dq_ref, dkv_ref, sum_ref
+    mine_ref, keys_ref, turned_ref, q_ref, grad_ref, log_ref, out_ref, dq_ref, d0_ref, d1_ref, d2_ref, d3_ref, sum_ref
 ):
     tile = pl.program_id(0)
 
@@ -325,9 +325,10 @@
     def _():
         for group in range(16):
             half, place = (0, group) if group < 8 else (1, 15 - group)
-            for y in range(4):
-                at = 256 * group + 64 * y
-                dkv_ref[y, half, place] = sum_ref[at : at + 64, :].astype(BF)
+            for r, dkv_ref in enumerate((d0_ref, d1_ref, d2_ref, d3_ref)):
+                at = 256 * group + 64 * lax.bitwise_xor(mine_ref[0], r)
+                part = sum_ref[pl.ds(pl.multiple_of(at, 64), 64), :]
+                dkv_ref[half, place] = part.astype(BF)
 
 
 def kernel_middle(
@@ -529,7 +530,9 @@
         grad_ref[128 * g : 128 * g + 128, 128:384] = part.astype(BF)
 
 
-def kernel_slices_back(dkv_ref, dq_ref, cos_ref, sin_ref, table_ref, msg_ref):
+def kernel_slices_back(
+    d0_ref, d1_ref, d2_ref, d3_ref, dq_ref, cos_ref, sin_ref, table_ref, msg_ref
+):
     def unrotate(w, cos, sin):
         partner = jnp.where(
             lane(w.shape) % 64 < 32, pltpu.roll(w, 96, 1), pltpu.roll(w, 32, 1)
@@ -539,7 +542,10 @@
     parts = []
     for half in range(2):
         at = slice(512 * half, 512 * half + 512)
-        parts.append(unrotate(dkv_ref[at, :].astype(F32), cos_ref[at, :], sin_ref[at, :]))
+        dkv = d0_ref[half].reshape(512, 128).astype(F32)
+        for d_ref in (d1_ref, d2_ref, d3_ref):
+            dkv = dkv + d_ref[half].reshape(512, 128).astype(F32)
+        parts.append(unrotate(dkv, cos_ref[at, :], sin_ref[at, :]))
     for half in range(2):
         at = slice(512 * half, 512 * half + 512)
         for head in range(2):
@@ -668,10 +674,10 @@
     return value, swap(value, "core"), swap(value, "zl")
 
 
-def cross(parts):
+def cross(parts, axes=FSDP):
     here = [parts[0]]
     for r in range(1, 4):
-        here.append(lax.ppermute(parts[r], FSDP, [(f, f ^ r) for f in range(4)]))
+        here.append(lax.ppermute(parts[r], axes, [(i, i ^ r) for i in range(4)]))
     return here
 
 
@@ -753,7 +759,6 @@
     cot_pair = jnp.concatenate(
         [jnp.where(first, cot, across), jnp.where(first, across, cot)], axis=0
     )
-    cot_all = gather(after(cot_pair, msg), ("x", "y")).reshape(4, 4, 2, 128, WIDTH)
     out_upper = neighbours(w_slice[0:512, 640:896])
     msg = exchange(msg, HEAD_AXES + FSDP)
 
@@ -787,6 +792,7 @@
         (kv, out_lower, cos_heads, sin_heads)
     )
     experts_all = neighbours(after(expert_weights, msg))
+    cot_all = gather(after(cot_pair, kv_copies), ("x", "y")).reshape(4, 4, 2, 128, WIDTH)
     out_upper = out_upper + (swap(after(out_upper[2], kv), "core"),)
     out_lower = out_lower + (swap(out_lower[2], "core"),)
     w_out = (*out_upper, *out_lower)
@@ -886,7 +892,10 @@
     dxs, o_all = lax.optimization_barrier((dxs, o_all))
     o_all = o_all + (swap(o_all[2], "core"),)
     dxs = exchange(dxs, CTX)
-    dxs, ys, expert_grads, o_all = lax.optimization_barrier((dxs, ys, expert_grads, o_all))
+    expert_own = lax.psum_scatter(
+        expert_grads.reshape(4 * 384, WIDTH), FSDP, scatter_dimension=0, tiled=True
+    ).astype(F32)
+    dxs, ys, o_all = lax.optimization_barrier((dxs, ys, o_all))
 
     dmid, da_parts, grad_msg, gain_ffn_part = call(
         kernel_middle_back,
@@ -918,9 +927,9 @@
     grad_heads = exchange(grad_msg, HEAD_AXES)
     ys, grad_heads = lax.optimization_barrier((ys, grad_heads))
     ys = exchange(ys, CTX)
-    dq, dkv = call(
+    dq, *dkv = call(
         kernel_attend_back,
-        (sds((2048, 128), F32), sds((4, 2, 8, 64, 128), BF)),
+        (sds((2048, 128), F32),) + (sds((2, 8, 64, 128), BF),) * 4,
         (2e10, 7e6),
         grid=(8,),
         in_specs=[
@@ -932,17 +941,12 @@
             log_spec,
             row_spec,
         ],
-        out_specs=(row_spec, whole((4, 2, 8, 64, 128))),
+        out_specs=(row_spec,) + (whole((2, 8, 64, 128)),) * 4,
         scratch_shapes=[pltpu.VMEM((4096, 128), F32)],
     )(mine_ref, keys, turned, queries, grad_heads, log_total, o_rows)
     da_here = cross(da_parts)
-    dkv = lax.psum_scatter(
-        dkv.reshape(4096, 128), ("y",), scatter_dimension=0, tiled=True
-    )
+    dkv = cross(dkv, ("y",))
     dkv, ys, da_here = lax.optimization_barrier((dkv, ys, da_here))
-    expert_own = lax.psum_scatter(
-        after(expert_grads, dkv).reshape(4 * 384, WIDTH), FSDP, scatter_dimension=0, tiled=True
-    ).astype(F32)
     rest_part = call(
         kernel_out_weight,
         sds((WIDTH, 384), BF),
@@ -969,9 +973,9 @@
         kernel_slices_back,
         sds((8, 4, 64, 128), BF),
         (4e8, 5e6),
-        in_specs=[VM] * 5,
+        in_specs=[VM] * 8,
         out_specs=VM,
-    )(dkv, dq.reshape(2, 8, 2, 64, 128), cos_heads, sin_heads, head_table)
+    )(*dkv, dq.reshape(2, 8, 2, 64, 128), cos_heads, sin_heads, head_table)
     back = exchange(back.reshape(32, 64, 128), HEAD_AXES + FSDP)
 
     grads, d_all = call(

time: 487 us -> 478 us (0.982)
  waiting for transfers between devices: 214 us -> 192 us
  starting transfers between devices: 79.6 us -> 91.3 us
    reduce_scatter x2 -> x1, waiting for transfers between devices: 17.1 us -> 0.02 us  [on_device(): lax.psum_scatter(expert_grads.reshape(4 * 384, WIDTH), FSDP, scatter_dime...]
    ppermute x6 -> x9, starting transfers between devices: 7.6 us -> 16.3 us  [cross(): here.append(lax.ppermute(parts[r], axes, [(i, i ^ r) for i in range(4)]))]
    all_to_all x9, waiting for transfers between devices: 165 us -> 158 us  [exchange(): return lax.all_to_all(value, axes, split_axis=0, concat_axis=0, tiled=True)]
    ppermute x6 -> x9, waiting for transfers between devices: 27.5 us -> 29.2 us  [cross(): here.append(lax.ppermute(parts[r], axes, [(i, i ^ r) for i in range(4)]))]
  transfers between devices with their start and end apart: 34 -> 36, of which waited for: 15 -> 14; matrix products, arithmetic and copies ran while one was open for 3% -> 4% of each run, Pallas kernels for 26% -> 27%
where the time goes in v4:
time: 478 us; the launch traced here: 470 us
  waiting for transfers between devices  192 us (40%)
  Pallas kernels  130 us (27%)
  starting transfers between devices  91.3 us (19%)
  local copies, waits for them, and re-layouts  16.9 us (4%)
  blocking collectives  15.8 us (3%)
  between operations  15.1 us (3%)
  other arithmetic  8.93 us (2%)
    all_to_all x9, waiting for transfers between devices, exchange(): return lax.all_to_all(value, axes, split_axis=0, concat_axis=0, tiled=True)  158 us
    all_to_all x9, starting transfers between devices, exchange(): return lax.all_to_all(value, axes, split_axis=0, concat_axis=0, tiled=True)  60.2 us
    ppermute x9, waiting for transfers between devices, cross(): here.append(lax.ppermute(parts[r], axes, [(i, i ^ r) for i in range(4)]))  29.2 us
    pallas_call x1, Pallas kernels, on_device(): call(kernel_attend_back, (sds((2048, 128), F32),) + (sds((2, 8, 64, 128),...  20.2 us
    ppermute x9, starting transfers between devices, cross(): here.append(lax.ppermute(parts[r], axes, [(i, i ^ r) for i in range(4)]))  16.3 us
    pallas_call x1, Pallas kernels, on_device(): call(kernel_attend, (sds((8, 2, 64, 128), BF), sds((8, 8, 256), F32), sds...  16 us
    pallas_call x1, Pallas kernels, on_device(): call(kernel_experts_after, (sds((32, 64, WIDTH), BF), sds((4, 384, WIDTH)...  15.9 us
    all_to_all x1, blocking collectives, exchange(): return lax.all_to_all(value, axes, split_axis=0, concat_axis=0, tiled=True)  15.8 us
  transfers between devices with their start and end apart: 36, of which 14 were waited for; matrix products, arithmetic and copies ran while one was open for 4% of the time, Pallas kernels for 27%

profile of v4, /device:TPU:1, one launch (start us, length us, event | category | flops | bytes accessed | tf_op | source)
XLA Modules:
  0.0 469.9 jit_solution(1545702427753288170)
XLA Ops:
  19.3 9.9 %all-to-all-start = ((bf16[128,8,896]{2,1,0:T(8,128)(2,1)}), bf16[128,8,896]{2,1,0:T(8,128)(2,1)S(1)}, u32[]{:S(2)}, u32[]{:S(2)}) async-start(bf16[128,8,896]{2,1,0:T(8,128)(2,1)} %bitcast.55), calls=%async_computation | async-start | bytes 3670016 | tf_op jit(solution)/shard_map/all_to_all | solution.py:658
  32.3 24.0 %all-to-all-done = bf16[128,8,896]{2,1,0:T(8,128)(2,1)S(1)} async-done(((bf16[128,8,896]{2,1,0:T(8,128)(2,1)}), bf16[128,8,896]{2,1,0:T(8,128)(2,1)S(1)}, u32[]{:S(2)}, u32[]{:S(2)}) %all-to-all-start) | async-done | bytes 1835040 | tf_op jit(solution)/shard_map/all_to_all | solution.py:658
  57.6 4.6 shard_map.198
  62.2 6.0 %all-to-all-start.1 = ((bf16[32,64,128]{2,1,0:T(8,128)(2,1)}), bf16[32,64,128]{2,1,0:T(8,128)(2,1)S(1)}, u32[]{:S(2)}, u32[]{:S(2)}) async-start(bf16[32,64,128]{2,1,0:T(8,128)(2,1)} %get-tuple-element.131), calls=%async_computation.1 | async-start | bytes 1048576 | tf_op jit(solution)/shard_map/all_to_all | solution.py:658
  72.2 7.7 %all-to-all-done.1 = bf16[32,64,128]{2,1,0:T(8,128)(2,1)S(1)} async-done(((bf16[32,64,128]{2,1,0:T(8,128)(2,1)}), bf16[32,64,128]{2,1,0:T(8,128)(2,1)S(1)}, u32[]{:S(2)}, u32[]{:S(2)}) %all-to-all-start.1) | async-done | bytes 524320 | tf_op jit(solution)/shard_map/all_to_all | solution.py:658
  84.4 3.7 all-to-all-start.2
  96.1 14.1 %all-to-all-done.2 = bf16[4,1024,128]{2,1,0:T(8,128)(2,1)S(1)} async-done(((bf16[4,1024,128]{2,1,0:T(8,128)(2,1)}), bf16[4,1024,128]{2,1,0:T(8,128)(2,1)S(1)}, u32[]{:S(2)}, u32[]{:S(2)}) %all-to-all-start.2) | async-done | bytes 1048608 | tf_op jit(solution)/shard_map/all_to_all | solution.py:658
  111.9 16.0 %shard_map.200 = (bf16[8,2,64,128]{3,2,1,0:T(8,128)(2,1)}, f32[8,8,256]{2,1,0:T(8,128)}, f32[2048,128]{1,0:T(8,128)}, bf16[4096,128]{1,0:T(8,128)(2,1)}, bf16[128,4096]{1,0:T(8,128)(2,1)}) custom-call(s32[1]{0:T(128)} %bitcast.mine_ref, bf16[4,2,8,64,128]{4,3,2,1,0:T(8,128)(2,1)} %bitcast.66, bf16[2048,128]{1,0:T(8,128)(2,1)} %bitcast.75), custom_call_target="tpu_custom_call" | custom-call | flops 10000000000 | bytes 5000000 | tf_op jit(solution)/shard_map/pallas_call | solution.py:802
  134.4 7.4 %all-to-all-done.3.o_ref.o0_ref = bf16[8,2,64,128]{3,2,1,0:T(8,128)(2,1)S(1)} async-done(((bf16[8,2,64,128]{3,2,1,0:T(8,128)(2,1)}), bf16[8,2,64,128]{3,2,1,0:T(8,128)(2,1)S(1)}, u32[]{:S(2)}, u32[]{:S(2)}) %all-to-all-start.3) | async-done | bytes 262176 | tf_op jit(solution)/shard_map/all_to_all | solution.py:658
  142.5 5.3 %shard_map.202 = (bf16[32,64,1024]{2,1,0:T(8,128)(2,1)}, f32[128,1024]{1,0:T(8,128)}) custom-call(s32[1]{0:T(128)} %bitcast.1.part_ref, bf16[8,2,64,128]{3,2,1,0:T(8,128)(2,1)} %copy-done.7, bf16[512,256]{1,0:T(8,128)(2,1)} %copy-done.6, bf16[512,256]{1,0:T(8,128)(2,1)} %copy-done.14, bf16[512,256]{1,0:T(8,128)(2,1)} %copy-done.15, ...), custom_call_target="tpu_custom_call" | custom-call | flops 900000000 | bytes 8000000 | tf_op jit(solution)/shard_map/pallas_call | solution.py:822
  148.6 5.5 %all-to-all-start.4 = ((bf16[32,64,1024]{2,1,0:T(8,128)(2,1)}), bf16[32,64,1024]{2,1,0:T(8,128)(2,1)}, u32[]{:S(2)}, u32[]{:S(2)}) async-start(bf16[32,64,1024]{2,1,0:T(8,128)(2,1)} %get-tuple-element.165), calls=%async_computation.4 | async-start | bytes 8388608 | tf_op jit(solution)/shard_map/all_to_all | solution.py:658
  158.8 12.5 %shard_map.203 = (bf16[32,64,1024]{2,1,0:T(8,128)(2,1)}, f32[2048,512]{1,0:T(8,128)}, bf16[512,1024]{1,0:T(8,128)(2,1)}, bf16[1024,1024]{1,0:T(8,128)(2,1)}) custom-call(s32[1]{0:T(128)} %bitcast.1.part_ref, bf16[4,4,2,128,1024]{4,3,2,1,0:T(8,128)(2,1)} %bitcast.74, bf16[32,8,128]{2,1,0:T(8,128)(2,1)} %dynamic-slice_bitcast_fusion.parts_ref, ...), custom_call_target="tpu_custom_call" | custom-call | flops 6000000000 | bytes 20000000 | tf_op jit(solution)/shard_map/pallas_call | solution.py:841
  171.3 46.2 %all-to-all-done.4.h_ref = bf16[32,64,1024]{2,1,0:T(8,128)(2,1)} async-done(((bf16[32,64,1024]{2,1,0:T(8,128)(2,1)}), bf16[32,64,1024]{2,1,0:T(8,128)(2,1)}, u32[]{:S(2)}, u32[]{:S(2)}) %all-to-all-start.4) | async-done | bytes 4194336 | tf_op jit(solution)/shard_map/all_to_all | solution.py:658
  217.5 13.8 %shard_map.204 = (bf16[2048,512]{1,0:T(8,128)(2,1)}, bf16[2048,1024]{1,0:T(8,128)(2,1)}, bf16[32,64,1024]{2,1,0:T(8,128)(2,1)}) custom-call(bf16[32,64,1024]{2,1,0:T(8,128)(2,1)} %all-to-all-done.4.h_ref, bf16[1024,1024]{1,0:T(8,128)(2,1)} %get-tuple-element.174.gu_ref, f32[2048,512]{1,0:T(8,128)} %get-tuple-element.175.dact_ref), custom_call_target="tpu_custom_call" | custom-call | flops 8999999488 | bytes 20000000 | tf_op jit(solution)/shard_map/pallas_call | solution.py:867
  232.1 7.0 %all-to-all-start.5 = ((bf16[32,64,1024]{2,1,0:T(8,128)(2,1)}), bf16[32,64,1024]{2,1,0:T(8,128)(2,1)}, u32[]{:S(2)}, u32[]{:S(2)}) async-start(bf16[32,64,1024]{2,1,0:T(8,128)(2,1)} %get-tuple-element.178), calls=%async_computation.5 | async-start | bytes 8388608 | tf_op jit(solution)/shard_map/all_to_all | solution.py:658
  240.9 15.9 %shard_map.205 = (bf16[32,64,1024]{2,1,0:T(8,128)(2,1)}, bf16[4,384,1024]{2,1,0:T(8,128)(2,1)}) custom-call(bf16[32,64,1024]{2,1,0:T(8,128)(2,1)} %all-to-all-done.4.h_ref, bf16[2048,512]{1,0:T(8,128)(2,1)} %get-tuple-element.179.act_ref, bf16[32,64,1024]{2,1,0:T(8,128)(2,1)} %get-tuple-element.180.dys_ref, bf16[2048,1024]{1,0:T(8,128)(2,1)} %get-tuple-element.181.dboth_ref, ...), custom_call_target="tpu_custom_call" | custom-call | flops 8999999488 | bytes 20000000 | tf_op jit(solution)/shard_map/pallas_call | solution.py:883
  256.9 37.9 %all-to-all-done.5.dxs_ref = bf16[32,64,1024]{2,1,0:T(8,128)(2,1)} async-done(((bf16[32,64,1024]{2,1,0:T(8,128)(2,1)}), bf16[32,64,1024]{2,1,0:T(8,128)(2,1)}, u32[]{:S(2)}, u32[]{:S(2)}) %all-to-all-start.5) | async-done | bytes 4194336 | tf_op jit(solution)/shard_map/all_to_all | solution.py:658
  294.8 5.8 %shard_map.206 = (f32[128,1024]{1,0:T(8,128)}, bf16[4,128,256]{2,1,0:T(8,128)(2,1)}, bf16[8,2,64,128]{3,2,1,0:T(8,128)(2,1)}, f32[8,1024]{1,0:T(8,128)}) custom-call(s32[1]{0:T(128)} %bitcast.1.part_ref, bf16[32,64,1024]{2,1,0:T(8,128)(2,1)} %all-to-all-done.5.dxs_ref, bf16[128,2048]{1,0:T(8,128)(2,1)} %get-tuple-element.189.pick_ref, ...), custom_call_target="tpu_custom_call" | custom-call | flops 900000000 | bytes 8000000 | tf_op jit(solution)/shard_map/pallas_call | solution.py:900
  300.6 15.8 %all_to_all.50.grad_ref = bf16[8,2,64,128]{3,2,1,0:T(8,128)(2,1)} all-to-all(bf16[8,2,64,128]{3,2,1,0:T(8,128)(2,1)} %get-tuple-element.190), channel_id=1, replica_groups=mesh['x'=4,'zh'=2,'y'=4,'zl'=2,'core'=2] {'x','zh'}, dimensions={0} | all-to-all | bytes 524288 | tf_op jit(solution)/shard_map/all_to_all | solution.py:658
  316.4 4.9 %all-to-all-start.7 = ((bf16[32,64,1024]{2,1,0:T(8,128)(2,1)}), bf16[32,64,1024]{2,1,0:T(8,128)(2,1)}, u32[]{:S(2)}, u32[]{:S(2)}) async-start(bf16[32,64,1024]{2,1,0:T(8,128)(2,1)} %get-tuple-element.198), calls=%async_computation.7 | async-start | bytes 8388608 | tf_op jit(solution)/shard_map/all_to_all | solution.py:658
  321.3 20.2 %shard_map.207 = (f32[2048,128]{1,0:T(8,128)}, bf16[2,8,64,128]{3,2,1,0:T(8,128)(2,1)}, bf16[2,8,64,128]{3,2,1,0:T(8,128)(2,1)}, bf16[2,8,64,128]{3,2,1,0:T(8,128)(2,1)}, bf16[2,8,64,128]{3,2,1,0:T(8,128)(2,1)}) custom-call(s32[1]{0:T(128)} %bitcast.mine_ref, bf16[4096,128]{1,0:T(8,128)(2,1)} %get-tuple-element.137.keys_ref, ...), custom_call_target="tpu_custom_call" | custom-call | flops 20000000000 | bytes 7000000 | tf_op jit(solution)/shard_map/pallas_call | solution.py:930
  346.1 5.1 %collective-permute-start.19 = (bf16[128,256]{1,0:T(8,128)(2,1)S(1)}, bf16[128,256]{1,0:T(8,128)(2,1)S(1)}, u32[]{:S(2)}, u32[]{:S(2)}) collective-permute-start(bf16[128,256]{1,0:T(8,128)(2,1)S(1)} %get-tuple-element.245), channel_id=1, source_target_pairs={{0,1},{1,0},{2,3},{3,2},{4,5},{5,4},{6,7},{7,6},{8,9},{9,8},{10,11... | collective-permute-start | bytes 196616 | tf_op jit(solution)/shard_map/ppermute | solution.py:680
  355.7 13.8 %collective-permute-done.20.da2_ref = bf16[128,256]{1,0:T(8,128)(2,1)S(1)} collective-permute-done((bf16[128,256]{1,0:T(8,128)(2,1)S(1)}, bf16[128,256]{1,0:T(8,128)(2,1)S(1)}, u32[]{:S(2)}, u32[]{:S(2)}) %collective-permute-start.20) | collective-permute-done | bytes 65568 | tf_op jit(solution)/shard_map/ppermute | solution.py:680
  372.6 9.5 %collective-permute-done.17.d2_ref = bf16[2,8,64,128]{3,2,1,0:T(8,128)(2,1)S(1)} collective-permute-done((bf16[2,8,64,128]{3,2,1,0:T(8,128)(2,1)}, bf16[2,8,64,128]{3,2,1,0:T(8,128)(2,1)S(1)}, u32[]{:S(2)}, u32[]{:S(2)}) %collective-permute-start.17) | collective-permute-done | bytes 262176 | tf_op jit(solution)/shard_map/ppermute | solution.py:680
  382.9 4.3 shard_map.209
  387.2 15.0 %all-to-all-start.8 = ((bf16[32,64,128]{2,1,0:T(8,128)(2,1)}), bf16[32,64,128]{2,1,0:T(8,128)(2,1)S(1)}, u32[]{:S(2)}, u32[]{:S(2)}) async-start(bf16[32,64,128]{2,1,0:T(8,128)(2,1)} %bitcast.58), calls=%async_computation.8 | async-start | bytes 1048576 | tf_op jit(solution)/shard_map/all_to_all | solution.py:658
  405.1 8.7 %all-to-all-done.8.msg_ref = bf16[32,64,128]{2,1,0:T(8,128)(2,1)S(1)} async-done(((bf16[32,64,128]{2,1,0:T(8,128)(2,1)}), bf16[32,64,128]{2,1,0:T(8,128)(2,1)S(1)}, u32[]{:S(2)}, u32[]{:S(2)}) %all-to-all-start.8) | async-done | bytes 524320 | tf_op jit(solution)/shard_map/all_to_all | solution.py:658
  414.6 5.3 %shard_map.211 = (bf16[1024,896]{1,0:T(8,128)(2,1)}, bf16[512,512]{1,0:T(8,128)(2,1)}) custom-call(bf16[32,64,128]{2,1,0:T(8,128)(2,1)} %copy-done.2, bf16[512,1024]{1,0:T(8,128)(2,1)} %get-tuple-element.210.hidden_ref, bf16[1024,896]{1,0:T(8,128)(2,1)} %bitcast.53, bf16[1024,384]{1,0:T(8,128)(2,1)} %shard_map.210.rest_ref), custom_call_target="tpu_custom_call" | custom-call | flops 600000000 | bytes 5000000 | tf_op jit(solution)/shard_map/pallas_call | solution.py:981
  419.9 4.8 %all-to-all-start.9 = ((bf16[128,8,896]{2,1,0:T(8,128)(2,1)}), bf16[128,8,896]{2,1,0:T(8,128)(2,1)S(1)}, u32[]{:S(2)}, u32[]{:S(2)}) async-start(bf16[128,8,896]{2,1,0:T(8,128)(2,1)} %bitcast.59), calls=%async_computation.9 | async-start | bytes 3670016 | tf_op jit(solution)/shard_map/all_to_all | solution.py:658
  427.1 3.9 shard_map.212
  434.5 5.0 %shard_map.208 = bf16[128,1024]{1,0:T(8,128)(2,1)} custom-call(bf16[32,64,1024]{2,1,0:T(8,128)(2,1)} %all-to-all-done.7.ys_ref, bf16[128,2048]{1,0:T(8,128)(2,1)} %get-tuple-element.201.high_ref, bf16[128,2048]{1,0:T(8,128)(2,1)} %get-tuple-element.202.rest_ref, f32[128,1024]{1,0:T(8,128)} %get-tuple-element.168.mid_ref), custom_call_target="tpu_custom_call" | custom-call | flops 1000000000 | bytes 5000000 | tf_op jit(solution)/shard_map/pallas_call | solution.py:957
  439.6 12.3 %all-to-all-done.9 = bf16[128,8,896]{2,1,0:T(8,128)(2,1)S(1)} async-done(((bf16[128,8,896]{2,1,0:T(8,128)(2,1)}), bf16[128,8,896]{2,1,0:T(8,128)(2,1)S(1)}, u32[]{:S(2)}, u32[]{:S(2)}) %all-to-all-start.9) | async-done | bytes 1835040 | tf_op jit(solution)/shard_map/all_to_all | solution.py:658
  (168 shorter events, 82.8 us)
Async XLA Ops:
  7.2 11.4 %collective-permute-start = (bf16[128,1024]{1,0:T(8,128)(2,1)}, bf16[128,1024]{1,0:T(8,128)(2,1)S(1)}, u32[]{:S(2)}, u32[]{:S(2)}) collective-permute-start(bf16[128,1024]{1,0:T(8,128)(2,1)} %bitcast.61), channel_id=1, source_target_pairs={{0,1},{1,0},{2,3},{3,2},{4,5},{5,4},{6,7},{7,6},{8,9},{9,8},{10,11... | collective-permute-start | bytes 786440 | tf_op jit(solution)/shard_map/ppermute | solution.py:670
  19.3 37.0 %all-to-all-start = ((bf16[128,8,896]{2,1,0:T(8,128)(2,1)}), bf16[128,8,896]{2,1,0:T(8,128)(2,1)S(1)}, u32[]{:S(2)}, u32[]{:S(2)}) async-start(bf16[128,8,896]{2,1,0:T(8,128)(2,1)} %bitcast.55), calls=%async_computation | async-start | bytes 3670016 | tf_op jit(solution)/shard_map/all_to_all | solution.py:658
  29.2 27.6 %collective-permute-start.2 = (bf16[128,1024]{1,0:T(8,128)(2,1)S(1)}, bf16[128,1024]{1,0:T(8,128)(2,1)S(1)}, u32[]{:S(2)}, u32[]{:S(2)}) collective-permute-start(bf16[128,1024]{1,0:T(8,128)(2,1)S(1)} %collective-permute-done.1.x2_ref), channel_id=1, source_target_pairs={{0,1},{1,0},{2,3},{3,2},{4,5},{5,4},{6,7},{7,6},{8,9},{9,8},{10,11... | collective-permute-start | bytes 786440 | tf_op jit(solution)/shard_map/ppermute | solution.py:670
  56.3 14.9 %collective-permute-start.12 = (bf16[128,1024]{1,0:T(8,128)(2,1)S(1)}, bf16[128,1024]{1,0:T(8,128)(2,1)S(1)}, u32[]{:S(2)}, u32[]{:S(2)}) collective-permute-start(bf16[128,1024]{1,0:T(8,128)(2,1)S(1)} %bitcast.68), channel_id=1, source_target_pairs={{0,16},{16,0},{1,17},{17,1},{2,18},{18,2},{3,19},{19,3},{4,20},{20... | collective-permute-start | bytes 786440 | tf_op jit(solution)/shard_map/ppermute | solution.py:670
  62.2 17.7 %all-to-all-start.1 = ((bf16[32,64,128]{2,1,0:T(8,128)(2,1)}), bf16[32,64,128]{2,1,0:T(8,128)(2,1)S(1)}, u32[]{:S(2)}, u32[]{:S(2)}) async-start(bf16[32,64,128]{2,1,0:T(8,128)(2,1)} %get-tuple-element.131), calls=%async_computation.1 | async-start | bytes 1048576 | tf_op jit(solution)/shard_map/all_to_all | solution.py:658
  68.3 90.6 %all-gather.2.cloned.1.call-start = ((), (), s32[]{:S(2)}) async-start(), calls=%async_computation.11 | async-start | bytes 8912896 | tf_op jit(solution)/shard_map/all_gather | solution.py:662
  69.4 14.5 %collective-permute-start.3 = (bf16[512,256]{1,0:T(8,128)(2,1)S(1)}, bf16[512,256]{1,0:T(8,128)(2,1)S(1)}, u32[]{:S(2)}, u32[]{:S(2)}) collective-permute-start(bf16[512,256]{1,0:T(8,128)(2,1)S(1)} %get-tuple-element.149.u0_ref), channel_id=1, source_target_pairs={{0,1},{1,0},{2,3},{3,2},{4,5},{5,4},{6,7},{7,6},{8,9},{9,8},{10,11... | collective-permute-start | bytes 786440 | tf_op jit(solution)/shard_map/ppermute | solution.py:670
  69.7 14.2 %collective-permute-start.4 = (bf16[512,256]{1,0:T(8,128)(2,1)S(1)}, bf16[512,256]{1,0:T(8,128)(2,1)S(1)}, u32[]{:S(2)}, u32[]{:S(2)}) collective-permute-start(bf16[512,256]{1,0:T(8,128)(2,1)S(1)} %get-tuple-element.149.u0_ref), channel_id=1, source_target_pairs={{0,2},{2,0},{1,3},{3,1},{4,6},{6,4},{5,7},{7,5},{8,10},{10,8},{9,1... | collective-permute-start | bytes 786440 | tf_op jit(solution)/shard_map/ppermute | solution.py:670
  84.4 25.7 %all-to-all-start.2 = ((bf16[4,1024,128]{2,1,0:T(8,128)(2,1)}), bf16[4,1024,128]{2,1,0:T(8,128)(2,1)S(1)}, u32[]{:S(2)}, u32[]{:S(2)}) async-start(bf16[4,1024,128]{2,1,0:T(8,128)(2,1)} %get-tuple-element.133), calls=%async_computation.2 | async-start | bytes 2097152 | tf_op jit(solution)/shard_map/all_to_all | solution.py:658
  91.8 36.2 %collective-permute-start.10 = (bf16[384,1024]{1,0:T(8,128)(2,1)S(1)}, bf16[384,1024]{1,0:T(8,128)(2,1)}, u32[]{:S(2)}, u32[]{:S(2)}) collective-permute-start(bf16[384,1024]{1,0:T(8,128)(2,1)S(1)} %pad_maximum_fusion.w0_ref), channel_id=1, source_target_pairs={{0,2},{2,0},{1,3},{3,1},{4,6},{6,4},{5,7},{7,5},{8,10},{10,8},{9,1... | collective-permute-start | bytes 2359304 | tf_op jit(solution)/shard_map/ppermute | solution.py:670
  93.1 34.9 %collective-permute-start.9 = (bf16[384,1024]{1,0:T(8,128)(2,1)S(1)}, bf16[384,1024]{1,0:T(8,128)(2,1)}, u32[]{:S(2)}, u32[]{:S(2)}) collective-permute-start(bf16[384,1024]{1,0:T(8,128)(2,1)S(1)} %pad_maximum_fusion.w0_ref), channel_id=1, source_target_pairs={{0,1},{1,0},{2,3},{3,2},{4,5},{5,4},{6,7},{7,6},{8,9},{9,8},{10,11... | collective-permute-start | bytes 2359304 | tf_op jit(solution)/shard_map/ppermute | solution.py:670
  110.1 17.9 %collective-permute-start.7 = (bf16[512,256]{1,0:T(8,128)(2,1)S(1)}, bf16[512,256]{1,0:T(8,128)(2,1)S(1)}, u32[]{:S(2)}, u32[]{:S(2)}) collective-permute-start(bf16[512,256]{1,0:T(8,128)(2,1)S(1)} %collective-permute-done.4.u2_ref), channel_id=1, source_target_pairs={{0,1},{1,0},{2,3},{3,2},{4,5},{5,4},{6,7},{7,6},{8,9},{9,8},{10,11... | collective-permute-start | bytes 786440 | tf_op jit(solution)/shard_map/ppermute | solution.py:670
  111.4 16.7 %collective-permute-start.8 = (bf16[512,256]{1,0:T(8,128)(2,1)S(1)}, bf16[512,256]{1,0:T(8,128)(2,1)S(1)}, u32[]{:S(2)}, u32[]{:S(2)}) collective-permute-start(bf16[512,256]{1,0:T(8,128)(2,1)S(1)} %collective-permute-done.6.l2_ref), channel_id=1, source_target_pairs={{0,1},{1,0},{2,3},{3,2},{4,5},{5,4},{6,7},{7,6},{8,9},{9,8},{10,11... | collective-permute-start | bytes 786440 | tf_op jit(solution)/shard_map/ppermute | solution.py:670
  128.0 19.7 %collective-permute-start.11 = (bf16[384,1024]{1,0:T(8,128)(2,1)}, bf16[384,1024]{1,0:T(8,128)(2,1)S(1)}, u32[]{:S(2)}, u32[]{:S(2)}) collective-permute-start(bf16[384,1024]{1,0:T(8,128)(2,1)} %collective-permute-done.10.w2_ref), channel_id=1, source_target_pairs={{0,1},{1,0},{2,3},{3,2},{4,5},{5,4},{6,7},{7,6},{8,9},{9,8},{10,11... | collective-permute-start | bytes 2359304 | tf_op jit(solution)/shard_map/ppermute | solution.py:670
  128.5 13.2 %all-to-all-start.3 = ((bf16[8,2,64,128]{3,2,1,0:T(8,128)(2,1)}), bf16[8,2,64,128]{3,2,1,0:T(8,128)(2,1)S(1)}, u32[]{:S(2)}, u32[]{:S(2)}) async-start(bf16[8,2,64,128]{3,2,1,0:T(8,128)(2,1)} %get-tuple-element.148), calls=%async_computation.3 | async-start | bytes 524288 | tf_op jit(solution)/shard_map/all_to_all | solution.py:658
  148.6 68.9 %all-to-all-start.4 = ((bf16[32,64,1024]{2,1,0:T(8,128)(2,1)}), bf16[32,64,1024]{2,1,0:T(8,128)(2,1)}, u32[]{:S(2)}, u32[]{:S(2)}) async-start(bf16[32,64,1024]{2,1,0:T(8,128)(2,1)} %get-tuple-element.165), calls=%async_computation.4 | async-start | bytes 8388608 | tf_op jit(solution)/shard_map/all_to_all | solution.py:658
  155.6 75.8 %collective-permute-start.13 = (bf16[8,2,64,128]{3,2,1,0:T(8,128)(2,1)S(1)}, bf16[8,2,64,128]{3,2,1,0:T(8,128)(2,1)S(1)}, u32[]{:S(2)}, u32[]{:S(2)}) collective-permute-start(bf16[8,2,64,128]{3,2,1,0:T(8,128)(2,1)S(1)} %copy-done.8), channel_id=1, source_target_pairs={{0,1},{1,0},{2,3},{3,2},{4,5},{5,4},{6,7},{7,6},{8,9},{9,8},{10,11... | collective-permute-start | bytes 786440 | tf_op jit(solution)/shard_map/ppermute | solution.py:670
  156.8 74.6 %collective-permute-start.14 = (bf16[8,2,64,128]{3,2,1,0:T(8,128)(2,1)S(1)}, bf16[8,2,64,128]{3,2,1,0:T(8,128)(2,1)S(1)}, u32[]{:S(2)}, u32[]{:S(2)}) collective-permute-start(bf16[8,2,64,128]{3,2,1,0:T(8,128)(2,1)S(1)} %copy-done.8), channel_id=1, source_target_pairs={{0,2},{2,0},{1,3},{3,1},{4,6},{6,4},{5,7},{7,5},{8,10},{10,8},{9,1... | collective-permute-start | bytes 786440 | tf_op jit(solution)/shard_map/ppermute | solution.py:670
  232.1 62.7 %all-to-all-start.5 = ((bf16[32,64,1024]{2,1,0:T(8,128)(2,1)}), bf16[32,64,1024]{2,1,0:T(8,128)(2,1)}, u32[]{:S(2)}, u32[]{:S(2)}) async-start(bf16[32,64,1024]{2,1,0:T(8,128)(2,1)} %get-tuple-element.178), calls=%async_computation.5 | async-start | bytes 8388608 | tf_op jit(solution)/shard_map/all_to_all | solution.py:658
  239.1 185.7 %reduce-scatter.2.cloned.1.call-start = ((), (), s32[]{:S(2)}) async-start(), calls=%async_computation.12 | async-start | bytes 3932160 | tf_op jit(solution)/shard_map/reduce_scatter | solution.py:895
  239.1 17.7 %collective-permute-start.15 = (bf16[8,2,64,128]{3,2,1,0:T(8,128)(2,1)S(1)}, bf16[8,2,64,128]{3,2,1,0:T(8,128)(2,1)S(1)}, u32[]{:S(2)}, u32[]{:S(2)}) collective-permute-start(bf16[8,2,64,128]{3,2,1,0:T(8,128)(2,1)S(1)} %collective-permute-done.14.o2_ref), channel_id=1, source_target_pairs={{0,1},{1,0},{2,3},{3,2},{4,5},{5,4},{6,7},{7,6},{8,9},{9,8},{10,11... | collective-permute-start | bytes 786440 | tf_op jit(solution)/shard_map/ppermute | solution.py:670
  316.4 65.7 %all-to-all-start.7 = ((bf16[32,64,1024]{2,1,0:T(8,128)(2,1)}), bf16[32,64,1024]{2,1,0:T(8,128)(2,1)}, u32[]{:S(2)}, u32[]{:S(2)}) async-start(bf16[32,64,1024]{2,1,0:T(8,128)(2,1)} %get-tuple-element.198), calls=%async_computation.7 | async-start | bytes 8388608 | tf_op jit(solution)/shard_map/all_to_all | solution.py:658
  341.5 31.1 %collective-permute-start.16 = (bf16[2,8,64,128]{3,2,1,0:T(8,128)(2,1)}, bf16[2,8,64,128]{3,2,1,0:T(8,128)(2,1)S(1)}, u32[]{:S(2)}, u32[]{:S(2)}) collective-permute-start(bf16[2,8,64,128]{3,2,1,0:T(8,128)(2,1)} %get-tuple-element.195), channel_id=1, source_target_pairs={{0,4},{4,0},{8,12},{12,8},{1,5},{5,1},{9,13},{13,9},{2,6},{6,2},{1... | collective-permute-start | bytes 786440 | tf_op jit(solution)/shard_map/ppermute | solution.py:680
  342.6 39.5 %collective-permute-start.17 = (bf16[2,8,64,128]{3,2,1,0:T(8,128)(2,1)}, bf16[2,8,64,128]{3,2,1,0:T(8,128)(2,1)S(1)}, u32[]{:S(2)}, u32[]{:S(2)}) collective-permute-start(bf16[2,8,64,128]{3,2,1,0:T(8,128)(2,1)} %get-tuple-element.196), channel_id=1, source_target_pairs={{0,8},{4,12},{8,0},{12,4},{1,9},{5,13},{9,1},{13,5},{2,10},{6,14},... | collective-permute-start | bytes 786440 | tf_op jit(solution)/shard_map/ppermute | solution.py:680
  345.0 37.1 %collective-permute-start.18 = (bf16[2,8,64,128]{3,2,1,0:T(8,128)(2,1)}, bf16[2,8,64,128]{3,2,1,0:T(8,128)(2,1)S(1)}, u32[]{:S(2)}, u32[]{:S(2)}) collective-permute-start(bf16[2,8,64,128]{3,2,1,0:T(8,128)(2,1)} %get-tuple-element.197), channel_id=1, source_target_pairs={{0,12},{4,8},{8,4},{12,0},{1,13},{5,9},{9,5},{13,1},{2,14},{6,10},... | collective-permute-start | bytes 786440 | tf_op jit(solution)/shard_map/ppermute | solution.py:680
  351.1 18.4 %collective-permute-start.20 = (bf16[128,256]{1,0:T(8,128)(2,1)S(1)}, bf16[128,256]{1,0:T(8,128)(2,1)S(1)}, u32[]{:S(2)}, u32[]{:S(2)}) collective-permute-start(bf16[128,256]{1,0:T(8,128)(2,1)S(1)} %get-tuple-element.244), channel_id=1, source_target_pairs={{0,2},{1,3},{2,0},{3,1},{4,6},{5,7},{6,4},{7,5},{8,10},{9,11},{10,... | collective-permute-start | bytes 196616 | tf_op jit(solution)/shard_map/ppermute | solution.py:680
  354.6 18.0 %collective-permute-start.21 = (bf16[128,256]{1,0:T(8,128)(2,1)S(1)}, bf16[128,256]{1,0:T(8,128)(2,1)S(1)}, u32[]{:S(2)}, u32[]{:S(2)}) collective-permute-start(bf16[128,256]{1,0:T(8,128)(2,1)S(1)} %get-tuple-element.243), channel_id=1, source_target_pairs={{0,3},{1,2},{2,1},{3,0},{4,7},{5,6},{6,5},{7,4},{8,11},{9,10},{10,... | collective-permute-start | bytes 196616 | tf_op jit(solution)/shard_map/ppermute | solution.py:680
  387.2 26.6 %all-to-all-start.8 = ((bf16[32,64,128]{2,1,0:T(8,128)(2,1)}), bf16[32,64,128]{2,1,0:T(8,128)(2,1)S(1)}, u32[]{:S(2)}, u32[]{:S(2)}) async-start(bf16[32,64,128]{2,1,0:T(8,128)(2,1)} %bitcast.58), calls=%async_computation.8 | async-start | bytes 1048576 | tf_op jit(solution)/shard_map/all_to_all | solution.py:658
  419.9 32.0 %all-to-all-start.9 = ((bf16[128,8,896]{2,1,0:T(8,128)(2,1)}), bf16[128,8,896]{2,1,0:T(8,128)(2,1)S(1)}, u32[]{:S(2)}, u32[]{:S(2)}) async-start(bf16[128,8,896]{2,1,0:T(8,128)(2,1)} %bitcast.59), calls=%async_computation.9 | async-start | bytes 3670016 | tf_op jit(solution)/shard_map/all_to_all | solution.py:658
  431.0 24.7 %collective-permute-start.22 = (bf16[128,1024]{1,0:T(8,128)(2,1)}, bf16[128,1024]{1,0:T(8,128)(2,1)S(1)}, u32[]{:S(2)}, u32[]{:S(2)}) collective-permute-start(bf16[128,1024]{1,0:T(8,128)(2,1)} %get-tuple-element.222), channel_id=1, source_target_pairs={{0,1},{1,0},{2,3},{3,2},{4,5},{5,4},{6,7},{7,6},{8,9},{9,8},{10,11... | collective-permute-start | bytes 786440 | tf_op jit(solution)/shard_map/ppermute | solution.py:680
  432.1 23.6 %collective-permute-start.23 = (bf16[128,1024]{1,0:T(8,128)(2,1)}, bf16[128,1024]{1,0:T(8,128)(2,1)S(1)}, u32[]{:S(2)}, u32[]{:S(2)}) collective-permute-start(bf16[128,1024]{1,0:T(8,128)(2,1)} %get-tuple-element.223), channel_id=1, source_target_pairs={{0,2},{1,3},{2,0},{3,1},{4,6},{5,7},{6,4},{7,5},{8,10},{9,11},{10,... | collective-permute-start | bytes 786440 | tf_op jit(solution)/shard_map/ppermute | solution.py:680
  432.9 25.7 %collective-permute-start.24 = (bf16[128,1024]{1,0:T(8,128)(2,1)}, bf16[128,1024]{1,0:T(8,128)(2,1)S(1)}, u32[]{:S(2)}, u32[]{:S(2)}) collective-permute-start(bf16[128,1024]{1,0:T(8,128)(2,1)} %get-tuple-element.224), channel_id=1, source_target_pairs={{0,3},{1,2},{2,1},{3,0},{4,7},{5,6},{6,5},{7,4},{8,11},{9,10},{10,... | collective-permute-start | bytes 786440 | tf_op jit(solution)/shard_map/ppermute | solution.py:680
  (41 other events, 509.8 us)
Sparse Core Ops, SparseCore 0:
  84.2 74.6 all-gather.1
  257.0 65.2 reduce-scatter.1

commit v5 on v4

--- a/solution.py
+++ b/solution.py
@@ -301,25 +301,20 @@
     log_total = log_ref[0][0:1]
 
     def step(c, dq, last):
-        at = 512 * c
-        keys = keys_ref[pl.ds(at, 512), :]
+        at = pl.ds(pl.multiple_of(c * 512, 512), 512)
+        keys = keys_ref[at, :]
         scores = mm(keys, q, NT)
         if last:
             scores = jnp.where(k_pos <= q_pos, scores, MASKED)
         weights = jnp.exp(scores - log_total)
         slope = (weights * (mm(keys, grad, NT) - delta)).astype(BF)
-        sum_ref[pl.ds(at, 512), :] += mm(slope, q) + mm(weights.astype(BF), grad)
-        return dq + mm(turned_ref[0:64, pl.ds(at, 512)], slope)
-
-    def run(count):
-        dq = jnp.zeros((64, 256), F32)
-        for c in range(count):
-            dq = step(c, dq, c == count - 1)
-        dq = jnp.concatenate([dq * 0.125, jnp.zeros((64, 256), F32)], axis=0)
-        dq_ref[...] = jnp.transpose(dq)
-
-    for t, count in enumerate(CHUNKS):
-        pl.when(tile == t)(functools.partial(run, count))
+        sum_ref[at, :] += mm(slope, q) + mm(weights.astype(BF), grad)
+        return dq + mm(turned_ref[0:64, at], slope)
+
+    count = jnp.where(tile < 4, tile + 1, 12 - tile)
+    dq = lax.fori_loop(0, count - 1, lambda c, v: step(c, v, False), jnp.zeros((64, 256), F32))
+    dq = step(count - 1, dq, True)
+    dq_ref[...] = jnp.transpose(jnp.concatenate([dq * 0.125, jnp.zeros((64, 256), F32)], axis=0))
 
     @pl.when(tile == 7)
     def _():

time: 478 us -> 478 us (level)
  transfers between devices with their start and end apart: 36 -> 36, of which waited for: 14 -> 14; matrix products, arithmetic and copies ran while one was open for 4% -> 4% of each run, Pallas kernels for 27% -> 28%
where the time goes in v5:
time: 478 us; the launch traced here: 470 us
  waiting for transfers between devices  188 us (39%)
  Pallas kernels  133 us (28%)
  starting transfers between devices  92.3 us (19%)
  local copies, waits for them, and re-layouts  16.9 us (4%)
  blocking collectives  15.7 us (3%)
  between operations  15.1 us (3%)
  other arithmetic  8.93 us (2%)
    all_to_all x9, waiting for transfers between devices, exchange(): return lax.all_to_all(value, axes, split_axis=0, concat_axis=0, tiled=True)  158 us
    all_to_all x9, starting transfers between devices, exchange(): return lax.all_to_all(value, axes, split_axis=0, concat_axis=0, tiled=True)  60.6 us
    ppermute x9, waiting for transfers between devices, cross(): here.append(lax.ppermute(parts[r], axes, [(i, i ^ r) for i in range(4)]))  26.1 us
    pallas_call x1, Pallas kernels, on_device(): call(kernel_attend_back, (sds((2048, 128), F32),) + (sds((2, 8, 64, 128),...  22.9 us
    ppermute x9, starting transfers between devices, cross(): here.append(lax.ppermute(parts[r], axes, [(i, i ^ r) for i in range(4)]))  16.9 us
    pallas_call x1, Pallas kernels, on_device(): call(kernel_attend, (sds((8, 2, 64, 128), BF), sds((8, 8, 256), F32), sds...  16 us
    pallas_call x1, Pallas kernels, on_device(): call(kernel_experts_after, (sds((32, 64, WIDTH), BF), sds((4, 384, WIDTH)...  15.9 us
    all_to_all x1, blocking collectives, exchange(): return lax.all_to_all(value, axes, split_axis=0, concat_axis=0, tiled=True)  15.7 us
  transfers between devices with their start and end apart: 36, of which 14 were waited for; matrix products, arithmetic and copies ran while one was open for 4% of the time, Pallas kernels for 28%

profile of v5, /device:TPU:1, one launch (start us, length us, event | category | flops | bytes accessed | tf_op | source)
XLA Modules:
  0.0 469.8 jit_solution(445339914103587233)
XLA Ops:
  19.3 9.9 %all-to-all-start = ((bf16[128,8,896]{2,1,0:T(8,128)(2,1)}), bf16[128,8,896]{2,1,0:T(8,128)(2,1)S(1)}, u32[]{:S(2)}, u32[]{:S(2)}) async-start(bf16[128,8,896]{2,1,0:T(8,128)(2,1)} %bitcast.55), calls=%async_computation | async-start | bytes 3670016 | tf_op jit(solution)/shard_map/all_to_all | solution.py:653
  32.3 24.0 %all-to-all-done = bf16[128,8,896]{2,1,0:T(8,128)(2,1)S(1)} async-done(((bf16[128,8,896]{2,1,0:T(8,128)(2,1)}), bf16[128,8,896]{2,1,0:T(8,128)(2,1)S(1)}, u32[]{:S(2)}, u32[]{:S(2)}) %all-to-all-start) | async-done | bytes 1835040 | tf_op jit(solution)/shard_map/all_to_all | solution.py:653
  57.6 4.6 shard_map.198
  62.2 6.0 %all-to-all-start.1 = ((bf16[32,64,128]{2,1,0:T(8,128)(2,1)}), bf16[32,64,128]{2,1,0:T(8,128)(2,1)S(1)}, u32[]{:S(2)}, u32[]{:S(2)}) async-start(bf16[32,64,128]{2,1,0:T(8,128)(2,1)} %get-tuple-element.131), calls=%async_computation.1 | async-start | bytes 1048576 | tf_op jit(solution)/shard_map/all_to_all | solution.py:653
  72.2 7.7 %all-to-all-done.1 = bf16[32,64,128]{2,1,0:T(8,128)(2,1)S(1)} async-done(((bf16[32,64,128]{2,1,0:T(8,128)(2,1)}), bf16[32,64,128]{2,1,0:T(8,128)(2,1)S(1)}, u32[]{:S(2)}, u32[]{:S(2)}) %all-to-all-start.1) | async-done | bytes 524320 | tf_op jit(solution)/shard_map/all_to_all | solution.py:653
  96.1 14.1 %all-to-all-done.2 = bf16[4,1024,128]{2,1,0:T(8,128)(2,1)S(1)} async-done(((bf16[4,1024,128]{2,1,0:T(8,128)(2,1)}), bf16[4,1024,128]{2,1,0:T(8,128)(2,1)S(1)}, u32[]{:S(2)}, u32[]{:S(2)}) %all-to-all-start.2) | async-done | bytes 1048608 | tf_op jit(solution)/shard_map/all_to_all | solution.py:653
  111.6 16.0 %shard_map.200 = (bf16[8,2,64,128]{3,2,1,0:T(8,128)(2,1)}, f32[8,8,256]{2,1,0:T(8,128)}, f32[2048,128]{1,0:T(8,128)}, bf16[4096,128]{1,0:T(8,128)(2,1)}, bf16[128,4096]{1,0:T(8,128)(2,1)}) custom-call(s32[1]{0:T(128)} %bitcast.mine_ref, bf16[4,2,8,64,128]{4,3,2,1,0:T(8,128)(2,1)} %bitcast.66, bf16[2048,128]{1,0:T(8,128)(2,1)} %bitcast.75), custom_call_target="tpu_custom_call" | custom-call | flops 10000000000 | bytes 5000000 | tf_op jit(solution)/shard_map/pallas_call | solution.py:797
  134.4 7.4 %all-to-all-done.3.o_ref.o0_ref = bf16[8,2,64,128]{3,2,1,0:T(8,128)(2,1)S(1)} async-done(((bf16[8,2,64,128]{3,2,1,0:T(8,128)(2,1)}), bf16[8,2,64,128]{3,2,1,0:T(8,128)(2,1)S(1)}, u32[]{:S(2)}, u32[]{:S(2)}) %all-to-all-start.3) | async-done | bytes 262176 | tf_op jit(solution)/shard_map/all_to_all | solution.py:653
  142.5 5.3 %shard_map.202 = (bf16[32,64,1024]{2,1,0:T(8,128)(2,1)}, f32[128,1024]{1,0:T(8,128)}) custom-call(s32[1]{0:T(128)} %bitcast.1.part_ref, bf16[8,2,64,128]{3,2,1,0:T(8,128)(2,1)} %copy-done.7, bf16[512,256]{1,0:T(8,128)(2,1)} %copy-done.6, bf16[512,256]{1,0:T(8,128)(2,1)} %copy-done.14, bf16[512,256]{1,0:T(8,128)(2,1)} %copy-done.15, ...), custom_call_target="tpu_custom_call" | custom-call | flops 900000000 | bytes 8000000 | tf_op jit(solution)/shard_map/pallas_call | solution.py:817
  148.6 5.5 %all-to-all-start.4 = ((bf16[32,64,1024]{2,1,0:T(8,128)(2,1)}), bf16[32,64,1024]{2,1,0:T(8,128)(2,1)}, u32[]{:S(2)}, u32[]{:S(2)}) async-start(bf16[32,64,1024]{2,1,0:T(8,128)(2,1)} %get-tuple-element.165), calls=%async_computation.4 | async-start | bytes 8388608 | tf_op jit(solution)/shard_map/all_to_all | solution.py:653
  158.8 12.5 %shard_map.203 = (bf16[32,64,1024]{2,1,0:T(8,128)(2,1)}, f32[2048,512]{1,0:T(8,128)}, bf16[512,1024]{1,0:T(8,128)(2,1)}, bf16[1024,1024]{1,0:T(8,128)(2,1)}) custom-call(s32[1]{0:T(128)} %bitcast.1.part_ref, bf16[4,4,2,128,1024]{4,3,2,1,0:T(8,128)(2,1)} %bitcast.74, bf16[32,8,128]{2,1,0:T(8,128)(2,1)} %dynamic-slice_bitcast_fusion.parts_ref, ...), custom_call_target="tpu_custom_call" | custom-call | flops 6000000000 | bytes 20000000 | tf_op jit(solution)/shard_map/pallas_call | solution.py:836
  171.3 45.7 %all-to-all-done.4.h_ref = bf16[32,64,1024]{2,1,0:T(8,128)(2,1)} async-done(((bf16[32,64,1024]{2,1,0:T(8,128)(2,1)}), bf16[32,64,1024]{2,1,0:T(8,128)(2,1)}, u32[]{:S(2)}, u32[]{:S(2)}) %all-to-all-start.4) | async-done | bytes 4194336 | tf_op jit(solution)/shard_map/all_to_all | solution.py:653
  217.0 13.8 %shard_map.204 = (bf16[2048,512]{1,0:T(8,128)(2,1)}, bf16[2048,1024]{1,0:T(8,128)(2,1)}, bf16[32,64,1024]{2,1,0:T(8,128)(2,1)}) custom-call(bf16[32,64,1024]{2,1,0:T(8,128)(2,1)} %all-to-all-done.4.h_ref, bf16[1024,1024]{1,0:T(8,128)(2,1)} %get-tuple-element.174.gu_ref, f32[2048,512]{1,0:T(8,128)} %get-tuple-element.175.dact_ref), custom_call_target="tpu_custom_call" | custom-call | flops 8999999488 | bytes 20000000 | tf_op jit(solution)/shard_map/pallas_call | solution.py:862
  231.6 7.0 %all-to-all-start.5 = ((bf16[32,64,1024]{2,1,0:T(8,128)(2,1)}), bf16[32,64,1024]{2,1,0:T(8,128)(2,1)}, u32[]{:S(2)}, u32[]{:S(2)}) async-start(bf16[32,64,1024]{2,1,0:T(8,128)(2,1)} %get-tuple-element.178), calls=%async_computation.5 | async-start | bytes 8388608 | tf_op jit(solution)/shard_map/all_to_all | solution.py:653
  240.4 15.9 %shard_map.205 = (bf16[32,64,1024]{2,1,0:T(8,128)(2,1)}, bf16[4,384,1024]{2,1,0:T(8,128)(2,1)}) custom-call(bf16[32,64,1024]{2,1,0:T(8,128)(2,1)} %all-to-all-done.4.h_ref, bf16[2048,512]{1,0:T(8,128)(2,1)} %get-tuple-element.179.act_ref, bf16[32,64,1024]{2,1,0:T(8,128)(2,1)} %get-tuple-element.180.dys_ref, bf16[2048,1024]{1,0:T(8,128)(2,1)} %get-tuple-element.181.dboth_ref, ...), custom_call_target="tpu_custom_call" | custom-call | flops 8999999488 | bytes 20000000 | tf_op jit(solution)/shard_map/pallas_call | solution.py:878
  256.3 37.9 %all-to-all-done.5.dxs_ref = bf16[32,64,1024]{2,1,0:T(8,128)(2,1)} async-done(((bf16[32,64,1024]{2,1,0:T(8,128)(2,1)}), bf16[32,64,1024]{2,1,0:T(8,128)(2,1)}, u32[]{:S(2)}, u32[]{:S(2)}) %all-to-all-start.5) | async-done | bytes 4194336 | tf_op jit(solution)/shard_map/all_to_all | solution.py:653
  294.2 5.8 %shard_map.206 = (f32[128,1024]{1,0:T(8,128)}, bf16[4,128,256]{2,1,0:T(8,128)(2,1)}, bf16[8,2,64,128]{3,2,1,0:T(8,128)(2,1)}, f32[8,1024]{1,0:T(8,128)}) custom-call(s32[1]{0:T(128)} %bitcast.1.part_ref, bf16[32,64,1024]{2,1,0:T(8,128)(2,1)} %all-to-all-done.5.dxs_ref, bf16[128,2048]{1,0:T(8,128)(2,1)} %get-tuple-element.189.pick_ref, ...), custom_call_target="tpu_custom_call" | custom-call | flops 900000000 | bytes 8000000 | tf_op jit(solution)/shard_map/pallas_call | solution.py:895
  300.0 15.7 %all_to_all.50.grad_ref = bf16[8,2,64,128]{3,2,1,0:T(8,128)(2,1)} all-to-all(bf16[8,2,64,128]{3,2,1,0:T(8,128)(2,1)} %get-tuple-element.190), channel_id=1, replica_groups=mesh['x'=4,'zh'=2,'y'=4,'zl'=2,'core'=2] {'x','zh'}, dimensions={0} | all-to-all | bytes 524288 | tf_op jit(solution)/shard_map/all_to_all | solution.py:653
  315.6 4.9 %all-to-all-start.7 = ((bf16[32,64,1024]{2,1,0:T(8,128)(2,1)}), bf16[32,64,1024]{2,1,0:T(8,128)(2,1)}, u32[]{:S(2)}, u32[]{:S(2)}) async-start(bf16[32,64,1024]{2,1,0:T(8,128)(2,1)} %get-tuple-element.198), calls=%async_computation.7 | async-start | bytes 8388608 | tf_op jit(solution)/shard_map/all_to_all | solution.py:653
  320.6 22.9 %shard_map.207 = (f32[2048,128]{1,0:T(8,128)}, bf16[2,8,64,128]{3,2,1,0:T(8,128)(2,1)}, bf16[2,8,64,128]{3,2,1,0:T(8,128)(2,1)}, bf16[2,8,64,128]{3,2,1,0:T(8,128)(2,1)}, bf16[2,8,64,128]{3,2,1,0:T(8,128)(2,1)}) custom-call(s32[1]{0:T(128)} %bitcast.mine_ref, bf16[4096,128]{1,0:T(8,128)(2,1)} %get-tuple-element.137.keys_ref, ...), custom_call_target="tpu_custom_call" | custom-call | flops 20000000000 | bytes 7000000 | tf_op jit(solution)/shard_map/pallas_call | solution.py:925
  348.0 5.1 %collective-permute-start.19 = (bf16[128,256]{1,0:T(8,128)(2,1)S(1)}, bf16[128,256]{1,0:T(8,128)(2,1)S(1)}, u32[]{:S(2)}, u32[]{:S(2)}) collective-permute-start(bf16[128,256]{1,0:T(8,128)(2,1)S(1)} %get-tuple-element.245), channel_id=1, source_target_pairs={{0,1},{1,0},{2,3},{3,2},{4,5},{5,4},{6,7},{7,6},{8,9},{9,8},{10,11... | collective-permute-start | bytes 196616 | tf_op jit(solution)/shard_map/ppermute | solution.py:675
  353.1 4.1 collective-permute-start.20
  358.3 11.1 %collective-permute-done.20.da2_ref = bf16[128,256]{1,0:T(8,128)(2,1)S(1)} collective-permute-done((bf16[128,256]{1,0:T(8,128)(2,1)S(1)}, bf16[128,256]{1,0:T(8,128)(2,1)S(1)}, u32[]{:S(2)}, u32[]{:S(2)}) %collective-permute-start.20) | collective-permute-done | bytes 65568 | tf_op jit(solution)/shard_map/ppermute | solution.py:675
  372.5 9.1 %collective-permute-done.17.d2_ref = bf16[2,8,64,128]{3,2,1,0:T(8,128)(2,1)S(1)} collective-permute-done((bf16[2,8,64,128]{3,2,1,0:T(8,128)(2,1)}, bf16[2,8,64,128]{3,2,1,0:T(8,128)(2,1)S(1)}, u32[]{:S(2)}, u32[]{:S(2)}) %collective-permute-start.17) | collective-permute-done | bytes 262176 | tf_op jit(solution)/shard_map/ppermute | solution.py:675
  382.4 4.3 shard_map.209
  386.7 15.1 %all-to-all-start.8 = ((bf16[32,64,128]{2,1,0:T(8,128)(2,1)}), bf16[32,64,128]{2,1,0:T(8,128)(2,1)S(1)}, u32[]{:S(2)}, u32[]{:S(2)}) async-start(bf16[32,64,128]{2,1,0:T(8,128)(2,1)} %bitcast.58), calls=%async_computation.8 | async-start | bytes 1048576 | tf_op jit(solution)/shard_map/all_to_all | solution.py:653
  404.7 8.7 %all-to-all-done.8.msg_ref = bf16[32,64,128]{2,1,0:T(8,128)(2,1)S(1)} async-done(((bf16[32,64,128]{2,1,0:T(8,128)(2,1)}), bf16[32,64,128]{2,1,0:T(8,128)(2,1)S(1)}, u32[]{:S(2)}, u32[]{:S(2)}) %all-to-all-start.8) | async-done | bytes 524320 | tf_op jit(solution)/shard_map/all_to_all | solution.py:653
  414.2 5.3 %shard_map.211 = (bf16[1024,896]{1,0:T(8,128)(2,1)}, bf16[512,512]{1,0:T(8,128)(2,1)}) custom-call(bf16[32,64,128]{2,1,0:T(8,128)(2,1)} %copy-done.2, bf16[512,1024]{1,0:T(8,128)(2,1)} %get-tuple-element.210.hidden_ref, bf16[1024,896]{1,0:T(8,128)(2,1)} %bitcast.53, bf16[1024,384]{1,0:T(8,128)(2,1)} %shard_map.210.rest_ref), custom_call_target="tpu_custom_call" | custom-call | flops 600000000 | bytes 5000000 | tf_op jit(solution)/shard_map/pallas_call | solution.py:976
  419.5 5.1 %all-to-all-start.9 = ((bf16[128,8,896]{2,1,0:T(8,128)(2,1)}), bf16[128,8,896]{2,1,0:T(8,128)(2,1)S(1)}, u32[]{:S(2)}, u32[]{:S(2)}) async-start(bf16[128,8,896]{2,1,0:T(8,128)(2,1)} %bitcast.59), calls=%async_computation.9 | async-start | bytes 3670016 | tf_op jit(solution)/shard_map/all_to_all | solution.py:653
  427.0 3.9 shard_map.212
  434.4 5.0 %shard_map.208 = bf16[128,1024]{1,0:T(8,128)(2,1)} custom-call(bf16[32,64,1024]{2,1,0:T(8,128)(2,1)} %all-to-all-done.7.ys_ref, bf16[128,2048]{1,0:T(8,128)(2,1)} %get-tuple-element.201.high_ref, bf16[128,2048]{1,0:T(8,128)(2,1)} %get-tuple-element.202.rest_ref, f32[128,1024]{1,0:T(8,128)} %get-tuple-element.168.mid_ref), custom_call_target="tpu_custom_call" | custom-call | flops 1000000000 | bytes 5000000 | tf_op jit(solution)/shard_map/pallas_call | solution.py:952
  439.5 12.3 %all-to-all-done.9 = bf16[128,8,896]{2,1,0:T(8,128)(2,1)S(1)} async-done(((bf16[128,8,896]{2,1,0:T(8,128)(2,1)}), bf16[128,8,896]{2,1,0:T(8,128)(2,1)S(1)}, u32[]{:S(2)}, u32[]{:S(2)}) %all-to-all-start.9) | async-done | bytes 1835040 | tf_op jit(solution)/shard_map/all_to_all | solution.py:653
  (168 shorter events, 83.0 us)
Async XLA Ops:
  7.2 11.4 %collective-permute-start = (bf16[128,1024]{1,0:T(8,128)(2,1)}, bf16[128,1024]{1,0:T(8,128)(2,1)S(1)}, u32[]{:S(2)}, u32[]{:S(2)}) collective-permute-start(bf16[128,1024]{1,0:T(8,128)(2,1)} %bitcast.61), channel_id=1, source_target_pairs={{0,1},{1,0},{2,3},{3,2},{4,5},{5,4},{6,7},{7,6},{8,9},{9,8},{10,11... | collective-permute-start | bytes 786440 | tf_op jit(solution)/shard_map/ppermute | solution.py:665
  19.3 37.0 %all-to-all-start = ((bf16[128,8,896]{2,1,0:T(8,128)(2,1)}), bf16[128,8,896]{2,1,0:T(8,128)(2,1)S(1)}, u32[]{:S(2)}, u32[]{:S(2)}) async-start(bf16[128,8,896]{2,1,0:T(8,128)(2,1)} %bitcast.55), calls=%async_computation | async-start | bytes 3670016 | tf_op jit(solution)/shard_map/all_to_all | solution.py:653
  29.2 27.6 %collective-permute-start.2 = (bf16[128,1024]{1,0:T(8,128)(2,1)S(1)}, bf16[128,1024]{1,0:T(8,128)(2,1)S(1)}, u32[]{:S(2)}, u32[]{:S(2)}) collective-permute-start(bf16[128,1024]{1,0:T(8,128)(2,1)S(1)} %collective-permute-done.1.x2_ref), channel_id=1, source_target_pairs={{0,1},{1,0},{2,3},{3,2},{4,5},{5,4},{6,7},{7,6},{8,9},{9,8},{10,11... | collective-permute-start | bytes 786440 | tf_op jit(solution)/shard_map/ppermute | solution.py:665
  56.3 14.9 %collective-permute-start.12 = (bf16[128,1024]{1,0:T(8,128)(2,1)S(1)}, bf16[128,1024]{1,0:T(8,128)(2,1)S(1)}, u32[]{:S(2)}, u32[]{:S(2)}) collective-permute-start(bf16[128,1024]{1,0:T(8,128)(2,1)S(1)} %bitcast.68), channel_id=1, source_target_pairs={{0,16},{16,0},{1,17},{17,1},{2,18},{18,2},{3,19},{19,3},{4,20},{20... | collective-permute-start | bytes 786440 | tf_op jit(solution)/shard_map/ppermute | solution.py:665
  62.2 17.7 %all-to-all-start.1 = ((bf16[32,64,128]{2,1,0:T(8,128)(2,1)}), bf16[32,64,128]{2,1,0:T(8,128)(2,1)S(1)}, u32[]{:S(2)}, u32[]{:S(2)}) async-start(bf16[32,64,128]{2,1,0:T(8,128)(2,1)} %get-tuple-element.131), calls=%async_computation.1 | async-start | bytes 1048576 | tf_op jit(solution)/shard_map/all_to_all | solution.py:653
  68.3 90.5 %all-gather.2.cloned.1.call-start = ((), (), s32[]{:S(2)}) async-start(), calls=%async_computation.11 | async-start | bytes 8912896 | tf_op jit(solution)/shard_map/all_gather | solution.py:657
  69.4 14.6 %collective-permute-start.3 = (bf16[512,256]{1,0:T(8,128)(2,1)S(1)}, bf16[512,256]{1,0:T(8,128)(2,1)S(1)}, u32[]{:S(2)}, u32[]{:S(2)}) collective-permute-start(bf16[512,256]{1,0:T(8,128)(2,1)S(1)} %get-tuple-element.149.u0_ref), channel_id=1, source_target_pairs={{0,1},{1,0},{2,3},{3,2},{4,5},{5,4},{6,7},{7,6},{8,9},{9,8},{10,11... | collective-permute-start | bytes 786440 | tf_op jit(solution)/shard_map/ppermute | solution.py:665
  69.7 14.2 %collective-permute-start.4 = (bf16[512,256]{1,0:T(8,128)(2,1)S(1)}, bf16[512,256]{1,0:T(8,128)(2,1)S(1)}, u32[]{:S(2)}, u32[]{:S(2)}) collective-permute-start(bf16[512,256]{1,0:T(8,128)(2,1)S(1)} %get-tuple-element.149.u0_ref), channel_id=1, source_target_pairs={{0,2},{2,0},{1,3},{3,1},{4,6},{6,4},{5,7},{7,5},{8,10},{10,8},{9,1... | collective-permute-start | bytes 786440 | tf_op jit(solution)/shard_map/ppermute | solution.py:665
  84.4 25.7 %all-to-all-start.2 = ((bf16[4,1024,128]{2,1,0:T(8,128)(2,1)}), bf16[4,1024,128]{2,1,0:T(8,128)(2,1)S(1)}, u32[]{:S(2)}, u32[]{:S(2)}) async-start(bf16[4,1024,128]{2,1,0:T(8,128)(2,1)} %get-tuple-element.133), calls=%async_computation.2 | async-start | bytes 2097152 | tf_op jit(solution)/shard_map/all_to_all | solution.py:653
  91.8 35.9 %collective-permute-start.10 = (bf16[384,1024]{1,0:T(8,128)(2,1)S(1)}, bf16[384,1024]{1,0:T(8,128)(2,1)}, u32[]{:S(2)}, u32[]{:S(2)}) collective-permute-start(bf16[384,1024]{1,0:T(8,128)(2,1)S(1)} %pad_maximum_fusion.w0_ref), channel_id=1, source_target_pairs={{0,2},{2,0},{1,3},{3,1},{4,6},{6,4},{5,7},{7,5},{8,10},{10,8},{9,1... | collective-permute-start | bytes 2359304 | tf_op jit(solution)/shard_map/ppermute | solution.py:665
  93.1 34.6 %collective-permute-start.9 = (bf16[384,1024]{1,0:T(8,128)(2,1)S(1)}, bf16[384,1024]{1,0:T(8,128)(2,1)}, u32[]{:S(2)}, u32[]{:S(2)}) collective-permute-start(bf16[384,1024]{1,0:T(8,128)(2,1)S(1)} %pad_maximum_fusion.w0_ref), channel_id=1, source_target_pairs={{0,1},{1,0},{2,3},{3,2},{4,5},{5,4},{6,7},{7,6},{8,9},{9,8},{10,11... | collective-permute-start | bytes 2359304 | tf_op jit(solution)/shard_map/ppermute | solution.py:665
  110.2 17.6 %collective-permute-start.7 = (bf16[512,256]{1,0:T(8,128)(2,1)S(1)}, bf16[512,256]{1,0:T(8,128)(2,1)S(1)}, u32[]{:S(2)}, u32[]{:S(2)}) collective-permute-start(bf16[512,256]{1,0:T(8,128)(2,1)S(1)} %collective-permute-done.4.u2_ref), channel_id=1, source_target_pairs={{0,1},{1,0},{2,3},{3,2},{4,5},{5,4},{6,7},{7,6},{8,9},{9,8},{10,11... | collective-permute-start | bytes 786440 | tf_op jit(solution)/shard_map/ppermute | solution.py:665
  111.4 16.4 %collective-permute-start.8 = (bf16[512,256]{1,0:T(8,128)(2,1)S(1)}, bf16[512,256]{1,0:T(8,128)(2,1)S(1)}, u32[]{:S(2)}, u32[]{:S(2)}) collective-permute-start(bf16[512,256]{1,0:T(8,128)(2,1)S(1)} %collective-permute-done.6.l2_ref), channel_id=1, source_target_pairs={{0,1},{1,0},{2,3},{3,2},{4,5},{5,4},{6,7},{7,6},{8,9},{9,8},{10,11... | collective-permute-start | bytes 786440 | tf_op jit(solution)/shard_map/ppermute | solution.py:665
  127.7 20.0 %collective-permute-start.11 = (bf16[384,1024]{1,0:T(8,128)(2,1)}, bf16[384,1024]{1,0:T(8,128)(2,1)S(1)}, u32[]{:S(2)}, u32[]{:S(2)}) collective-permute-start(bf16[384,1024]{1,0:T(8,128)(2,1)} %collective-permute-done.10.w2_ref), channel_id=1, source_target_pairs={{0,1},{1,0},{2,3},{3,2},{4,5},{5,4},{6,7},{7,6},{8,9},{9,8},{10,11... | collective-permute-start | bytes 2359304 | tf_op jit(solution)/shard_map/ppermute | solution.py:665
  128.5 13.2 %all-to-all-start.3 = ((bf16[8,2,64,128]{3,2,1,0:T(8,128)(2,1)}), bf16[8,2,64,128]{3,2,1,0:T(8,128)(2,1)S(1)}, u32[]{:S(2)}, u32[]{:S(2)}) async-start(bf16[8,2,64,128]{3,2,1,0:T(8,128)(2,1)} %get-tuple-element.148), calls=%async_computation.3 | async-start | bytes 524288 | tf_op jit(solution)/shard_map/all_to_all | solution.py:653
  148.6 68.4 %all-to-all-start.4 = ((bf16[32,64,1024]{2,1,0:T(8,128)(2,1)}), bf16[32,64,1024]{2,1,0:T(8,128)(2,1)}, u32[]{:S(2)}, u32[]{:S(2)}) async-start(bf16[32,64,1024]{2,1,0:T(8,128)(2,1)} %get-tuple-element.165), calls=%async_computation.4 | async-start | bytes 8388608 | tf_op jit(solution)/shard_map/all_to_all | solution.py:653
  155.6 75.2 %collective-permute-start.13 = (bf16[8,2,64,128]{3,2,1,0:T(8,128)(2,1)S(1)}, bf16[8,2,64,128]{3,2,1,0:T(8,128)(2,1)S(1)}, u32[]{:S(2)}, u32[]{:S(2)}) collective-permute-start(bf16[8,2,64,128]{3,2,1,0:T(8,128)(2,1)S(1)} %copy-done.8), channel_id=1, source_target_pairs={{0,1},{1,0},{2,3},{3,2},{4,5},{5,4},{6,7},{7,6},{8,9},{9,8},{10,11... | collective-permute-start | bytes 786440 | tf_op jit(solution)/shard_map/ppermute | solution.py:665
  156.8 74.1 %collective-permute-start.14 = (bf16[8,2,64,128]{3,2,1,0:T(8,128)(2,1)S(1)}, bf16[8,2,64,128]{3,2,1,0:T(8,128)(2,1)S(1)}, u32[]{:S(2)}, u32[]{:S(2)}) collective-permute-start(bf16[8,2,64,128]{3,2,1,0:T(8,128)(2,1)S(1)} %copy-done.8), channel_id=1, source_target_pairs={{0,2},{2,0},{1,3},{3,1},{4,6},{6,4},{5,7},{7,5},{8,10},{10,8},{9,1... | collective-permute-start | bytes 786440 | tf_op jit(solution)/shard_map/ppermute | solution.py:665
  231.6 62.7 %all-to-all-start.5 = ((bf16[32,64,1024]{2,1,0:T(8,128)(2,1)}), bf16[32,64,1024]{2,1,0:T(8,128)(2,1)}, u32[]{:S(2)}, u32[]{:S(2)}) async-start(bf16[32,64,1024]{2,1,0:T(8,128)(2,1)} %get-tuple-element.178), calls=%async_computation.5 | async-start | bytes 8388608 | tf_op jit(solution)/shard_map/all_to_all | solution.py:653
  238.6 186.1 %reduce-scatter.2.cloned.1.call-start = ((), (), s32[]{:S(2)}) async-start(), calls=%async_computation.12 | async-start | bytes 3932160 | tf_op jit(solution)/shard_map/reduce_scatter | solution.py:890
  238.6 17.7 %collective-permute-start.15 = (bf16[8,2,64,128]{3,2,1,0:T(8,128)(2,1)S(1)}, bf16[8,2,64,128]{3,2,1,0:T(8,128)(2,1)S(1)}, u32[]{:S(2)}, u32[]{:S(2)}) collective-permute-start(bf16[8,2,64,128]{3,2,1,0:T(8,128)(2,1)S(1)} %collective-permute-done.14.o2_ref), channel_id=1, source_target_pairs={{0,1},{1,0},{2,3},{3,2},{4,5},{5,4},{6,7},{7,6},{8,9},{9,8},{10,11... | collective-permute-start | bytes 786440 | tf_op jit(solution)/shard_map/ppermute | solution.py:665
  315.6 66.0 %all-to-all-start.7 = ((bf16[32,64,1024]{2,1,0:T(8,128)(2,1)}), bf16[32,64,1024]{2,1,0:T(8,128)(2,1)}, u32[]{:S(2)}, u32[]{:S(2)}) async-start(bf16[32,64,1024]{2,1,0:T(8,128)(2,1)} %get-tuple-element.198), calls=%async_computation.7 | async-start | bytes 8388608 | tf_op jit(solution)/shard_map/all_to_all | solution.py:653
  343.4 29.0 %collective-permute-start.16 = (bf16[2,8,64,128]{3,2,1,0:T(8,128)(2,1)}, bf16[2,8,64,128]{3,2,1,0:T(8,128)(2,1)S(1)}, u32[]{:S(2)}, u32[]{:S(2)}) collective-permute-start(bf16[2,8,64,128]{3,2,1,0:T(8,128)(2,1)} %get-tuple-element.195), channel_id=1, source_target_pairs={{0,4},{4,0},{8,12},{12,8},{1,5},{5,1},{9,13},{13,9},{2,6},{6,2},{1... | collective-permute-start | bytes 786440 | tf_op jit(solution)/shard_map/ppermute | solution.py:675
  344.7 36.9 %collective-permute-start.17 = (bf16[2,8,64,128]{3,2,1,0:T(8,128)(2,1)}, bf16[2,8,64,128]{3,2,1,0:T(8,128)(2,1)S(1)}, u32[]{:S(2)}, u32[]{:S(2)}) collective-permute-start(bf16[2,8,64,128]{3,2,1,0:T(8,128)(2,1)} %get-tuple-element.196), channel_id=1, source_target_pairs={{0,8},{4,12},{8,0},{12,4},{1,9},{5,13},{9,1},{13,5},{2,10},{6,14},... | collective-permute-start | bytes 786440 | tf_op jit(solution)/shard_map/ppermute | solution.py:675
  347.1 34.5 %collective-permute-start.18 = (bf16[2,8,64,128]{3,2,1,0:T(8,128)(2,1)}, bf16[2,8,64,128]{3,2,1,0:T(8,128)(2,1)S(1)}, u32[]{:S(2)}, u32[]{:S(2)}) collective-permute-start(bf16[2,8,64,128]{3,2,1,0:T(8,128)(2,1)} %get-tuple-element.197), channel_id=1, source_target_pairs={{0,12},{4,8},{8,4},{12,0},{1,13},{5,9},{9,5},{13,1},{2,14},{6,10},... | collective-permute-start | bytes 786440 | tf_op jit(solution)/shard_map/ppermute | solution.py:675
  353.1 16.3 %collective-permute-start.20 = (bf16[128,256]{1,0:T(8,128)(2,1)S(1)}, bf16[128,256]{1,0:T(8,128)(2,1)S(1)}, u32[]{:S(2)}, u32[]{:S(2)}) collective-permute-start(bf16[128,256]{1,0:T(8,128)(2,1)S(1)} %get-tuple-element.244), channel_id=1, source_target_pairs={{0,2},{1,3},{2,0},{3,1},{4,6},{5,7},{6,4},{7,5},{8,10},{9,11},{10,... | collective-permute-start | bytes 196616 | tf_op jit(solution)/shard_map/ppermute | solution.py:675
  357.2 15.2 %collective-permute-start.21 = (bf16[128,256]{1,0:T(8,128)(2,1)S(1)}, bf16[128,256]{1,0:T(8,128)(2,1)S(1)}, u32[]{:S(2)}, u32[]{:S(2)}) collective-permute-start(bf16[128,256]{1,0:T(8,128)(2,1)S(1)} %get-tuple-element.243), channel_id=1, source_target_pairs={{0,3},{1,2},{2,1},{3,0},{4,7},{5,6},{6,5},{7,4},{8,11},{9,10},{10,... | collective-permute-start | bytes 196616 | tf_op jit(solution)/shard_map/ppermute | solution.py:675
  386.7 26.7 %all-to-all-start.8 = ((bf16[32,64,128]{2,1,0:T(8,128)(2,1)}), bf16[32,64,128]{2,1,0:T(8,128)(2,1)S(1)}, u32[]{:S(2)}, u32[]{:S(2)}) async-start(bf16[32,64,128]{2,1,0:T(8,128)(2,1)} %bitcast.58), calls=%async_computation.8 | async-start | bytes 1048576 | tf_op jit(solution)/shard_map/all_to_all | solution.py:653
  419.5 32.3 %all-to-all-start.9 = ((bf16[128,8,896]{2,1,0:T(8,128)(2,1)}), bf16[128,8,896]{2,1,0:T(8,128)(2,1)S(1)}, u32[]{:S(2)}, u32[]{:S(2)}) async-start(bf16[128,8,896]{2,1,0:T(8,128)(2,1)} %bitcast.59), calls=%async_computation.9 | async-start | bytes 3670016 | tf_op jit(solution)/shard_map/all_to_all | solution.py:653
  430.9 24.7 %collective-permute-start.22 = (bf16[128,1024]{1,0:T(8,128)(2,1)}, bf16[128,1024]{1,0:T(8,128)(2,1)S(1)}, u32[]{:S(2)}, u32[]{:S(2)}) collective-permute-start(bf16[128,1024]{1,0:T(8,128)(2,1)} %get-tuple-element.222), channel_id=1, source_target_pairs={{0,1},{1,0},{2,3},{3,2},{4,5},{5,4},{6,7},{7,6},{8,9},{9,8},{10,11... | collective-permute-start | bytes 786440 | tf_op jit(solution)/shard_map/ppermute | solution.py:675
  432.0 23.6 %collective-permute-start.23 = (bf16[128,1024]{1,0:T(8,128)(2,1)}, bf16[128,1024]{1,0:T(8,128)(2,1)S(1)}, u32[]{:S(2)}, u32[]{:S(2)}) collective-permute-start(bf16[128,1024]{1,0:T(8,128)(2,1)} %get-tuple-element.223), channel_id=1, source_target_pairs={{0,2},{1,3},{2,0},{3,1},{4,6},{5,7},{6,4},{7,5},{8,10},{9,11},{10,... | collective-permute-start | bytes 786440 | tf_op jit(solution)/shard_map/ppermute | solution.py:675
  432.8 25.7 %collective-permute-start.24 = (bf16[128,1024]{1,0:T(8,128)(2,1)}, bf16[128,1024]{1,0:T(8,128)(2,1)S(1)}, u32[]{:S(2)}, u32[]{:S(2)}) collective-permute-start(bf16[128,1024]{1,0:T(8,128)(2,1)} %get-tuple-element.224), channel_id=1, source_target_pairs={{0,3},{1,2},{2,1},{3,0},{4,7},{5,6},{6,5},{7,4},{8,11},{9,10},{10,... | collective-permute-start | bytes 786440 | tf_op jit(solution)/shard_map/ppermute | solution.py:675
  (41 other events, 508.6 us)
Sparse Core Ops, SparseCore 0:
  84.2 74.6 all-gather.1
  256.4 66.0 reduce-scatter.1

commit v6 on v5

--- a/solution.py
+++ b/solution.py
@@ -155,15 +155,17 @@
 
 def kernel_picks(rank_ref, gate_ref, pick_ref, turned_ref, high_ref, rest_ref):
     slot = lax.broadcasted_iota(jnp.int32, (64, 128), 0).astype(F32)
-    for p in range(16):
+
+    @pl.loop(0, 16)
+    def _(p):
         picks, weights = [], []
         for e in (2 * p, 2 * p + 1):
-            hit = slot == rank_ref[e : e + 1, :]
+            hit = slot == rank_ref[pl.ds(e, 1), :]
             picks.append(jnp.where(hit, 1.0, 0.0))
-            weights.append(jnp.where(hit, gate_ref[e : e + 1, :], 0.0))
+            weights.append(jnp.where(hit, gate_ref[pl.ds(e, 1), :], 0.0))
         picks = jnp.concatenate(picks, axis=0)
         weights = jnp.transpose(jnp.concatenate(weights, axis=0))
-        at = slice(128 * p, 128 * p + 128)
+        at = pl.ds(pl.multiple_of(128 * p, 128), 128)
         pick_ref[at, :] = picks.astype(BF)
         turned_ref[:, at] = jnp.transpose(picks).astype(BF)
         high = weights.astype(BF)
@@ -212,9 +214,6 @@
             q_ref[half, :, head] = queries[:, at : at + 128].reshape(8, 64, 128)
 
 
-CHUNKS = (1, 2, 3, 4, 8, 7, 6, 5)
-
-
 def tile_positions(tile, mine):
     front = tile < 4
     i = jnp.where(front, tile, tile - 4)
@@ -227,7 +226,19 @@
     return jnp.where(front, q_front, q_back), jnp.where(front, k_front, k_back)
 
 
-def kernel_attend(mine_ref, kv_ref, q_ref, msg_ref, log_ref, out_ref, keys_ref, turned_ref):
+def kernel_attend(
+    mine_ref,
+    kv_ref,
+    q_ref,
+    msg_ref,
+    log_ref,
+    out_ref,
+    keys_ref,
+    turned_ref,
+    peak_ref,
+    total_ref,
+    mixed_ref,
+):
     tile = pl.program_id(0)
 
     @pl.when(tile == 0)
@@ -245,37 +256,53 @@
     q = q_ref[...]
     q_pos, k_pos = tile_positions(tile, mine_ref[0])
 
-    def run(count):
-        peak = jnp.full((1, 256), MASKED, F32)
-        total = jnp.zeros((1, 256), F32)
-        mixed = jnp.zeros((64, 256), F32)
-        later = mm(keys_ref[0:512, :], q, NT)
+    def run(first, count, last):
+        def keys(c):
+            return pl.ds(pl.multiple_of(first + 512 * c, 512), 512)
+
+        peak = peak_ref[0:1]
+        total = total_ref[0:1]
+        mixed = mixed_ref[...]
+        later = mm(keys_ref[keys(0), :], q, NT)
         for c in range(count):
             scores = later
             if c + 1 < count:
-                later = mm(keys_ref[512 * c + 512 : 512 * c + 1024, :], q, NT)
-            else:
+                later = mm(keys_ref[keys(c + 1), :], q, NT)
+            elif last:
                 scores = jnp.where(k_pos <= q_pos, scores, MASKED)
             higher = jnp.maximum(peak, jnp.max(scores, axis=0, keepdims=True))
             weights = jnp.exp(scores - higher)
             fade = jnp.exp(peak - higher)
             total = total * fade + jnp.sum(weights, axis=0, keepdims=True)
-            mixed = mixed * fade + mm(
-                turned_ref[64:128, 512 * c : 512 * c + 512], weights.astype(BF)
-            )
+            mixed = mixed * fade + mm(turned_ref[64:128, keys(c)], weights.astype(BF))
             peak = higher
-        log_ref[0] = jnp.broadcast_to(peak + jnp.log(total), (8, 256))
-        mixed = mixed / total
-        out = jnp.transpose(jnp.concatenate([jnp.zeros((64, 256), F32), mixed], axis=0))
-        out_ref[...] = out
-        low = lane((64, 128)) < 64
-        for a in range(2):
-            first = out[128 * a : 128 * a + 64]
-            second = out[128 * a + 64 : 128 * a + 128]
-            msg_ref[a, 0] = jnp.where(low, pltpu.roll(first, 64, 1), second).astype(BF)
-
-    for t, count in enumerate(CHUNKS):
-        pl.when(tile == t)(functools.partial(run, count))
+        peak_ref[...] = jnp.broadcast_to(peak, (8, 256))
+        total_ref[...] = jnp.broadcast_to(total, (8, 256))
+        mixed_ref[...] = mixed
+
+    peak_ref[...] = jnp.full((8, 256), MASKED, F32)
+    total_ref[...] = jnp.zeros((8, 256), F32)
+    mixed_ref[...] = jnp.zeros((64, 256), F32)
+
+    @pl.when(tile >= 4)
+    def _():
+        run(0, 4, False)
+
+    first = jnp.where(tile >= 4, 2048, 0)
+    rest = jnp.where(tile >= 4, 8 - tile, tile + 1)
+    for count in range(1, 5):
+        pl.when(rest == count)(functools.partial(run, first, count, True))
+
+    total = total_ref[0:1]
+    log_ref[0] = jnp.broadcast_to(peak_ref[0:1] + jnp.log(total), (8, 256))
+    mixed = mixed_ref[...] / total
+    out = jnp.transpose(jnp.concatenate([jnp.zeros((64, 256), F32), mixed], axis=0))
+    out_ref[...] = out
+    low = lane((64, 128)) < 64
+    for a in range(2):
+        one = out[128 * a : 128 * a + 64]
+        two = out[128 * a + 64 : 128 * a + 128]
+        msg_ref[a, 0] = jnp.where(low, pltpu.roll(one, 64, 1), two).astype(BF)
 
 
 def kernel_attend_back(
@@ -440,7 +467,13 @@
 
     act = act_ref[...]
     ys_ref[...] = mm(act, v_ref[...]).astype(BF).reshape(4, 64, WIDTH)
-    ggu_ref[...] += mm(h_ref[...].reshape(256, WIDTH), dboth_ref[...], TN)
+    h = h_ref[...].reshape(256, WIDTH)
+
+    @pl.loop(0, 4)
+    def _(c):
+        at = pl.ds(pl.multiple_of(256 * c, 256), 256)
+        ggu_ref[:, at] += mm(h, dboth_ref[:, at], TN)
+
     gv_ref[...] += mm(act, dys_ref[...].reshape(256, WIDTH), TN)
 
     @pl.when(step == 7)
@@ -518,11 +551,13 @@
     which = lax.broadcasted_iota(jnp.int32, (128, WIDTH), 0)
     grad_ref[:, 0:128] = jnp.transpose(jnp.where(which == 1, gain_ref[0:1], 0.0)).astype(BF)
     pairs = ((o0_ref, da0_ref), (o1_ref, da1_ref), (o2_ref, da2_ref), (o3_ref, da3_ref))
-    for g in range(8):
+
+    @pl.loop(0, 8)
+    def _(g):
         part = jnp.zeros((128, 256), F32)
         for o_ref, da_ref in pairs:
             part = part + mm(o_ref[g].reshape(128, 128), da_ref[...], TN)
-        grad_ref[128 * g : 128 * g + 128, 128:384] = part.astype(BF)
+        grad_ref[pl.ds(pl.multiple_of(128 * g, 128), 128), 128:384] = part.astype(BF)
 
 
 def kernel_slices_back(
@@ -807,6 +842,11 @@
         grid=(8,),
         in_specs=[SM, whole((4, 2, 8, 64, 128)), row_spec],
         out_specs=(msg_spec, log_spec, row_spec, whole((4096, 128)), whole((128, 4096))),
+        scratch_shapes=[
+            pltpu.VMEM((8, 256), F32),
+            pltpu.VMEM((8, 256), F32),
+            pltpu.VMEM((64, 256), F32),
+        ],
     )(mine_ref, kv, queries)
     o_msg, w_out, experts_all = lax.optimization_barrier((o_msg, w_out, experts_all))
     experts_all = experts_all + (swap(experts_all[2], "core"),)

time: 478 us -> 472 us (0.987); the launches traced: 470 us -> 471 us
  waiting for transfers between devices: 188 us -> 174 us
  Pallas kernels: 133 us -> 144 us
    all_to_all x9, waiting for transfers between devices: 158 us -> 147 us  [exchange(): return lax.all_to_all(value, axes, split_axis=0, concat_axis=0, tiled=True)]
    pallas_call x1, Pallas kernels: 15.9 us -> 23.6 us  [on_device(): call(kernel_experts_after, (sds((32, 64, WIDTH), BF), sds((4, 384, WIDTH)...]
  transfers between devices with their start and end apart: 36 -> 36, of which waited for: 14 -> 14; matrix products, arithmetic and copies ran while one was open for 4% -> 4% of each run, Pallas kernels for 28% -> 30%
where the time goes in v6:
time: 472 us; the launch traced here: 471 us
  waiting for transfers between devices  174 us (37%)
  Pallas kernels  144 us (31%)
  starting transfers between devices  96.9 us (21%)
  local copies, waits for them, and re-layouts  16.9 us (4%)
  between operations  14.6 us (3%)
  blocking collectives  14.5 us (3%)
  other arithmetic  8.93 us (2%)
    all_to_all x9, waiting for transfers between devices, exchange(): return lax.all_to_all(value, axes, split_axis=0, concat_axis=0, tiled=True)  147 us
    all_to_all x9, starting transfers between devices, exchange(): return lax.all_to_all(value, axes, split_axis=0, concat_axis=0, tiled=True)  65.2 us
    ppermute x9, waiting for transfers between devices, cross(): here.append(lax.ppermute(parts[r], axes, [(i, i ^ r) for i in range(4)]))  25.1 us
    pallas_call x1, Pallas kernels, on_device(): call(kernel_experts_after, (sds((32, 64, WIDTH), BF), sds((4, 384, WIDTH)...  23.6 us
    pallas_call x1, Pallas kernels, on_device(): call(kernel_attend_back, (sds((2048, 128), F32),) + (sds((2, 8, 64, 128),...  22.9 us
    ppermute x9, starting transfers between devices, cross(): here.append(lax.ppermute(parts[r], axes, [(i, i ^ r) for i in range(4)]))  17.7 us
    pallas_call x1, Pallas kernels, on_device(): call(kernel_attend, (sds((8, 2, 64, 128), BF), sds((8, 8, 256), F32), sds...  17.1 us
    all_to_all x1, blocking collectives, exchange(): return lax.all_to_all(value, axes, split_axis=0, concat_axis=0, tiled=True)  14.5 us
  transfers between devices with their start and end apart: 36, of which 14 were waited for; matrix products, arithmetic and copies ran while one was open for 4% of the time, Pallas kernels for 30%

profile of v6, /device:TPU:1, one launch (start us, length us, event | category | flops | bytes accessed | tf_op | source)
XLA Modules:
  0.0 470.6 jit_solution(7062773920439815951)
XLA Ops:
  19.3 9.9 %all-to-all-start = ((bf16[128,8,896]{2,1,0:T(8,128)(2,1)}), bf16[128,8,896]{2,1,0:T(8,128)(2,1)S(1)}, u32[]{:S(2)}, u32[]{:S(2)}) async-start(bf16[128,8,896]{2,1,0:T(8,128)(2,1)} %bitcast.55), calls=%async_computation | async-start | bytes 3670016 | tf_op jit(solution)/shard_map/all_to_all | solution.py:688
  32.3 24.0 %all-to-all-done = bf16[128,8,896]{2,1,0:T(8,128)(2,1)S(1)} async-done(((bf16[128,8,896]{2,1,0:T(8,128)(2,1)}), bf16[128,8,896]{2,1,0:T(8,128)(2,1)S(1)}, u32[]{:S(2)}, u32[]{:S(2)}) %all-to-all-start) | async-done | bytes 1835040 | tf_op jit(solution)/shard_map/all_to_all | solution.py:688
  57.6 4.6 shard_map.198
  62.2 6.0 %all-to-all-start.1 = ((bf16[32,64,128]{2,1,0:T(8,128)(2,1)}), bf16[32,64,128]{2,1,0:T(8,128)(2,1)S(1)}, u32[]{:S(2)}, u32[]{:S(2)}) async-start(bf16[32,64,128]{2,1,0:T(8,128)(2,1)} %get-tuple-element.131), calls=%async_computation.1 | async-start | bytes 1048576 | tf_op jit(solution)/shard_map/all_to_all | solution.py:688
  72.2 7.7 %all-to-all-done.1 = bf16[32,64,128]{2,1,0:T(8,128)(2,1)S(1)} async-done(((bf16[32,64,128]{2,1,0:T(8,128)(2,1)}), bf16[32,64,128]{2,1,0:T(8,128)(2,1)S(1)}, u32[]{:S(2)}, u32[]{:S(2)}) %all-to-all-start.1) | async-done | bytes 524320 | tf_op jit(solution)/shard_map/all_to_all | solution.py:688
  96.1 14.1 %all-to-all-done.2 = bf16[4,1024,128]{2,1,0:T(8,128)(2,1)S(1)} async-done(((bf16[4,1024,128]{2,1,0:T(8,128)(2,1)}), bf16[4,1024,128]{2,1,0:T(8,128)(2,1)S(1)}, u32[]{:S(2)}, u32[]{:S(2)}) %all-to-all-start.2) | async-done | bytes 1048608 | tf_op jit(solution)/shard_map/all_to_all | solution.py:688
  111.6 17.1 %shard_map.200 = (bf16[8,2,64,128]{3,2,1,0:T(8,128)(2,1)}, f32[8,8,256]{2,1,0:T(8,128)}, f32[2048,128]{1,0:T(8,128)}, bf16[4096,128]{1,0:T(8,128)(2,1)}, bf16[128,4096]{1,0:T(8,128)(2,1)}) custom-call(s32[1]{0:T(128)} %bitcast.mine_ref, bf16[4,2,8,64,128]{4,3,2,1,0:T(8,128)(2,1)} %bitcast.66, bf16[2048,128]{1,0:T(8,128)(2,1)} %bitcast.75), custom_call_target="tpu_custom_call" | custom-call | flops 10000000000 | bytes 5000000 | tf_op jit(solution)/shard_map/pallas_call | solution.py:832
  136.7 6.2 %all-to-all-done.3.o_ref.o0_ref = bf16[8,2,64,128]{3,2,1,0:T(8,128)(2,1)S(1)} async-done(((bf16[8,2,64,128]{3,2,1,0:T(8,128)(2,1)}), bf16[8,2,64,128]{3,2,1,0:T(8,128)(2,1)S(1)}, u32[]{:S(2)}, u32[]{:S(2)}) %all-to-all-start.3) | async-done | bytes 262176 | tf_op jit(solution)/shard_map/all_to_all | solution.py:688
  143.6 5.2 %shard_map.202 = (bf16[32,64,1024]{2,1,0:T(8,128)(2,1)}, f32[128,1024]{1,0:T(8,128)}) custom-call(s32[1]{0:T(128)} %bitcast.1.part_ref, bf16[8,2,64,128]{3,2,1,0:T(8,128)(2,1)} %copy-done.7, bf16[512,256]{1,0:T(8,128)(2,1)} %copy-done.6, bf16[512,256]{1,0:T(8,128)(2,1)} %copy-done.14, bf16[512,256]{1,0:T(8,128)(2,1)} %copy-done.15, ...), custom_call_target="tpu_custom_call" | custom-call | flops 900000000 | bytes 8000000 | tf_op jit(solution)/shard_map/pallas_call | solution.py:857
  149.7 5.6 %all-to-all-start.4 = ((bf16[32,64,1024]{2,1,0:T(8,128)(2,1)}), bf16[32,64,1024]{2,1,0:T(8,128)(2,1)}, u32[]{:S(2)}, u32[]{:S(2)}) async-start(bf16[32,64,1024]{2,1,0:T(8,128)(2,1)} %get-tuple-element.165), calls=%async_computation.4 | async-start | bytes 8388608 | tf_op jit(solution)/shard_map/all_to_all | solution.py:688
  158.6 12.5 %shard_map.203 = (bf16[32,64,1024]{2,1,0:T(8,128)(2,1)}, f32[2048,512]{1,0:T(8,128)}, bf16[512,1024]{1,0:T(8,128)(2,1)}, bf16[1024,1024]{1,0:T(8,128)(2,1)}) custom-call(s32[1]{0:T(128)} %bitcast.1.part_ref, bf16[4,4,2,128,1024]{4,3,2,1,0:T(8,128)(2,1)} %bitcast.74, bf16[32,8,128]{2,1,0:T(8,128)(2,1)} %dynamic-slice_bitcast_fusion.parts_ref, ...), custom_call_target="tpu_custom_call" | custom-call | flops 6000000000 | bytes 20000000 | tf_op jit(solution)/shard_map/pallas_call | solution.py:876
  171.1 41.8 %all-to-all-done.4.h_ref = bf16[32,64,1024]{2,1,0:T(8,128)(2,1)} async-done(((bf16[32,64,1024]{2,1,0:T(8,128)(2,1)}), bf16[32,64,1024]{2,1,0:T(8,128)(2,1)}, u32[]{:S(2)}, u32[]{:S(2)}) %all-to-all-start.4) | async-done | bytes 4194336 | tf_op jit(solution)/shard_map/all_to_all | solution.py:688
  212.9 13.8 %shard_map.204 = (bf16[2048,512]{1,0:T(8,128)(2,1)}, bf16[2048,1024]{1,0:T(8,128)(2,1)}, bf16[32,64,1024]{2,1,0:T(8,128)(2,1)}) custom-call(bf16[32,64,1024]{2,1,0:T(8,128)(2,1)} %all-to-all-done.4.h_ref, bf16[1024,1024]{1,0:T(8,128)(2,1)} %get-tuple-element.174.gu_ref, f32[2048,512]{1,0:T(8,128)} %get-tuple-element.175.dact_ref), custom_call_target="tpu_custom_call" | custom-call | flops 8999999488 | bytes 20000000 | tf_op jit(solution)/shard_map/pallas_call | solution.py:902
  227.4 9.1 %all-to-all-start.5 = ((bf16[32,64,1024]{2,1,0:T(8,128)(2,1)}), bf16[32,64,1024]{2,1,0:T(8,128)(2,1)}, u32[]{:S(2)}, u32[]{:S(2)}) async-start(bf16[32,64,1024]{2,1,0:T(8,128)(2,1)} %get-tuple-element.178), calls=%async_computation.5 | async-start | bytes 8388608 | tf_op jit(solution)/shard_map/all_to_all | solution.py:688
  237.9 23.6 %shard_map.205 = (bf16[32,64,1024]{2,1,0:T(8,128)(2,1)}, bf16[4,384,1024]{2,1,0:T(8,128)(2,1)}) custom-call(bf16[32,64,1024]{2,1,0:T(8,128)(2,1)} %all-to-all-done.4.h_ref, bf16[2048,512]{1,0:T(8,128)(2,1)} %get-tuple-element.179.act_ref, bf16[32,64,1024]{2,1,0:T(8,128)(2,1)} %get-tuple-element.180.dys_ref, bf16[2048,1024]{1,0:T(8,128)(2,1)} %get-tuple-element.181.dboth_ref, ...), custom_call_target="tpu_custom_call" | custom-call | flops 8999999488 | bytes 20000000 | tf_op jit(solution)/shard_map/pallas_call | solution.py:918
  261.5 33.2 %all-to-all-done.5.dxs_ref = bf16[32,64,1024]{2,1,0:T(8,128)(2,1)} async-done(((bf16[32,64,1024]{2,1,0:T(8,128)(2,1)}), bf16[32,64,1024]{2,1,0:T(8,128)(2,1)}, u32[]{:S(2)}, u32[]{:S(2)}) %all-to-all-start.5) | async-done | bytes 4194336 | tf_op jit(solution)/shard_map/all_to_all | solution.py:688
  294.7 5.7 %shard_map.206 = (f32[128,1024]{1,0:T(8,128)}, bf16[4,128,256]{2,1,0:T(8,128)(2,1)}, bf16[8,2,64,128]{3,2,1,0:T(8,128)(2,1)}, f32[8,1024]{1,0:T(8,128)}) custom-call(s32[1]{0:T(128)} %bitcast.1.part_ref, bf16[32,64,1024]{2,1,0:T(8,128)(2,1)} %all-to-all-done.5.dxs_ref, bf16[128,2048]{1,0:T(8,128)(2,1)} %get-tuple-element.189.pick_ref, ...), custom_call_target="tpu_custom_call" | custom-call | flops 900000000 | bytes 8000000 | tf_op jit(solution)/shard_map/pallas_call | solution.py:935
  300.4 14.5 %all_to_all.50.grad_ref = bf16[8,2,64,128]{3,2,1,0:T(8,128)(2,1)} all-to-all(bf16[8,2,64,128]{3,2,1,0:T(8,128)(2,1)} %get-tuple-element.190), channel_id=1, replica_groups=mesh['x'=4,'zh'=2,'y'=4,'zl'=2,'core'=2] {'x','zh'}, dimensions={0} | all-to-all | bytes 524288 | tf_op jit(solution)/shard_map/all_to_all | solution.py:688
  314.9 6.3 %all-to-all-start.7 = ((bf16[32,64,1024]{2,1,0:T(8,128)(2,1)}), bf16[32,64,1024]{2,1,0:T(8,128)(2,1)}, u32[]{:S(2)}, u32[]{:S(2)}) async-start(bf16[32,64,1024]{2,1,0:T(8,128)(2,1)} %get-tuple-element.198), calls=%async_computation.7 | async-start | bytes 8388608 | tf_op jit(solution)/shard_map/all_to_all | solution.py:688
  321.2 22.9 %shard_map.207 = (f32[2048,128]{1,0:T(8,128)}, bf16[2,8,64,128]{3,2,1,0:T(8,128)(2,1)}, bf16[2,8,64,128]{3,2,1,0:T(8,128)(2,1)}, bf16[2,8,64,128]{3,2,1,0:T(8,128)(2,1)}, bf16[2,8,64,128]{3,2,1,0:T(8,128)(2,1)}) custom-call(s32[1]{0:T(128)} %bitcast.mine_ref, bf16[4096,128]{1,0:T(8,128)(2,1)} %get-tuple-element.137.keys_ref, ...), custom_call_target="tpu_custom_call" | custom-call | flops 20000000000 | bytes 7000000 | tf_op jit(solution)/shard_map/pallas_call | solution.py:965
  352.9 5.7 %collective-permute-start.20 = (bf16[128,256]{1,0:T(8,128)(2,1)S(1)}, bf16[128,256]{1,0:T(8,128)(2,1)S(1)}, u32[]{:S(2)}, u32[]{:S(2)}) collective-permute-start(bf16[128,256]{1,0:T(8,128)(2,1)S(1)} %get-tuple-element.244), channel_id=1, source_target_pairs={{0,2},{1,3},{2,0},{3,1},{4,6},{5,7},{6,4},{7,5},{8,10},{9,11},{10,... | collective-permute-start | bytes 196616 | tf_op jit(solution)/shard_map/ppermute | solution.py:710
  359.7 11.7 %collective-permute-done.20.da2_ref = bf16[128,256]{1,0:T(8,128)(2,1)S(1)} collective-permute-done((bf16[128,256]{1,0:T(8,128)(2,1)S(1)}, bf16[128,256]{1,0:T(8,128)(2,1)S(1)}, u32[]{:S(2)}, u32[]{:S(2)}) %collective-permute-start.20) | collective-permute-done | bytes 65568 | tf_op jit(solution)/shard_map/ppermute | solution.py:710
  371.4 5.7 %collective-permute-done.21.da3_ref = bf16[128,256]{1,0:T(8,128)(2,1)S(1)} collective-permute-done((bf16[128,256]{1,0:T(8,128)(2,1)S(1)}, bf16[128,256]{1,0:T(8,128)(2,1)S(1)}, u32[]{:S(2)}, u32[]{:S(2)}) %collective-permute-start.21) | collective-permute-done | bytes 65568 | tf_op jit(solution)/shard_map/ppermute | solution.py:710
  377.1 4.8 %collective-permute-done.17.d2_ref = bf16[2,8,64,128]{3,2,1,0:T(8,128)(2,1)S(1)} collective-permute-done((bf16[2,8,64,128]{3,2,1,0:T(8,128)(2,1)}, bf16[2,8,64,128]{3,2,1,0:T(8,128)(2,1)S(1)}, u32[]{:S(2)}, u32[]{:S(2)}) %collective-permute-start.17) | collective-permute-done | bytes 262176 | tf_op jit(solution)/shard_map/ppermute | solution.py:710
  382.7 4.3 shard_map.209
  387.0 16.2 %all-to-all-start.8 = ((bf16[32,64,128]{2,1,0:T(8,128)(2,1)}), bf16[32,64,128]{2,1,0:T(8,128)(2,1)S(1)}, u32[]{:S(2)}, u32[]{:S(2)}) async-start(bf16[32,64,128]{2,1,0:T(8,128)(2,1)} %bitcast.58), calls=%async_computation.8 | async-start | bytes 1048576 | tf_op jit(solution)/shard_map/all_to_all | solution.py:688
  403.3 4.3 shard_map.210.rest_ref
  407.6 7.3 %all-to-all-done.8.msg_ref = bf16[32,64,128]{2,1,0:T(8,128)(2,1)S(1)} async-done(((bf16[32,64,128]{2,1,0:T(8,128)(2,1)}), bf16[32,64,128]{2,1,0:T(8,128)(2,1)S(1)}, u32[]{:S(2)}, u32[]{:S(2)}) %all-to-all-start.8) | async-done | bytes 524320 | tf_op jit(solution)/shard_map/all_to_all | solution.py:688
  415.7 5.3 %shard_map.211 = (bf16[1024,896]{1,0:T(8,128)(2,1)}, bf16[512,512]{1,0:T(8,128)(2,1)}) custom-call(bf16[32,64,128]{2,1,0:T(8,128)(2,1)} %copy-done.2, bf16[512,1024]{1,0:T(8,128)(2,1)} %get-tuple-element.210.hidden_ref, bf16[1024,896]{1,0:T(8,128)(2,1)} %bitcast.53, bf16[1024,384]{1,0:T(8,128)(2,1)} %shard_map.210.rest_ref), custom_call_target="tpu_custom_call" | custom-call | flops 600000000 | bytes 5000000 | tf_op jit(solution)/shard_map/pallas_call | solution.py:1016
  421.0 4.9 %all-to-all-start.9 = ((bf16[128,8,896]{2,1,0:T(8,128)(2,1)}), bf16[128,8,896]{2,1,0:T(8,128)(2,1)S(1)}, u32[]{:S(2)}, u32[]{:S(2)}) async-start(bf16[128,8,896]{2,1,0:T(8,128)(2,1)} %bitcast.59), calls=%async_computation.9 | async-start | bytes 3670016 | tf_op jit(solution)/shard_map/all_to_all | solution.py:688
  435.7 5.0 %shard_map.208 = bf16[128,1024]{1,0:T(8,128)(2,1)} custom-call(bf16[32,64,1024]{2,1,0:T(8,128)(2,1)} %all-to-all-done.7.ys_ref, bf16[128,2048]{1,0:T(8,128)(2,1)} %get-tuple-element.201.high_ref, bf16[128,2048]{1,0:T(8,128)(2,1)} %get-tuple-element.202.rest_ref, f32[128,1024]{1,0:T(8,128)} %get-tuple-element.168.mid_ref), custom_call_target="tpu_custom_call" | custom-call | flops 1000000000 | bytes 5000000 | tf_op jit(solution)/shard_map/pallas_call | solution.py:992
  440.8 12.3 %all-to-all-done.9 = bf16[128,8,896]{2,1,0:T(8,128)(2,1)S(1)} async-done(((bf16[128,8,896]{2,1,0:T(8,128)(2,1)}), bf16[128,8,896]{2,1,0:T(8,128)(2,1)S(1)}, u32[]{:S(2)}, u32[]{:S(2)}) %all-to-all-start.9) | async-done | bytes 1835040 | tf_op jit(solution)/shard_map/all_to_all | solution.py:688
  (168 shorter events, 84.6 us)
Async XLA Ops:
  7.2 11.4 %collective-permute-start = (bf16[128,1024]{1,0:T(8,128)(2,1)}, bf16[128,1024]{1,0:T(8,128)(2,1)S(1)}, u32[]{:S(2)}, u32[]{:S(2)}) collective-permute-start(bf16[128,1024]{1,0:T(8,128)(2,1)} %bitcast.61), channel_id=1, source_target_pairs={{0,1},{1,0},{2,3},{3,2},{4,5},{5,4},{6,7},{7,6},{8,9},{9,8},{10,11... | collective-permute-start | bytes 786440 | tf_op jit(solution)/shard_map/ppermute | solution.py:700
  19.3 37.0 %all-to-all-start = ((bf16[128,8,896]{2,1,0:T(8,128)(2,1)}), bf16[128,8,896]{2,1,0:T(8,128)(2,1)S(1)}, u32[]{:S(2)}, u32[]{:S(2)}) async-start(bf16[128,8,896]{2,1,0:T(8,128)(2,1)} %bitcast.55), calls=%async_computation | async-start | bytes 3670016 | tf_op jit(solution)/shard_map/all_to_all | solution.py:688
  29.2 27.6 %collective-permute-start.2 = (bf16[128,1024]{1,0:T(8,128)(2,1)S(1)}, bf16[128,1024]{1,0:T(8,128)(2,1)S(1)}, u32[]{:S(2)}, u32[]{:S(2)}) collective-permute-start(bf16[128,1024]{1,0:T(8,128)(2,1)S(1)} %collective-permute-done.1.x2_ref), channel_id=1, source_target_pairs={{0,1},{1,0},{2,3},{3,2},{4,5},{5,4},{6,7},{7,6},{8,9},{9,8},{10,11... | collective-permute-start | bytes 786440 | tf_op jit(solution)/shard_map/ppermute | solution.py:700
  56.3 14.9 %collective-permute-start.12 = (bf16[128,1024]{1,0:T(8,128)(2,1)S(1)}, bf16[128,1024]{1,0:T(8,128)(2,1)S(1)}, u32[]{:S(2)}, u32[]{:S(2)}) collective-permute-start(bf16[128,1024]{1,0:T(8,128)(2,1)S(1)} %bitcast.68), channel_id=1, source_target_pairs={{0,16},{16,0},{1,17},{17,1},{2,18},{18,2},{3,19},{19,3},{4,20},{20... | collective-permute-start | bytes 786440 | tf_op jit(solution)/shard_map/ppermute | solution.py:700
  62.2 17.7 %all-to-all-start.1 = ((bf16[32,64,128]{2,1,0:T(8,128)(2,1)}), bf16[32,64,128]{2,1,0:T(8,128)(2,1)S(1)}, u32[]{:S(2)}, u32[]{:S(2)}) async-start(bf16[32,64,128]{2,1,0:T(8,128)(2,1)} %get-tuple-element.131), calls=%async_computation.1 | async-start | bytes 1048576 | tf_op jit(solution)/shard_map/all_to_all | solution.py:688
  68.3 90.4 %all-gather.2.cloned.1.call-start = ((), (), s32[]{:S(2)}) async-start(), calls=%async_computation.11 | async-start | bytes 8912896 | tf_op jit(solution)/shard_map/all_gather | solution.py:692
  69.4 14.5 %collective-permute-start.3 = (bf16[512,256]{1,0:T(8,128)(2,1)S(1)}, bf16[512,256]{1,0:T(8,128)(2,1)S(1)}, u32[]{:S(2)}, u32[]{:S(2)}) collective-permute-start(bf16[512,256]{1,0:T(8,128)(2,1)S(1)} %get-tuple-element.149.u0_ref), channel_id=1, source_target_pairs={{0,1},{1,0},{2,3},{3,2},{4,5},{5,4},{6,7},{7,6},{8,9},{9,8},{10,11... | collective-permute-start | bytes 786440 | tf_op jit(solution)/shard_map/ppermute | solution.py:700
  69.7 14.2 %collective-permute-start.4 = (bf16[512,256]{1,0:T(8,128)(2,1)S(1)}, bf16[512,256]{1,0:T(8,128)(2,1)S(1)}, u32[]{:S(2)}, u32[]{:S(2)}) collective-permute-start(bf16[512,256]{1,0:T(8,128)(2,1)S(1)} %get-tuple-element.149.u0_ref), channel_id=1, source_target_pairs={{0,2},{2,0},{1,3},{3,1},{4,6},{6,4},{5,7},{7,5},{8,10},{10,8},{9,1... | collective-permute-start | bytes 786440 | tf_op jit(solution)/shard_map/ppermute | solution.py:700
  84.4 25.7 %all-to-all-start.2 = ((bf16[4,1024,128]{2,1,0:T(8,128)(2,1)}), bf16[4,1024,128]{2,1,0:T(8,128)(2,1)S(1)}, u32[]{:S(2)}, u32[]{:S(2)}) async-start(bf16[4,1024,128]{2,1,0:T(8,128)(2,1)} %get-tuple-element.133), calls=%async_computation.2 | async-start | bytes 2097152 | tf_op jit(solution)/shard_map/all_to_all | solution.py:688
  91.8 37.0 %collective-permute-start.10 = (bf16[384,1024]{1,0:T(8,128)(2,1)S(1)}, bf16[384,1024]{1,0:T(8,128)(2,1)}, u32[]{:S(2)}, u32[]{:S(2)}) collective-permute-start(bf16[384,1024]{1,0:T(8,128)(2,1)S(1)} %pad_maximum_fusion.w0_ref), channel_id=1, source_target_pairs={{0,2},{2,0},{1,3},{3,1},{4,6},{6,4},{5,7},{7,5},{8,10},{10,8},{9,1... | collective-permute-start | bytes 2359304 | tf_op jit(solution)/shard_map/ppermute | solution.py:700
  93.1 35.7 %collective-permute-start.9 = (bf16[384,1024]{1,0:T(8,128)(2,1)S(1)}, bf16[384,1024]{1,0:T(8,128)(2,1)}, u32[]{:S(2)}, u32[]{:S(2)}) collective-permute-start(bf16[384,1024]{1,0:T(8,128)(2,1)S(1)} %pad_maximum_fusion.w0_ref), channel_id=1, source_target_pairs={{0,1},{1,0},{2,3},{3,2},{4,5},{5,4},{6,7},{7,6},{8,9},{9,8},{10,11... | collective-permute-start | bytes 2359304 | tf_op jit(solution)/shard_map/ppermute | solution.py:700
  110.1 18.6 %collective-permute-start.7 = (bf16[512,256]{1,0:T(8,128)(2,1)S(1)}, bf16[512,256]{1,0:T(8,128)(2,1)S(1)}, u32[]{:S(2)}, u32[]{:S(2)}) collective-permute-start(bf16[512,256]{1,0:T(8,128)(2,1)S(1)} %collective-permute-done.4.u2_ref), channel_id=1, source_target_pairs={{0,1},{1,0},{2,3},{3,2},{4,5},{5,4},{6,7},{7,6},{8,9},{9,8},{10,11... | collective-permute-start | bytes 786440 | tf_op jit(solution)/shard_map/ppermute | solution.py:700
  111.4 17.4 %collective-permute-start.8 = (bf16[512,256]{1,0:T(8,128)(2,1)S(1)}, bf16[512,256]{1,0:T(8,128)(2,1)S(1)}, u32[]{:S(2)}, u32[]{:S(2)}) collective-permute-start(bf16[512,256]{1,0:T(8,128)(2,1)S(1)} %collective-permute-done.6.l2_ref), channel_id=1, source_target_pairs={{0,1},{1,0},{2,3},{3,2},{4,5},{5,4},{6,7},{7,6},{8,9},{9,8},{10,11... | collective-permute-start | bytes 786440 | tf_op jit(solution)/shard_map/ppermute | solution.py:700
  128.8 20.0 %collective-permute-start.11 = (bf16[384,1024]{1,0:T(8,128)(2,1)}, bf16[384,1024]{1,0:T(8,128)(2,1)S(1)}, u32[]{:S(2)}, u32[]{:S(2)}) collective-permute-start(bf16[384,1024]{1,0:T(8,128)(2,1)} %collective-permute-done.10.w2_ref), channel_id=1, source_target_pairs={{0,1},{1,0},{2,3},{3,2},{4,5},{5,4},{6,7},{7,6},{8,9},{9,8},{10,11... | collective-permute-start | bytes 2359304 | tf_op jit(solution)/shard_map/ppermute | solution.py:700
  129.6 13.2 %all-to-all-start.3 = ((bf16[8,2,64,128]{3,2,1,0:T(8,128)(2,1)}), bf16[8,2,64,128]{3,2,1,0:T(8,128)(2,1)S(1)}, u32[]{:S(2)}, u32[]{:S(2)}) async-start(bf16[8,2,64,128]{3,2,1,0:T(8,128)(2,1)} %get-tuple-element.148), calls=%async_computation.3 | async-start | bytes 524288 | tf_op jit(solution)/shard_map/all_to_all | solution.py:688
  149.7 63.2 %all-to-all-start.4 = ((bf16[32,64,1024]{2,1,0:T(8,128)(2,1)}), bf16[32,64,1024]{2,1,0:T(8,128)(2,1)}, u32[]{:S(2)}, u32[]{:S(2)}) async-start(bf16[32,64,1024]{2,1,0:T(8,128)(2,1)} %get-tuple-element.165), calls=%async_computation.4 | async-start | bytes 8388608 | tf_op jit(solution)/shard_map/all_to_all | solution.py:688
  156.8 69.9 %collective-permute-start.13 = (bf16[8,2,64,128]{3,2,1,0:T(8,128)(2,1)S(1)}, bf16[8,2,64,128]{3,2,1,0:T(8,128)(2,1)S(1)}, u32[]{:S(2)}, u32[]{:S(2)}) collective-permute-start(bf16[8,2,64,128]{3,2,1,0:T(8,128)(2,1)S(1)} %copy-done.8), channel_id=1, source_target_pairs={{0,1},{1,0},{2,3},{3,2},{4,5},{5,4},{6,7},{7,6},{8,9},{9,8},{10,11... | collective-permute-start | bytes 786440 | tf_op jit(solution)/shard_map/ppermute | solution.py:700
  158.0 68.8 %collective-permute-start.14 = (bf16[8,2,64,128]{3,2,1,0:T(8,128)(2,1)S(1)}, bf16[8,2,64,128]{3,2,1,0:T(8,128)(2,1)S(1)}, u32[]{:S(2)}, u32[]{:S(2)}) collective-permute-start(bf16[8,2,64,128]{3,2,1,0:T(8,128)(2,1)S(1)} %copy-done.8), channel_id=1, source_target_pairs={{0,2},{2,0},{1,3},{3,1},{4,6},{6,4},{5,7},{7,5},{8,10},{10,8},{9,1... | collective-permute-start | bytes 786440 | tf_op jit(solution)/shard_map/ppermute | solution.py:700
  227.4 67.3 %all-to-all-start.5 = ((bf16[32,64,1024]{2,1,0:T(8,128)(2,1)}), bf16[32,64,1024]{2,1,0:T(8,128)(2,1)}, u32[]{:S(2)}, u32[]{:S(2)}) async-start(bf16[32,64,1024]{2,1,0:T(8,128)(2,1)} %get-tuple-element.178), calls=%async_computation.5 | async-start | bytes 8388608 | tf_op jit(solution)/shard_map/all_to_all | solution.py:688
  236.6 189.4 %reduce-scatter.2.cloned.1.call-start = ((), (), s32[]{:S(2)}) async-start(), calls=%async_computation.12 | async-start | bytes 3932160 | tf_op jit(solution)/shard_map/reduce_scatter | solution.py:930
  236.6 24.9 %collective-permute-start.15 = (bf16[8,2,64,128]{3,2,1,0:T(8,128)(2,1)S(1)}, bf16[8,2,64,128]{3,2,1,0:T(8,128)(2,1)S(1)}, u32[]{:S(2)}, u32[]{:S(2)}) collective-permute-start(bf16[8,2,64,128]{3,2,1,0:T(8,128)(2,1)S(1)} %collective-permute-done.14.o2_ref), channel_id=1, source_target_pairs={{0,1},{1,0},{2,3},{3,2},{4,5},{5,4},{6,7},{7,6},{8,9},{9,8},{10,11... | collective-permute-start | bytes 786440 | tf_op jit(solution)/shard_map/ppermute | solution.py:700
  314.9 67.0 %all-to-all-start.7 = ((bf16[32,64,1024]{2,1,0:T(8,128)(2,1)}), bf16[32,64,1024]{2,1,0:T(8,128)(2,1)}, u32[]{:S(2)}, u32[]{:S(2)}) async-start(bf16[32,64,1024]{2,1,0:T(8,128)(2,1)} %get-tuple-element.198), calls=%async_computation.7 | async-start | bytes 8388608 | tf_op jit(solution)/shard_map/all_to_all | solution.py:688
  344.1 33.1 %collective-permute-start.16 = (bf16[2,8,64,128]{3,2,1,0:T(8,128)(2,1)}, bf16[2,8,64,128]{3,2,1,0:T(8,128)(2,1)S(1)}, u32[]{:S(2)}, u32[]{:S(2)}) collective-permute-start(bf16[2,8,64,128]{3,2,1,0:T(8,128)(2,1)} %get-tuple-element.195), channel_id=1, source_target_pairs={{0,4},{4,0},{8,12},{12,8},{1,5},{5,1},{9,13},{13,9},{2,6},{6,2},{1... | collective-permute-start | bytes 786440 | tf_op jit(solution)/shard_map/ppermute | solution.py:710
  345.4 36.6 %collective-permute-start.17 = (bf16[2,8,64,128]{3,2,1,0:T(8,128)(2,1)}, bf16[2,8,64,128]{3,2,1,0:T(8,128)(2,1)S(1)}, u32[]{:S(2)}, u32[]{:S(2)}) collective-permute-start(bf16[2,8,64,128]{3,2,1,0:T(8,128)(2,1)} %get-tuple-element.196), channel_id=1, source_target_pairs={{0,8},{4,12},{8,0},{12,4},{1,9},{5,13},{9,1},{13,5},{2,10},{6,14},... | collective-permute-start | bytes 786440 | tf_op jit(solution)/shard_map/ppermute | solution.py:710
  347.8 34.2 %collective-permute-start.18 = (bf16[2,8,64,128]{3,2,1,0:T(8,128)(2,1)}, bf16[2,8,64,128]{3,2,1,0:T(8,128)(2,1)S(1)}, u32[]{:S(2)}, u32[]{:S(2)}) collective-permute-start(bf16[2,8,64,128]{3,2,1,0:T(8,128)(2,1)} %get-tuple-element.197), channel_id=1, source_target_pairs={{0,12},{4,8},{8,4},{12,0},{1,13},{5,9},{9,5},{13,1},{2,14},{6,10},... | collective-permute-start | bytes 786440 | tf_op jit(solution)/shard_map/ppermute | solution.py:710
  352.9 18.5 %collective-permute-start.20 = (bf16[128,256]{1,0:T(8,128)(2,1)S(1)}, bf16[128,256]{1,0:T(8,128)(2,1)S(1)}, u32[]{:S(2)}, u32[]{:S(2)}) collective-permute-start(bf16[128,256]{1,0:T(8,128)(2,1)S(1)} %get-tuple-element.244), channel_id=1, source_target_pairs={{0,2},{1,3},{2,0},{3,1},{4,6},{5,7},{6,4},{7,5},{8,10},{9,11},{10,... | collective-permute-start | bytes 196616 | tf_op jit(solution)/shard_map/ppermute | solution.py:710
  358.6 18.6 %collective-permute-start.21 = (bf16[128,256]{1,0:T(8,128)(2,1)S(1)}, bf16[128,256]{1,0:T(8,128)(2,1)S(1)}, u32[]{:S(2)}, u32[]{:S(2)}) collective-permute-start(bf16[128,256]{1,0:T(8,128)(2,1)S(1)} %get-tuple-element.243), channel_id=1, source_target_pairs={{0,3},{1,2},{2,1},{3,0},{4,7},{5,6},{6,5},{7,4},{8,11},{9,10},{10,... | collective-permute-start | bytes 196616 | tf_op jit(solution)/shard_map/ppermute | solution.py:710
  387.0 27.9 %all-to-all-start.8 = ((bf16[32,64,128]{2,1,0:T(8,128)(2,1)}), bf16[32,64,128]{2,1,0:T(8,128)(2,1)S(1)}, u32[]{:S(2)}, u32[]{:S(2)}) async-start(bf16[32,64,128]{2,1,0:T(8,128)(2,1)} %bitcast.58), calls=%async_computation.8 | async-start | bytes 1048576 | tf_op jit(solution)/shard_map/all_to_all | solution.py:688
  421.0 32.1 %all-to-all-start.9 = ((bf16[128,8,896]{2,1,0:T(8,128)(2,1)}), bf16[128,8,896]{2,1,0:T(8,128)(2,1)S(1)}, u32[]{:S(2)}, u32[]{:S(2)}) async-start(bf16[128,8,896]{2,1,0:T(8,128)(2,1)} %bitcast.59), calls=%async_computation.9 | async-start | bytes 3670016 | tf_op jit(solution)/shard_map/all_to_all | solution.py:688
  432.2 24.7 %collective-permute-start.22 = (bf16[128,1024]{1,0:T(8,128)(2,1)}, bf16[128,1024]{1,0:T(8,128)(2,1)S(1)}, u32[]{:S(2)}, u32[]{:S(2)}) collective-permute-start(bf16[128,1024]{1,0:T(8,128)(2,1)} %get-tuple-element.222), channel_id=1, source_target_pairs={{0,1},{1,0},{2,3},{3,2},{4,5},{5,4},{6,7},{7,6},{8,9},{9,8},{10,11... | collective-permute-start | bytes 786440 | tf_op jit(solution)/shard_map/ppermute | solution.py:710
  433.2 23.6 %collective-permute-start.23 = (bf16[128,1024]{1,0:T(8,128)(2,1)}, bf16[128,1024]{1,0:T(8,128)(2,1)S(1)}, u32[]{:S(2)}, u32[]{:S(2)}) collective-permute-start(bf16[128,1024]{1,0:T(8,128)(2,1)} %get-tuple-element.223), channel_id=1, source_target_pairs={{0,2},{1,3},{2,0},{3,1},{4,6},{5,7},{6,4},{7,5},{8,10},{9,11},{10,... | collective-permute-start | bytes 786440 | tf_op jit(solution)/shard_map/ppermute | solution.py:710
  434.0 25.7 %collective-permute-start.24 = (bf16[128,1024]{1,0:T(8,128)(2,1)}, bf16[128,1024]{1,0:T(8,128)(2,1)S(1)}, u32[]{:S(2)}, u32[]{:S(2)}) collective-permute-start(bf16[128,1024]{1,0:T(8,128)(2,1)} %get-tuple-element.224), channel_id=1, source_target_pairs={{0,3},{1,2},{2,1},{3,0},{4,7},{5,6},{6,5},{7,4},{8,11},{9,10},{10,... | collective-permute-start | bytes 786440 | tf_op jit(solution)/shard_map/ppermute | solution.py:710
  (41 other events, 504.6 us)
Sparse Core Ops, SparseCore 0:
  84.2 74.4 all-gather.1
  261.6 61.9 reduce-scatter.1

commit v7 on v6

--- a/solution.py
+++ b/solution.py
@@ -442,17 +442,26 @@
 
 
 def kernel_experts(h_ref, gu_ref, dact_ref, act_ref, dboth_ref, dxs_ref):
-    both = mm(h_ref[...].reshape(512, WIDTH), gu_ref[...])
-    gate_h, up_h = both[:, :512], both[:, 512:]
-    sig = jax.nn.sigmoid(gate_h)
-    swished = gate_h * sig
-    act_ref[...] = (swished * up_h).astype(BF)
-    dact = dact_ref[...]
-    dgate = (dact * up_h * sig * (1.0 + gate_h * (1.0 - sig))).astype(BF)
-    dup = (dact * swished).astype(BF)
-    dboth = jnp.concatenate([dgate, dup], axis=1)
-    dboth_ref[...] = dboth
-    dxs_ref[...] = mm(dboth, gu_ref[...], NT).astype(BF).reshape(8, 64, WIDTH)
+    def project(part):
+        return mm(h_ref[4 * part : 4 * part + 4].reshape(256, WIDTH), gu_ref[...])
+
+    later = project(0)
+    for part in range(2):
+        both = later
+        if part == 0:
+            later = project(1)
+        at = slice(256 * part, 256 * part + 256)
+        gate_h, up_h = both[:, :512], both[:, 512:]
+        sig = 0.5 * jnp.tanh(0.5 * gate_h) + 0.5
+        swished = gate_h * sig
+        act_ref[at, :] = (swished * up_h).astype(BF)
+        dact = dact_ref[at, :]
+        dgate = (dact * up_h * (sig + swished * (1.0 - sig))).astype(BF)
+        dup = (dact * swished).astype(BF)
+        dboth = jnp.concatenate([dgate, dup], axis=1)
+        dboth_ref[at, :] = dboth
+        dxs = mm(dboth, gu_ref[...], NT).astype(BF)
+        dxs_ref[4 * part : 4 * part + 4] = dxs.reshape(4, 64, WIDTH)
 
 
 def kernel_experts_after(
@@ -560,15 +569,32 @@
         grad_ref[pl.ds(pl.multiple_of(128 * g, 128), 128), 128:384] = part.astype(BF)
 
 
+def unrotate(w, cos, sin):
+    partner = jnp.where(lane(w.shape) % 64 < 32, pltpu.roll(w, 96, 1), pltpu.roll(w, 32, 1))
+    return (w * cos - partner * sin).astype(BF)
+
+
+def kernel_queries_back(
+    dq_ref, cos_ref, sin_ref, table_ref, hidden_ref, msg_ref, hidden_turned_ref
+):
+    for s in range(4):
+        at = slice(128 * s, 128 * s + 128)
+        hidden_turned_ref[:, at] = jnp.transpose(hidden_ref[at, :].astype(F32)).astype(BF)
+    parts = []
+    for half in range(2):
+        at = slice(512 * half, 512 * half + 512)
+        for head in range(2):
+            dq = dq_ref[half, :, head].reshape(512, 128)
+            parts.append(unrotate(dq, cos_ref[at, :], sin_ref[at, :]))
+    whole = jnp.concatenate(parts, axis=1)
+    for f in range(4):
+        rows = mm(whole, table_ref[f, :, 256:768], NT)
+        msg_ref[:, f] = rows.astype(BF).reshape(8, 64, 128)
+
+
 def kernel_slices_back(
-    d0_ref, d1_ref, d2_ref, d3_ref, dq_ref, cos_ref, sin_ref, table_ref, msg_ref
+    d0_ref, d1_ref, d2_ref, d3_ref, queries_ref, cos_ref, sin_ref, table_ref, msg_ref
 ):
-    def unrotate(w, cos, sin):
-        partner = jnp.where(
-            lane(w.shape) % 64 < 32, pltpu.roll(w, 96, 1), pltpu.roll(w, 32, 1)
-        )
-        return (w * cos - partner * sin).astype(BF)
-
     parts = []
     for half in range(2):
         at = slice(512 * half, 512 * half + 512)
@@ -576,15 +602,10 @@
         for d_ref in (d1_ref, d2_ref, d3_ref):
             dkv = dkv + d_ref[half].reshape(512, 128).astype(F32)
         parts.append(unrotate(dkv, cos_ref[at, :], sin_ref[at, :]))
-    for half in range(2):
-        at = slice(512 * half, 512 * half + 512)
-        for head in range(2):
-            parts.append(
-                unrotate(dq_ref[half, :, head].reshape(512, 128), cos_ref[at, :], sin_ref[at, :])
-            )
     whole = jnp.concatenate(parts, axis=1)
     for f in range(4):
-        msg_ref[:, f] = mm(whole, table_ref[f], NT).astype(BF).reshape(8, 64, 128)
+        rows = mm(whole, table_ref[f, :, 0:256], NT) + queries_ref[:, f].reshape(512, 128)
+        msg_ref[:, f] = rows.astype(BF).reshape(8, 64, 128)
 
 
 def kernel_hidden_grad(part_ref, d_ref, w_ref, h0_ref, h1_ref, h2_ref, h3_ref):
@@ -604,7 +625,7 @@
             d_ref[128 * s + 64 : 128 * s + 128, 128 * p : 128 * p + 128] = jnp.where(
                 low, pltpu.roll(even, 64, 1), odd
             ).astype(BF)
-    total = mm(hidden_ref[...], d_ref[...], TN)
+    total = mm(hidden_ref[...], d_ref[...])
     grads_ref[:, 0:512] = total.astype(BF)
     gain = jnp.sum(total * w_ref[:, 0:512].astype(F32), axis=1, keepdims=True)
     gain = gain / w_ref[:, 512:640].astype(F32)[:, 0:1]
@@ -871,7 +892,6 @@
     )(part_ref, o_heads, *w_out, x, gains, picks)
     cot_all = after(cot_all, mid)
     slots, experts_all = lax.optimization_barrier((slots, experts_all))
-    o_all = neighbours(after(o_heads, mid))
     slots = exchange(slots, CTX)
     dys, dact, down, gate_up = call(
         kernel_experts_ready,
@@ -924,13 +944,12 @@
         out_specs=(slot_spec, whole((4, 384, WIDTH))),
         scratch_shapes=[pltpu.VMEM((WIDTH, WIDTH), F32), pltpu.VMEM((512, WIDTH), F32)],
     )(slots, act, dys, dboth, down)
-    dxs, o_all = lax.optimization_barrier((dxs, o_all))
-    o_all = o_all + (swap(o_all[2], "core"),)
+    o_all = neighbours(after(o_heads, dxs))
     dxs = exchange(dxs, CTX)
     expert_own = lax.psum_scatter(
         expert_grads.reshape(4 * 384, WIDTH), FSDP, scatter_dimension=0, tiled=True
     ).astype(F32)
-    dxs, ys, o_all = lax.optimization_barrier((dxs, ys, o_all))
+    dxs, ys = lax.optimization_barrier((dxs, ys))
 
     dmid, da_parts, grad_msg, gain_ffn_part = call(
         kernel_middle_back,
@@ -960,7 +979,8 @@
         scratch_shapes=[pltpu.VMEM((128, WIDTH), F32), pltpu.VMEM((128, WIDTH), BF)],
     )(part_ref, dxs, picks_turned, mid, cot, gains, *w_out)
     grad_heads = exchange(grad_msg, HEAD_AXES)
-    ys, grad_heads = lax.optimization_barrier((ys, grad_heads))
+    ys, grad_heads, o_all = lax.optimization_barrier((ys, grad_heads, o_all))
+    o_all = o_all + (swap(o_all[2], "core"),)
     ys = exchange(ys, CTX)
     dq, *dkv = call(
         kernel_attend_back,
@@ -981,7 +1001,14 @@
     )(mine_ref, keys, turned, queries, grad_heads, log_total, o_rows)
     da_here = cross(da_parts)
     dkv = cross(dkv, ("y",))
-    dkv, ys, da_here = lax.optimization_barrier((dkv, ys, da_here))
+    queries_back, hidden_turned = call(
+        kernel_queries_back,
+        (sds((8, 4, 64, 128), BF), sds((WIDTH, 512), BF)),
+        (3e8, 4e6),
+        in_specs=[VM] * 5,
+        out_specs=(VM, VM),
+    )(dq.reshape(2, 8, 2, 64, 128), cos_heads, sin_heads, head_table, hidden)
+    dkv, ys, da_here, queries_back = lax.optimization_barrier((dkv, ys, da_here, queries_back))
     rest_part = call(
         kernel_out_weight,
         sds((WIDTH, 384), BF),
@@ -1007,10 +1034,10 @@
     back = call(
         kernel_slices_back,
         sds((8, 4, 64, 128), BF),
-        (4e8, 5e6),
+        (2e8, 3e6),
         in_specs=[VM] * 8,
         out_specs=VM,
-    )(*dkv, dq.reshape(2, 8, 2, 64, 128), cos_heads, sin_heads, head_table)
+    )(*dkv, queries_back, cos_heads, sin_heads, head_table)
     back = exchange(back.reshape(32, 64, 128), HEAD_AXES + FSDP)
 
     grads, d_all = call(
@@ -1019,7 +1046,7 @@
         (6e8, 5e6),
         in_specs=[VM] * 4,
         out_specs=(VM, VM),
-    )(back, hidden, w_slice, rest_part)
+    )(back, hidden_turned, w_slice, rest_part)
     dh_parts = call(
         kernel_hidden_grad,
         (sds((128, WIDTH), BF),) * 4,

time: 472 us -> 468 us (level)
  blocking collectives: 14.5 us -> 0 us
  starting transfers between devices: 96.9 us -> 102 us
    all_to_all x1 -> x0, blocking collectives: 14.5 us -> none  [exchange(): return lax.all_to_all(value, axes, split_axis=0, concat_axis=0, tiled=True)]
    ppermute x16, starting transfers between devices: 14 us -> 20.1 us  [swap(): return lax.ppermute(value, axis, [(0, 1), (1, 0)])]
    all_to_all x9 -> x10, waiting for transfers between devices: 147 us -> 143 us  [exchange(): return lax.all_to_all(value, axes, split_axis=0, concat_axis=0, tiled=True)]
    unnamed x76 -> x78, local copies, waits for them, and re-layouts: 8.82 us -> 11.2 us
    all_to_all x9 -> x10, starting transfers between devices: 65.2 us -> 66.7 us  [exchange(): return lax.all_to_all(value, axes, split_axis=0, concat_axis=0, tiled=True)]
  transfers between devices with their start and end apart: 36 -> 37, of which waited for: 14 -> 16; matrix products, arithmetic and copies ran while one was open for 4% -> 4% of each run, Pallas kernels for 30% -> 28%
where the time goes in v7:
time: 468 us; the launch traced here: 467 us
  waiting for transfers between devices  175 us (37%)
  Pallas kernels  147 us (31%)
  starting transfers between devices  102 us (22%)
  local copies, waits for them, and re-layouts  19.3 us (4%)
  between operations  14.6 us (3%)
  other arithmetic  8.98 us (2%)
    all_to_all x10, waiting for transfers between devices, exchange(): return lax.all_to_all(value, axes, split_axis=0, concat_axis=0, tiled=True)  143 us
    all_to_all x10, starting transfers between devices, exchange(): return lax.all_to_all(value, axes, split_axis=0, concat_axis=0, tiled=True)  66.7 us
    ppermute x9, waiting for transfers between devices, cross(): here.append(lax.ppermute(parts[r], axes, [(i, i ^ r) for i in range(4)]))  26 us
    pallas_call x1, Pallas kernels, on_device(): call(kernel_experts_after, (sds((32, 64, WIDTH), BF), sds((4, 384, WIDTH)...  23.6 us
    pallas_call x1, Pallas kernels, on_device(): call(kernel_attend_back, (sds((2048, 128), F32),) + (sds((2, 8, 64, 128),...  22.9 us
    ppermute x16, starting transfers between devices, swap(): return lax.ppermute(value, axis, [(0, 1), (1, 0)])  20.1 us
    pallas_call x1, Pallas kernels, on_device(): call(kernel_attend, (sds((8, 2, 64, 128), BF), sds((8, 8, 256), F32), sds...  17.1 us
    ppermute x9, starting transfers between devices, cross(): here.append(lax.ppermute(parts[r], axes, [(i, i ^ r) for i in range(4)]))  14.9 us
  transfers between devices with their start and end apart: 37, of which 16 were waited for; matrix products, arithmetic and copies ran while one was open for 4% of the time, Pallas kernels for 28%

profile of v7, /device:TPU:1, one launch (start us, length us, event | category | flops | bytes accessed | tf_op | source)
XLA Modules:
  0.0 466.7 jit_solution(3847442982676003030)
XLA Ops:
  19.6 9.7 %all-to-all-start = ((bf16[128,8,896]{2,1,0:T(8,128)(2,1)}), bf16[128,8,896]{2,1,0:T(8,128)(2,1)S(1)}, u32[]{:S(2)}, u32[]{:S(2)}) async-start(bf16[128,8,896]{2,1,0:T(8,128)(2,1)} %bitcast.55), calls=%async_computation | async-start | bytes 3670016 | tf_op jit(solution)/shard_map/all_to_all | solution.py:709
  32.4 24.0 %all-to-all-done = bf16[128,8,896]{2,1,0:T(8,128)(2,1)S(1)} async-done(((bf16[128,8,896]{2,1,0:T(8,128)(2,1)}), bf16[128,8,896]{2,1,0:T(8,128)(2,1)S(1)}, u32[]{:S(2)}, u32[]{:S(2)}) %all-to-all-start) | async-done | bytes 1835040 | tf_op jit(solution)/shard_map/all_to_all | solution.py:709
  57.7 4.6 shard_map.198
  62.3 6.0 %all-to-all-start.1 = ((bf16[32,64,128]{2,1,0:T(8,128)(2,1)}), bf16[32,64,128]{2,1,0:T(8,128)(2,1)S(1)}, u32[]{:S(2)}, u32[]{:S(2)}) async-start(bf16[32,64,128]{2,1,0:T(8,128)(2,1)} %get-tuple-element.129), calls=%async_computation.1 | async-start | bytes 1048576 | tf_op jit(solution)/shard_map/all_to_all | solution.py:709
  72.5 7.4 %all-to-all-done.1 = bf16[32,64,128]{2,1,0:T(8,128)(2,1)S(1)} async-done(((bf16[32,64,128]{2,1,0:T(8,128)(2,1)}), bf16[32,64,128]{2,1,0:T(8,128)(2,1)S(1)}, u32[]{:S(2)}, u32[]{:S(2)}) %all-to-all-start.1) | async-done | bytes 524320 | tf_op jit(solution)/shard_map/all_to_all | solution.py:709
  96.6 13.6 %all-to-all-done.2 = bf16[4,1024,128]{2,1,0:T(8,128)(2,1)S(1)} async-done(((bf16[4,1024,128]{2,1,0:T(8,128)(2,1)}), bf16[4,1024,128]{2,1,0:T(8,128)(2,1)S(1)}, u32[]{:S(2)}, u32[]{:S(2)}) %all-to-all-start.2) | async-done | bytes 1048608 | tf_op jit(solution)/shard_map/all_to_all | solution.py:709
  111.7 17.1 %shard_map.200 = (bf16[8,2,64,128]{3,2,1,0:T(8,128)(2,1)}, f32[8,8,256]{2,1,0:T(8,128)}, f32[2048,128]{1,0:T(8,128)}, bf16[4096,128]{1,0:T(8,128)(2,1)}, bf16[128,4096]{1,0:T(8,128)(2,1)}) custom-call(s32[1]{0:T(128)} %bitcast.mine_ref, bf16[4,2,8,64,128]{4,3,2,1,0:T(8,128)(2,1)} %bitcast.65, bf16[2048,128]{1,0:T(8,128)(2,1)} %bitcast.75), custom_call_target="tpu_custom_call" | custom-call | flops 10000000000 | bytes 5000000 | tf_op jit(solution)/shard_map/pallas_call | solution.py:853
  136.8 6.2 %all-to-all-done.3.o_ref.o0_ref = bf16[8,2,64,128]{3,2,1,0:T(8,128)(2,1)S(1)} async-done(((bf16[8,2,64,128]{3,2,1,0:T(8,128)(2,1)}), bf16[8,2,64,128]{3,2,1,0:T(8,128)(2,1)S(1)}, u32[]{:S(2)}, u32[]{:S(2)}) %all-to-all-start.3) | async-done | bytes 262176 | tf_op jit(solution)/shard_map/all_to_all | solution.py:709
  143.6 5.2 %shard_map.202 = (bf16[32,64,1024]{2,1,0:T(8,128)(2,1)}, f32[128,1024]{1,0:T(8,128)}) custom-call(s32[1]{0:T(128)} %bitcast.1.part_ref, bf16[8,2,64,128]{3,2,1,0:T(8,128)(2,1)} %copy-done.7, bf16[512,256]{1,0:T(8,128)(2,1)} %copy-done.6, bf16[512,256]{1,0:T(8,128)(2,1)} %copy-done.15, bf16[512,256]{1,0:T(8,128)(2,1)} %copy-done.14, ...), custom_call_target="tpu_custom_call" | custom-call | flops 900000000 | bytes 8000000 | tf_op jit(solution)/shard_map/pallas_call | solution.py:878
  149.8 5.6 %all-to-all-start.4 = ((bf16[32,64,1024]{2,1,0:T(8,128)(2,1)}), bf16[32,64,1024]{2,1,0:T(8,128)(2,1)}, u32[]{:S(2)}, u32[]{:S(2)}) async-start(bf16[32,64,1024]{2,1,0:T(8,128)(2,1)} %get-tuple-element.163), calls=%async_computation.4 | async-start | bytes 8388608 | tf_op jit(solution)/shard_map/all_to_all | solution.py:709
  158.7 12.5 %shard_map.203 = (bf16[32,64,1024]{2,1,0:T(8,128)(2,1)}, f32[2048,512]{1,0:T(8,128)}, bf16[512,1024]{1,0:T(8,128)(2,1)}, bf16[1024,1024]{1,0:T(8,128)(2,1)}) custom-call(s32[1]{0:T(128)} %bitcast.1.part_ref, bf16[4,4,2,128,1024]{4,3,2,1,0:T(8,128)(2,1)} %bitcast.74, bf16[32,8,128]{2,1,0:T(8,128)(2,1)} %dynamic-slice_bitcast_fusion.parts_ref, ...), custom_call_target="tpu_custom_call" | custom-call | flops 6000000000 | bytes 20000000 | tf_op jit(solution)/shard_map/pallas_call | solution.py:896
  171.3 41.6 %all-to-all-done.4.h_ref = bf16[32,64,1024]{2,1,0:T(8,128)(2,1)} async-done(((bf16[32,64,1024]{2,1,0:T(8,128)(2,1)}), bf16[32,64,1024]{2,1,0:T(8,128)(2,1)}, u32[]{:S(2)}, u32[]{:S(2)}) %all-to-all-start.4) | async-done | bytes 4194336 | tf_op jit(solution)/shard_map/all_to_all | solution.py:709
  212.9 13.2 %shard_map.204 = (bf16[2048,512]{1,0:T(8,128)(2,1)}, bf16[2048,1024]{1,0:T(8,128)(2,1)}, bf16[32,64,1024]{2,1,0:T(8,128)(2,1)}) custom-call(bf16[32,64,1024]{2,1,0:T(8,128)(2,1)} %all-to-all-done.4.h_ref, bf16[1024,1024]{1,0:T(8,128)(2,1)} %get-tuple-element.172.gu_ref, f32[2048,512]{1,0:T(8,128)} %get-tuple-element.173.dact_ref), custom_call_target="tpu_custom_call" | custom-call | flops 8999999488 | bytes 20000000 | tf_op jit(solution)/shard_map/pallas_call | solution.py:922
  226.1 9.1 %all-to-all-start.5 = ((bf16[32,64,1024]{2,1,0:T(8,128)(2,1)}), bf16[32,64,1024]{2,1,0:T(8,128)(2,1)}, u32[]{:S(2)}, u32[]{:S(2)}) async-start(bf16[32,64,1024]{2,1,0:T(8,128)(2,1)} %get-tuple-element.174), calls=%async_computation.5 | async-start | bytes 8388608 | tf_op jit(solution)/shard_map/all_to_all | solution.py:709
  235.3 23.6 %shard_map.205 = (bf16[32,64,1024]{2,1,0:T(8,128)(2,1)}, bf16[4,384,1024]{2,1,0:T(8,128)(2,1)}) custom-call(bf16[32,64,1024]{2,1,0:T(8,128)(2,1)} %all-to-all-done.4.h_ref, bf16[2048,512]{1,0:T(8,128)(2,1)} %get-tuple-element.175.act_ref, bf16[32,64,1024]{2,1,0:T(8,128)(2,1)} %get-tuple-element.176.dys_ref, bf16[2048,1024]{1,0:T(8,128)(2,1)} %get-tuple-element.177.dboth_ref, ...), custom_call_target="tpu_custom_call" | custom-call | flops 8999999488 | bytes 20000000 | tf_op jit(solution)/shard_map/pallas_call | solution.py:938
  259.8 6.4 %collective-permute-start.14 = (bf16[8,2,64,128]{3,2,1,0:T(8,128)(2,1)S(1)}, bf16[8,2,64,128]{3,2,1,0:T(8,128)(2,1)S(1)}, u32[]{:S(2)}, u32[]{:S(2)}) collective-permute-start(bf16[8,2,64,128]{3,2,1,0:T(8,128)(2,1)S(1)} %copy-done.8), channel_id=1, source_target_pairs={{0,2},{2,0},{1,3},{3,1},{4,6},{6,4},{5,7},{7,5},{8,10},{10,8},{9,1... | collective-permute-start | bytes 786440 | tf_op jit(solution)/shard_map/ppermute | solution.py:721
  267.7 25.8 %all-to-all-done.5.dxs_ref = bf16[32,64,1024]{2,1,0:T(8,128)(2,1)} async-done(((bf16[32,64,1024]{2,1,0:T(8,128)(2,1)}), bf16[32,64,1024]{2,1,0:T(8,128)(2,1)}, u32[]{:S(2)}, u32[]{:S(2)}) %all-to-all-start.5) | async-done | bytes 4194336 | tf_op jit(solution)/shard_map/all_to_all | solution.py:709
  293.5 5.7 %shard_map.206 = (f32[128,1024]{1,0:T(8,128)}, bf16[4,128,256]{2,1,0:T(8,128)(2,1)}, bf16[8,2,64,128]{3,2,1,0:T(8,128)(2,1)}, f32[8,1024]{1,0:T(8,128)}) custom-call(s32[1]{0:T(128)} %bitcast.1.part_ref, bf16[32,64,1024]{2,1,0:T(8,128)(2,1)} %all-to-all-done.5.dxs_ref, bf16[128,2048]{1,0:T(8,128)(2,1)} %get-tuple-element.182.pick_ref, ...), custom_call_target="tpu_custom_call" | custom-call | flops 900000000 | bytes 8000000 | tf_op jit(solution)/shard_map/pallas_call | solution.py:954
  299.2 6.8 %all-to-all-start.6 = ((bf16[8,2,64,128]{3,2,1,0:T(8,128)(2,1)}), bf16[8,2,64,128]{3,2,1,0:T(8,128)(2,1)S(1)}, u32[]{:S(2)}, u32[]{:S(2)}) async-start(bf16[8,2,64,128]{3,2,1,0:T(8,128)(2,1)} %get-tuple-element.183), calls=%async_computation.6 | async-start | bytes 524288 | tf_op jit(solution)/shard_map/all_to_all | solution.py:709
  306.1 7.3 %all-to-all-done.6.grad_ref = bf16[8,2,64,128]{3,2,1,0:T(8,128)(2,1)S(1)} async-done(((bf16[8,2,64,128]{3,2,1,0:T(8,128)(2,1)}), bf16[8,2,64,128]{3,2,1,0:T(8,128)(2,1)S(1)}, u32[]{:S(2)}, u32[]{:S(2)}) %all-to-all-start.6) | async-done | bytes 262176 | tf_op jit(solution)/shard_map/all_to_all | solution.py:709
  314.0 7.6 %all-to-all-start.7 = ((bf16[32,64,1024]{2,1,0:T(8,128)(2,1)}), bf16[32,64,1024]{2,1,0:T(8,128)(2,1)}, u32[]{:S(2)}, u32[]{:S(2)}) async-start(bf16[32,64,1024]{2,1,0:T(8,128)(2,1)} %get-tuple-element.192), calls=%async_computation.7 | async-start | bytes 8388608 | tf_op jit(solution)/shard_map/all_to_all | solution.py:709
  321.7 22.9 %shard_map.207 = (f32[2048,128]{1,0:T(8,128)}, bf16[2,8,64,128]{3,2,1,0:T(8,128)(2,1)}, bf16[2,8,64,128]{3,2,1,0:T(8,128)(2,1)}, bf16[2,8,64,128]{3,2,1,0:T(8,128)(2,1)}, bf16[2,8,64,128]{3,2,1,0:T(8,128)(2,1)}) custom-call(s32[1]{0:T(128)} %bitcast.mine_ref, bf16[4096,128]{1,0:T(8,128)(2,1)} %get-tuple-element.135.keys_ref, ...), custom_call_target="tpu_custom_call" | custom-call | flops 20000000000 | bytes 7000000 | tf_op jit(solution)/shard_map/pallas_call | solution.py:985
  349.2 8.0 %collective-permute-start.20 = (bf16[128,256]{1,0:T(8,128)(2,1)S(1)}, bf16[128,256]{1,0:T(8,128)(2,1)S(1)}, u32[]{:S(2)}, u32[]{:S(2)}) collective-permute-start(bf16[128,256]{1,0:T(8,128)(2,1)S(1)} %get-tuple-element.239), channel_id=1, source_target_pairs={{0,3},{1,2},{2,1},{3,0},{4,7},{5,6},{6,5},{7,4},{8,11},{9,10},{10,... | collective-permute-start | bytes 196616 | tf_op jit(solution)/shard_map/ppermute | solution.py:731
  357.2 12.5 %collective-permute-done.20.da3_ref = bf16[128,256]{1,0:T(8,128)(2,1)S(1)} collective-permute-done((bf16[128,256]{1,0:T(8,128)(2,1)S(1)}, bf16[128,256]{1,0:T(8,128)(2,1)S(1)}, u32[]{:S(2)}, u32[]{:S(2)}) %collective-permute-start.20) | collective-permute-done | bytes 65568 | tf_op jit(solution)/shard_map/ppermute | solution.py:731
  374.7 11.8 %collective-permute-done.16.d2_ref = bf16[2,8,64,128]{3,2,1,0:T(8,128)(2,1)S(1)} collective-permute-done((bf16[2,8,64,128]{3,2,1,0:T(8,128)(2,1)}, bf16[2,8,64,128]{3,2,1,0:T(8,128)(2,1)S(1)}, u32[]{:S(2)}, u32[]{:S(2)}) %collective-permute-start.16) | collective-permute-done | bytes 262176 | tf_op jit(solution)/shard_map/ppermute | solution.py:731
  390.6 10.3 %all-to-all-start.8 = ((bf16[32,64,128]{2,1,0:T(8,128)(2,1)}), bf16[32,64,128]{2,1,0:T(8,128)(2,1)S(1)}, u32[]{:S(2)}, u32[]{:S(2)}) async-start(bf16[32,64,128]{2,1,0:T(8,128)(2,1)} %bitcast.58), calls=%async_computation.8 | async-start | bytes 1048576 | tf_op jit(solution)/shard_map/all_to_all | solution.py:709
  403.2 4.4 shard_map.211.rest_ref
  407.6 4.9 %all-to-all-done.8.msg_ref = bf16[32,64,128]{2,1,0:T(8,128)(2,1)S(1)} async-done(((bf16[32,64,128]{2,1,0:T(8,128)(2,1)}), bf16[32,64,128]{2,1,0:T(8,128)(2,1)S(1)}, u32[]{:S(2)}, u32[]{:S(2)}) %all-to-all-start.8) | async-done | bytes 524320 | tf_op jit(solution)/shard_map/all_to_all | solution.py:709
  413.3 5.0 %shard_map.212 = (bf16[1024,896]{1,0:T(8,128)(2,1)}, bf16[512,512]{1,0:T(8,128)(2,1)}) custom-call(bf16[32,64,128]{2,1,0:T(8,128)(2,1)} %copy-done.2, bf16[1024,512]{1,0:T(8,128)(2,1)} %get-tuple-element.207.hidden_ref, bf16[1024,896]{1,0:T(8,128)(2,1)} %bitcast.53, bf16[1024,384]{1,0:T(8,128)(2,1)} %shard_map.211.rest_ref), custom_call_target="tpu_custom_call" | custom-call | flops 600000000 | bytes 5000000 | tf_op jit(solution)/shard_map/pallas_call | solution.py:1043
  418.3 4.5 all-to-all-start.9
  432.6 5.0 %shard_map.209 = bf16[128,1024]{1,0:T(8,128)(2,1)} custom-call(bf16[32,64,1024]{2,1,0:T(8,128)(2,1)} %all-to-all-done.7.ys_ref, bf16[128,2048]{1,0:T(8,128)(2,1)} %get-tuple-element.200.high_ref, bf16[128,2048]{1,0:T(8,128)(2,1)} %get-tuple-element.201.rest_ref, f32[128,1024]{1,0:T(8,128)} %get-tuple-element.166.mid_ref), custom_call_target="tpu_custom_call" | custom-call | flops 1000000000 | bytes 5000000 | tf_op jit(solution)/shard_map/pallas_call | solution.py:1019
  437.7 12.3 %all-to-all-done.9 = bf16[128,8,896]{2,1,0:T(8,128)(2,1)S(1)} async-done(((bf16[128,8,896]{2,1,0:T(8,128)(2,1)}), bf16[128,8,896]{2,1,0:T(8,128)(2,1)S(1)}, u32[]{:S(2)}, u32[]{:S(2)}) %all-to-all-start.9) | async-done | bytes 1835040 | tf_op jit(solution)/shard_map/all_to_all | solution.py:709
  (172 shorter events, 91.3 us)
Async XLA Ops:
  7.2 11.7 %collective-permute-start.1 = (bf16[128,1024]{1,0:T(8,128)(2,1)}, bf16[128,1024]{1,0:T(8,128)(2,1)S(1)}, u32[]{:S(2)}, u32[]{:S(2)}) collective-permute-start(bf16[128,1024]{1,0:T(8,128)(2,1)} %bitcast.60), channel_id=1, source_target_pairs={{0,2},{2,0},{1,3},{3,1},{4,6},{6,4},{5,7},{7,5},{8,10},{10,8},{9,1... | collective-permute-start | bytes 786440 | tf_op jit(solution)/shard_map/ppermute | solution.py:721
  19.6 36.8 %all-to-all-start = ((bf16[128,8,896]{2,1,0:T(8,128)(2,1)}), bf16[128,8,896]{2,1,0:T(8,128)(2,1)S(1)}, u32[]{:S(2)}, u32[]{:S(2)}) async-start(bf16[128,8,896]{2,1,0:T(8,128)(2,1)} %bitcast.55), calls=%async_computation | async-start | bytes 3670016 | tf_op jit(solution)/shard_map/all_to_all | solution.py:709
  29.3 27.6 %collective-permute-start.2 = (bf16[128,1024]{1,0:T(8,128)(2,1)S(1)}, bf16[128,1024]{1,0:T(8,128)(2,1)S(1)}, u32[]{:S(2)}, u32[]{:S(2)}) collective-permute-start(bf16[128,1024]{1,0:T(8,128)(2,1)S(1)} %collective-permute-done.1.x2_ref), channel_id=1, source_target_pairs={{0,1},{1,0},{2,3},{3,2},{4,5},{5,4},{6,7},{7,6},{8,9},{9,8},{10,11... | collective-permute-start | bytes 786440 | tf_op jit(solution)/shard_map/ppermute | solution.py:721
  56.4 15.2 %collective-permute-start.12 = (bf16[128,1024]{1,0:T(8,128)(2,1)S(1)}, bf16[128,1024]{1,0:T(8,128)(2,1)S(1)}, u32[]{:S(2)}, u32[]{:S(2)}) collective-permute-start(bf16[128,1024]{1,0:T(8,128)(2,1)S(1)} %bitcast.67), channel_id=1, source_target_pairs={{0,16},{16,0},{1,17},{17,1},{2,18},{18,2},{3,19},{19,3},{4,20},{20... | collective-permute-start | bytes 786440 | tf_op jit(solution)/shard_map/ppermute | solution.py:721
  62.3 17.7 %all-to-all-start.1 = ((bf16[32,64,128]{2,1,0:T(8,128)(2,1)}), bf16[32,64,128]{2,1,0:T(8,128)(2,1)S(1)}, u32[]{:S(2)}, u32[]{:S(2)}) async-start(bf16[32,64,128]{2,1,0:T(8,128)(2,1)} %get-tuple-element.129), calls=%async_computation.1 | async-start | bytes 1048576 | tf_op jit(solution)/shard_map/all_to_all | solution.py:709
  68.4 90.4 %all-gather.2.cloned.1.call-start = ((), (), s32[]{:S(2)}) async-start(), calls=%async_computation.11 | async-start | bytes 8912896 | tf_op jit(solution)/shard_map/all_gather | solution.py:713
  69.5 14.5 %collective-permute-start.4 = (bf16[512,256]{1,0:T(8,128)(2,1)S(1)}, bf16[512,256]{1,0:T(8,128)(2,1)S(1)}, u32[]{:S(2)}, u32[]{:S(2)}) collective-permute-start(bf16[512,256]{1,0:T(8,128)(2,1)S(1)} %get-tuple-element.147.u0_ref), channel_id=1, source_target_pairs={{0,2},{2,0},{1,3},{3,1},{4,6},{6,4},{5,7},{7,5},{8,10},{10,8},{9,1... | collective-permute-start | bytes 786440 | tf_op jit(solution)/shard_map/ppermute | solution.py:721
  71.0 13.1 %collective-permute-start.3 = (bf16[512,256]{1,0:T(8,128)(2,1)S(1)}, bf16[512,256]{1,0:T(8,128)(2,1)S(1)}, u32[]{:S(2)}, u32[]{:S(2)}) collective-permute-start(bf16[512,256]{1,0:T(8,128)(2,1)S(1)} %get-tuple-element.147.u0_ref), channel_id=1, source_target_pairs={{0,1},{1,0},{2,3},{3,2},{4,5},{5,4},{6,7},{7,6},{8,9},{9,8},{10,11... | collective-permute-start | bytes 786440 | tf_op jit(solution)/shard_map/ppermute | solution.py:721
  84.5 25.7 %all-to-all-start.2 = ((bf16[4,1024,128]{2,1,0:T(8,128)(2,1)}), bf16[4,1024,128]{2,1,0:T(8,128)(2,1)S(1)}, u32[]{:S(2)}, u32[]{:S(2)}) async-start(bf16[4,1024,128]{2,1,0:T(8,128)(2,1)} %get-tuple-element.131), calls=%async_computation.2 | async-start | bytes 2097152 | tf_op jit(solution)/shard_map/all_to_all | solution.py:709
  92.2 36.7 %collective-permute-start.10 = (bf16[384,1024]{1,0:T(8,128)(2,1)S(1)}, bf16[384,1024]{1,0:T(8,128)(2,1)}, u32[]{:S(2)}, u32[]{:S(2)}) collective-permute-start(bf16[384,1024]{1,0:T(8,128)(2,1)S(1)} %pad_maximum_fusion.w0_ref), channel_id=1, source_target_pairs={{0,2},{2,0},{1,3},{3,1},{4,6},{6,4},{5,7},{7,5},{8,10},{10,8},{9,1... | collective-permute-start | bytes 2359304 | tf_op jit(solution)/shard_map/ppermute | solution.py:721
  93.2 35.7 %collective-permute-start.9 = (bf16[384,1024]{1,0:T(8,128)(2,1)S(1)}, bf16[384,1024]{1,0:T(8,128)(2,1)}, u32[]{:S(2)}, u32[]{:S(2)}) collective-permute-start(bf16[384,1024]{1,0:T(8,128)(2,1)S(1)} %pad_maximum_fusion.w0_ref), channel_id=1, source_target_pairs={{0,1},{1,0},{2,3},{3,2},{4,5},{5,4},{6,7},{7,6},{8,9},{9,8},{10,11... | collective-permute-start | bytes 2359304 | tf_op jit(solution)/shard_map/ppermute | solution.py:721
  110.2 18.7 %collective-permute-start.7 = (bf16[512,256]{1,0:T(8,128)(2,1)S(1)}, bf16[512,256]{1,0:T(8,128)(2,1)S(1)}, u32[]{:S(2)}, u32[]{:S(2)}) collective-permute-start(bf16[512,256]{1,0:T(8,128)(2,1)S(1)} %collective-permute-done.4.u2_ref), channel_id=1, source_target_pairs={{0,1},{1,0},{2,3},{3,2},{4,5},{5,4},{6,7},{7,6},{8,9},{9,8},{10,11... | collective-permute-start | bytes 786440 | tf_op jit(solution)/shard_map/ppermute | solution.py:721
  111.4 17.4 %collective-permute-start.8 = (bf16[512,256]{1,0:T(8,128)(2,1)S(1)}, bf16[512,256]{1,0:T(8,128)(2,1)S(1)}, u32[]{:S(2)}, u32[]{:S(2)}) collective-permute-start(bf16[512,256]{1,0:T(8,128)(2,1)S(1)} %collective-permute-done.6.l2_ref), channel_id=1, source_target_pairs={{0,1},{1,0},{2,3},{3,2},{4,5},{5,4},{6,7},{7,6},{8,9},{9,8},{10,11... | collective-permute-start | bytes 786440 | tf_op jit(solution)/shard_map/ppermute | solution.py:721
  128.9 20.0 %collective-permute-start.11 = (bf16[384,1024]{1,0:T(8,128)(2,1)}, bf16[384,1024]{1,0:T(8,128)(2,1)S(1)}, u32[]{:S(2)}, u32[]{:S(2)}) collective-permute-start(bf16[384,1024]{1,0:T(8,128)(2,1)} %collective-permute-done.10.w2_ref), channel_id=1, source_target_pairs={{0,1},{1,0},{2,3},{3,2},{4,5},{5,4},{6,7},{7,6},{8,9},{9,8},{10,11... | collective-permute-start | bytes 2359304 | tf_op jit(solution)/shard_map/ppermute | solution.py:721
  129.7 13.2 %all-to-all-start.3 = ((bf16[8,2,64,128]{3,2,1,0:T(8,128)(2,1)}), bf16[8,2,64,128]{3,2,1,0:T(8,128)(2,1)S(1)}, u32[]{:S(2)}, u32[]{:S(2)}) async-start(bf16[8,2,64,128]{3,2,1,0:T(8,128)(2,1)} %get-tuple-element.146), calls=%async_computation.3 | async-start | bytes 524288 | tf_op jit(solution)/shard_map/all_to_all | solution.py:709
  149.8 63.1 %all-to-all-start.4 = ((bf16[32,64,1024]{2,1,0:T(8,128)(2,1)}), bf16[32,64,1024]{2,1,0:T(8,128)(2,1)}, u32[]{:S(2)}, u32[]{:S(2)}) async-start(bf16[32,64,1024]{2,1,0:T(8,128)(2,1)} %get-tuple-element.163), calls=%async_computation.4 | async-start | bytes 8388608 | tf_op jit(solution)/shard_map/all_to_all | solution.py:709
  226.1 67.4 %all-to-all-start.5 = ((bf16[32,64,1024]{2,1,0:T(8,128)(2,1)}), bf16[32,64,1024]{2,1,0:T(8,128)(2,1)}, u32[]{:S(2)}, u32[]{:S(2)}) async-start(bf16[32,64,1024]{2,1,0:T(8,128)(2,1)} %get-tuple-element.174), calls=%async_computation.5 | async-start | bytes 8388608 | tf_op jit(solution)/shard_map/all_to_all | solution.py:709
  235.2 187.6 %reduce-scatter.2.cloned.1.call-start = ((), (), s32[]{:S(2)}) async-start(), calls=%async_computation.12 | async-start | bytes 3932160 | tf_op jit(solution)/shard_map/reduce_scatter | solution.py:949
  259.8 46.2 %collective-permute-start.14 = (bf16[8,2,64,128]{3,2,1,0:T(8,128)(2,1)S(1)}, bf16[8,2,64,128]{3,2,1,0:T(8,128)(2,1)S(1)}, u32[]{:S(2)}, u32[]{:S(2)}) collective-permute-start(bf16[8,2,64,128]{3,2,1,0:T(8,128)(2,1)S(1)} %copy-done.8), channel_id=1, source_target_pairs={{0,2},{2,0},{1,3},{3,1},{4,6},{6,4},{5,7},{7,5},{8,10},{10,8},{9,1... | collective-permute-start | bytes 786440 | tf_op jit(solution)/shard_map/ppermute | solution.py:721
  266.2 39.9 %collective-permute-start.13 = (bf16[8,2,64,128]{3,2,1,0:T(8,128)(2,1)S(1)}, bf16[8,2,64,128]{3,2,1,0:T(8,128)(2,1)S(1)}, u32[]{:S(2)}, u32[]{:S(2)}) collective-permute-start(bf16[8,2,64,128]{3,2,1,0:T(8,128)(2,1)S(1)} %copy-done.8), channel_id=1, source_target_pairs={{0,1},{1,0},{2,3},{3,2},{4,5},{5,4},{6,7},{7,6},{8,9},{9,8},{10,11... | collective-permute-start | bytes 786440 | tf_op jit(solution)/shard_map/ppermute | solution.py:721
  299.2 14.1 %all-to-all-start.6 = ((bf16[8,2,64,128]{3,2,1,0:T(8,128)(2,1)}), bf16[8,2,64,128]{3,2,1,0:T(8,128)(2,1)S(1)}, u32[]{:S(2)}, u32[]{:S(2)}) async-start(bf16[8,2,64,128]{3,2,1,0:T(8,128)(2,1)} %get-tuple-element.183), calls=%async_computation.6 | async-start | bytes 524288 | tf_op jit(solution)/shard_map/all_to_all | solution.py:709
  314.0 72.4 %all-to-all-start.7 = ((bf16[32,64,1024]{2,1,0:T(8,128)(2,1)}), bf16[32,64,1024]{2,1,0:T(8,128)(2,1)}, u32[]{:S(2)}, u32[]{:S(2)}) async-start(bf16[32,64,1024]{2,1,0:T(8,128)(2,1)} %get-tuple-element.192), calls=%async_computation.7 | async-start | bytes 8388608 | tf_op jit(solution)/shard_map/all_to_all | solution.py:709
  344.6 30.0 %collective-permute-start.15 = (bf16[2,8,64,128]{3,2,1,0:T(8,128)(2,1)}, bf16[2,8,64,128]{3,2,1,0:T(8,128)(2,1)S(1)}, u32[]{:S(2)}, u32[]{:S(2)}) collective-permute-start(bf16[2,8,64,128]{3,2,1,0:T(8,128)(2,1)} %get-tuple-element.189), channel_id=1, source_target_pairs={{0,4},{4,0},{8,12},{12,8},{1,5},{5,1},{9,13},{13,9},{2,6},{6,2},{1... | collective-permute-start | bytes 786440 | tf_op jit(solution)/shard_map/ppermute | solution.py:731
  345.8 40.6 %collective-permute-start.16 = (bf16[2,8,64,128]{3,2,1,0:T(8,128)(2,1)}, bf16[2,8,64,128]{3,2,1,0:T(8,128)(2,1)S(1)}, u32[]{:S(2)}, u32[]{:S(2)}) collective-permute-start(bf16[2,8,64,128]{3,2,1,0:T(8,128)(2,1)} %get-tuple-element.190), channel_id=1, source_target_pairs={{0,8},{4,12},{8,0},{12,4},{1,9},{5,13},{9,1},{13,5},{2,10},{6,14},... | collective-permute-start | bytes 786440 | tf_op jit(solution)/shard_map/ppermute | solution.py:731
  348.3 38.2 %collective-permute-start.17 = (bf16[2,8,64,128]{3,2,1,0:T(8,128)(2,1)}, bf16[2,8,64,128]{3,2,1,0:T(8,128)(2,1)S(1)}, u32[]{:S(2)}, u32[]{:S(2)}) collective-permute-start(bf16[2,8,64,128]{3,2,1,0:T(8,128)(2,1)} %get-tuple-element.191), channel_id=1, source_target_pairs={{0,12},{4,8},{8,4},{12,0},{1,13},{5,9},{9,5},{13,1},{2,14},{6,10},... | collective-permute-start | bytes 786440 | tf_op jit(solution)/shard_map/ppermute | solution.py:731
  349.2 20.5 %collective-permute-start.20 = (bf16[128,256]{1,0:T(8,128)(2,1)S(1)}, bf16[128,256]{1,0:T(8,128)(2,1)S(1)}, u32[]{:S(2)}, u32[]{:S(2)}) collective-permute-start(bf16[128,256]{1,0:T(8,128)(2,1)S(1)} %get-tuple-element.239), channel_id=1, source_target_pairs={{0,3},{1,2},{2,1},{3,0},{4,7},{5,6},{6,5},{7,4},{8,11},{9,10},{10,... | collective-permute-start | bytes 196616 | tf_op jit(solution)/shard_map/ppermute | solution.py:731
  357.2 17.1 %collective-permute-start.19 = (bf16[128,256]{1,0:T(8,128)(2,1)S(1)}, bf16[128,256]{1,0:T(8,128)(2,1)S(1)}, u32[]{:S(2)}, u32[]{:S(2)}) collective-permute-start(bf16[128,256]{1,0:T(8,128)(2,1)S(1)} %get-tuple-element.240), channel_id=1, source_target_pairs={{0,2},{1,3},{2,0},{3,1},{4,6},{5,7},{6,4},{7,5},{8,10},{9,11},{10,... | collective-permute-start | bytes 196616 | tf_op jit(solution)/shard_map/ppermute | solution.py:731
  390.6 21.9 %all-to-all-start.8 = ((bf16[32,64,128]{2,1,0:T(8,128)(2,1)}), bf16[32,64,128]{2,1,0:T(8,128)(2,1)S(1)}, u32[]{:S(2)}, u32[]{:S(2)}) async-start(bf16[32,64,128]{2,1,0:T(8,128)(2,1)} %bitcast.58), calls=%async_computation.8 | async-start | bytes 1048576 | tf_op jit(solution)/shard_map/all_to_all | solution.py:709
  418.3 31.6 %all-to-all-start.9 = ((bf16[128,8,896]{2,1,0:T(8,128)(2,1)}), bf16[128,8,896]{2,1,0:T(8,128)(2,1)S(1)}, u32[]{:S(2)}, u32[]{:S(2)}) async-start(bf16[128,8,896]{2,1,0:T(8,128)(2,1)} %bitcast.59), calls=%async_computation.9 | async-start | bytes 3670016 | tf_op jit(solution)/shard_map/all_to_all | solution.py:709
  429.1 26.2 %collective-permute-start.22 = (bf16[128,1024]{1,0:T(8,128)(2,1)}, bf16[128,1024]{1,0:T(8,128)(2,1)S(1)}, u32[]{:S(2)}, u32[]{:S(2)}) collective-permute-start(bf16[128,1024]{1,0:T(8,128)(2,1)} %get-tuple-element.218), channel_id=1, source_target_pairs={{0,1},{1,0},{2,3},{3,2},{4,5},{5,4},{6,7},{7,6},{8,9},{9,8},{10,11... | collective-permute-start | bytes 786440 | tf_op jit(solution)/shard_map/ppermute | solution.py:731
  430.1 25.1 %collective-permute-start.23 = (bf16[128,1024]{1,0:T(8,128)(2,1)}, bf16[128,1024]{1,0:T(8,128)(2,1)S(1)}, u32[]{:S(2)}, u32[]{:S(2)}) collective-permute-start(bf16[128,1024]{1,0:T(8,128)(2,1)} %get-tuple-element.219), channel_id=1, source_target_pairs={{0,2},{1,3},{2,0},{3,1},{4,6},{5,7},{6,4},{7,5},{8,10},{9,11},{10,... | collective-permute-start | bytes 786440 | tf_op jit(solution)/shard_map/ppermute | solution.py:731
  430.9 25.7 %collective-permute-start.24 = (bf16[128,1024]{1,0:T(8,128)(2,1)}, bf16[128,1024]{1,0:T(8,128)(2,1)S(1)}, u32[]{:S(2)}, u32[]{:S(2)}) collective-permute-start(bf16[128,1024]{1,0:T(8,128)(2,1)} %get-tuple-element.220), channel_id=1, source_target_pairs={{0,3},{1,2},{2,1},{3,0},{4,7},{5,6},{6,5},{7,4},{8,11},{9,10},{10,... | collective-permute-start | bytes 786440 | tf_op jit(solution)/shard_map/ppermute | solution.py:731
  (43 other events, 505.4 us)
Sparse Core Ops, SparseCore 0:
  84.2 74.4 all-gather.1
  259.0 68.0 reduce-scatter.1

commit v8 on v7

--- a/solution.py
+++ b/solution.py
@@ -613,7 +613,7 @@
         h_ref[...] = mm(d_ref[place(part_ref, r, 128), :], w_ref[:, 0:512], NT).astype(BF)
 
 
-def kernel_grads(msg_ref, hidden_ref, w_ref, rest_ref, grads_ref, d_ref):
+def kernel_grads(msg_ref, hidden_ref, rest_ref, grads_ref, d_ref):
     low = lane((64, 128)) < 64
     for s in range(4):
         for p in range(4):
@@ -627,11 +627,7 @@
             ).astype(BF)
     total = mm(hidden_ref[...], d_ref[...])
     grads_ref[:, 0:512] = total.astype(BF)
-    gain = jnp.sum(total * w_ref[:, 0:512].astype(F32), axis=1, keepdims=True)
-    gain = gain / w_ref[:, 512:640].astype(F32)[:, 0:1]
-    rest = rest_ref[:, 0:128]
-    grads_ref[:, 512:640] = jnp.where(lane((WIDTH, 128)) == 0, gain.astype(BF), rest)
-    grads_ref[:, 640:896] = rest_ref[:, 128:384]
+    grads_ref[:, 512:896] = rest_ref[...]
 
 
 def kernel_input_grad(d0_ref, d1_ref, d2_ref, d3_ref, x_ref, dmid_ref, gains_ref, out_ref):
@@ -648,7 +644,7 @@
     )
 
 
-def kernel_total(parts_ref, table_ref, qkv_ref, out_ref, gains_ref, sum_ref):
+def kernel_total(parts_ref, table_ref, w_ref, rows_ref, qkv_ref, out_ref, gains_ref, sum_ref):
     total = parts_ref[0].astype(F32)
     for c in range(1, 32):
         total = total + parts_ref[c].astype(F32)
@@ -673,12 +669,16 @@
         qkv_ref[:, 1536 + 128 * p : 1664 + 128 * p] = piece[:, 384:512]
     for f in range(4):
         out_ref[:, 256 * f : 256 * f + 256] = sum_ref[f, :, 640:896]
-    gains_ref[...] = (
+    gains = (
         sum_ref[0, :, 512:640]
         + sum_ref[1, :, 512:640]
         + sum_ref[2, :, 512:640]
         + sum_ref[3, :, 512:640]
     )
+    w = w_ref[...].astype(BF).astype(F32)
+    first = jnp.sum(w * qkv_ref[...], axis=1, keepdims=True)
+    first = first / rows_ref[:, 0:1].astype(BF).astype(F32)
+    gains_ref[...] = jnp.where(lane((8, 128)) == 0, first, gains)
 
 
 def kernel_output(ys_ref, high_ref, rest_ref, mid_ref, out_ref, sum_ref):
@@ -1044,9 +1044,9 @@
         kernel_grads,
         (sds((WIDTH, 896), BF), sds((512, 512), BF)),
         (6e8, 5e6),
-        in_specs=[VM] * 4,
+        in_specs=[VM] * 3,
         out_specs=(VM, VM),
-    )(back, hidden_turned, w_slice, rest_part)
+    )(back, hidden_turned, rest_part)
     dh_parts = call(
         kernel_hidden_grad,
         (sds((128, WIDTH), BF),) * 4,
@@ -1059,10 +1059,10 @@
         kernel_total,
         (sds((8, 2048), F32), sds((8, WIDTH), F32), sds((8, 128), F32)),
         (1e8, 4e6),
-        in_specs=[VM, VM],
+        in_specs=[VM] * 4,
         out_specs=(VM, VM, VM),
         scratch_shapes=[pltpu.VMEM((4, 8, 896), F32)],
-    )(grads.reshape(32, 4, 8, 896), slice_table)
+    )(grads.reshape(32, 4, 8, 896), slice_table, query_key_value_weight, gain_rows)
     dh_here = cross(dh_parts)
     input_grad = call(
         kernel_input_grad,

time: 468 us -> 467 us (level)
  transfers between devices with their start and end apart: 37 -> 37, of which waited for: 16 -> 15; matrix products, arithmetic and copies ran while one was open for 4% -> 4% of each run, Pallas kernels for 28% -> 28%
where the time goes in v8:
time: 467 us; the launch traced here: 465 us
  waiting for transfers between devices  176 us (38%)
  Pallas kernels  146 us (31%)
  starting transfers between devices  101 us (22%)
  local copies, waits for them, and re-layouts  19.3 us (4%)
  between operations  14.6 us (3%)
  other arithmetic  8.98 us (2%)
    all_to_all x10, waiting for transfers between devices, exchange(): return lax.all_to_all(value, axes, split_axis=0, concat_axis=0, tiled=True)  143 us
    all_to_all x10, starting transfers between devices, exchange(): return lax.all_to_all(value, axes, split_axis=0, concat_axis=0, tiled=True)  66.2 us
    ppermute x9, waiting for transfers between devices, cross(): here.append(lax.ppermute(parts[r], axes, [(i, i ^ r) for i in range(4)]))  26.7 us
    pallas_call x1, Pallas kernels, on_device(): call(kernel_experts_after, (sds((32, 64, WIDTH), BF), sds((4, 384, WIDTH)...  23.6 us
    pallas_call x1, Pallas kernels, on_device(): call(kernel_attend_back, (sds((2048, 128), F32),) + (sds((2, 8, 64, 128),...  23 us
    ppermute x16, starting transfers between devices, swap(): return lax.ppermute(value, axis, [(0, 1), (1, 0)])  20 us
    pallas_call x1, Pallas kernels, on_device(): call(kernel_attend, (sds((8, 2, 64, 128), BF), sds((8, 8, 256), F32), sds...  17.1 us
    ppermute x9, starting transfers between devices, cross(): here.append(lax.ppermute(parts[r], axes, [(i, i ^ r) for i in range(4)]))  14.4 us
  transfers between devices with their start and end apart: 37, of which 15 were waited for; matrix products, arithmetic and copies ran while one was open for 4% of the time, Pallas kernels for 28%

profile of v8, /device:TPU:1, one launch (start us, length us, event | category | flops | bytes accessed | tf_op | source)
XLA Modules:
  0.0 465.5 jit_solution(928346350325274092)
XLA Ops:
  19.6 9.7 %all-to-all-start = ((bf16[128,8,896]{2,1,0:T(8,128)(2,1)}), bf16[128,8,896]{2,1,0:T(8,128)(2,1)S(1)}, u32[]{:S(2)}, u32[]{:S(2)}) async-start(bf16[128,8,896]{2,1,0:T(8,128)(2,1)} %bitcast.54), calls=%async_computation | async-start | bytes 3670016 | tf_op jit(solution)/shard_map/all_to_all | solution.py:709
  32.4 24.0 %all-to-all-done = bf16[128,8,896]{2,1,0:T(8,128)(2,1)S(1)} async-done(((bf16[128,8,896]{2,1,0:T(8,128)(2,1)}), bf16[128,8,896]{2,1,0:T(8,128)(2,1)S(1)}, u32[]{:S(2)}, u32[]{:S(2)}) %all-to-all-start) | async-done | bytes 1835040 | tf_op jit(solution)/shard_map/all_to_all | solution.py:709
  57.7 4.6 shard_map.198
  62.3 6.0 %all-to-all-start.1 = ((bf16[32,64,128]{2,1,0:T(8,128)(2,1)}), bf16[32,64,128]{2,1,0:T(8,128)(2,1)S(1)}, u32[]{:S(2)}, u32[]{:S(2)}) async-start(bf16[32,64,128]{2,1,0:T(8,128)(2,1)} %get-tuple-element.129), calls=%async_computation.1 | async-start | bytes 1048576 | tf_op jit(solution)/shard_map/all_to_all | solution.py:709
  72.5 7.4 %all-to-all-done.1 = bf16[32,64,128]{2,1,0:T(8,128)(2,1)S(1)} async-done(((bf16[32,64,128]{2,1,0:T(8,128)(2,1)}), bf16[32,64,128]{2,1,0:T(8,128)(2,1)S(1)}, u32[]{:S(2)}, u32[]{:S(2)}) %all-to-all-start.1) | async-done | bytes 524320 | tf_op jit(solution)/shard_map/all_to_all | solution.py:709
  96.6 13.6 %all-to-all-done.2 = bf16[4,1024,128]{2,1,0:T(8,128)(2,1)S(1)} async-done(((bf16[4,1024,128]{2,1,0:T(8,128)(2,1)}), bf16[4,1024,128]{2,1,0:T(8,128)(2,1)S(1)}, u32[]{:S(2)}, u32[]{:S(2)}) %all-to-all-start.2) | async-done | bytes 1048608 | tf_op jit(solution)/shard_map/all_to_all | solution.py:709
  111.7 17.1 %shard_map.200 = (bf16[8,2,64,128]{3,2,1,0:T(8,128)(2,1)}, f32[8,8,256]{2,1,0:T(8,128)}, f32[2048,128]{1,0:T(8,128)}, bf16[4096,128]{1,0:T(8,128)(2,1)}, bf16[128,4096]{1,0:T(8,128)(2,1)}) custom-call(s32[1]{0:T(128)} %bitcast.mine_ref, bf16[4,2,8,64,128]{4,3,2,1,0:T(8,128)(2,1)} %bitcast.64, bf16[2048,128]{1,0:T(8,128)(2,1)} %bitcast.74), custom_call_target="tpu_custom_call" | custom-call | flops 10000000000 | bytes 5000000 | tf_op jit(solution)/shard_map/pallas_call | solution.py:853
  136.7 6.2 %all-to-all-done.3.o_ref.o0_ref = bf16[8,2,64,128]{3,2,1,0:T(8,128)(2,1)S(1)} async-done(((bf16[8,2,64,128]{3,2,1,0:T(8,128)(2,1)}), bf16[8,2,64,128]{3,2,1,0:T(8,128)(2,1)S(1)}, u32[]{:S(2)}, u32[]{:S(2)}) %all-to-all-start.3) | async-done | bytes 262176 | tf_op jit(solution)/shard_map/all_to_all | solution.py:709
  143.6 5.2 %shard_map.202 = (bf16[32,64,1024]{2,1,0:T(8,128)(2,1)}, f32[128,1024]{1,0:T(8,128)}) custom-call(s32[1]{0:T(128)} %bitcast.1.part_ref, bf16[8,2,64,128]{3,2,1,0:T(8,128)(2,1)} %copy-done.7, bf16[512,256]{1,0:T(8,128)(2,1)} %copy-done.6, bf16[512,256]{1,0:T(8,128)(2,1)} %copy-done.15, bf16[512,256]{1,0:T(8,128)(2,1)} %copy-done.14, ...), custom_call_target="tpu_custom_call" | custom-call | flops 900000000 | bytes 8000000 | tf_op jit(solution)/shard_map/pallas_call | solution.py:878
  149.7 5.6 %all-to-all-start.4 = ((bf16[32,64,1024]{2,1,0:T(8,128)(2,1)}), bf16[32,64,1024]{2,1,0:T(8,128)(2,1)}, u32[]{:S(2)}, u32[]{:S(2)}) async-start(bf16[32,64,1024]{2,1,0:T(8,128)(2,1)} %get-tuple-element.163), calls=%async_computation.4 | async-start | bytes 8388608 | tf_op jit(solution)/shard_map/all_to_all | solution.py:709
  158.7 12.5 %shard_map.203 = (bf16[32,64,1024]{2,1,0:T(8,128)(2,1)}, f32[2048,512]{1,0:T(8,128)}, bf16[512,1024]{1,0:T(8,128)(2,1)}, bf16[1024,1024]{1,0:T(8,128)(2,1)}) custom-call(s32[1]{0:T(128)} %bitcast.1.part_ref, bf16[4,4,2,128,1024]{4,3,2,1,0:T(8,128)(2,1)} %bitcast.73, bf16[32,8,128]{2,1,0:T(8,128)(2,1)} %dynamic-slice_bitcast_fusion.parts_ref, ...), custom_call_target="tpu_custom_call" | custom-call | flops 6000000000 | bytes 20000000 | tf_op jit(solution)/shard_map/pallas_call | solution.py:896
  171.2 41.7 %all-to-all-done.4.h_ref = bf16[32,64,1024]{2,1,0:T(8,128)(2,1)} async-done(((bf16[32,64,1024]{2,1,0:T(8,128)(2,1)}), bf16[32,64,1024]{2,1,0:T(8,128)(2,1)}, u32[]{:S(2)}, u32[]{:S(2)}) %all-to-all-start.4) | async-done | bytes 4194336 | tf_op jit(solution)/shard_map/all_to_all | solution.py:709
  212.9 13.2 %shard_map.204 = (bf16[2048,512]{1,0:T(8,128)(2,1)}, bf16[2048,1024]{1,0:T(8,128)(2,1)}, bf16[32,64,1024]{2,1,0:T(8,128)(2,1)}) custom-call(bf16[32,64,1024]{2,1,0:T(8,128)(2,1)} %all-to-all-done.4.h_ref, bf16[1024,1024]{1,0:T(8,128)(2,1)} %get-tuple-element.172.gu_ref, f32[2048,512]{1,0:T(8,128)} %get-tuple-element.173.dact_ref), custom_call_target="tpu_custom_call" | custom-call | flops 8999999488 | bytes 20000000 | tf_op jit(solution)/shard_map/pallas_call | solution.py:922
  226.1 9.1 %all-to-all-start.5 = ((bf16[32,64,1024]{2,1,0:T(8,128)(2,1)}), bf16[32,64,1024]{2,1,0:T(8,128)(2,1)}, u32[]{:S(2)}, u32[]{:S(2)}) async-start(bf16[32,64,1024]{2,1,0:T(8,128)(2,1)} %get-tuple-element.174), calls=%async_computation.5 | async-start | bytes 8388608 | tf_op jit(solution)/shard_map/all_to_all | solution.py:709
  235.3 23.6 %shard_map.205 = (bf16[32,64,1024]{2,1,0:T(8,128)(2,1)}, bf16[4,384,1024]{2,1,0:T(8,128)(2,1)}) custom-call(bf16[32,64,1024]{2,1,0:T(8,128)(2,1)} %all-to-all-done.4.h_ref, bf16[2048,512]{1,0:T(8,128)(2,1)} %get-tuple-element.175.act_ref, bf16[32,64,1024]{2,1,0:T(8,128)(2,1)} %get-tuple-element.176.dys_ref, bf16[2048,1024]{1,0:T(8,128)(2,1)} %get-tuple-element.177.dboth_ref, ...), custom_call_target="tpu_custom_call" | custom-call | flops 8999999488 | bytes 20000000 | tf_op jit(solution)/shard_map/pallas_call | solution.py:938
  259.9 6.3 %collective-permute-start.14 = (bf16[8,2,64,128]{3,2,1,0:T(8,128)(2,1)S(1)}, bf16[8,2,64,128]{3,2,1,0:T(8,128)(2,1)S(1)}, u32[]{:S(2)}, u32[]{:S(2)}) collective-permute-start(bf16[8,2,64,128]{3,2,1,0:T(8,128)(2,1)S(1)} %copy-done.8), channel_id=1, source_target_pairs={{0,2},{2,0},{1,3},{3,1},{4,6},{6,4},{5,7},{7,5},{8,10},{10,8},{9,1... | collective-permute-start | bytes 786440 | tf_op jit(solution)/shard_map/ppermute | solution.py:721
  267.7 25.8 %all-to-all-done.5.dxs_ref = bf16[32,64,1024]{2,1,0:T(8,128)(2,1)} async-done(((bf16[32,64,1024]{2,1,0:T(8,128)(2,1)}), bf16[32,64,1024]{2,1,0:T(8,128)(2,1)}, u32[]{:S(2)}, u32[]{:S(2)}) %all-to-all-start.5) | async-done | bytes 4194336 | tf_op jit(solution)/shard_map/all_to_all | solution.py:709
  293.5 5.7 %shard_map.206 = (f32[128,1024]{1,0:T(8,128)}, bf16[4,128,256]{2,1,0:T(8,128)(2,1)}, bf16[8,2,64,128]{3,2,1,0:T(8,128)(2,1)}, f32[8,1024]{1,0:T(8,128)}) custom-call(s32[1]{0:T(128)} %bitcast.1.part_ref, bf16[32,64,1024]{2,1,0:T(8,128)(2,1)} %all-to-all-done.5.dxs_ref, bf16[128,2048]{1,0:T(8,128)(2,1)} %get-tuple-element.182.pick_ref, ...), custom_call_target="tpu_custom_call" | custom-call | flops 900000000 | bytes 8000000 | tf_op jit(solution)/shard_map/pallas_call | solution.py:954
  299.2 6.9 %all-to-all-start.6 = ((bf16[8,2,64,128]{3,2,1,0:T(8,128)(2,1)}), bf16[8,2,64,128]{3,2,1,0:T(8,128)(2,1)S(1)}, u32[]{:S(2)}, u32[]{:S(2)}) async-start(bf16[8,2,64,128]{3,2,1,0:T(8,128)(2,1)} %get-tuple-element.183), calls=%async_computation.6 | async-start | bytes 524288 | tf_op jit(solution)/shard_map/all_to_all | solution.py:709
  306.2 7.3 %all-to-all-done.6.grad_ref = bf16[8,2,64,128]{3,2,1,0:T(8,128)(2,1)S(1)} async-done(((bf16[8,2,64,128]{3,2,1,0:T(8,128)(2,1)}), bf16[8,2,64,128]{3,2,1,0:T(8,128)(2,1)S(1)}, u32[]{:S(2)}, u32[]{:S(2)}) %all-to-all-start.6) | async-done | bytes 262176 | tf_op jit(solution)/shard_map/all_to_all | solution.py:709
  314.1 7.7 %all-to-all-start.7 = ((bf16[32,64,1024]{2,1,0:T(8,128)(2,1)}), bf16[32,64,1024]{2,1,0:T(8,128)(2,1)}, u32[]{:S(2)}, u32[]{:S(2)}) async-start(bf16[32,64,1024]{2,1,0:T(8,128)(2,1)} %get-tuple-element.192), calls=%async_computation.7 | async-start | bytes 8388608 | tf_op jit(solution)/shard_map/all_to_all | solution.py:709
  321.9 23.0 %shard_map.207 = (f32[2048,128]{1,0:T(8,128)}, bf16[2,8,64,128]{3,2,1,0:T(8,128)(2,1)}, bf16[2,8,64,128]{3,2,1,0:T(8,128)(2,1)}, bf16[2,8,64,128]{3,2,1,0:T(8,128)(2,1)}, bf16[2,8,64,128]{3,2,1,0:T(8,128)(2,1)}) custom-call(s32[1]{0:T(128)} %bitcast.mine_ref, bf16[4096,128]{1,0:T(8,128)(2,1)} %get-tuple-element.135.keys_ref, ...), custom_call_target="tpu_custom_call" | custom-call | flops 20000000000 | bytes 7000000 | tf_op jit(solution)/shard_map/pallas_call | solution.py:985
  349.4 7.7 %collective-permute-start.20 = (bf16[128,256]{1,0:T(8,128)(2,1)S(1)}, bf16[128,256]{1,0:T(8,128)(2,1)S(1)}, u32[]{:S(2)}, u32[]{:S(2)}) collective-permute-start(bf16[128,256]{1,0:T(8,128)(2,1)S(1)} %get-tuple-element.239), channel_id=1, source_target_pairs={{0,3},{1,2},{2,1},{3,0},{4,7},{5,6},{6,5},{7,4},{8,11},{9,10},{10,... | collective-permute-start | bytes 196616 | tf_op jit(solution)/shard_map/ppermute | solution.py:731
  357.2 15.7 %collective-permute-done.20.da3_ref = bf16[128,256]{1,0:T(8,128)(2,1)S(1)} collective-permute-done((bf16[128,256]{1,0:T(8,128)(2,1)S(1)}, bf16[128,256]{1,0:T(8,128)(2,1)S(1)}, u32[]{:S(2)}, u32[]{:S(2)}) %collective-permute-start.20) | collective-permute-done | bytes 65568 | tf_op jit(solution)/shard_map/ppermute | solution.py:731
  372.9 4.3 shard_map.208
  377.2 9.9 %collective-permute-done.16.d2_ref = bf16[2,8,64,128]{3,2,1,0:T(8,128)(2,1)S(1)} collective-permute-done((bf16[2,8,64,128]{3,2,1,0:T(8,128)(2,1)}, bf16[2,8,64,128]{3,2,1,0:T(8,128)(2,1)S(1)}, u32[]{:S(2)}, u32[]{:S(2)}) %collective-permute-start.16) | collective-permute-done | bytes 262176 | tf_op jit(solution)/shard_map/ppermute | solution.py:731
  391.3 9.6 %all-to-all-start.8 = ((bf16[32,64,128]{2,1,0:T(8,128)(2,1)}), bf16[32,64,128]{2,1,0:T(8,128)(2,1)S(1)}, u32[]{:S(2)}, u32[]{:S(2)}) async-start(bf16[32,64,128]{2,1,0:T(8,128)(2,1)} %bitcast.57), calls=%async_computation.8 | async-start | bytes 1048576 | tf_op jit(solution)/shard_map/all_to_all | solution.py:709
  403.2 4.4 shard_map.211.rest_ref
  407.6 4.9 %all-to-all-done.8.msg_ref = bf16[32,64,128]{2,1,0:T(8,128)(2,1)S(1)} async-done(((bf16[32,64,128]{2,1,0:T(8,128)(2,1)}), bf16[32,64,128]{2,1,0:T(8,128)(2,1)S(1)}, u32[]{:S(2)}, u32[]{:S(2)}) %all-to-all-start.8) | async-done | bytes 524320 | tf_op jit(solution)/shard_map/all_to_all | solution.py:709
  417.1 4.5 all-to-all-start.9
  431.4 5.0 %shard_map.209 = bf16[128,1024]{1,0:T(8,128)(2,1)} custom-call(bf16[32,64,1024]{2,1,0:T(8,128)(2,1)} %all-to-all-done.7.ys_ref, bf16[128,2048]{1,0:T(8,128)(2,1)} %get-tuple-element.200.high_ref, bf16[128,2048]{1,0:T(8,128)(2,1)} %get-tuple-element.201.rest_ref, f32[128,1024]{1,0:T(8,128)} %get-tuple-element.166.mid_ref), custom_call_target="tpu_custom_call" | custom-call | flops 1000000000 | bytes 5000000 | tf_op jit(solution)/shard_map/pallas_call | solution.py:1019
  436.4 12.3 %all-to-all-done.9 = bf16[128,8,896]{2,1,0:T(8,128)(2,1)S(1)} async-done(((bf16[128,8,896]{2,1,0:T(8,128)(2,1)}), bf16[128,8,896]{2,1,0:T(8,128)(2,1)S(1)}, u32[]{:S(2)}, u32[]{:S(2)}) %all-to-all-start.9) | async-done | bytes 1835040 | tf_op jit(solution)/shard_map/all_to_all | solution.py:709
  (172 shorter events, 90.2 us)
Async XLA Ops:
  7.2 11.6 %collective-permute-start.1 = (bf16[128,1024]{1,0:T(8,128)(2,1)}, bf16[128,1024]{1,0:T(8,128)(2,1)S(1)}, u32[]{:S(2)}, u32[]{:S(2)}) collective-permute-start(bf16[128,1024]{1,0:T(8,128)(2,1)} %bitcast.59), channel_id=1, source_target_pairs={{0,2},{2,0},{1,3},{3,1},{4,6},{6,4},{5,7},{7,5},{8,10},{10,8},{9,1... | collective-permute-start | bytes 786440 | tf_op jit(solution)/shard_map/ppermute | solution.py:721
  19.6 36.8 %all-to-all-start = ((bf16[128,8,896]{2,1,0:T(8,128)(2,1)}), bf16[128,8,896]{2,1,0:T(8,128)(2,1)S(1)}, u32[]{:S(2)}, u32[]{:S(2)}) async-start(bf16[128,8,896]{2,1,0:T(8,128)(2,1)} %bitcast.54), calls=%async_computation | async-start | bytes 3670016 | tf_op jit(solution)/shard_map/all_to_all | solution.py:709
  29.3 27.6 %collective-permute-start.2 = (bf16[128,1024]{1,0:T(8,128)(2,1)S(1)}, bf16[128,1024]{1,0:T(8,128)(2,1)S(1)}, u32[]{:S(2)}, u32[]{:S(2)}) collective-permute-start(bf16[128,1024]{1,0:T(8,128)(2,1)S(1)} %collective-permute-done.1.x2_ref), channel_id=1, source_target_pairs={{0,1},{1,0},{2,3},{3,2},{4,5},{5,4},{6,7},{7,6},{8,9},{9,8},{10,11... | collective-permute-start | bytes 786440 | tf_op jit(solution)/shard_map/ppermute | solution.py:721
  56.4 15.2 %collective-permute-start.12 = (bf16[128,1024]{1,0:T(8,128)(2,1)S(1)}, bf16[128,1024]{1,0:T(8,128)(2,1)S(1)}, u32[]{:S(2)}, u32[]{:S(2)}) collective-permute-start(bf16[128,1024]{1,0:T(8,128)(2,1)S(1)} %bitcast.66), channel_id=1, source_target_pairs={{0,16},{16,0},{1,17},{17,1},{2,18},{18,2},{3,19},{19,3},{4,20},{20... | collective-permute-start | bytes 786440 | tf_op jit(solution)/shard_map/ppermute | solution.py:721
  62.3 17.7 %all-to-all-start.1 = ((bf16[32,64,128]{2,1,0:T(8,128)(2,1)}), bf16[32,64,128]{2,1,0:T(8,128)(2,1)S(1)}, u32[]{:S(2)}, u32[]{:S(2)}) async-start(bf16[32,64,128]{2,1,0:T(8,128)(2,1)} %get-tuple-element.129), calls=%async_computation.1 | async-start | bytes 1048576 | tf_op jit(solution)/shard_map/all_to_all | solution.py:709
  68.3 90.4 %all-gather.2.cloned.1.call-start = ((), (), s32[]{:S(2)}) async-start(), calls=%async_computation.11 | async-start | bytes 8912896 | tf_op jit(solution)/shard_map/all_gather | solution.py:713
  69.5 14.5 %collective-permute-start.4 = (bf16[512,256]{1,0:T(8,128)(2,1)S(1)}, bf16[512,256]{1,0:T(8,128)(2,1)S(1)}, u32[]{:S(2)}, u32[]{:S(2)}) collective-permute-start(bf16[512,256]{1,0:T(8,128)(2,1)S(1)} %get-tuple-element.147.u0_ref), channel_id=1, source_target_pairs={{0,2},{2,0},{1,3},{3,1},{4,6},{6,4},{5,7},{7,5},{8,10},{10,8},{9,1... | collective-permute-start | bytes 786440 | tf_op jit(solution)/shard_map/ppermute | solution.py:721
  71.0 13.1 %collective-permute-start.3 = (bf16[512,256]{1,0:T(8,128)(2,1)S(1)}, bf16[512,256]{1,0:T(8,128)(2,1)S(1)}, u32[]{:S(2)}, u32[]{:S(2)}) collective-permute-start(bf16[512,256]{1,0:T(8,128)(2,1)S(1)} %get-tuple-element.147.u0_ref), channel_id=1, source_target_pairs={{0,1},{1,0},{2,3},{3,2},{4,5},{5,4},{6,7},{7,6},{8,9},{9,8},{10,11... | collective-permute-start | bytes 786440 | tf_op jit(solution)/shard_map/ppermute | solution.py:721
  84.5 25.7 %all-to-all-start.2 = ((bf16[4,1024,128]{2,1,0:T(8,128)(2,1)}), bf16[4,1024,128]{2,1,0:T(8,128)(2,1)S(1)}, u32[]{:S(2)}, u32[]{:S(2)}) async-start(bf16[4,1024,128]{2,1,0:T(8,128)(2,1)} %get-tuple-element.131), calls=%async_computation.2 | async-start | bytes 2097152 | tf_op jit(solution)/shard_map/all_to_all | solution.py:709
  92.1 36.7 %collective-permute-start.10 = (bf16[384,1024]{1,0:T(8,128)(2,1)S(1)}, bf16[384,1024]{1,0:T(8,128)(2,1)}, u32[]{:S(2)}, u32[]{:S(2)}) collective-permute-start(bf16[384,1024]{1,0:T(8,128)(2,1)S(1)} %pad_maximum_fusion.w0_ref), channel_id=1, source_target_pairs={{0,2},{2,0},{1,3},{3,1},{4,6},{6,4},{5,7},{7,5},{8,10},{10,8},{9,1... | collective-permute-start | bytes 2359304 | tf_op jit(solution)/shard_map/ppermute | solution.py:721
  93.2 35.6 %collective-permute-start.9 = (bf16[384,1024]{1,0:T(8,128)(2,1)S(1)}, bf16[384,1024]{1,0:T(8,128)(2,1)}, u32[]{:S(2)}, u32[]{:S(2)}) collective-permute-start(bf16[384,1024]{1,0:T(8,128)(2,1)S(1)} %pad_maximum_fusion.w0_ref), channel_id=1, source_target_pairs={{0,1},{1,0},{2,3},{3,2},{4,5},{5,4},{6,7},{7,6},{8,9},{9,8},{10,11... | collective-permute-start | bytes 2359304 | tf_op jit(solution)/shard_map/ppermute | solution.py:721
  110.2 18.7 %collective-permute-start.7 = (bf16[512,256]{1,0:T(8,128)(2,1)S(1)}, bf16[512,256]{1,0:T(8,128)(2,1)S(1)}, u32[]{:S(2)}, u32[]{:S(2)}) collective-permute-start(bf16[512,256]{1,0:T(8,128)(2,1)S(1)} %collective-permute-done.4.u2_ref), channel_id=1, source_target_pairs={{0,1},{1,0},{2,3},{3,2},{4,5},{5,4},{6,7},{7,6},{8,9},{9,8},{10,11... | collective-permute-start | bytes 786440 | tf_op jit(solution)/shard_map/ppermute | solution.py:721
  111.4 17.4 %collective-permute-start.8 = (bf16[512,256]{1,0:T(8,128)(2,1)S(1)}, bf16[512,256]{1,0:T(8,128)(2,1)S(1)}, u32[]{:S(2)}, u32[]{:S(2)}) collective-permute-start(bf16[512,256]{1,0:T(8,128)(2,1)S(1)} %collective-permute-done.6.l2_ref), channel_id=1, source_target_pairs={{0,1},{1,0},{2,3},{3,2},{4,5},{5,4},{6,7},{7,6},{8,9},{9,8},{10,11... | collective-permute-start | bytes 786440 | tf_op jit(solution)/shard_map/ppermute | solution.py:721
  128.9 20.0 %collective-permute-start.11 = (bf16[384,1024]{1,0:T(8,128)(2,1)}, bf16[384,1024]{1,0:T(8,128)(2,1)S(1)}, u32[]{:S(2)}, u32[]{:S(2)}) collective-permute-start(bf16[384,1024]{1,0:T(8,128)(2,1)} %collective-permute-done.10.w2_ref), channel_id=1, source_target_pairs={{0,1},{1,0},{2,3},{3,2},{4,5},{5,4},{6,7},{7,6},{8,9},{9,8},{10,11... | collective-permute-start | bytes 2359304 | tf_op jit(solution)/shard_map/ppermute | solution.py:721
  129.7 13.2 %all-to-all-start.3 = ((bf16[8,2,64,128]{3,2,1,0:T(8,128)(2,1)}), bf16[8,2,64,128]{3,2,1,0:T(8,128)(2,1)S(1)}, u32[]{:S(2)}, u32[]{:S(2)}) async-start(bf16[8,2,64,128]{3,2,1,0:T(8,128)(2,1)} %get-tuple-element.146), calls=%async_computation.3 | async-start | bytes 524288 | tf_op jit(solution)/shard_map/all_to_all | solution.py:709
  149.7 63.2 %all-to-all-start.4 = ((bf16[32,64,1024]{2,1,0:T(8,128)(2,1)}), bf16[32,64,1024]{2,1,0:T(8,128)(2,1)}, u32[]{:S(2)}, u32[]{:S(2)}) async-start(bf16[32,64,1024]{2,1,0:T(8,128)(2,1)} %get-tuple-element.163), calls=%async_computation.4 | async-start | bytes 8388608 | tf_op jit(solution)/shard_map/all_to_all | solution.py:709
  226.1 67.4 %all-to-all-start.5 = ((bf16[32,64,1024]{2,1,0:T(8,128)(2,1)}), bf16[32,64,1024]{2,1,0:T(8,128)(2,1)}, u32[]{:S(2)}, u32[]{:S(2)}) async-start(bf16[32,64,1024]{2,1,0:T(8,128)(2,1)} %get-tuple-element.174), calls=%async_computation.5 | async-start | bytes 8388608 | tf_op jit(solution)/shard_map/all_to_all | solution.py:709
  235.2 186.4 %reduce-scatter.2.cloned.1.call-start = ((), (), s32[]{:S(2)}) async-start(), calls=%async_computation.12 | async-start | bytes 3932160 | tf_op jit(solution)/shard_map/reduce_scatter | solution.py:949
  259.9 46.3 %collective-permute-start.14 = (bf16[8,2,64,128]{3,2,1,0:T(8,128)(2,1)S(1)}, bf16[8,2,64,128]{3,2,1,0:T(8,128)(2,1)S(1)}, u32[]{:S(2)}, u32[]{:S(2)}) collective-permute-start(bf16[8,2,64,128]{3,2,1,0:T(8,128)(2,1)S(1)} %copy-done.8), channel_id=1, source_target_pairs={{0,2},{2,0},{1,3},{3,1},{4,6},{6,4},{5,7},{7,5},{8,10},{10,8},{9,1... | collective-permute-start | bytes 786440 | tf_op jit(solution)/shard_map/ppermute | solution.py:721
  266.2 39.9 %collective-permute-start.13 = (bf16[8,2,64,128]{3,2,1,0:T(8,128)(2,1)S(1)}, bf16[8,2,64,128]{3,2,1,0:T(8,128)(2,1)S(1)}, u32[]{:S(2)}, u32[]{:S(2)}) collective-permute-start(bf16[8,2,64,128]{3,2,1,0:T(8,128)(2,1)S(1)} %copy-done.8), channel_id=1, source_target_pairs={{0,1},{1,0},{2,3},{3,2},{4,5},{5,4},{6,7},{7,6},{8,9},{9,8},{10,11... | collective-permute-start | bytes 786440 | tf_op jit(solution)/shard_map/ppermute | solution.py:721
  299.2 14.2 %all-to-all-start.6 = ((bf16[8,2,64,128]{3,2,1,0:T(8,128)(2,1)}), bf16[8,2,64,128]{3,2,1,0:T(8,128)(2,1)S(1)}, u32[]{:S(2)}, u32[]{:S(2)}) async-start(bf16[8,2,64,128]{3,2,1,0:T(8,128)(2,1)} %get-tuple-element.183), calls=%async_computation.6 | async-start | bytes 524288 | tf_op jit(solution)/shard_map/all_to_all | solution.py:709
  314.1 73.0 %all-to-all-start.7 = ((bf16[32,64,1024]{2,1,0:T(8,128)(2,1)}), bf16[32,64,1024]{2,1,0:T(8,128)(2,1)}, u32[]{:S(2)}, u32[]{:S(2)}) async-start(bf16[32,64,1024]{2,1,0:T(8,128)(2,1)} %get-tuple-element.192), calls=%async_computation.7 | async-start | bytes 8388608 | tf_op jit(solution)/shard_map/all_to_all | solution.py:709
  344.8 32.3 %collective-permute-start.15 = (bf16[2,8,64,128]{3,2,1,0:T(8,128)(2,1)}, bf16[2,8,64,128]{3,2,1,0:T(8,128)(2,1)S(1)}, u32[]{:S(2)}, u32[]{:S(2)}) collective-permute-start(bf16[2,8,64,128]{3,2,1,0:T(8,128)(2,1)} %get-tuple-element.189), channel_id=1, source_target_pairs={{0,4},{4,0},{8,12},{12,8},{1,5},{5,1},{9,13},{13,9},{2,6},{6,2},{1... | collective-permute-start | bytes 786440 | tf_op jit(solution)/shard_map/ppermute | solution.py:731
  346.1 41.0 %collective-permute-start.16 = (bf16[2,8,64,128]{3,2,1,0:T(8,128)(2,1)}, bf16[2,8,64,128]{3,2,1,0:T(8,128)(2,1)S(1)}, u32[]{:S(2)}, u32[]{:S(2)}) collective-permute-start(bf16[2,8,64,128]{3,2,1,0:T(8,128)(2,1)} %get-tuple-element.190), channel_id=1, source_target_pairs={{0,8},{4,12},{8,0},{12,4},{1,9},{5,13},{9,1},{13,5},{2,10},{6,14},... | collective-permute-start | bytes 786440 | tf_op jit(solution)/shard_map/ppermute | solution.py:731
  348.4 38.7 %collective-permute-start.17 = (bf16[2,8,64,128]{3,2,1,0:T(8,128)(2,1)}, bf16[2,8,64,128]{3,2,1,0:T(8,128)(2,1)S(1)}, u32[]{:S(2)}, u32[]{:S(2)}) collective-permute-start(bf16[2,8,64,128]{3,2,1,0:T(8,128)(2,1)} %get-tuple-element.191), channel_id=1, source_target_pairs={{0,12},{4,8},{8,4},{12,0},{1,13},{5,9},{9,5},{13,1},{2,14},{6,10},... | collective-permute-start | bytes 786440 | tf_op jit(solution)/shard_map/ppermute | solution.py:731
  349.4 23.4 %collective-permute-start.20 = (bf16[128,256]{1,0:T(8,128)(2,1)S(1)}, bf16[128,256]{1,0:T(8,128)(2,1)S(1)}, u32[]{:S(2)}, u32[]{:S(2)}) collective-permute-start(bf16[128,256]{1,0:T(8,128)(2,1)S(1)} %get-tuple-element.239), channel_id=1, source_target_pairs={{0,3},{1,2},{2,1},{3,0},{4,7},{5,6},{6,5},{7,4},{8,11},{9,10},{10,... | collective-permute-start | bytes 196616 | tf_op jit(solution)/shard_map/ppermute | solution.py:731
  357.2 20.0 %collective-permute-start.19 = (bf16[128,256]{1,0:T(8,128)(2,1)S(1)}, bf16[128,256]{1,0:T(8,128)(2,1)S(1)}, u32[]{:S(2)}, u32[]{:S(2)}) collective-permute-start(bf16[128,256]{1,0:T(8,128)(2,1)S(1)} %get-tuple-element.240), channel_id=1, source_target_pairs={{0,2},{1,3},{2,0},{3,1},{4,6},{5,7},{6,4},{7,5},{8,10},{9,11},{10,... | collective-permute-start | bytes 196616 | tf_op jit(solution)/shard_map/ppermute | solution.py:731
  391.3 21.3 %all-to-all-start.8 = ((bf16[32,64,128]{2,1,0:T(8,128)(2,1)}), bf16[32,64,128]{2,1,0:T(8,128)(2,1)S(1)}, u32[]{:S(2)}, u32[]{:S(2)}) async-start(bf16[32,64,128]{2,1,0:T(8,128)(2,1)} %bitcast.57), calls=%async_computation.8 | async-start | bytes 1048576 | tf_op jit(solution)/shard_map/all_to_all | solution.py:709
  417.1 31.7 %all-to-all-start.9 = ((bf16[128,8,896]{2,1,0:T(8,128)(2,1)}), bf16[128,8,896]{2,1,0:T(8,128)(2,1)S(1)}, u32[]{:S(2)}, u32[]{:S(2)}) async-start(bf16[128,8,896]{2,1,0:T(8,128)(2,1)} %bitcast.58), calls=%async_computation.9 | async-start | bytes 3670016 | tf_op jit(solution)/shard_map/all_to_all | solution.py:709
  427.8 26.4 %collective-permute-start.22 = (bf16[128,1024]{1,0:T(8,128)(2,1)}, bf16[128,1024]{1,0:T(8,128)(2,1)S(1)}, u32[]{:S(2)}, u32[]{:S(2)}) collective-permute-start(bf16[128,1024]{1,0:T(8,128)(2,1)} %get-tuple-element.218), channel_id=1, source_target_pairs={{0,1},{1,0},{2,3},{3,2},{4,5},{5,4},{6,7},{7,6},{8,9},{9,8},{10,11... | collective-permute-start | bytes 786440 | tf_op jit(solution)/shard_map/ppermute | solution.py:731
  428.9 25.3 %collective-permute-start.23 = (bf16[128,1024]{1,0:T(8,128)(2,1)}, bf16[128,1024]{1,0:T(8,128)(2,1)S(1)}, u32[]{:S(2)}, u32[]{:S(2)}) collective-permute-start(bf16[128,1024]{1,0:T(8,128)(2,1)} %get-tuple-element.219), channel_id=1, source_target_pairs={{0,2},{1,3},{2,0},{3,1},{4,6},{5,7},{6,4},{7,5},{8,10},{9,11},{10,... | collective-permute-start | bytes 786440 | tf_op jit(solution)/shard_map/ppermute | solution.py:731
  429.7 25.7 %collective-permute-start.24 = (bf16[128,1024]{1,0:T(8,128)(2,1)}, bf16[128,1024]{1,0:T(8,128)(2,1)S(1)}, u32[]{:S(2)}, u32[]{:S(2)}) collective-permute-start(bf16[128,1024]{1,0:T(8,128)(2,1)} %get-tuple-element.220), channel_id=1, source_target_pairs={{0,3},{1,2},{2,1},{3,0},{4,7},{5,6},{6,5},{7,4},{8,11},{9,10},{10,... | collective-permute-start | bytes 786440 | tf_op jit(solution)/shard_map/ppermute | solution.py:731
  (43 other events, 496.8 us)
Sparse Core Ops, SparseCore 0:
  84.2 74.4 all-gather.1
  259.1 68.0 reduce-scatter.1

commit v9 on v8

--- a/solution.py
+++ b/solution.py
@@ -199,9 +199,8 @@
 
 
 def kernel_heads(msg_ref, table_ref, kv_ref, q_ref):
-    out = jnp.zeros((512, 768), F32)
-    for f in range(4):
-        out = out + mm(msg_ref[:, f].reshape(512, 128), table_ref[f])
+    rows = jnp.concatenate([msg_ref[:, f].reshape(512, 128) for f in range(4)], axis=1)
+    out = mm(rows, table_ref[...].reshape(512, 768))
     pairs = out[:, 0:256].astype(BF)
     for half in range(2):
         block = pairs[:, 128 * half : 128 * half + 128]
@@ -603,8 +602,9 @@
             dkv = dkv + d_ref[half].reshape(512, 128).astype(F32)
         parts.append(unrotate(dkv, cos_ref[at, :], sin_ref[at, :]))
     whole = jnp.concatenate(parts, axis=1)
+    cut = mm(whole, table_ref[:, :, 0:256].reshape(512, 256), NT)
     for f in range(4):
-        rows = mm(whole, table_ref[f, :, 0:256], NT) + queries_ref[:, f].reshape(512, 128)
+        rows = cut[:, 128 * f : 128 * f + 128] + queries_ref[:, f].reshape(512, 128)
         msg_ref[:, f] = rows.astype(BF).reshape(8, 64, 128)
 
 

time: 467 us -> 462 us (0.989)
  starting transfers between devices: 101 us -> 91.7 us
  waiting for transfers between devices: 176 us -> 181 us
    all_to_all x10, waiting for transfers between devices: 143 us -> 150 us  [exchange(): return lax.all_to_all(value, axes, split_axis=0, concat_axis=0, tiled=True)]
    ppermute x16, starting transfers between devices: 20 us -> 13.9 us  [swap(): return lax.ppermute(value, axis, [(0, 1), (1, 0)])]
  transfers between devices with their start and end apart: 37 -> 37, of which waited for: 15 -> 16; matrix products, arithmetic and copies ran while one was open for 4% -> 4% of each run, Pallas kernels for 28% -> 28%
where the time goes in v9:
time: 462 us; the launch traced here: 461 us
  waiting for transfers between devices  181 us (39%)
  Pallas kernels  145 us (31%)
  starting transfers between devices  91.7 us (20%)
  local copies, waits for them, and re-layouts  19.3 us (4%)
  between operations  14.6 us (3%)
  other arithmetic  8.98 us (2%)
    all_to_all x10, waiting for transfers between devices, exchange(): return lax.all_to_all(value, axes, split_axis=0, concat_axis=0, tiled=True)  150 us
    all_to_all x10, starting transfers between devices, exchange(): return lax.all_to_all(value, axes, split_axis=0, concat_axis=0, tiled=True)  64.1 us
    pallas_call x1, Pallas kernels, on_device(): call(kernel_experts_after, (sds((32, 64, WIDTH), BF), sds((4, 384, WIDTH)...  23.6 us
    ppermute x9, waiting for transfers between devices, cross(): here.append(lax.ppermute(parts[r], axes, [(i, i ^ r) for i in range(4)]))  23.5 us
    pallas_call x1, Pallas kernels, on_device(): call(kernel_attend_back, (sds((2048, 128), F32),) + (sds((2, 8, 64, 128),...  22.9 us
    pallas_call x1, Pallas kernels, on_device(): call(kernel_attend, (sds((8, 2, 64, 128), BF), sds((8, 8, 256), F32), sds...  17.1 us
    ppermute x16, starting transfers between devices, swap(): return lax.ppermute(value, axis, [(0, 1), (1, 0)])  13.9 us
    ppermute x9, starting transfers between devices, cross(): here.append(lax.ppermute(parts[r], axes, [(i, i ^ r) for i in range(4)]))  13.6 us
  transfers between devices with their start and end apart: 37, of which 16 were waited for; matrix products, arithmetic and copies ran while one was open for 4% of the time, Pallas kernels for 28%

profile of v9, /device:TPU:1, one launch (start us, length us, event | category | flops | bytes accessed | tf_op | source)
XLA Modules:
  0.0 460.5 jit_solution(5541506224093045140)
XLA Ops:
  19.6 9.7 %all-to-all-start = ((bf16[128,8,896]{2,1,0:T(8,128)(2,1)}), bf16[128,8,896]{2,1,0:T(8,128)(2,1)S(1)}, u32[]{:S(2)}, u32[]{:S(2)}) async-start(bf16[128,8,896]{2,1,0:T(8,128)(2,1)} %bitcast.54), calls=%async_computation | async-start | bytes 3670016 | tf_op jit(solution)/shard_map/all_to_all | solution.py:709
  32.4 24.0 %all-to-all-done = bf16[128,8,896]{2,1,0:T(8,128)(2,1)S(1)} async-done(((bf16[128,8,896]{2,1,0:T(8,128)(2,1)}), bf16[128,8,896]{2,1,0:T(8,128)(2,1)S(1)}, u32[]{:S(2)}, u32[]{:S(2)}) %all-to-all-start) | async-done | bytes 1835040 | tf_op jit(solution)/shard_map/all_to_all | solution.py:709
  57.7 4.6 shard_map.198
  62.3 6.0 %all-to-all-start.1 = ((bf16[32,64,128]{2,1,0:T(8,128)(2,1)}), bf16[32,64,128]{2,1,0:T(8,128)(2,1)S(1)}, u32[]{:S(2)}, u32[]{:S(2)}) async-start(bf16[32,64,128]{2,1,0:T(8,128)(2,1)} %get-tuple-element.129), calls=%async_computation.1 | async-start | bytes 1048576 | tf_op jit(solution)/shard_map/all_to_all | solution.py:709
  72.5 7.4 %all-to-all-done.1 = bf16[32,64,128]{2,1,0:T(8,128)(2,1)S(1)} async-done(((bf16[32,64,128]{2,1,0:T(8,128)(2,1)}), bf16[32,64,128]{2,1,0:T(8,128)(2,1)S(1)}, u32[]{:S(2)}, u32[]{:S(2)}) %all-to-all-start.1) | async-done | bytes 524320 | tf_op jit(solution)/shard_map/all_to_all | solution.py:709
  96.1 13.0 %all-to-all-done.2 = bf16[4,1024,128]{2,1,0:T(8,128)(2,1)S(1)} async-done(((bf16[4,1024,128]{2,1,0:T(8,128)(2,1)}), bf16[4,1024,128]{2,1,0:T(8,128)(2,1)S(1)}, u32[]{:S(2)}, u32[]{:S(2)}) %all-to-all-start.2) | async-done | bytes 1048608 | tf_op jit(solution)/shard_map/all_to_all | solution.py:709
  110.6 17.1 %shard_map.200 = (bf16[8,2,64,128]{3,2,1,0:T(8,128)(2,1)}, f32[8,8,256]{2,1,0:T(8,128)}, f32[2048,128]{1,0:T(8,128)}, bf16[4096,128]{1,0:T(8,128)(2,1)}, bf16[128,4096]{1,0:T(8,128)(2,1)}) custom-call(s32[1]{0:T(128)} %bitcast.mine_ref, bf16[4,2,8,64,128]{4,3,2,1,0:T(8,128)(2,1)} %bitcast.64, bf16[2048,128]{1,0:T(8,128)(2,1)} %bitcast.74), custom_call_target="tpu_custom_call" | custom-call | flops 10000000000 | bytes 5000000 | tf_op jit(solution)/shard_map/pallas_call | solution.py:853
  135.7 6.1 %all-to-all-done.3.o_ref.o0_ref = bf16[8,2,64,128]{3,2,1,0:T(8,128)(2,1)S(1)} async-done(((bf16[8,2,64,128]{3,2,1,0:T(8,128)(2,1)}), bf16[8,2,64,128]{3,2,1,0:T(8,128)(2,1)S(1)}, u32[]{:S(2)}, u32[]{:S(2)}) %all-to-all-start.3) | async-done | bytes 262176 | tf_op jit(solution)/shard_map/all_to_all | solution.py:709
  142.5 5.3 %shard_map.202 = (bf16[32,64,1024]{2,1,0:T(8,128)(2,1)}, f32[128,1024]{1,0:T(8,128)}) custom-call(s32[1]{0:T(128)} %bitcast.1.part_ref, bf16[8,2,64,128]{3,2,1,0:T(8,128)(2,1)} %copy-done.7, bf16[512,256]{1,0:T(8,128)(2,1)} %copy-done.6, bf16[512,256]{1,0:T(8,128)(2,1)} %copy-done.15, bf16[512,256]{1,0:T(8,128)(2,1)} %copy-done.14, ...), custom_call_target="tpu_custom_call" | custom-call | flops 900000000 | bytes 8000000 | tf_op jit(solution)/shard_map/pallas_call | solution.py:878
  148.7 5.5 %all-to-all-start.4 = ((bf16[32,64,1024]{2,1,0:T(8,128)(2,1)}), bf16[32,64,1024]{2,1,0:T(8,128)(2,1)}, u32[]{:S(2)}, u32[]{:S(2)}) async-start(bf16[32,64,1024]{2,1,0:T(8,128)(2,1)} %get-tuple-element.163), calls=%async_computation.4 | async-start | bytes 8388608 | tf_op jit(solution)/shard_map/all_to_all | solution.py:709
  158.9 12.5 %shard_map.203 = (bf16[32,64,1024]{2,1,0:T(8,128)(2,1)}, f32[2048,512]{1,0:T(8,128)}, bf16[512,1024]{1,0:T(8,128)(2,1)}, bf16[1024,1024]{1,0:T(8,128)(2,1)}) custom-call(s32[1]{0:T(128)} %bitcast.1.part_ref, bf16[4,4,2,128,1024]{4,3,2,1,0:T(8,128)(2,1)} %bitcast.73, bf16[32,8,128]{2,1,0:T(8,128)(2,1)} %dynamic-slice_bitcast_fusion.parts_ref, ...), custom_call_target="tpu_custom_call" | custom-call | flops 6000000000 | bytes 20000000 | tf_op jit(solution)/shard_map/pallas_call | solution.py:896
  171.5 45.3 %all-to-all-done.4.h_ref = bf16[32,64,1024]{2,1,0:T(8,128)(2,1)} async-done(((bf16[32,64,1024]{2,1,0:T(8,128)(2,1)}), bf16[32,64,1024]{2,1,0:T(8,128)(2,1)}, u32[]{:S(2)}, u32[]{:S(2)}) %all-to-all-start.4) | async-done | bytes 4194336 | tf_op jit(solution)/shard_map/all_to_all | solution.py:709
  216.8 13.2 %shard_map.204 = (bf16[2048,512]{1,0:T(8,128)(2,1)}, bf16[2048,1024]{1,0:T(8,128)(2,1)}, bf16[32,64,1024]{2,1,0:T(8,128)(2,1)}) custom-call(bf16[32,64,1024]{2,1,0:T(8,128)(2,1)} %all-to-all-done.4.h_ref, bf16[1024,1024]{1,0:T(8,128)(2,1)} %get-tuple-element.172.gu_ref, f32[2048,512]{1,0:T(8,128)} %get-tuple-element.173.dact_ref), custom_call_target="tpu_custom_call" | custom-call | flops 8999999488 | bytes 20000000 | tf_op jit(solution)/shard_map/pallas_call | solution.py:922
  230.0 7.0 %all-to-all-start.5 = ((bf16[32,64,1024]{2,1,0:T(8,128)(2,1)}), bf16[32,64,1024]{2,1,0:T(8,128)(2,1)}, u32[]{:S(2)}, u32[]{:S(2)}) async-start(bf16[32,64,1024]{2,1,0:T(8,128)(2,1)} %get-tuple-element.174), calls=%async_computation.5 | async-start | bytes 8388608 | tf_op jit(solution)/shard_map/all_to_all | solution.py:709
  237.1 23.6 %shard_map.205 = (bf16[32,64,1024]{2,1,0:T(8,128)(2,1)}, bf16[4,384,1024]{2,1,0:T(8,128)(2,1)}) custom-call(bf16[32,64,1024]{2,1,0:T(8,128)(2,1)} %all-to-all-done.4.h_ref, bf16[2048,512]{1,0:T(8,128)(2,1)} %get-tuple-element.175.act_ref, bf16[32,64,1024]{2,1,0:T(8,128)(2,1)} %get-tuple-element.176.dys_ref, bf16[2048,1024]{1,0:T(8,128)(2,1)} %get-tuple-element.177.dboth_ref, ...), custom_call_target="tpu_custom_call" | custom-call | flops 8999999488 | bytes 20000000 | tf_op jit(solution)/shard_map/pallas_call | solution.py:938
  263.3 29.4 %all-to-all-done.5.dxs_ref = bf16[32,64,1024]{2,1,0:T(8,128)(2,1)} async-done(((bf16[32,64,1024]{2,1,0:T(8,128)(2,1)}), bf16[32,64,1024]{2,1,0:T(8,128)(2,1)}, u32[]{:S(2)}, u32[]{:S(2)}) %all-to-all-start.5) | async-done | bytes 4194336 | tf_op jit(solution)/shard_map/all_to_all | solution.py:709
  292.7 5.7 %shard_map.206 = (f32[128,1024]{1,0:T(8,128)}, bf16[4,128,256]{2,1,0:T(8,128)(2,1)}, bf16[8,2,64,128]{3,2,1,0:T(8,128)(2,1)}, f32[8,1024]{1,0:T(8,128)}) custom-call(s32[1]{0:T(128)} %bitcast.1.part_ref, bf16[32,64,1024]{2,1,0:T(8,128)(2,1)} %all-to-all-done.5.dxs_ref, bf16[128,2048]{1,0:T(8,128)(2,1)} %get-tuple-element.182.pick_ref, ...), custom_call_target="tpu_custom_call" | custom-call | flops 900000000 | bytes 8000000 | tf_op jit(solution)/shard_map/pallas_call | solution.py:954
  298.5 8.4 %all-to-all-start.6 = ((bf16[8,2,64,128]{3,2,1,0:T(8,128)(2,1)}), bf16[8,2,64,128]{3,2,1,0:T(8,128)(2,1)S(1)}, u32[]{:S(2)}, u32[]{:S(2)}) async-start(bf16[8,2,64,128]{3,2,1,0:T(8,128)(2,1)} %get-tuple-element.183), calls=%async_computation.6 | async-start | bytes 524288 | tf_op jit(solution)/shard_map/all_to_all | solution.py:709
  306.9 7.3 %all-to-all-done.6.grad_ref = bf16[8,2,64,128]{3,2,1,0:T(8,128)(2,1)S(1)} async-done(((bf16[8,2,64,128]{3,2,1,0:T(8,128)(2,1)}), bf16[8,2,64,128]{3,2,1,0:T(8,128)(2,1)S(1)}, u32[]{:S(2)}, u32[]{:S(2)}) %all-to-all-start.6) | async-done | bytes 262176 | tf_op jit(solution)/shard_map/all_to_all | solution.py:709
  314.9 4.9 %all-to-all-start.7 = ((bf16[32,64,1024]{2,1,0:T(8,128)(2,1)}), bf16[32,64,1024]{2,1,0:T(8,128)(2,1)}, u32[]{:S(2)}, u32[]{:S(2)}) async-start(bf16[32,64,1024]{2,1,0:T(8,128)(2,1)} %get-tuple-element.192), calls=%async_computation.7 | async-start | bytes 8388608 | tf_op jit(solution)/shard_map/all_to_all | solution.py:709
  319.8 22.9 %shard_map.207 = (f32[2048,128]{1,0:T(8,128)}, bf16[2,8,64,128]{3,2,1,0:T(8,128)(2,1)}, bf16[2,8,64,128]{3,2,1,0:T(8,128)(2,1)}, bf16[2,8,64,128]{3,2,1,0:T(8,128)(2,1)}, bf16[2,8,64,128]{3,2,1,0:T(8,128)(2,1)}) custom-call(s32[1]{0:T(128)} %bitcast.mine_ref, bf16[4096,128]{1,0:T(8,128)(2,1)} %get-tuple-element.135.keys_ref, ...), custom_call_target="tpu_custom_call" | custom-call | flops 20000000000 | bytes 7000000 | tf_op jit(solution)/shard_map/pallas_call | solution.py:985
  347.3 4.6 %collective-permute-start.20 = (bf16[128,256]{1,0:T(8,128)(2,1)S(1)}, bf16[128,256]{1,0:T(8,128)(2,1)S(1)}, u32[]{:S(2)}, u32[]{:S(2)}) collective-permute-start(bf16[128,256]{1,0:T(8,128)(2,1)S(1)} %get-tuple-element.239), channel_id=1, source_target_pairs={{0,3},{1,2},{2,1},{3,0},{4,7},{5,6},{6,5},{7,4},{8,11},{9,10},{10,... | collective-permute-start | bytes 196616 | tf_op jit(solution)/shard_map/ppermute | solution.py:731
  353.9 10.6 %collective-permute-done.20.da3_ref = bf16[128,256]{1,0:T(8,128)(2,1)S(1)} collective-permute-done((bf16[128,256]{1,0:T(8,128)(2,1)S(1)}, bf16[128,256]{1,0:T(8,128)(2,1)S(1)}, u32[]{:S(2)}, u32[]{:S(2)}) %collective-permute-start.20) | collective-permute-done | bytes 65568 | tf_op jit(solution)/shard_map/ppermute | solution.py:731
  364.9 4.3 shard_map.208
  370.5 10.4 %collective-permute-done.16.d2_ref = bf16[2,8,64,128]{3,2,1,0:T(8,128)(2,1)S(1)} collective-permute-done((bf16[2,8,64,128]{3,2,1,0:T(8,128)(2,1)}, bf16[2,8,64,128]{3,2,1,0:T(8,128)(2,1)S(1)}, u32[]{:S(2)}, u32[]{:S(2)}) %collective-permute-start.16) | collective-permute-done | bytes 262176 | tf_op jit(solution)/shard_map/ppermute | solution.py:731
  384.9 10.4 %all-to-all-start.8 = ((bf16[32,64,128]{2,1,0:T(8,128)(2,1)}), bf16[32,64,128]{2,1,0:T(8,128)(2,1)S(1)}, u32[]{:S(2)}, u32[]{:S(2)}) async-start(bf16[32,64,128]{2,1,0:T(8,128)(2,1)} %bitcast.57), calls=%async_computation.8 | async-start | bytes 1048576 | tf_op jit(solution)/shard_map/all_to_all | solution.py:709
  397.6 4.4 shard_map.211.rest_ref
  402.0 4.9 %all-to-all-done.8.msg_ref = bf16[32,64,128]{2,1,0:T(8,128)(2,1)S(1)} async-done(((bf16[32,64,128]{2,1,0:T(8,128)(2,1)}), bf16[32,64,128]{2,1,0:T(8,128)(2,1)S(1)}, u32[]{:S(2)}, u32[]{:S(2)}) %all-to-all-start.8) | async-done | bytes 524320 | tf_op jit(solution)/shard_map/all_to_all | solution.py:709
  411.4 5.2 %all-to-all-start.9 = ((bf16[128,8,896]{2,1,0:T(8,128)(2,1)}), bf16[128,8,896]{2,1,0:T(8,128)(2,1)S(1)}, u32[]{:S(2)}, u32[]{:S(2)}) async-start(bf16[128,8,896]{2,1,0:T(8,128)(2,1)} %bitcast.58), calls=%async_computation.9 | async-start | bytes 3670016 | tf_op jit(solution)/shard_map/all_to_all | solution.py:709
  419.0 3.9 shard_map.213
  426.4 5.0 %shard_map.209 = bf16[128,1024]{1,0:T(8,128)(2,1)} custom-call(bf16[32,64,1024]{2,1,0:T(8,128)(2,1)} %all-to-all-done.7.ys_ref, bf16[128,2048]{1,0:T(8,128)(2,1)} %get-tuple-element.200.high_ref, bf16[128,2048]{1,0:T(8,128)(2,1)} %get-tuple-element.201.rest_ref, f32[128,1024]{1,0:T(8,128)} %get-tuple-element.166.mid_ref), custom_call_target="tpu_custom_call" | custom-call | flops 1000000000 | bytes 5000000 | tf_op jit(solution)/shard_map/pallas_call | solution.py:1019
  431.5 12.3 %all-to-all-done.9 = bf16[128,8,896]{2,1,0:T(8,128)(2,1)S(1)} async-done(((bf16[128,8,896]{2,1,0:T(8,128)(2,1)}), bf16[128,8,896]{2,1,0:T(8,128)(2,1)S(1)}, u32[]{:S(2)}, u32[]{:S(2)}) %all-to-all-start.9) | async-done | bytes 1835040 | tf_op jit(solution)/shard_map/all_to_all | solution.py:709
  (172 shorter events, 90.9 us)
Async XLA Ops:
  7.2 11.6 %collective-permute-start.1 = (bf16[128,1024]{1,0:T(8,128)(2,1)}, bf16[128,1024]{1,0:T(8,128)(2,1)S(1)}, u32[]{:S(2)}, u32[]{:S(2)}) collective-permute-start(bf16[128,1024]{1,0:T(8,128)(2,1)} %bitcast.59), channel_id=1, source_target_pairs={{0,2},{2,0},{1,3},{3,1},{4,6},{6,4},{5,7},{7,5},{8,10},{10,8},{9,1... | collective-permute-start | bytes 786440 | tf_op jit(solution)/shard_map/ppermute | solution.py:721
  19.6 36.8 %all-to-all-start = ((bf16[128,8,896]{2,1,0:T(8,128)(2,1)}), bf16[128,8,896]{2,1,0:T(8,128)(2,1)S(1)}, u32[]{:S(2)}, u32[]{:S(2)}) async-start(bf16[128,8,896]{2,1,0:T(8,128)(2,1)} %bitcast.54), calls=%async_computation | async-start | bytes 3670016 | tf_op jit(solution)/shard_map/all_to_all | solution.py:709
  29.3 27.6 %collective-permute-start.2 = (bf16[128,1024]{1,0:T(8,128)(2,1)S(1)}, bf16[128,1024]{1,0:T(8,128)(2,1)S(1)}, u32[]{:S(2)}, u32[]{:S(2)}) collective-permute-start(bf16[128,1024]{1,0:T(8,128)(2,1)S(1)} %collective-permute-done.1.x2_ref), channel_id=1, source_target_pairs={{0,1},{1,0},{2,3},{3,2},{4,5},{5,4},{6,7},{7,6},{8,9},{9,8},{10,11... | collective-permute-start | bytes 786440 | tf_op jit(solution)/shard_map/ppermute | solution.py:721
  56.4 15.2 %collective-permute-start.12 = (bf16[128,1024]{1,0:T(8,128)(2,1)S(1)}, bf16[128,1024]{1,0:T(8,128)(2,1)S(1)}, u32[]{:S(2)}, u32[]{:S(2)}) collective-permute-start(bf16[128,1024]{1,0:T(8,128)(2,1)S(1)} %bitcast.66), channel_id=1, source_target_pairs={{0,16},{16,0},{1,17},{17,1},{2,18},{18,2},{3,19},{19,3},{4,20},{20... | collective-permute-start | bytes 786440 | tf_op jit(solution)/shard_map/ppermute | solution.py:721
  62.3 17.7 %all-to-all-start.1 = ((bf16[32,64,128]{2,1,0:T(8,128)(2,1)}), bf16[32,64,128]{2,1,0:T(8,128)(2,1)S(1)}, u32[]{:S(2)}, u32[]{:S(2)}) async-start(bf16[32,64,128]{2,1,0:T(8,128)(2,1)} %get-tuple-element.129), calls=%async_computation.1 | async-start | bytes 1048576 | tf_op jit(solution)/shard_map/all_to_all | solution.py:709
  68.3 90.6 %all-gather.2.cloned.1.call-start = ((), (), s32[]{:S(2)}) async-start(), calls=%async_computation.11 | async-start | bytes 8912896 | tf_op jit(solution)/shard_map/all_gather | solution.py:713
  69.5 14.0 %collective-permute-start.4 = (bf16[512,256]{1,0:T(8,128)(2,1)S(1)}, bf16[512,256]{1,0:T(8,128)(2,1)S(1)}, u32[]{:S(2)}, u32[]{:S(2)}) collective-permute-start(bf16[512,256]{1,0:T(8,128)(2,1)S(1)} %get-tuple-element.147.u0_ref), channel_id=1, source_target_pairs={{0,2},{2,0},{1,3},{3,1},{4,6},{6,4},{5,7},{7,5},{8,10},{10,8},{9,1... | collective-permute-start | bytes 786440 | tf_op jit(solution)/shard_map/ppermute | solution.py:721
  71.0 12.6 %collective-permute-start.3 = (bf16[512,256]{1,0:T(8,128)(2,1)S(1)}, bf16[512,256]{1,0:T(8,128)(2,1)S(1)}, u32[]{:S(2)}, u32[]{:S(2)}) collective-permute-start(bf16[512,256]{1,0:T(8,128)(2,1)S(1)} %get-tuple-element.147.u0_ref), channel_id=1, source_target_pairs={{0,1},{1,0},{2,3},{3,2},{4,5},{5,4},{6,7},{7,6},{8,9},{9,8},{10,11... | collective-permute-start | bytes 786440 | tf_op jit(solution)/shard_map/ppermute | solution.py:721
  84.0 25.2 %all-to-all-start.2 = ((bf16[4,1024,128]{2,1,0:T(8,128)(2,1)}), bf16[4,1024,128]{2,1,0:T(8,128)(2,1)S(1)}, u32[]{:S(2)}, u32[]{:S(2)}) async-start(bf16[4,1024,128]{2,1,0:T(8,128)(2,1)} %get-tuple-element.131), calls=%async_computation.2 | async-start | bytes 2097152 | tf_op jit(solution)/shard_map/all_to_all | solution.py:709
  91.6 36.2 %collective-permute-start.10 = (bf16[384,1024]{1,0:T(8,128)(2,1)S(1)}, bf16[384,1024]{1,0:T(8,128)(2,1)}, u32[]{:S(2)}, u32[]{:S(2)}) collective-permute-start(bf16[384,1024]{1,0:T(8,128)(2,1)S(1)} %pad_maximum_fusion.w0_ref), channel_id=1, source_target_pairs={{0,2},{2,0},{1,3},{3,1},{4,6},{6,4},{5,7},{7,5},{8,10},{10,8},{9,1... | collective-permute-start | bytes 2359304 | tf_op jit(solution)/shard_map/ppermute | solution.py:721
  92.6 35.1 %collective-permute-start.9 = (bf16[384,1024]{1,0:T(8,128)(2,1)S(1)}, bf16[384,1024]{1,0:T(8,128)(2,1)}, u32[]{:S(2)}, u32[]{:S(2)}) collective-permute-start(bf16[384,1024]{1,0:T(8,128)(2,1)S(1)} %pad_maximum_fusion.w0_ref), channel_id=1, source_target_pairs={{0,1},{1,0},{2,3},{3,2},{4,5},{5,4},{6,7},{7,6},{8,9},{9,8},{10,11... | collective-permute-start | bytes 2359304 | tf_op jit(solution)/shard_map/ppermute | solution.py:721
  109.1 18.7 %collective-permute-start.7 = (bf16[512,256]{1,0:T(8,128)(2,1)S(1)}, bf16[512,256]{1,0:T(8,128)(2,1)S(1)}, u32[]{:S(2)}, u32[]{:S(2)}) collective-permute-start(bf16[512,256]{1,0:T(8,128)(2,1)S(1)} %collective-permute-done.4.u2_ref), channel_id=1, source_target_pairs={{0,1},{1,0},{2,3},{3,2},{4,5},{5,4},{6,7},{7,6},{8,9},{9,8},{10,11... | collective-permute-start | bytes 786440 | tf_op jit(solution)/shard_map/ppermute | solution.py:721
  110.4 17.4 %collective-permute-start.8 = (bf16[512,256]{1,0:T(8,128)(2,1)S(1)}, bf16[512,256]{1,0:T(8,128)(2,1)S(1)}, u32[]{:S(2)}, u32[]{:S(2)}) collective-permute-start(bf16[512,256]{1,0:T(8,128)(2,1)S(1)} %collective-permute-done.6.l2_ref), channel_id=1, source_target_pairs={{0,1},{1,0},{2,3},{3,2},{4,5},{5,4},{6,7},{7,6},{8,9},{9,8},{10,11... | collective-permute-start | bytes 786440 | tf_op jit(solution)/shard_map/ppermute | solution.py:721
  127.8 19.9 %collective-permute-start.11 = (bf16[384,1024]{1,0:T(8,128)(2,1)}, bf16[384,1024]{1,0:T(8,128)(2,1)S(1)}, u32[]{:S(2)}, u32[]{:S(2)}) collective-permute-start(bf16[384,1024]{1,0:T(8,128)(2,1)} %collective-permute-done.10.w2_ref), channel_id=1, source_target_pairs={{0,1},{1,0},{2,3},{3,2},{4,5},{5,4},{6,7},{7,6},{8,9},{9,8},{10,11... | collective-permute-start | bytes 2359304 | tf_op jit(solution)/shard_map/ppermute | solution.py:721
  128.6 13.2 %all-to-all-start.3 = ((bf16[8,2,64,128]{3,2,1,0:T(8,128)(2,1)}), bf16[8,2,64,128]{3,2,1,0:T(8,128)(2,1)S(1)}, u32[]{:S(2)}, u32[]{:S(2)}) async-start(bf16[8,2,64,128]{3,2,1,0:T(8,128)(2,1)} %get-tuple-element.146), calls=%async_computation.3 | async-start | bytes 524288 | tf_op jit(solution)/shard_map/all_to_all | solution.py:709
  148.7 68.2 %all-to-all-start.4 = ((bf16[32,64,1024]{2,1,0:T(8,128)(2,1)}), bf16[32,64,1024]{2,1,0:T(8,128)(2,1)}, u32[]{:S(2)}, u32[]{:S(2)}) async-start(bf16[32,64,1024]{2,1,0:T(8,128)(2,1)} %get-tuple-element.163), calls=%async_computation.4 | async-start | bytes 8388608 | tf_op jit(solution)/shard_map/all_to_all | solution.py:709
  230.0 62.7 %all-to-all-start.5 = ((bf16[32,64,1024]{2,1,0:T(8,128)(2,1)}), bf16[32,64,1024]{2,1,0:T(8,128)(2,1)}, u32[]{:S(2)}, u32[]{:S(2)}) async-start(bf16[32,64,1024]{2,1,0:T(8,128)(2,1)} %get-tuple-element.174), calls=%async_computation.5 | async-start | bytes 8388608 | tf_op jit(solution)/shard_map/all_to_all | solution.py:709
  237.0 179.7 %reduce-scatter.2.cloned.1.call-start = ((), (), s32[]{:S(2)}) async-start(), calls=%async_computation.12 | async-start | bytes 3932160 | tf_op jit(solution)/shard_map/reduce_scatter | solution.py:949
  261.6 45.3 %collective-permute-start.14 = (bf16[8,2,64,128]{3,2,1,0:T(8,128)(2,1)S(1)}, bf16[8,2,64,128]{3,2,1,0:T(8,128)(2,1)S(1)}, u32[]{:S(2)}, u32[]{:S(2)}) collective-permute-start(bf16[8,2,64,128]{3,2,1,0:T(8,128)(2,1)S(1)} %copy-done.8), channel_id=1, source_target_pairs={{0,2},{2,0},{1,3},{3,1},{4,6},{6,4},{5,7},{7,5},{8,10},{10,8},{9,1... | collective-permute-start | bytes 786440 | tf_op jit(solution)/shard_map/ppermute | solution.py:721
  261.6 45.3 %collective-permute-start.13 = (bf16[8,2,64,128]{3,2,1,0:T(8,128)(2,1)S(1)}, bf16[8,2,64,128]{3,2,1,0:T(8,128)(2,1)S(1)}, u32[]{:S(2)}, u32[]{:S(2)}) collective-permute-start(bf16[8,2,64,128]{3,2,1,0:T(8,128)(2,1)S(1)} %copy-done.8), channel_id=1, source_target_pairs={{0,1},{1,0},{2,3},{3,2},{4,5},{5,4},{6,7},{7,6},{8,9},{9,8},{10,11... | collective-permute-start | bytes 786440 | tf_op jit(solution)/shard_map/ppermute | solution.py:721
  298.5 15.8 %all-to-all-start.6 = ((bf16[8,2,64,128]{3,2,1,0:T(8,128)(2,1)}), bf16[8,2,64,128]{3,2,1,0:T(8,128)(2,1)S(1)}, u32[]{:S(2)}, u32[]{:S(2)}) async-start(bf16[8,2,64,128]{3,2,1,0:T(8,128)(2,1)} %get-tuple-element.183), calls=%async_computation.6 | async-start | bytes 524288 | tf_op jit(solution)/shard_map/all_to_all | solution.py:709
  314.9 65.9 %all-to-all-start.7 = ((bf16[32,64,1024]{2,1,0:T(8,128)(2,1)}), bf16[32,64,1024]{2,1,0:T(8,128)(2,1)}, u32[]{:S(2)}, u32[]{:S(2)}) async-start(bf16[32,64,1024]{2,1,0:T(8,128)(2,1)} %get-tuple-element.192), calls=%async_computation.7 | async-start | bytes 8388608 | tf_op jit(solution)/shard_map/all_to_all | solution.py:709
  342.7 27.7 %collective-permute-start.15 = (bf16[2,8,64,128]{3,2,1,0:T(8,128)(2,1)}, bf16[2,8,64,128]{3,2,1,0:T(8,128)(2,1)S(1)}, u32[]{:S(2)}, u32[]{:S(2)}) collective-permute-start(bf16[2,8,64,128]{3,2,1,0:T(8,128)(2,1)} %get-tuple-element.189), channel_id=1, source_target_pairs={{0,4},{4,0},{8,12},{12,8},{1,5},{5,1},{9,13},{13,9},{2,6},{6,2},{1... | collective-permute-start | bytes 786440 | tf_op jit(solution)/shard_map/ppermute | solution.py:731
  343.9 37.0 %collective-permute-start.16 = (bf16[2,8,64,128]{3,2,1,0:T(8,128)(2,1)}, bf16[2,8,64,128]{3,2,1,0:T(8,128)(2,1)S(1)}, u32[]{:S(2)}, u32[]{:S(2)}) collective-permute-start(bf16[2,8,64,128]{3,2,1,0:T(8,128)(2,1)} %get-tuple-element.190), channel_id=1, source_target_pairs={{0,8},{4,12},{8,0},{12,4},{1,9},{5,13},{9,1},{13,5},{2,10},{6,14},... | collective-permute-start | bytes 786440 | tf_op jit(solution)/shard_map/ppermute | solution.py:731
  346.3 34.6 %collective-permute-start.17 = (bf16[2,8,64,128]{3,2,1,0:T(8,128)(2,1)}, bf16[2,8,64,128]{3,2,1,0:T(8,128)(2,1)S(1)}, u32[]{:S(2)}, u32[]{:S(2)}) collective-permute-start(bf16[2,8,64,128]{3,2,1,0:T(8,128)(2,1)} %get-tuple-element.191), channel_id=1, source_target_pairs={{0,12},{4,8},{8,4},{12,0},{1,13},{5,9},{9,5},{13,1},{2,14},{6,10},... | collective-permute-start | bytes 786440 | tf_op jit(solution)/shard_map/ppermute | solution.py:731
  347.3 17.2 %collective-permute-start.20 = (bf16[128,256]{1,0:T(8,128)(2,1)S(1)}, bf16[128,256]{1,0:T(8,128)(2,1)S(1)}, u32[]{:S(2)}, u32[]{:S(2)}) collective-permute-start(bf16[128,256]{1,0:T(8,128)(2,1)S(1)} %get-tuple-element.239), channel_id=1, source_target_pairs={{0,3},{1,2},{2,1},{3,0},{4,7},{5,6},{6,5},{7,4},{8,11},{9,10},{10,... | collective-permute-start | bytes 196616 | tf_op jit(solution)/shard_map/ppermute | solution.py:731
  352.0 17.2 %collective-permute-start.19 = (bf16[128,256]{1,0:T(8,128)(2,1)S(1)}, bf16[128,256]{1,0:T(8,128)(2,1)S(1)}, u32[]{:S(2)}, u32[]{:S(2)}) collective-permute-start(bf16[128,256]{1,0:T(8,128)(2,1)S(1)} %get-tuple-element.240), channel_id=1, source_target_pairs={{0,2},{1,3},{2,0},{3,1},{4,6},{5,7},{6,4},{7,5},{8,10},{9,11},{10,... | collective-permute-start | bytes 196616 | tf_op jit(solution)/shard_map/ppermute | solution.py:731
  384.9 22.0 %all-to-all-start.8 = ((bf16[32,64,128]{2,1,0:T(8,128)(2,1)}), bf16[32,64,128]{2,1,0:T(8,128)(2,1)S(1)}, u32[]{:S(2)}, u32[]{:S(2)}) async-start(bf16[32,64,128]{2,1,0:T(8,128)(2,1)} %bitcast.57), calls=%async_computation.8 | async-start | bytes 1048576 | tf_op jit(solution)/shard_map/all_to_all | solution.py:709
  411.4 32.4 %all-to-all-start.9 = ((bf16[128,8,896]{2,1,0:T(8,128)(2,1)}), bf16[128,8,896]{2,1,0:T(8,128)(2,1)S(1)}, u32[]{:S(2)}, u32[]{:S(2)}) async-start(bf16[128,8,896]{2,1,0:T(8,128)(2,1)} %bitcast.58), calls=%async_computation.9 | async-start | bytes 3670016 | tf_op jit(solution)/shard_map/all_to_all | solution.py:709
  422.9 26.4 %collective-permute-start.22 = (bf16[128,1024]{1,0:T(8,128)(2,1)}, bf16[128,1024]{1,0:T(8,128)(2,1)S(1)}, u32[]{:S(2)}, u32[]{:S(2)}) collective-permute-start(bf16[128,1024]{1,0:T(8,128)(2,1)} %get-tuple-element.218), channel_id=1, source_target_pairs={{0,1},{1,0},{2,3},{3,2},{4,5},{5,4},{6,7},{7,6},{8,9},{9,8},{10,11... | collective-permute-start | bytes 786440 | tf_op jit(solution)/shard_map/ppermute | solution.py:731
  423.9 25.3 %collective-permute-start.23 = (bf16[128,1024]{1,0:T(8,128)(2,1)}, bf16[128,1024]{1,0:T(8,128)(2,1)S(1)}, u32[]{:S(2)}, u32[]{:S(2)}) collective-permute-start(bf16[128,1024]{1,0:T(8,128)(2,1)} %get-tuple-element.219), channel_id=1, source_target_pairs={{0,2},{1,3},{2,0},{3,1},{4,6},{5,7},{6,4},{7,5},{8,10},{9,11},{10,... | collective-permute-start | bytes 786440 | tf_op jit(solution)/shard_map/ppermute | solution.py:731
  424.8 25.7 %collective-permute-start.24 = (bf16[128,1024]{1,0:T(8,128)(2,1)}, bf16[128,1024]{1,0:T(8,128)(2,1)S(1)}, u32[]{:S(2)}, u32[]{:S(2)}) collective-permute-start(bf16[128,1024]{1,0:T(8,128)(2,1)} %get-tuple-element.220), channel_id=1, source_target_pairs={{0,3},{1,2},{2,1},{3,0},{4,7},{5,6},{6,5},{7,4},{8,11},{9,10},{10,... | collective-permute-start | bytes 786440 | tf_op jit(solution)/shard_map/ppermute | solution.py:731
  (43 other events, 492.4 us)
Sparse Core Ops, SparseCore 0:
  83.7 75.2 all-gather.1
  260.8 61.4 reduce-scatter.1
